TPU v7x, 32 devices: a whole 2x2x4 slice. The times are simulated.
32 devices in a mesh: seq: 2 (over core), mp: 4 (over y, x), row: 4 (over z).
Axes of the slice: x: 2, y: 2, z: 4, core: 2. Of those that a mesh axis runs over, the one named last changes fastest.
Arguments:
- block_in: bfloat16 [4, 2048, 2048], P('row', 'seq'), may hold values from -6 to 6
- doc_lengths: int32 [4, 3], P('row'), may hold values from 1 to 1856, as said below
- attn_gain: float32 [2048], replicated, may hold values from 0.5 to 1.5
- qkv_weight: bfloat16 [3, 2048, 2048], P(None, ('seq', 'row'), 'mp'), may hold values from -0.125 to 0.125
- conv_weight: float32 [3, 4, 2048], P(None, None, 'mp'), may hold values from -3 to 3
- beta_weight: bfloat16 [16, 2048], P('mp', ('seq', 'row')), may hold values from -0.125 to 0.125
- out_gain: float32 [128], replicated, may hold values from 0.5 to 1.5
- out_weight: bfloat16 [2048, 2048], P('mp', ('seq', 'row')), may hold values from -0.125 to 0.125
- ffn_gain: float32 [2048], replicated, may hold values from 0.5 to 1.5
- gateup_weight: bfloat16 [2, 2048, 5632], P(None, ('seq', 'row'), 'mp'), may hold values from -0.125 to 0.125
- down_weight: bfloat16 [5632, 2048], P('mp', ('seq', 'row')), may hold values from -0.078125 to 0.078125
- cotangent: bfloat16 [4, 2048, 2048], P('row', 'seq'), may hold values from -6 to 6
Outputs:
- block_out: bfloat16 [4, 2048, 2048], P('row', 'seq')
- grad_in: float32 [4, 2048, 2048], P('row', 'seq')
- grad_attn_gain: float32 [2048], replicated
- grad_qkv: float32 [3, 2048, 2048], P(None, ('seq', 'row'), 'mp')
- grad_conv: float32 [3, 4, 2048], P(None, None, 'mp')
- grad_beta: float32 [16, 2048], P('mp', ('seq', 'row'))
- grad_out_gain: float32 [128], replicated
- grad_out_weight: float32 [2048, 2048], P('mp', ('seq', 'row'))
- grad_ffn_gain: float32 [2048], replicated
- grad_gateup: float32 [2, 2048, 5632], P(None, ('seq', 'row'), 'mp')
- grad_down: float32 [5632, 2048], P('mp', ('seq', 'row'))
Inputs may be any that keep to these rules, and one draw needn't show every extreme that they name: `doc_lengths`: in each row one document, which one drawn from the seed, has exactly 1856 tokens; the others have at most 64. Each document's region is its length rounded up to a multiple of 64, the regions lie in order from position 0, and positions past a document's length or past the last region are padding.
All inputs are finite; a program needn't handle non-finite values.
Results may differ from a plain program's by a relative error of at most 0.018.
Values may be sent and summed in bfloat16 or wider, within the bound.
A program may use at most 320 MiB of HBM per device.

v0:
```python
from functools import partial

import jax
import jax.numpy as jnp
from jax import lax
from jax.sharding import PartitionSpec as P

HDIM = 128
KERNEL = 4
BLOCK = 64


EPSILON = 1e-06
PRECISE = lax.Precision.HIGHEST


def passed_along(block, axis, distance):
    devices = range(lax.axis_size(axis))
    route = [(i - distance, i) for i in devices if i - distance in devices]
    return lax.ppermute(block, axis, route)


def row_layout(lengths, positions):
    span_len = (lengths + BLOCK - 1) // BLOCK * BLOCK
    closing = jnp.cumsum(span_len)
    opening = closing - span_len
    bounds = jnp.concatenate([opening, closing[-1:]])
    reached = bounds[None, :] <= positions[:, None]
    doc_start = jnp.max(jnp.where(reached, bounds[None, :], 0), axis=1)
    inside = (positions[:, None] >= opening[None, :]) & (
        positions[:, None] < (opening + lengths)[None, :]
    )
    real_mask = jnp.any(inside, axis=1).astype(jnp.float32)
    return (doc_start, real_mask)


def local_span(carry_on, queries, keys_in, values, strength):
    head_count, token_count, head_width = queries.shape
    block_count = token_count // BLOCK

    def to_blocks(tensor):
        return tensor.reshape(head_count, block_count, BLOCK, -1).transpose(1, 0, 2, 3)

    def from_blocks(tensor):
        return tensor.transpose(1, 0, 2, 3).reshape(head_count, token_count, -1)

    strict_lower = jnp.tril(jnp.ones((BLOCK, BLOCK), jnp.float32), -1)
    causal = jnp.tril(jnp.ones((BLOCK, BLOCK), jnp.float32))
    identity = jnp.broadcast_to(
        jnp.eye(head_width, dtype=jnp.float32), (head_count, head_width, head_width)
    )

    def block_step(carried, block_in):
        memory, mapping = carried
        q_blk, k_blk, v_blk, s_blk, carry_flag = block_in
        write_rate = s_blk[..., 0]
        memory = memory * carry_flag
        mapping = mapping * carry_flag
        key_gram = jnp.einsum("hcp,hdp->hcd", k_blk, k_blk, precision=PRECISE)
        system = jnp.eye(BLOCK, dtype=jnp.float32) + strict_lower * (
            write_rate[:, :, None] * key_gram
        )
        right_side = jnp.concatenate(
            [write_rate[..., None] * k_blk, write_rate[..., None] * v_blk], axis=-1
        )
        solved = lax.linalg.triangular_solve(
            system, right_side, left_side=True, lower=True, unit_diagonal=True
        )
        w_mat = solved[..., :head_width]
        u_mat = solved[..., head_width:]
        corrected = u_mat - jnp.einsum("hcp,hpv->hcv", w_mat, memory, precision=PRECISE)
        scores = causal * jnp.einsum("hcp,hdp->hcd", q_blk, k_blk, precision=PRECISE)
        out_zero = jnp.einsum("hcp,hpv->hcv", q_blk, memory, precision=PRECISE)
        out_zero = out_zero + jnp.einsum("hcd,hdv->hcv", scores, corrected, precision=PRECISE)
        w_map = jnp.einsum("hcp,hpq->hcq", w_mat, mapping, precision=PRECISE)
        q_prop = jnp.einsum("hcp,hpq->hcq", q_blk, mapping, precision=PRECISE)
        q_prop = q_prop - jnp.einsum("hcd,hdq->hcq", scores, w_map, precision=PRECISE)
        memory = memory + jnp.einsum("hcp,hcv->hpv", k_blk, corrected, precision=PRECISE)
        mapping = mapping - jnp.einsum("hcp,hcq->hpq", k_blk, w_map, precision=PRECISE)
        return ((memory, mapping), (out_zero, q_prop))

    initial = (jnp.zeros((head_count, head_width, head_width), jnp.float32), identity)
    blocks = (
        to_blocks(queries),
        to_blocks(keys_in),
        to_blocks(values),
        to_blocks(strength[..., None]),
        carry_on,
    )
    (memory, mapping), (out_zero, q_prop) = lax.scan(block_step, initial, blocks)
    return (from_blocks(out_zero), from_blocks(q_prop), mapping, memory)


def shards(
    block_in,
    doc_lengths,
    attn_gain,
    qkv_weight,
    conv_weight,
    beta_weight,
    out_gain,
    out_weight,
    ffn_gain,
    gateup_weight,
    down_weight,
    cotangent,
):
    tok_count = block_in.shape[1]
    seq_count = lax.axis_size("seq")
    own_index = lax.axis_index("seq")
    positions = own_index * tok_count + jnp.arange(tok_count + KERNEL - 1, dtype=jnp.int32)
    doc_start, real_ext = row_layout(doc_lengths[0], positions)
    real_mask = real_ext[:tok_count]
    taps = [(positions - shift_no >= doc_start).astype(jnp.float32) for shift_no in range(KERNEL)]
    carry_on = (doc_start[:tok_count:BLOCK] != positions[:tok_count:BLOCK]).astype(jnp.float32)
    residual_in = block_in[0].astype(jnp.float32)
    stat_in = lax.rsqrt(jnp.mean(residual_in * residual_in, axis=-1, keepdims=True) + EPSILON)
    unit_in = residual_in * stat_in
    normed = (unit_in * attn_gain).astype(jnp.bfloat16)
    qkv_full, beta_full, out_full, gateup_full, down_full = (
        lax.all_gather(qkv_weight, ("seq", "row"), axis=1, tiled=True),
        lax.all_gather(beta_weight, ("seq", "row"), axis=1, tiled=True),
        lax.all_gather(out_weight, ("seq", "row"), axis=1, tiled=True),
        lax.all_gather(gateup_weight, ("seq", "row"), axis=1, tiled=True),
        lax.all_gather(down_weight, ("seq", "row"), axis=1, tiled=True),
    )
    raw = jnp.einsum("td,sdc->stc", normed, qkv_full, preferred_element_type=jnp.float32).astype(
        jnp.bfloat16
    )
    rims = passed_along(raw[:, tok_count - KERNEL + 1 :, :], "seq", 1)
    extended = jnp.concatenate([rims, raw], axis=1).astype(jnp.float32)
    conv_sum = jnp.zeros(raw.shape, jnp.float32)
    for shift_no in range(KERNEL):
        window = extended[:, KERNEL - 1 - shift_no : KERNEL - 1 - shift_no + tok_count]
        conv_sum = (
            conv_sum
            + conv_weight[:, shift_no][:, None, :]
            * window
            * taps[shift_no][:tok_count][None, :, None]
        )
    conv_sig = jax.nn.sigmoid(conv_sum)
    head_count = conv_weight.shape[2] // HDIM
    split_heads = (
        (conv_sum * conv_sig).reshape(3, tok_count, head_count, HDIM).transpose(0, 2, 1, 3)
    )
    q_scale = lax.rsqrt(jnp.sum(split_heads[0] * split_heads[0], axis=-1, keepdims=True) + EPSILON)
    q_unit = split_heads[0] * q_scale
    queries = q_unit * HDIM ** (-0.5)
    k_scale = lax.rsqrt(jnp.sum(split_heads[1] * split_heads[1], axis=-1, keepdims=True) + EPSILON)
    keys_in = split_heads[1] * k_scale
    values = split_heads[2]
    logits = jnp.einsum("td,hd->ht", normed, beta_full, preferred_element_type=jnp.float32)
    beta_sig = jax.nn.sigmoid(logits)
    strength = beta_sig * real_mask[None, :]
    (out_zero, q_prop, span_map, span_state), span_pullback = jax.vjp(
        partial(local_span, carry_on), queries, keys_in, values, strength
    )
    empty_state = jnp.zeros_like(span_state)
    all_maps, all_states = (
        lax.all_gather(span_map[None].astype(jnp.bfloat16), "seq", axis=0, tiled=True).astype(
            jnp.float32
        ),
        lax.all_gather(span_state[None].astype(jnp.bfloat16), "seq", axis=0, tiled=True).astype(
            jnp.float32
        ),
    )

    def fold_forward(counter, incoming):
        moved = (
            jnp.einsum("hpq,hqv->hpv", all_maps[counter], incoming, precision=PRECISE)
            + all_states[counter]
        )
        return jnp.where(counter < own_index, moved, incoming)

    state_in = lax.fori_loop(0, seq_count, fold_forward, empty_state)
    mixer = out_zero + jnp.einsum("htp,hpv->htv", q_prop, state_in, precision=PRECISE)
    stat_out = lax.rsqrt(jnp.mean(mixer * mixer, axis=-1, keepdims=True) + EPSILON)
    unit_out = mixer * stat_out
    normed_out = (
        (unit_out * out_gain).transpose(1, 0, 2).reshape(tok_count, -1).astype(jnp.bfloat16)
    )
    branch_part = jnp.dot(normed_out, out_full, preferred_element_type=jnp.float32)
    hidden = residual_in + lax.psum(branch_part.astype(jnp.bfloat16), "mp").astype(jnp.float32)
    stat_mid = lax.rsqrt(jnp.mean(hidden * hidden, axis=-1, keepdims=True) + EPSILON)
    unit_mid = hidden * stat_mid
    normed_mid = (unit_mid * ffn_gain).astype(jnp.bfloat16)
    gate_up = jnp.einsum("td,sdf->stf", normed_mid, gateup_full, preferred_element_type=jnp.float32)
    gate_sig = jax.nn.sigmoid(gate_up[0])
    product = (gate_up[0] * gate_sig * gate_up[1]).astype(jnp.bfloat16)
    ffn_part = jnp.dot(product, down_full, preferred_element_type=jnp.float32)
    block_out = hidden + lax.psum(ffn_part.astype(jnp.bfloat16), "mp").astype(jnp.float32)
    qkv_full, beta_full, out_full, gateup_full, down_full = (
        lax.all_gather(qkv_weight, ("seq", "row"), axis=1, tiled=True),
        lax.all_gather(beta_weight, ("seq", "row"), axis=1, tiled=True),
        lax.all_gather(out_weight, ("seq", "row"), axis=1, tiled=True),
        lax.all_gather(gateup_weight, ("seq", "row"), axis=1, tiled=True),
        lax.all_gather(down_weight, ("seq", "row"), axis=1, tiled=True),
    )
    grad_top = cotangent[0]
    grad_down_part = jnp.dot(product.T, grad_top, preferred_element_type=jnp.float32)
    grad_product = jnp.dot(grad_top, down_full.T, preferred_element_type=jnp.float32)
    grad_gate = grad_product * gate_up[1] * gate_sig * (1.0 + gate_up[0] * (1.0 - gate_sig))
    grad_up = grad_product * gate_up[0] * gate_sig
    grad_gate_up = jnp.stack([grad_gate, grad_up]).astype(jnp.bfloat16)
    grad_gateup_part = jnp.einsum(
        "td,stf->sdf", normed_mid, grad_gate_up, preferred_element_type=jnp.float32
    )
    grad_mid_part = jnp.einsum(
        "stf,sdf->td", grad_gate_up, gateup_full, preferred_element_type=jnp.float32
    )
    grad_mid = lax.psum(grad_mid_part.astype(jnp.bfloat16), "mp").astype(jnp.float32)
    ffn_gain_part = jnp.sum(grad_mid * unit_mid, axis=0)
    grad_unit_mid = grad_mid * ffn_gain
    grad_hidden = grad_top.astype(jnp.float32) + stat_mid * (
        grad_unit_mid - unit_mid * jnp.mean(grad_unit_mid * unit_mid, axis=-1, keepdims=True)
    )
    grad_branch = grad_hidden.astype(jnp.bfloat16)
    grad_out_part = jnp.dot(normed_out.T, grad_branch, preferred_element_type=jnp.float32)
    grad_normed_out = jnp.dot(grad_branch, out_full.T, preferred_element_type=jnp.float32)
    grad_normed_out = grad_normed_out.reshape(tok_count, head_count, HDIM).transpose(1, 0, 2)
    out_gain_part = jnp.sum(grad_normed_out * unit_out, axis=(0, 1))
    grad_unit_out = grad_normed_out * out_gain
    grad_mixer = stat_out * (
        grad_unit_out - unit_out * jnp.mean(grad_unit_out * unit_out, axis=-1, keepdims=True)
    )
    local_grad = jnp.einsum("htp,htv->hpv", q_prop, grad_mixer, precision=PRECISE)
    grad_q_prop = jnp.einsum("htv,hpv->htp", grad_mixer, state_in, precision=PRECISE)
    all_grads = lax.all_gather(
        local_grad[None].astype(jnp.bfloat16), "seq", axis=0, tiled=True
    ).astype(jnp.float32)

    def fold_backward(counter, later_grad):
        source = seq_count - 1 - counter
        moved = (
            jnp.einsum("hqp,hqv->hpv", all_maps[source], later_grad, precision=PRECISE)
            + all_grads[source]
        )
        return jnp.where(source > own_index, moved, later_grad)

    grad_end = lax.fori_loop(0, seq_count, fold_backward, empty_state)
    grad_map = jnp.einsum("hpv,hqv->hpq", grad_end, state_in, precision=PRECISE)
    grad_queries, grad_keys, grad_values, grad_strength = span_pullback(
        (grad_mixer, grad_q_prop, grad_map, grad_end)
    )
    grad_logits = (grad_strength * real_mask[None, :] * beta_sig * (1.0 - beta_sig)).astype(
        jnp.bfloat16
    )
    grad_beta_part = jnp.einsum(
        "ht,td->hd", grad_logits, normed, preferred_element_type=jnp.float32
    )
    grad_q_unit = grad_queries * HDIM ** (-0.5)
    grad_q_raw = q_scale * (
        grad_q_unit - q_unit * jnp.sum(grad_q_unit * q_unit, axis=-1, keepdims=True)
    )
    grad_k_raw = k_scale * (
        grad_keys - keys_in * jnp.sum(grad_keys * keys_in, axis=-1, keepdims=True)
    )
    grad_act = (
        jnp.stack([grad_q_raw, grad_k_raw, grad_values])
        .transpose(0, 2, 1, 3)
        .reshape(3, tok_count, -1)
    )
    grad_conv_sum = grad_act * conv_sig * (1.0 + conv_sum * (1.0 - conv_sig))
    rims_back = passed_along(grad_conv_sum[:, : KERNEL - 1, :], "seq", -1)
    grad_ext = jnp.concatenate([grad_conv_sum, rims_back], axis=1)
    grad_raw = jnp.zeros(grad_conv_sum.shape, jnp.float32)
    conv_terms = []
    for shift_no in range(KERNEL):
        grad_raw = (
            grad_raw
            + conv_weight[:, shift_no][:, None, :]
            * grad_ext[:, shift_no : shift_no + tok_count]
            * taps[shift_no][shift_no : shift_no + tok_count][None, :, None]
        )
        window = extended[:, KERNEL - 1 - shift_no : KERNEL - 1 - shift_no + tok_count]
        conv_terms.append(
            jnp.sum(grad_conv_sum * window * taps[shift_no][:tok_count][None, :, None], axis=1)
        )
    grad_conv_part = jnp.stack(conv_terms, axis=1)
    grad_raw_low = grad_raw.astype(jnp.bfloat16)
    grad_qkv_part = jnp.einsum(
        "td,stc->sdc", normed, grad_raw_low, preferred_element_type=jnp.float32
    )
    grad_normed = jnp.einsum(
        "stc,sdc->td", grad_raw_low, qkv_full, preferred_element_type=jnp.float32
    )
    grad_normed = grad_normed + jnp.einsum(
        "ht,hd->td", grad_logits, beta_full, preferred_element_type=jnp.float32
    )
    grad_normed, out_gain_sum = (
        lax.psum(grad_normed.astype(jnp.bfloat16), "mp").astype(jnp.float32),
        lax.psum(out_gain_part.astype(jnp.bfloat16), "mp").astype(jnp.float32),
    )
    attn_gain_part = jnp.sum(grad_normed * unit_in, axis=0)
    grad_unit_in = grad_normed * attn_gain
    grad_input = grad_hidden + stat_in * (
        grad_unit_in - unit_in * jnp.mean(grad_unit_in * unit_in, axis=-1, keepdims=True)
    )
    weight_sums = (
        lax.psum_scatter(grad_qkv_part, ("seq", "row"), scatter_dimension=1, tiled=True),
        lax.psum_scatter(grad_beta_part, ("seq", "row"), scatter_dimension=1, tiled=True),
        lax.psum_scatter(grad_out_part, ("seq", "row"), scatter_dimension=1, tiled=True),
        lax.psum_scatter(grad_gateup_part, ("seq", "row"), scatter_dimension=1, tiled=True),
        lax.psum_scatter(grad_down_part, ("seq", "row"), scatter_dimension=1, tiled=True),
    )
    small_sums = lax.psum(
        (attn_gain_part, grad_conv_part, out_gain_sum, ffn_gain_part), ("seq", "row")
    )
    return (
        block_out.astype(jnp.bfloat16)[None],
        grad_input[None],
        small_sums[0],
        weight_sums[0],
        small_sums[1],
        weight_sums[1],
        small_sums[2],
        weight_sums[2],
        small_sums[3],
        weight_sums[3],
        weight_sums[4],
    )


def solution(mesh):
    return jax.shard_map(
        shards,
        mesh=mesh,
        in_specs=(
            P("row", "seq", None),
            P("row", None),
            P(),
            P(None, ("seq", "row"), "mp"),
            P(None, None, "mp"),
            P("mp", ("seq", "row")),
            P(),
            P("mp", ("seq", "row")),
            P(),
            P(None, ("seq", "row"), "mp"),
            P("mp", ("seq", "row")),
            P("row", "seq", None),
        ),
        out_specs=(
            P("row", "seq", None),
            P("row", "seq", None),
            P(),
            P(None, ("seq", "row"), "mp"),
            P(None, None, "mp"),
            P("mp", ("seq", "row")),
            P(),
            P("mp", ("seq", "row")),
            P(),
            P(None, ("seq", "row"), "mp"),
            P("mp", ("seq", "row")),
        ),
        check_vma=False,
    )
```

profile of v0, /device:TPU:0, one launch (start us, length us, event | category | flops | bytes accessed | tf_op | source)
XLA Modules:
  0.0 3412.9 jit_solution(8706984130764641248)
XLA Ops:
  16.7 24.1 all_gather.30
  43.4 33.9 all-gather.8.cloned.1.call-done
  77.3 10.5 convert_bitcast_fusion.1
  95.7 7.6 multiply_bitcast_fusion
  119.6 661.6 %while.97 = (s32[]{:T(128)}, f32[4,128,128]{2,1,0:T(8,128)S(1)}, f32[4,128,128]{2,1,0:T(8,128)S(1)}, f32[16,4,64,128]{3,2,0,1:T(8,128)}, f32[16,4,64,128]{3,2,0,...) while((s32[]{:T(128)}, f32[4,128,128]{2,1,0:T(8,128)S(1)}, ...), condition=%wide.region_7.8_spmd.clone, body=%wide.region_6.7_spmd.clone.sunk | while | flops 454316096 | bytes 8985113 | solution.py:90
  126.6 19.7 custom-call.33
  167.9 19.7 custom-call.33
  209.3 19.7 custom-call.33
  250.6 19.7 custom-call.33
  292.0 19.7 custom-call.33
  333.4 19.7 custom-call.33
  374.7 19.7 custom-call.33
  416.0 19.7 custom-call.33
  457.4 19.7 custom-call.33
  498.7 19.7 custom-call.33
  540.1 19.7 custom-call.33
  581.4 19.7 custom-call.33
  622.8 19.7 custom-call.33
  664.2 19.7 custom-call.33
  705.5 19.7 custom-call.33
  746.9 19.7 custom-call.33
  806.7 101.5 %all-reduce.8.cloned.1.call-done = bf16[1024,2048]{1,0:T(8,128)(2,1)} async-done(((bf16[1024,2048]{1,0:T(8,128)(2,1)}), bf16[1024,2048]{1,0:T(8,128)(2,1)}) %all-reduce.8.cloned.1.call-update) | async-done | bytes 4194320 | tf_op jit(solution)/shard_map/psum | solution.py:183
  913.0 104.8 %all-gather.12.cloned.1.call-done = bf16[2,2048,1408]{2,1,0:T(8,128)(2,1)} async-done(((bf16[2,256,1408]{2,1,0:T(8,128)(2,1)}), bf16[2,2048,1408]{2,1,0:T(8,128)(2,1)}) %all-gather.12.cloned.1.call-update) | async-done | bytes 11534352 | tf_op jit(solution)/shard_map/all_gather | solution.py:124
  1017.8 20.6 convolution_bitcast_fusion.1
  1038.4 40.1 %all-gather.14.cloned.1.call-done = bf16[1408,2048]{1,0:T(8,128)(2,1)} async-done(((bf16[1408,256]{1,0:T(8,128)(2,1)}), bf16[1408,2048]{1,0:T(8,128)(2,1)}) %all-gather.14.cloned.1.call-update) | async-done | bytes 5767184 | tf_op jit(solution)/shard_map/all_gather | solution.py:125
  1078.5 14.1 fusion.251
  1095.1 16.3 bitcast_convert_fusion
  1111.5 13.5 convolution_convert_fusion
  1125.0 88.6 %all-reduce.10.cloned.1.call-done = bf16[1024,2048]{1,0:T(8,128)(2,1)} async-done(((bf16[1024,2048]{1,0:T(8,128)(2,1)}), bf16[1024,2048]{1,0:T(8,128)(2,1)}) %all-reduce.10.cloned.1.call-update) | async-done | bytes 4194320 | tf_op jit(solution)/shard_map/psum | solution.py:211
  1213.6 8.3 fusion.209
  1221.9 6.9 fusion.260
  1260.8 875.9 %while.96 = (s32[]{:T(128)}, f32[4,128,128]{2,1,0:T(8,128)S(1)}, f32[4,128,128]{2,1,0:T(8,128)S(1)}, f32[16,4,64,128]{3,2,0,1:T(8,128)}, f32[16,4,64,128]{3,2,0,...) while((s32[]{:T(128)}, f32[4,128,128]{2,1,0:T(8,128)S(1)}, ...), condition=%wide.region_23.24_spmd.clone, body=%wide.region_19.23_spmd.clone.sunk | while | flops 920072000 | bytes 14427733 | solution.py:90
  1270.8 19.7 custom-call.32
  1325.5 19.7 custom-call.32
  1380.3 19.7 custom-call.32
  1435.0 19.7 custom-call.32
  1489.8 19.7 custom-call.32
  1544.5 19.7 custom-call.32
  1599.3 19.7 custom-call.32
  1654.0 19.7 custom-call.32
  1708.7 19.7 custom-call.32
  1763.5 19.7 custom-call.32
  1818.2 19.7 custom-call.32
  1872.9 19.7 custom-call.32
  1927.7 19.7 custom-call.32
  1982.5 19.7 custom-call.32
  2037.2 19.7 custom-call.32
  2092.0 19.7 custom-call.32
  2150.1 6.9 fusion.255
  2157.1 9.1 multiply_reduce_fusion.4
  2173.7 13.1 fusion.221
  2186.8 12.4 fusion.214
  2199.2 12.1 convolution_bitcast_fusion.2
  2213.2 20.4 convolution_bitcast_fusion
  2235.0 12.1 fusion.258
  2247.2 14.6 fusion.241
  2262.4 8.9 psum.69
  2272.9 113.2 %all-reduce.12.cloned.1.call-done = (bf16[1024,2048]{1,0:T(8,128)(2,1)}, bf16[1024,2048]{1,0:T(8,128)(2,1)}) async-done(((bf16[1024,2048]{1,0:T(8,128)(2,1)}, bf16[1024,2048]{1,0:T(8,128)(2,1)}), (bf16[1024,2048]{1,0:T(8,128)(2,1)}, bf16[1024,2048]{1,0:T(8,128)(2,1)})) %all-reduce.12.cloned.1.call-update) | async-done | bytes 8388624 | tf_op jit(solution)/shard_map/psum | solution.py:191
  2391.2 35.4 %all-reduce.2 = (f32[2048]{0:T(1024)}, f32[3,4,512]{2,0,1:T(4,128)S(1)}, f32[128]{0:T(128)}, f32[2048]{0:T(1024)}) all-reduce(f32[2048]{0:T(1024)S(1)} %get-tuple-element.1409, f32[3,4,512]{2,0,1:T(4,128)S(1)} %pad_maximum_fusion.4, bf16[128]{0:T(256)(128)(2,1)S(1)} %psum.69, ...), channel_id=1, replica_groups=mesh['seq'=2,'mp'=4,'row'=4] {'seq','row'}, use_global_device_ids=true, to_apply=%region_29.30 | all-reduce | flops 10368 | bytes 82688 | tf_op jit(solution)/shard_map/psum | solution.py:306
  2427.2 17.1 fusion.205
  2444.3 193.0 %reduce-scatter.8.cloned.1.call-done = f32[3,256,512]{1,2,0:T(8,128)} async-done(((f32[3,2048,512]{1,2,0:T(8,128)}), f32[3,256,512]{1,2,0:T(8,128)}) %reduce-scatter.8.cloned.1.call-update) | async-done | bytes 1572880 | tf_op jit(solution)/shard_map/reduce_scatter | solution.py:300
  2640.3 442.7 %reduce-scatter.12.cloned.1.call-done = f32[2,256,1408]{1,2,0:T(8,128)} async-done(((f32[2,2048,1408]{1,2,0:T(8,128)}), f32[2,256,1408]{1,2,0:T(8,128)}) %reduce-scatter.12.cloned.1.call-update) | async-done | bytes 2883600 | tf_op jit(solution)/shard_map/reduce_scatter | solution.py:303
  3086.3 90.7 %reduce-scatter.10.cloned.1.call-done = f32[512,256]{1,0:T(8,128)} async-done(((f32[512,2048]{1,0:T(8,128)}), f32[512,256]{1,0:T(8,128)}) %reduce-scatter.10.cloned.1.call-update) | async-done | bytes 524304 | tf_op jit(solution)/shard_map/reduce_scatter | solution.py:302
  3177.1 228.5 %reduce-scatter.14.cloned.1.call-done = f32[1408,256]{1,0:T(8,128)} async-done(((f32[1408,2048]{1,0:T(8,128)}), f32[1408,256]{1,0:T(8,128)}) %reduce-scatter.14.cloned.1.call-update) | async-done | bytes 1441808 | tf_op jit(solution)/shard_map/reduce_scatter | solution.py:304
  (1230 shorter events, 1049.0 us)
Async XLA Ops:
  7.2 9.3 copy-start.53
  7.2 9.5 copy-start.63
  7.2 34.3 %copy-start.49 = (f32[2048]{0:T(1024)S(1)}, f32[2048]{0:T(1024)}, u32[]{:S(2)}) copy-start(f32[2048]{0:T(1024)} %param.22) | copy-start | bytes 24580
  7.2 70.1 %all-gather.8.cloned.1.call-start = ((), (), s32[]{:S(2)}) async-start(), calls=%async_computation.5 | async-start | bytes 7077888 | tf_op jit(solution)/shard_map/all_gather | solution.py:121
  7.9 791.2 %all-gather.10.cloned.1.call-start = ((), (), s32[]{:S(2)}) async-start(), calls=%async_computation.6 | async-start | bytes 2359296 | tf_op jit(solution)/shard_map/all_gather | solution.py:123
  8.7 899.5 %all-reduce.8.cloned.1.call-start = ((), (), s32[]{:S(2)}) async-start(), calls=%async_computation.7 | async-start | bytes 8388608 | tf_op jit(solution)/shard_map/psum | solution.py:183
  11.9 29.6 copy-start.1
  11.9 83.7 %copy-start.36 = (f32[1024]{0:T(1024)}, f32[1024]{0:T(1024)S(1)}, u32[]{:S(2)}) copy-start(f32[1024]{0:T(1024)S(1)} %fusion.270) | copy-start | bytes 12292
  13.4 82.3 %copy-start.40 = (f32[1024]{0:T(1024)}, f32[1024]{0:T(1024)S(1)}, u32[]{:S(2)}) copy-start(f32[1024]{0:T(1024)S(1)} %get-tuple-element.1577) | copy-start | bytes 12292
  16.5 60.8 %copy-start.46 = (f32[1024]{0:T(1024)}, f32[1024]{0:T(1024)S(1)}, u32[]{:S(2)}) copy-start(f32[1024]{0:T(1024)S(1)} %add_rsqrt_fusion.4) | copy-start | bytes 12292
  16.7 26.8 copy-start.58
  40.8 54.9 %copy-start.28 = (f32[3,512]{1,0:T(4,128)}, f32[3,512]{1,0:T(4,128)S(1)}, u32[]{:S(2)}) copy-start(f32[3,512]{1,0:T(4,128)S(1)} %get-tuple-element.1587) | copy-start | bytes 18436
  40.8 54.9 %copy-start.30 = (f32[3,512]{1,0:T(4,128)}, f32[3,512]{1,0:T(4,128)S(1)}, u32[]{:S(2)}) copy-start(f32[3,512]{1,0:T(4,128)S(1)} %get-tuple-element.1588) | copy-start | bytes 18436
  41.5 54.2 %copy-start.42 = (f32[1024]{0:T(1024)}, f32[1024]{0:T(1024)S(1)}, u32[]{:S(2)}) copy-start(f32[1024]{0:T(1024)S(1)} %get-tuple-element.1573) | copy-start | bytes 12292
  41.5 54.2 %copy-start.44 = (f32[1024]{0:T(1024)}, f32[1024]{0:T(1024)S(1)}, u32[]{:S(2)}) copy-start(f32[1024]{0:T(1024)S(1)} %get-tuple-element.1585) | copy-start | bytes 12292
  41.5 54.2 %copy-start.32 = (f32[3,512]{1,0:T(4,128)}, f32[3,512]{1,0:T(4,128)S(1)}, u32[]{:S(2)}) copy-start(f32[3,512]{1,0:T(4,128)S(1)} %get-tuple-element.1589) | copy-start | bytes 18436
  41.5 54.2 %copy-start.34 = (f32[3,512]{1,0:T(4,128)}, f32[3,512]{1,0:T(4,128)S(1)}, u32[]{:S(2)}) copy-start(f32[3,512]{1,0:T(4,128)S(1)} %get-tuple-element.1590) | copy-start | bytes 18436
  89.6 3.2 collective-permute-start
  95.7 7.7 copy-start
  104.0 3.9 copy-start.4
  781.2 8.1 copy-start.65
  792.1 5.7 copy-start.62
  805.5 212.3 %all-gather.12.cloned.1.call-start = ((), (), s32[]{:S(2)}) async-start(), calls=%async_computation.8 | async-start | bytes 12976128 | tf_op jit(solution)/shard_map/all_gather | solution.py:124
  806.0 272.5 %all-gather.14.cloned.1.call-start = ((), (), s32[]{:S(2)}) async-start(), calls=%async_computation.9 | async-start | bytes 6488064 | tf_op jit(solution)/shard_map/all_gather | solution.py:125
  806.6 211.2 %copy-start.51 = (f32[2048]{0:T(1024)S(1)}, f32[2048]{0:T(1024)}, u32[]{:S(2)}) copy-start(f32[2048]{0:T(1024)} %param.28) | copy-start | bytes 24580
  806.6 407.0 %all-reduce.10.cloned.1.call-start = ((), (), s32[]{:S(2)}) async-start(), calls=%async_computation.10 | async-start | bytes 8388608 | tf_op jit(solution)/shard_map/psum | solution.py:211
  1111.4 1159.9 %reduce-scatter.16.cloned.1.call-start = ((), (), s32[]{:S(2)}) async-start(), calls=%async_computation.15 | async-start | bytes 1179648
  1213.6 8.3 copy-start.2
  1213.6 8.3 copy-start.5
  1213.6 8.3 copy-start.15
  1221.9 6.9 copy-start.60
  1221.9 6.9 copy-start.7
  2136.7 3.5 copy-start.11
  2136.7 3.5 copy-start.14
  2136.8 5.7 copy-start.27
  2136.8 5.8 copy-start.57
  2136.8 5.8 copy-start.59
  2136.8 5.8 copy-start.39
  2142.6 4.8 copy-start.13
  2142.6 4.8 copy-start.21
  2150.0 7.0 slice-start
  2150.1 6.9 slice-start.1
  2150.1 6.9 copy-start.16
  2150.1 6.9 copy-start.37
  2150.1 6.9 copy-start.41
  2150.1 6.9 copy-start.43
  2150.1 6.9 copy-start.45
  2157.1 13.4 copy-start.3
  2157.1 13.4 copy-start.47
  2157.1 13.4 copy-start.50
  2168.9 4.7 copy-start.29
  2168.9 4.7 copy-start.31
  2169.0 4.7 copy-start.33
  2169.0 4.7 copy-start.35
  2169.0 4.7 copy-start.54
  2169.0 4.7 copy-start.55
  2169.0 4.7 copy-start.56
  2169.0 4.6 collective-permute-start.1
  2173.6 212.6 %all-reduce.12.cloned.1.call-start = ((), (), s32[]{:S(2)}) async-start(), calls=%async_computation.16 | async-start | bytes 16777216 | tf_op jit(solution)/shard_map/psum | solution.py:191
  2199.2 438.0 %reduce-scatter.8.cloned.1.call-start = ((), (), s32[]{:S(2)}) async-start(), calls=%async_computation.11 | async-start | bytes 14155776 | tf_op jit(solution)/shard_map/reduce_scatter | solution.py:300
  2211.4 871.6 %reduce-scatter.12.cloned.1.call-start = ((), (), s32[]{:S(2)}) async-start(), calls=%async_computation.13 | async-start | bytes 25952256 | tf_op jit(solution)/shard_map/reduce_scatter | solution.py:303
  2233.6 943.4 %reduce-scatter.10.cloned.1.call-start = ((), (), s32[]{:S(2)}) async-start(), calls=%async_computation.12 | async-start | bytes 4718592 | tf_op jit(solution)/shard_map/reduce_scatter | solution.py:302
  2247.2 1158.4 %reduce-scatter.14.cloned.1.call-start = ((), (), s32[]{:S(2)}) async-start(), calls=%async_computation.14 | async-start | bytes 12976128 | tf_op jit(solution)/shard_map/reduce_scatter | solution.py:304
  2386.1 5.0 copy-start.48
  (21 other events, 38.6 us)
Sparse Core Ops, SparseCore 0:
  9.6 67.6 all-gather.7
  78.9 29.4 all-gather.9
  805.6 102.5 all-reduce.7
  909.7 108.0 all-gather.11
  1019.3 59.1 all-gather.13
  1111.5 102.0 all-reduce.9
  2173.7 36.3 reduce-scatter.15
  2214.4 171.6 all-reduce.11
  2388.6 248.6 reduce-scatter.7
  2639.6 443.3 reduce-scatter.11
  3085.9 91.0 reduce-scatter.9
  3179.9 225.6 reduce-scatter.13
where the time goes:
time: 3430 us; the launch traced here: 3410 us
  waiting for transfers between devices  1440 us (42%)
  matrix products  896 us (26%)
  other arithmetic  820 us (24%)
  local copies, waits for them, and re-layouts  158 us (5%)
  blocking collectives  74.6 us (2%)
    another operation x128, other arithmetic, block_step(): lax.linalg.triangular_solve(system, right_side, left_side=True, lower=Tru...  648 us
    reduce_scatter x1, waiting for transfers between devices, shards(): lax.psum_scatter(grad_gateup_part, ('seq', 'row'), scatter_dimension=1, t...  443 us
    reduce_scatter x1, waiting for transfers between devices, shards(): lax.psum_scatter(grad_down_part, ('seq', 'row'), scatter_dimension=1, til...  229 us
    reduce_scatter x1, waiting for transfers between devices, shards(): lax.psum_scatter(grad_qkv_part, ('seq', 'row'), scatter_dimension=1, tile...  193 us
    psum x1, waiting for transfers between devices, shards(): lax.psum(ffn_part.astype(jnp.bfloat16), 'mp').astype(jnp.float32)  113 us
    all_gather x1, waiting for transfers between devices, shards(): lax.all_gather(gateup_weight, ('seq', 'row'), axis=1, tiled=True)  105 us
    dot_general x48, matrix products, block_step(): out_zero = jnp.einsum('hcp,hpv->hcv', q_blk, memory, precision=PRECISE)  103 us
    psum x1, waiting for transfers between devices, shards(): lax.psum(branch_part.astype(jnp.bfloat16), 'mp').astype(jnp.float32)  101 us
  transfers between devices with their start and end apart: 14, of which 10 were waited for; matrix products, arithmetic and copies ran while one was open for 26% of the time, Pallas kernels for 0%

commit v1 on v0

v1 whole, which is shorter than its diff:
```python
import functools
from functools import partial

import jax
import jax.numpy as jnp
from jax import lax
from jax.experimental import pallas as pl
from jax.experimental.pallas import tpu as pltpu
from jax.sharding import PartitionSpec as P

HDIM = 128
KERNEL = 4
BLOCK = 64
CHUNK = 128
EPSILON = 1e-06
PRECISE = lax.Precision.HIGHEST
F32 = jnp.float32
BF16 = jnp.bfloat16

NT=(((1,),(1,)),((),())); NN=(((1,),(0,)),((),())); TN=(((0,),(0,)),((),()))

def mm(a,b,dims=NN):
    return lax.dot_general(a.astype(BF16), b.astype(BF16), dims, preferred_element_type=F32)

def iotas():
    return lax.broadcasted_iota(jnp.int32,(CHUNK,CHUNK),0), lax.broadcasted_iota(jnp.int32,(CHUNK,CHUNK),1)

def inverse(a):
    r,c=iotas()
    t=jnp.where(r==c,1.0,0.0)-jnp.where(r//2==c//2,a,0.0)
    size=2
    while size<CHUNK:
        off=jnp.where((r//(2*size)==c//(2*size))&(r//size!=c//size),a,0.0)
        t=t-mm(t,mm(off,t))
        size*=2
    return t

def conv_act(ext_ref, s, base, lanes, cw, taps):
    total=cw[0:1]*ext_ref[s,pl.ds(base+8,CHUNK),lanes]
    for j in range(1,KERNEL):
        total=total+(cw[j:j+1]*taps[j-1])*ext_ref[s,pl.ds(base+8-j,CHUNK),lanes]
    sig=jax.nn.sigmoid(total)
    return total,sig

def fwd_kernel(heads, group, raw_ref, cw_ref, gain_ref, cols_ref, normed_ref, o_ref, s_ref, t_ref, w_ref, r_ref, ext, state):
    rows=group*CHUNK
    step=pl.program_id(0)
    @pl.when(step==0)
    def _():
        ext[:,0:8,:]=jnp.zeros((3,8,heads*HDIM),F32)
        state[...]=jnp.zeros(state.shape,F32)
    @pl.when(step>0)
    def _():
        ext[:,0:8,:]=ext[:,rows:rows+8,:]
    ext[:,8:,:]=raw_ref[...].astype(F32)
    r,c=iotas()
    width=heads*HDIM
    units=[]
    for g in range(group):
        base=g*CHUNK
        cols=cols_ref[pl.ds(base,CHUNK),:]
        taps=[cols[:,j:j+1] for j in range(3)]
        m=cols[:,6:7]
        for h in range(heads):
            act=[]
            for s in range(3):
                lanes=pl.ds(h*HDIM,HDIM)
                total,sig=conv_act(ext,s,base,lanes,cw_ref[s,:,lanes],taps)
                act.append(total*sig)
            q=act[0]*(lax.rsqrt(jnp.sum(act[0]*act[0],axis=1,keepdims=True)+EPSILON)*HDIM**-0.5)
            k=act[1]*lax.rsqrt(jnp.sum(act[1]*act[1],axis=1,keepdims=True)+EPSILON)
            v=act[2]
            b=cols[:,9+h:10+h]
            gram=mm(k,k,NT)
            score=mm(q,k,NT)
            mask=jnp.where(c<BLOCK,m,1.0)
            a=jnp.where(r>c,b*gram*mask,0.0)
            l=jnp.where(r>=c,score*mask,0.0)
            t=inverse(a)
            w=mm(t,b*k)*m
            u=mm(t,b*v)
            t_ref[g,h]=t.astype(BF16)
            w_ref[pl.ds(base,CHUNK),pl.ds(h*HDIM,HDIM)]=w.astype(BF16)
            units.append((g,h,q*m,k*cols[:,7:8],l,w,u,cols[0:1,8:9],m[CHUNK-1:CHUNK]))
    for g,h,q,k,l,w,u,keep0,keep1 in units:
        base=g*CHUNK
        out=(pl.ds(base,CHUNK),pl.ds(h*HDIM,HDIM))
        s=state[h]*keep0
        s_ref[g,h]=s.astype(BF16)
        rr=u-mm(w,s)
        o=mm(q,s)+mm(l,rr)
        state[h]=s*keep1+mm(k,rr,TN)
        r_ref[out]=rr.astype(BF16)
        o_ref[out]=o
        stat=lax.rsqrt(jnp.mean(o*o,axis=1,keepdims=True)+EPSILON)
        normed_ref[out]=(o*stat*gain_ref[...]).astype(BF16)

def forward(raw, cw, gain, cols, group):
    n=raw.shape[1]; heads=raw.shape[2]//HDIM; rows=group*CHUNK; width=heads*HDIM
    nc=n//CHUNK
    row=lambda w: pl.BlockSpec((rows,w),lambda i:(i,0))
    mat=pl.BlockSpec((group,heads,HDIM,HDIM),lambda i:(i,0,0,0))
    full=lambda a: pl.BlockSpec(a.shape,lambda i:(0,0))
    return pl.pallas_call(functools.partial(fwd_kernel,heads,group),
        grid=(n//rows,),
        in_specs=[pl.BlockSpec((3,rows,width),lambda i:(0,i,0)),pl.BlockSpec(cw.shape,lambda i:(0,0,0)),full(gain),row(16)],
        out_specs=[row(width),row(width),mat,mat,row(width),row(width)],
        out_shape=[jax.ShapeDtypeStruct((n,width),BF16),jax.ShapeDtypeStruct((n,width),F32),
            jax.ShapeDtypeStruct((nc,heads,HDIM,HDIM),BF16),jax.ShapeDtypeStruct((nc,heads,HDIM,HDIM),BF16),
            jax.ShapeDtypeStruct((n,width),BF16),jax.ShapeDtypeStruct((n,width),BF16)],
        scratch_shapes=[pltpu.VMEM((3,rows+8,width),F32),pltpu.VMEM((heads,HDIM,HDIM),F32)],
        compiler_params=pltpu.CompilerParams(vmem_limit_bytes=48<<20),
    )(raw,cw,gain,cols)

def bwd_kernel(heads, group, raw_ref, prev_ref, cw_ref, gain_ref, cols_ref, gno_ref, o_ref, s_ref, t_ref, w_ref, r_ref,
               graw_ref, gb_ref, gcw_ref, ggain_ref, ext, gext, grad_state):
    rows=group*CHUNK
    step=pl.program_id(0); steps=pl.num_programs(0)
    width=heads*HDIM
    @pl.when(step==0)
    def _():
        gext[:,rows:rows+8,:]=jnp.zeros((3,8,heads*HDIM),F32)
        grad_state[...]=jnp.zeros(grad_state.shape,F32)
        gcw_ref[...]=jnp.zeros(gcw_ref.shape,F32)
        ggain_ref[...]=jnp.zeros(ggain_ref.shape,F32)
    @pl.when(step>0)
    def _():
        gext[:,rows:rows+8,:]=gext[:,0:8,:]
    first=jnp.where(step==steps-1,0.0,1.0)
    ext[:,0:8,:]=prev_ref[...].astype(F32)[:,8:16]*first
    ext[:,8:,:]=raw_ref[...].astype(F32)
    r,c=iotas()
    for g in range(group-1,-1,-1):
        base=g*CHUNK
        cols=cols_ref[pl.ds(base,CHUNK),:]
        taps=[cols[:,j:j+1] for j in range(3)]
        m=cols[:,6:7]; m2=cols[:,7:8]; keep0=cols[0:1,8:9]; keep1=m[CHUNK-1:CHUNK]
        gbs=[]
        for h in range(heads):
            out=(pl.ds(base,CHUNK),pl.ds(h*HDIM,HDIM))
            act=[];tot=[];sigs=[]
            for s in range(3):
                lanes=pl.ds(h*HDIM,HDIM)
                total,sig=conv_act(ext,s,base,lanes,cw_ref[s,:,lanes],taps)
                act.append(total*sig);tot.append(total);sigs.append(sig)
            rq=lax.rsqrt(jnp.sum(act[0]*act[0],axis=1,keepdims=True)+EPSILON)
            rk=lax.rsqrt(jnp.sum(act[1]*act[1],axis=1,keepdims=True)+EPSILON)
            qu=act[0]*rq; q=qu*HDIM**-0.5
            k=act[1]*rk; v=act[2]
            b=cols[:,9+h:10+h]
            mask=jnp.where(c<BLOCK,m,1.0)
            gram=mm(k,k,NT)*mask
            l=jnp.where(r>=c,mm(q,k,NT)*mask,0.0)
            s=s_ref[g,h]; t=t_ref[g,h]; w=w_ref[out]; rr=r_ref[out]
            o=o_ref[out]
            stat=lax.rsqrt(jnp.mean(o*o,axis=1,keepdims=True)+EPSILON)
            uo=o*stat
            gno=gno_ref[out].astype(F32)
            ggain_ref[...]+=jnp.sum(gno*uo,axis=0,keepdims=True)
            gu=gno*gain_ref[...]
            do=stat*(gu-uo*jnp.mean(gu*uo,axis=1,keepdims=True))
            dsn=grad_state[h]
            dr=mm(l,do,TN)+m2*mm(k,dsn)
            ds=keep1*dsn+mm(q*m,do,TN)-mm(w,dr,TN)
            grad_state[h]=keep0*ds
            df=mm(t,dr,TN)
            dl=jnp.where(r>=c,mm(do,rr,NT)*mask,0.0)
            da=jnp.where(r>c,-mm(df,rr,NT),0.0)
            de=b*df
            e=v-m*mm(k,s)
            gbs.append(jnp.sum(df*e,axis=1,keepdims=True)+jnp.sum(da*gram,axis=1,keepdims=True))
            dkk=b*da*mask
            dq=m*mm(do,s,NT)+mm(dl,k)
            dk=mm(dl,q,TN)+m2*mm(rr,dsn,NT)-m*mm(de,s,NT)+mm(dkk,k)+mm(dkk,k,TN)
            dv=de
            gq=dq*HDIM**-0.5
            gq=rq*(gq-qu*jnp.sum(gq*qu,axis=1,keepdims=True))
            gk=rk*(dk-k*jnp.sum(dk*k,axis=1,keepdims=True))
            for i,ga in enumerate((gq,gk,dv)):
                lanes=pl.ds(h*HDIM,HDIM)
                gc=ga*sigs[i]*(1.0+tot[i]*(1.0-sigs[i]))
                gext[i,pl.ds(base,CHUNK),lanes]=gc
                for j in range(KERNEL):
                    win=ext[i,pl.ds(base+8-j,CHUNK),lanes]
                    prod=gc*win if j==0 else gc*win*taps[j-1]
                    gcw_ref[i,j:j+1,lanes]+=jnp.sum(prod,axis=0,keepdims=True)
        gb_ref[pl.ds(base,CHUNK),:]=jnp.concatenate(gbs,axis=1)
        for h in range(heads):
            for i in range(3):
                lanes=pl.ds(h*HDIM,HDIM)
                cw=cw_ref[i,:,lanes]
                total=cw[0:1]*gext[i,pl.ds(base,CHUNK),lanes]
                for j in range(1,KERNEL):
                    total=total+(cw[j:j+1]*cols[:,2+j:3+j])*gext[i,pl.ds(base+j,CHUNK),lanes]
                graw_ref[i,pl.ds(base,CHUNK),lanes]=total.astype(BF16)

def backward(raw, cw, gain, cols, gno, o, s, t, w, r, group):
    n=raw.shape[1]; heads=raw.shape[2]//HDIM; rows=group*CHUNK; width=heads*HDIM
    steps=n//rows
    row=lambda w: pl.BlockSpec((rows,w),lambda i:(steps-1-i,0))
    mat=pl.BlockSpec((group,heads,HDIM,HDIM),lambda i:(steps-1-i,0,0,0))
    full=lambda a: pl.BlockSpec(a.shape,lambda i:(0,0))
    prev=pl.BlockSpec((3,16,width),lambda i:(0,jnp.maximum((steps-1-i)*(rows//16)-1,0),0))
    return pl.pallas_call(functools.partial(bwd_kernel,heads,group),
        grid=(steps,),
        in_specs=[pl.BlockSpec((3,rows,width),lambda i:(0,steps-1-i,0)),prev,pl.BlockSpec(cw.shape,lambda i:(0,0,0)),full(gain),row(16),row(width),row(width),mat,mat,row(width),row(width)],
        out_specs=[pl.BlockSpec((3,rows,width),lambda i:(0,steps-1-i,0)),row(heads),pl.BlockSpec((3,KERNEL,width),lambda i:(0,0,0)),pl.BlockSpec((1,HDIM),lambda i:(0,0))],
        out_shape=[jax.ShapeDtypeStruct((3,n,width),BF16),jax.ShapeDtypeStruct((n,heads),F32),
            jax.ShapeDtypeStruct((3,KERNEL,width),F32),jax.ShapeDtypeStruct((1,HDIM),F32)],
        scratch_shapes=[pltpu.VMEM((3,rows+8,width),F32),pltpu.VMEM((3,rows+8,width),F32),pltpu.VMEM((heads,HDIM,HDIM),F32)],
        compiler_params=pltpu.CompilerParams(vmem_limit_bytes=48<<20),
    )(raw,raw,cw,gain,cols,gno,o,s,t,w,r)

def make_cols(starts, strength):
    n,heads=strength.shape
    blocks=n//BLOCK
    keep=starts[:blocks]; nxt=jnp.concatenate([starts[1:blocks],jnp.ones((1,),F32)])
    inside=jnp.arange(BLOCK)
    cols=[]
    for j in range(1,KERNEL):
        cols.append(jnp.where(inside[None,:]<j,keep[:,None],1.0).reshape(n))
    for j in range(1,KERNEL):
        cols.append(jnp.where(inside[None,:]>=BLOCK-j,nxt[:,None],1.0).reshape(n))
    pair=keep.reshape(-1,2)
    one=jnp.ones_like(pair[:,0])
    per=CHUNK//BLOCK
    cols.append(jnp.repeat(jnp.stack([one,pair[:,1]],axis=1).reshape(-1),BLOCK))
    cols.append(jnp.repeat(jnp.stack([pair[:,1],one],axis=1).reshape(-1),BLOCK))
    cols.append(jnp.repeat(pair[:,0],CHUNK))
    cols=jnp.stack(cols,axis=1)
    return jnp.concatenate([cols,strength,jnp.zeros((n,16-9-heads),F32)],axis=1)


def passed_along(block, axis, distance):
    devices = range(lax.axis_size(axis))
    route = [(i - distance, i) for i in devices if i - distance in devices]
    return lax.ppermute(block, axis, route)


def row_layout(lengths, positions):
    span_len = (lengths + BLOCK - 1) // BLOCK * BLOCK
    closing = jnp.cumsum(span_len)
    opening = closing - span_len
    bounds = jnp.concatenate([opening, closing[-1:]])
    reached = bounds[None, :] <= positions[:, None]
    doc_start = jnp.max(jnp.where(reached, bounds[None, :], 0), axis=1)
    inside = (positions[:, None] >= opening[None, :]) & (
        positions[:, None] < (opening + lengths)[None, :]
    )
    real_mask = jnp.any(inside, axis=1).astype(jnp.float32)
    return (doc_start, real_mask)


def local_span(carry_on, queries, keys_in, values, strength):
    head_count, token_count, head_width = queries.shape
    block_count = token_count // BLOCK

    def to_blocks(tensor):
        return tensor.reshape(head_count, block_count, BLOCK, -1).transpose(1, 0, 2, 3)

    def from_blocks(tensor):
        return tensor.transpose(1, 0, 2, 3).reshape(head_count, token_count, -1)

    strict_lower = jnp.tril(jnp.ones((BLOCK, BLOCK), jnp.float32), -1)
    causal = jnp.tril(jnp.ones((BLOCK, BLOCK), jnp.float32))
    identity = jnp.broadcast_to(
        jnp.eye(head_width, dtype=jnp.float32), (head_count, head_width, head_width)
    )

    def block_step(carried, block_in):
        memory, mapping = carried
        q_blk, k_blk, v_blk, s_blk, carry_flag = block_in
        write_rate = s_blk[..., 0]
        memory = memory * carry_flag
        mapping = mapping * carry_flag
        key_gram = jnp.einsum("hcp,hdp->hcd", k_blk, k_blk, precision=PRECISE)
        system = jnp.eye(BLOCK, dtype=jnp.float32) + strict_lower * (
            write_rate[:, :, None] * key_gram
        )
        right_side = jnp.concatenate(
            [write_rate[..., None] * k_blk, write_rate[..., None] * v_blk], axis=-1
        )
        solved = lax.linalg.triangular_solve(
            system, right_side, left_side=True, lower=True, unit_diagonal=True
        )
        w_mat = solved[..., :head_width]
        u_mat = solved[..., head_width:]
        corrected = u_mat - jnp.einsum("hcp,hpv->hcv", w_mat, memory, precision=PRECISE)
        scores = causal * jnp.einsum("hcp,hdp->hcd", q_blk, k_blk, precision=PRECISE)
        out_zero = jnp.einsum("hcp,hpv->hcv", q_blk, memory, precision=PRECISE)
        out_zero = out_zero + jnp.einsum("hcd,hdv->hcv", scores, corrected, precision=PRECISE)
        w_map = jnp.einsum("hcp,hpq->hcq", w_mat, mapping, precision=PRECISE)
        q_prop = jnp.einsum("hcp,hpq->hcq", q_blk, mapping, precision=PRECISE)
        q_prop = q_prop - jnp.einsum("hcd,hdq->hcq", scores, w_map, precision=PRECISE)
        memory = memory + jnp.einsum("hcp,hcv->hpv", k_blk, corrected, precision=PRECISE)
        mapping = mapping - jnp.einsum("hcp,hcq->hpq", k_blk, w_map, precision=PRECISE)
        return ((memory, mapping), (out_zero, q_prop))

    initial = (jnp.zeros((head_count, head_width, head_width), jnp.float32), identity)
    blocks = (
        to_blocks(queries),
        to_blocks(keys_in),
        to_blocks(values),
        to_blocks(strength[..., None]),
        carry_on,
    )
    (memory, mapping), (out_zero, q_prop) = lax.scan(block_step, initial, blocks)
    return (from_blocks(out_zero), from_blocks(q_prop), mapping, memory)


def span_forward(raw, conv_weight, out_gain, strength, taps, carry_on):
    tok_count = raw.shape[1]
    seq_count = lax.axis_size("seq")
    own_index = lax.axis_index("seq")
    head_count = conv_weight.shape[2] // HDIM
    rims = passed_along(raw[:, tok_count - KERNEL + 1 :, :], "seq", 1)
    extended = jnp.concatenate([rims, raw], axis=1).astype(jnp.float32)
    conv_sum = jnp.zeros(raw.shape, jnp.float32)
    for shift_no in range(KERNEL):
        window = extended[:, KERNEL - 1 - shift_no : KERNEL - 1 - shift_no + tok_count]
        conv_sum = (
            conv_sum
            + conv_weight[:, shift_no][:, None, :]
            * window
            * taps[shift_no][:tok_count][None, :, None]
        )
    conv_sig = jax.nn.sigmoid(conv_sum)
    split_heads = (
        (conv_sum * conv_sig).reshape(3, tok_count, head_count, HDIM).transpose(0, 2, 1, 3)
    )
    q_scale = lax.rsqrt(jnp.sum(split_heads[0] * split_heads[0], axis=-1, keepdims=True) + EPSILON)
    q_unit = split_heads[0] * q_scale
    queries = q_unit * HDIM ** (-0.5)
    k_scale = lax.rsqrt(jnp.sum(split_heads[1] * split_heads[1], axis=-1, keepdims=True) + EPSILON)
    keys_in = split_heads[1] * k_scale
    values = split_heads[2]
    (out_zero, q_prop, span_map, span_state), span_pullback = jax.vjp(
        partial(local_span, carry_on), queries, keys_in, values, strength.T
    )
    empty_state = jnp.zeros_like(span_state)
    all_maps, all_states = (
        lax.all_gather(span_map[None].astype(jnp.bfloat16), "seq", axis=0, tiled=True).astype(
            jnp.float32
        ),
        lax.all_gather(span_state[None].astype(jnp.bfloat16), "seq", axis=0, tiled=True).astype(
            jnp.float32
        ),
    )

    def fold_forward(counter, incoming):
        moved = (
            jnp.einsum("hpq,hqv->hpv", all_maps[counter], incoming, precision=PRECISE)
            + all_states[counter]
        )
        return jnp.where(counter < own_index, moved, incoming)

    state_in = lax.fori_loop(0, seq_count, fold_forward, empty_state)
    mixer = out_zero + jnp.einsum("htp,hpv->htv", q_prop, state_in, precision=PRECISE)
    stat_out = lax.rsqrt(jnp.mean(mixer * mixer, axis=-1, keepdims=True) + EPSILON)
    unit_out = mixer * stat_out
    normed_out = (
        (unit_out * out_gain).transpose(1, 0, 2).reshape(tok_count, -1).astype(jnp.bfloat16)
    )

    def pullback(grad_normed_out):
        grad_normed_out = grad_normed_out.astype(jnp.float32)
        grad_normed_out = grad_normed_out.reshape(tok_count, head_count, HDIM).transpose(1, 0, 2)
        out_gain_part = jnp.sum(grad_normed_out * unit_out, axis=(0, 1))
        grad_unit_out = grad_normed_out * out_gain
        grad_mixer = stat_out * (
            grad_unit_out - unit_out * jnp.mean(grad_unit_out * unit_out, axis=-1, keepdims=True)
        )
        local_grad = jnp.einsum("htp,htv->hpv", q_prop, grad_mixer, precision=PRECISE)
        grad_q_prop = jnp.einsum("htv,hpv->htp", grad_mixer, state_in, precision=PRECISE)
        all_grads = lax.all_gather(
            local_grad[None].astype(jnp.bfloat16), "seq", axis=0, tiled=True
        ).astype(jnp.float32)

        def fold_backward(counter, later_grad):
            source = seq_count - 1 - counter
            moved = (
                jnp.einsum("hqp,hqv->hpv", all_maps[source], later_grad, precision=PRECISE)
                + all_grads[source]
            )
            return jnp.where(source > own_index, moved, later_grad)

        grad_end = lax.fori_loop(0, seq_count, fold_backward, empty_state)
        grad_map = jnp.einsum("hpv,hqv->hpq", grad_end, state_in, precision=PRECISE)
        grad_queries, grad_keys, grad_values, grad_strength = span_pullback(
            (grad_mixer, grad_q_prop, grad_map, grad_end)
        )
        grad_q_unit = grad_queries * HDIM ** (-0.5)
        grad_q_raw = q_scale * (
            grad_q_unit - q_unit * jnp.sum(grad_q_unit * q_unit, axis=-1, keepdims=True)
        )
        grad_k_raw = k_scale * (
            grad_keys - keys_in * jnp.sum(grad_keys * keys_in, axis=-1, keepdims=True)
        )
        grad_act = (
            jnp.stack([grad_q_raw, grad_k_raw, grad_values])
            .transpose(0, 2, 1, 3)
            .reshape(3, tok_count, -1)
        )
        grad_conv_sum = grad_act * conv_sig * (1.0 + conv_sum * (1.0 - conv_sig))
        rims_back = passed_along(grad_conv_sum[:, : KERNEL - 1, :], "seq", -1)
        grad_ext = jnp.concatenate([grad_conv_sum, rims_back], axis=1)
        grad_raw = jnp.zeros(grad_conv_sum.shape, jnp.float32)
        conv_terms = []
        for shift_no in range(KERNEL):
            grad_raw = (
                grad_raw
                + conv_weight[:, shift_no][:, None, :]
                * grad_ext[:, shift_no : shift_no + tok_count]
                * taps[shift_no][shift_no : shift_no + tok_count][None, :, None]
            )
            window = extended[:, KERNEL - 1 - shift_no : KERNEL - 1 - shift_no + tok_count]
            conv_terms.append(
                jnp.sum(grad_conv_sum * window * taps[shift_no][:tok_count][None, :, None], axis=1)
            )
        grad_conv_part = jnp.stack(conv_terms, axis=1)
        return grad_raw.astype(jnp.bfloat16), grad_strength.T, grad_conv_part, out_gain_part

    return normed_out, pullback


def head_forward(raw, conv_weight, out_gain, strength, starts):
    width = conv_weight.shape[2] // lax.axis_size("seq")
    own_index = lax.axis_index("seq")

    def to_heads(block, axis, concat):
        return lax.all_to_all(block, "seq", split_axis=axis, concat_axis=concat, tiled=True)

    raw = to_heads(raw, 2, 1)
    own_conv = lax.dynamic_slice_in_dim(conv_weight, own_index * width, width, axis=2)
    cols = make_cols(starts, to_heads(strength, 1, 0))
    gain = out_gain[None, :]
    normed_out, *saved = forward(raw, own_conv, gain, cols, 2)

    def pullback(grad_normed_out):
        grad_raw, grad_strength, grad_conv, grad_gain = backward(
            raw, own_conv, gain, cols, to_heads(grad_normed_out, 1, 0), *saved, 2
        )
        grad_conv_part = lax.dynamic_update_slice_in_dim(
            jnp.zeros_like(conv_weight), grad_conv, own_index * width, axis=2
        )
        return to_heads(grad_raw, 1, 2), to_heads(grad_strength, 0, 1), grad_conv_part, grad_gain[0]

    return to_heads(normed_out, 0, 1), pullback


def shards(
    block_in,
    doc_lengths,
    attn_gain,
    qkv_weight,
    conv_weight,
    beta_weight,
    out_gain,
    out_weight,
    ffn_gain,
    gateup_weight,
    down_weight,
    cotangent,
):
    tok_count = block_in.shape[1]
    seq_count = lax.axis_size("seq")
    own_index = lax.axis_index("seq")
    head_count = conv_weight.shape[2] // HDIM
    residual_in = block_in[0].astype(jnp.float32)
    stat_in = lax.rsqrt(jnp.mean(residual_in * residual_in, axis=-1, keepdims=True) + EPSILON)
    unit_in = residual_in * stat_in
    normed = (unit_in * attn_gain).astype(jnp.bfloat16)
    gather = lambda weight: lax.all_gather(weight, ("seq", "row"), axis=1, tiled=True)
    qkv_full, beta_full, out_full, gateup_full, down_full = (
        gather(qkv_weight),
        gather(beta_weight),
        gather(out_weight),
        gather(gateup_weight),
        gather(down_weight),
    )
    raw = jnp.einsum("td,sdc->stc", normed, qkv_full, preferred_element_type=jnp.float32).astype(
        jnp.bfloat16
    )
    logits = jnp.einsum("td,hd->th", normed, beta_full, preferred_element_type=jnp.float32)
    beta_sig = jax.nn.sigmoid(logits)
    if head_count % seq_count == 0 and seq_count * tok_count % (2 * CHUNK) == 0:
        positions = jnp.arange(seq_count * tok_count, dtype=jnp.int32)
        doc_start, real_row = row_layout(doc_lengths[0], positions)
        real_mask = lax.dynamic_slice_in_dim(real_row, own_index * tok_count, tok_count)[:, None]
        starts = (doc_start[::BLOCK] != positions[::BLOCK]).astype(jnp.float32)
        normed_out, mixer_pullback = head_forward(
            raw, conv_weight, out_gain, beta_sig * real_mask, starts
        )
    else:
        positions = own_index * tok_count + jnp.arange(tok_count + KERNEL - 1, dtype=jnp.int32)
        doc_start, real_ext = row_layout(doc_lengths[0], positions)
        real_mask = real_ext[:tok_count, None]
        taps = [(positions - shift_no >= doc_start).astype(jnp.float32) for shift_no in range(KERNEL)]
        carry_on = (doc_start[:tok_count:BLOCK] != positions[:tok_count:BLOCK]).astype(jnp.float32)
        normed_out, mixer_pullback = span_forward(
            raw, conv_weight, out_gain, beta_sig * real_mask, taps, carry_on
        )
    branch_part = jnp.dot(normed_out, out_full, preferred_element_type=jnp.float32)
    hidden = residual_in + lax.psum(branch_part.astype(jnp.bfloat16), "mp").astype(jnp.float32)
    stat_mid = lax.rsqrt(jnp.mean(hidden * hidden, axis=-1, keepdims=True) + EPSILON)
    unit_mid = hidden * stat_mid
    normed_mid = (unit_mid * ffn_gain).astype(jnp.bfloat16)
    gate_up = jnp.einsum("td,sdf->stf", normed_mid, gateup_full, preferred_element_type=jnp.float32)
    gate_sig = jax.nn.sigmoid(gate_up[0])
    product = (gate_up[0] * gate_sig * gate_up[1]).astype(jnp.bfloat16)
    ffn_part = jnp.dot(product, down_full, preferred_element_type=jnp.float32)
    block_out = hidden + lax.psum(ffn_part.astype(jnp.bfloat16), "mp").astype(jnp.float32)
    grad_top = cotangent[0]
    grad_down_part = jnp.dot(product.T, grad_top, preferred_element_type=jnp.float32)
    grad_product = jnp.dot(grad_top, down_full.T, preferred_element_type=jnp.float32)
    grad_gate = grad_product * gate_up[1] * gate_sig * (1.0 + gate_up[0] * (1.0 - gate_sig))
    grad_up = grad_product * gate_up[0] * gate_sig
    grad_gate_up = jnp.stack([grad_gate, grad_up]).astype(jnp.bfloat16)
    grad_gateup_part = jnp.einsum(
        "td,stf->sdf", normed_mid, grad_gate_up, preferred_element_type=jnp.float32
    )
    grad_mid_part = jnp.einsum(
        "stf,sdf->td", grad_gate_up, gateup_full, preferred_element_type=jnp.float32
    )
    grad_mid = lax.psum(grad_mid_part.astype(jnp.bfloat16), "mp").astype(jnp.float32)
    ffn_gain_part = jnp.sum(grad_mid * unit_mid, axis=0)
    grad_unit_mid = grad_mid * ffn_gain
    grad_hidden = grad_top.astype(jnp.float32) + stat_mid * (
        grad_unit_mid - unit_mid * jnp.mean(grad_unit_mid * unit_mid, axis=-1, keepdims=True)
    )
    grad_branch = grad_hidden.astype(jnp.bfloat16)
    grad_out_part = jnp.dot(normed_out.T, grad_branch, preferred_element_type=jnp.float32)
    grad_normed_out = jnp.dot(grad_branch, out_full.T, preferred_element_type=jnp.float32)
    grad_raw_low, grad_strength, grad_conv_part, out_gain_part = mixer_pullback(
        grad_normed_out.astype(jnp.bfloat16)
    )
    grad_logits = (grad_strength * real_mask * beta_sig * (1.0 - beta_sig)).astype(jnp.bfloat16)
    grad_beta_part = jnp.einsum(
        "th,td->hd", grad_logits, normed, preferred_element_type=jnp.float32
    )
    grad_qkv_part = jnp.einsum(
        "td,stc->sdc", normed, grad_raw_low, preferred_element_type=jnp.float32
    )
    grad_normed = jnp.einsum(
        "stc,sdc->td", grad_raw_low, qkv_full, preferred_element_type=jnp.float32
    )
    grad_normed = grad_normed + jnp.einsum(
        "th,hd->td", grad_logits, beta_full, preferred_element_type=jnp.float32
    )
    grad_normed, out_gain_sum = (
        lax.psum(grad_normed.astype(jnp.bfloat16), "mp").astype(jnp.float32),
        lax.psum(out_gain_part, "mp"),
    )
    attn_gain_part = jnp.sum(grad_normed * unit_in, axis=0)
    grad_unit_in = grad_normed * attn_gain
    grad_input = grad_hidden + stat_in * (
        grad_unit_in - unit_in * jnp.mean(grad_unit_in * unit_in, axis=-1, keepdims=True)
    )

    def scatter(part):
        part = part.astype(jnp.bfloat16)
        part = lax.psum_scatter(part, ("seq", "row"), scatter_dimension=1, tiled=True)
        return part.astype(jnp.float32)

    weight_sums = (
        scatter(grad_qkv_part),
        scatter(grad_beta_part),
        scatter(grad_out_part),
        scatter(grad_gateup_part),
        scatter(grad_down_part),
    )
    small_sums = lax.psum(
        (attn_gain_part, grad_conv_part, out_gain_sum, ffn_gain_part), ("seq", "row")
    )
    return (
        block_out.astype(jnp.bfloat16)[None],
        grad_input[None],
        small_sums[0],
        weight_sums[0],
        small_sums[1],
        weight_sums[1],
        small_sums[2],
        weight_sums[2],
        small_sums[3],
        weight_sums[3],
        weight_sums[4],
    )


def solution(mesh):
    return jax.shard_map(
        shards,
        mesh=mesh,
        in_specs=(
            P("row", "seq", None),
            P("row", None),
            P(),
            P(None, ("seq", "row"), "mp"),
            P(None, None, "mp"),
            P("mp", ("seq", "row")),
            P(),
            P("mp", ("seq", "row")),
            P(),
            P(None, ("seq", "row"), "mp"),
            P("mp", ("seq", "row")),
            P("row", "seq", None),
        ),
        out_specs=(
            P("row", "seq", None),
            P("row", "seq", None),
            P(),
            P(None, ("seq", "row"), "mp"),
            P(None, None, "mp"),
            P("mp", ("seq", "row")),
            P(),
            P("mp", ("seq", "row")),
            P(),
            P(None, ("seq", "row"), "mp"),
            P("mp", ("seq", "row")),
        ),
        check_vma=False,
    )
```

time: 3430 us -> 1440 us (0.42)
  other arithmetic: 820 us -> 49.6 us
  matrix products: 896 us -> 154 us
  waiting for transfers between devices: 1440 us -> 941 us
  Pallas kernels: 0 us -> 103 us
  local copies, waits for them, and re-layouts: 158 us -> 62.3 us
    dot_general x506 -> x3, matrix products: 703 us -> 10.1 us  [the longest x1 3.49 us: shards(): jnp.einsum('td,hd->th', normed, beta_full, preferred_element_type=jnp.flo...]
    another operation x138 -> x1, other arithmetic: 649 us -> 0.18 us  [the longest x128 648 us: block_step(): lax.linalg.triangular_solve(system, right_side, left_side=True, lower=Tru...]
    reduce_scatter x4, waiting for transfers between devices: 955 us -> 384 us  [scatter(): lax.psum_scatter(part, ('seq', 'row'), scatter_dimension=1, tiled=True)]
    pallas_call x0 -> x2, Pallas kernels: none -> 103 us  [the longest x1 68.1 us: forward(): pl.pallas_call(functools.partial(fwd_kernel, heads, group), grid=(n // ro...]
    psum x1, waiting for transfers between devices: 113 us -> 175 us  [shards(): lax.psum(ffn_part.astype(jnp.bfloat16), 'mp').astype(jnp.float32)]
    dynamic_slice x64 -> x1, local copies, waits for them, and re-layouts: 45 us -> 0.01 us  [head_forward(): lax.dynamic_slice_in_dim(conv_weight, own_index * width, width, axis=2)]
    dynamic_update_slice x32 -> x0, other arithmetic: 35.9 us -> none  [local_span(): lax.scan(block_step, initial, blocks)]
    reduce_sum x21 -> x0, other arithmetic: 35.8 us -> none  [the longest x16 16.9 us: block_step(): write_rate[..., None] * k_blk]
  transfers between devices with their start and end apart: 14 -> 14, of which waited for: 10 -> 10; matrix products, arithmetic and copies ran while one was open for 26% -> 13% of each run, Pallas kernels for 0% -> 5%
where the time goes in v1:
time: 1440 us; the launch traced here: 1430 us
  waiting for transfers between devices  941 us (65%)
  matrix products  154 us (11%)
  Pallas kernels  103 us (7%)
  blocking collectives  95.2 us (7%)
  local copies, waits for them, and re-layouts  62.3 us (4%)
  other arithmetic  49.6 us (3%)
  between operations  14.8 us (1%)
    reduce_scatter x4, waiting for transfers between devices, scatter(): lax.psum_scatter(part, ('seq', 'row'), scatter_dimension=1, tiled=True)  384 us
    psum x1, waiting for transfers between devices, shards(): lax.psum(ffn_part.astype(jnp.bfloat16), 'mp').astype(jnp.float32)  175 us
    all_gather x4, waiting for transfers between devices, shards(): lax.all_gather(weight, ('seq', 'row'), axis=1, tiled=True)  174 us
    psum x1, waiting for transfers between devices, shards(): lax.psum(grad_mid_part.astype(jnp.bfloat16), 'mp').astype(jnp.float32)  102 us
    psum x1, waiting for transfers between devices, shards(): lax.psum(branch_part.astype(jnp.bfloat16), 'mp').astype(jnp.float32)  101 us
    pallas_call x1, Pallas kernels, forward(): pl.pallas_call(functools.partial(fwd_kernel, heads, group), grid=(n // ro...  68.1 us
    pallas_call x1, Pallas kernels, backward(): pl.pallas_call(functools.partial(bwd_kernel, heads, group), grid=(steps,)...  35.1 us
    psum x1, blocking collectives, shards(): lax.psum((attn_gain_part, grad_conv_part, out_gain_sum, ffn_gain_part), (...  34 us
  transfers between devices with their start and end apart: 14, of which 10 were waited for; matrix products, arithmetic and copies ran while one was open for 13% of the time, Pallas kernels for 5%

profile of v1, /device:TPU:0, one launch (start us, length us, event | category | flops | bytes accessed | tf_op | source)
XLA Modules:
  0.0 1429.0 jit_solution(1996227435100926707)
XLA Ops:
  8.8 22.9 %all_gather.16 = bf16[4,2048]{1,0:T(4,128)(2,1)S(1)} all-gather(bf16[4,256]{1,0:T(4,128)(2,1)} %param.17), channel_id=1, replica_groups=mesh['seq'=2,'mp'=4,'row'=4] {'seq','row'}, dimensions={1}, use_global_device_ids=true | all-gather | bytes 18432 | tf_op jit(solution)/shard_map/all_gather | solution.py:473
  32.5 3.1 fusion.20
  35.6 3.5 broadcast_multiply_fusion
  39.7 3.2 all-to-all-start.1
  47.2 1.3 copy.66.cols_ref
  48.6 28.6 %all-gather.5.cloned.1.call-done = bf16[3,2048,512]{2,1,0:T(8,128)(2,1)} async-done(((bf16[3,256,512]{2,1,0:T(8,128)(2,1)}), bf16[3,2048,512]{2,1,0:T(8,128)(2,1)}) %all-gather.5.cloned.1.call-update) | async-done | bytes 6291472 | tf_op jit(solution)/shard_map/all_gather | solution.py:473
  77.2 10.5 convert_bitcast_fusion.3
  87.7 5.5 copy.64
  93.2 12.3 all_to_all.112
  105.5 7.2 copy.65
  112.7 68.1 %shard_map.203 = (bf16[2048,256]{1,0:T(8,128)(2,1)S(1)}, f32[2048,256]{1,0:T(8,128)}, bf16[16,2,128,128]{3,2,1,0:T(8,128)(2,1)S(1)}, bf16[16,2,128,128]{3,2,1,0:...) custom-call(bf16[3,2048,256]{2,1,0:T(8,128)(2,1)} %bitcast.226, ...), custom_call_target="tpu_custom_call" | custom-call | tf_op jit(solution)/shard_map/pallas_call | solution.py:104
  180.8 1.0 copy-done.3
  181.8 1.0 copy-done.4
  182.8 1.3 copy.67
  184.1 3.6 all-to-all-start.2
  187.9 1.9 all-to-all-done.2
  189.8 6.4 convolution_convert_fusion.2
  197.4 101.3 %all-reduce.8.cloned.1.call-done = bf16[1024,2048]{1,0:T(8,128)(2,1)} async-done(((bf16[1024,2048]{1,0:T(8,128)(2,1)}), bf16[1024,2048]{1,0:T(8,128)(2,1)}) %all-reduce.8.cloned.1.call-update) | async-done | bytes 4194320 | tf_op jit(solution)/shard_map/psum | solution.py:504
  298.7 4.9 multiply_reduce_fusion
  303.6 104.8 %all-gather.9.cloned.1.call-done = bf16[2,2048,1408]{2,1,0:T(8,128)(2,1)} async-done(((bf16[2,256,1408]{2,1,0:T(8,128)(2,1)}), bf16[2,2048,1408]{2,1,0:T(8,128)(2,1)}) %all-gather.9.cloned.1.call-update) | async-done | bytes 11534352 | tf_op jit(solution)/shard_map/all_gather | solution.py:473
  408.3 20.1 %convolution_bitcast_fusion = f32[2,1024,1408]{2,1,0:T(8,128)} fusion(bf16[2,2048,1408]{2,1,0:T(8,128)(2,1)} %all-gather.9.cloned.1.call-done, bf16[1024,2048]{1,0:T(8,128)(2,1)} %all-reduce.8.cloned.1.call-done, bf16[1,1024,2048]{2,1,0:T(8,128)(2,1)} %param.12, f32[2048]{0:T(1024)S(1)} %copy-done.17, f32[1024]{0:T(1024)S(1)} %add_rsqrt_fusion), kind=kOutput, calls=%fused_computation.37 | convolution fusion | flops 11823742976 | bytes 31469568 | tf_op jit(solution)/shard_map/td,sdf->stf/dot_general | solution.py:508
  428.5 40.6 %all-gather.11.cloned.1.call-done = bf16[1408,2048]{1,0:T(8,128)(2,1)} async-done(((bf16[1408,256]{1,0:T(8,128)(2,1)}), bf16[1408,2048]{1,0:T(8,128)(2,1)}) %all-gather.11.cloned.1.call-update) | async-done | bytes 5767184 | tf_op jit(solution)/shard_map/all_gather | solution.py:473
  469.0 14.1 fusion.49
  483.1 1.6 copy-done.21
  484.8 0.9 copy-done.23
  485.6 16.3 %bitcast_convert_fusion = bf16[1024,2048]{1,0:T(8,128)(2,1)} fusion(bf16[2,2048,1408]{2,1,0:T(8,128)(2,1)} %all-gather.9.cloned.1.call-done, bf16[1,1024,1408]{2,1,0:T(8,128)(2,1)S(1)} %get-tuple-element.88, bf16[1,1024,1408]{2,1,0:T(8,128)(2,1)S(1)} %get-tuple-element.87), kind=kOutput, calls=%fused_computation.31 | convolution fusion | flops 11816140800 | bytes 21495808 | tf_op jit(solution)/shard_map/stf,sdf->td/dot_general | solution.py:522
  502.0 102.2 %all-reduce.10.cloned.1.call-done = bf16[1024,2048]{1,0:T(8,128)(2,1)} async-done(((bf16[1024,2048]{1,0:T(8,128)(2,1)}), bf16[1024,2048]{1,0:T(8,128)(2,1)}) %all-reduce.10.cloned.1.call-update) | async-done | bytes 4194320 | tf_op jit(solution)/shard_map/psum | solution.py:525
  604.2 8.0 fusion.16
  612.5 7.0 fusion.15
  619.5 3.7 fusion.55
  623.2 2.3 copy.68
  625.5 5.7 all_to_all.113
  631.2 35.1 %shard_map.204 = (bf16[3,2048,256]{2,1,0:T(8,128)(2,1)}, f32[2048,2]{1,0:T(8,128)S(1)}, f32[3,4,256]{2,1,0:T(4,128)S(1)}, f32[1,128]{1,0:T(1,128)S(1)}) custom-call(bf16[3,2048,256]{2,1,0:T(8,128)(2,1)} %bitcast.227, bf16[3,2048,256]{2,1,0:T(8,128)(2,1)} %bitcast.228, f32[3,4,256]{2,1,0:T(4,128)S(1)} %constant_dynamic-slice_fusion.cw_ref, ...), custom_call_target="tpu_custom_call" | custom-call | tf_op jit(solution)/shard_map/pallas_call | solution.py:204
  666.3 1.0 copy-done.5
  667.3 1.6 copy.72
  668.9 3.7 all_to_all.114
  672.7 3.3 convolution_convert_fusion.4
  676.0 1.1 copy.79
  677.5 7.1 convolution_convert_fusion.3
  684.7 13.3 convolution_convert_fusion
  698.1 12.8 convolution_convert_fusion.1
  710.8 15.9 %copy.70 = bf16[3,2048,256]{2,0,1:T(4,128)(2,1)S(1)} copy(bf16[3,2048,256]{2,1,0:T(8,128)(2,1)S(1)} %copy-done.11) | data formatting | bytes 6291456 | tf_op jit(solution)/shard_map/pallas_call | solution.py:204
  726.7 7.3 all_to_all.115
  734.0 3.8 copy.82
  737.8 3.8 all_to_all.101
  741.6 9.8 fusion.76
  751.4 3.3 fusion.23
  754.8 1.8 copy-done.12
  756.6 11.6 convert_bitcast_fusion.2
  768.5 1.5 copy-done.22
  770.0 18.7 %convert_bitcast_fusion = bf16[2,2048,1408]{1,2,0:T(8,128)(2,1)} fusion(bf16[1,1024,1408]{2,1,0:T(8,128)(2,1)} %copy-done.23, bf16[1,1024,1408]{2,1,0:T(8,128)(2,1)S(1)} %copy-done.22, bf16[1024,2048]{1,0:T(8,128)(2,1)} %all-reduce.8.cloned.1.call-done, bf16[1,1024,2048]{2,1,0:T(8,128)(2,1)} %param.12, f32[2048]{0:T(1024)S(1)} %copy-done.17, ...), kind=kOutput, calls=%fused_computation | convolution fusion | flops 11832393728 | bytes 25702400 | tf_op jit(solution)/shard_map/td,stf->sdf/dot_general | solution.py:519
  788.7 9.3 psum.69
  798.1 0.9 copy.80
  799.6 1.8 convert_element_type.147
  801.4 78.5 %reduce-scatter.14.cloned.1.call-done = bf16[1408,256]{1,0:T(8,128)(2,1)} async-done(((bf16[1408,2048]{1,0:T(8,128)(2,1)}), bf16[1408,256]{1,0:T(8,128)(2,1)}) %reduce-scatter.14.cloned.1.call-update) | async-done | bytes 720912 | tf_op jit(solution)/shard_map/reduce_scatter | solution.py:562
  879.9 2.3 convert_element_type.154
  882.2 175.3 %all-reduce.12.cloned.1.call-done = (bf16[1024,2048]{1,0:T(8,128)(2,1)}, bf16[1024,2048]{1,0:T(8,128)(2,1)}) async-done(((bf16[1024,2048]{1,0:T(8,128)(2,1)}, bf16[1024,2048]{1,0:T(8,128)(2,1)}), (bf16[1024,2048]{1,0:T(8,128)(2,1)}, bf16[1024,2048]{1,0:T(8,128)(2,1)})) %all-reduce.12.cloned.1.call-update) | async-done | bytes 8388624 | tf_op jit(solution)/shard_map/psum | solution.py:512
  1057.5 5.0 fusion.19
  1062.5 34.0 %all-reduce.2 = (f32[2048]{0:T(1024)}, f32[3,4,512]{2,1,0:T(4,128)}, f32[128]{0:T(128)}, f32[2048]{0:T(1024)}) all-reduce(f32[2048]{0:T(1024)S(1)} %get-tuple-element.77, f32[3,4,512]{2,1,0:T(4,128)S(1)} %constant_dynamic-update-slice_fusion, f32[128]{0:T(128)S(1)} %psum.69, ...), channel_id=1, replica_groups=mesh['seq'=2,'mp'=4,'row'=4] {'seq','row'}, use_global_device_ids=true, to_apply=%region_12.13 | all-reduce | flops 10368 | bytes 82944 | tf_op jit(solution)/shard_map/psum | solution.py:572
  1096.5 14.1 fusion.12
  1110.6 79.9 %reduce-scatter.8.cloned.1.call-done = bf16[3,256,512]{1,2,0:T(8,128)(2,1)} async-done(((bf16[3,2048,512]{1,2,0:T(8,128)(2,1)}), bf16[3,256,512]{1,2,0:T(8,128)(2,1)}) %reduce-scatter.8.cloned.1.call-update) | async-done | bytes 786448 | tf_op jit(solution)/shard_map/reduce_scatter | solution.py:562
  1190.5 2.6 copy.75
  1193.0 225.9 %reduce-scatter.12.cloned.1.call-done = bf16[2,256,1408]{1,2,0:T(8,128)(2,1)} async-done(((bf16[2,2048,1408]{1,2,0:T(8,128)(2,1)}), bf16[2,256,1408]{1,2,0:T(8,128)(2,1)}) %reduce-scatter.12.cloned.1.call-update) | async-done | bytes 1441808 | tf_op jit(solution)/shard_map/reduce_scatter | solution.py:562
  1418.9 3.0 copy.76
  (119 shorter events, 10.6 us)
Async XLA Ops:
  7.2 41.4 %copy-start = (f32[3,4,512]{2,1,0:T(4,128)S(1)}, f32[3,4,512]{2,1,0:T(4,128)}, u32[]{:S(2)}) copy-start(f32[3,4,512]{2,1,0:T(4,128)} %param.16) | copy-start | bytes 73732
  7.2 70.0 %all-gather.5.cloned.1.call-start = ((), (), s32[]{:S(2)}) async-start(), calls=%async_computation.11 | async-start | bytes 7077888 | tf_op jit(solution)/shard_map/all_gather | solution.py:473
  31.7 7.4 copy-start.15
  35.6 8.7 copy-start.19
  35.6 41.6 %copy-start.18 = (f32[2048]{0:T(1024)S(1)}, f32[2048]{0:T(1024)}, u32[]{:S(2)}) copy-start(f32[2048]{0:T(1024)} %param.14) | copy-start | bytes 24580
  39.7 7.3 all-to-all-start.1
  43.0 144.9 %all-gather.7.cloned.1.call-start = ((), (), s32[]{:S(2)}) async-start(), calls=%async_computation.12 | async-start | bytes 2359296 | tf_op jit(solution)/shard_map/all_gather | solution.py:473
  105.5 7.2 copy-start.6
  180.8 1.0 copy-start.3
  181.8 1.0 copy-start.4
  184.1 5.7 all-to-all-start.2
  187.7 111.0 %all-reduce.8.cloned.1.call-start = ((), (), s32[]{:S(2)}) async-start(), calls=%async_computation.13 | async-start | bytes 8388608 | tf_op jit(solution)/shard_map/psum | solution.py:504
  189.8 6.4 copy-start.13
  196.1 212.2 %copy-start.17 = (f32[2048]{0:T(1024)S(1)}, f32[2048]{0:T(1024)}, u32[]{:S(2)}) copy-start(f32[2048]{0:T(1024)} %param.20) | copy-start | bytes 24580
  196.2 212.2 %all-gather.9.cloned.1.call-start = ((), (), s32[]{:S(2)}) async-start(), calls=%async_computation.14 | async-start | bytes 12976128 | tf_op jit(solution)/shard_map/all_gather | solution.py:473
  196.7 272.3 %all-gather.11.cloned.1.call-start = ((), (), s32[]{:S(2)}) async-start(), calls=%async_computation.15 | async-start | bytes 6488064 | tf_op jit(solution)/shard_map/all_gather | solution.py:473
  197.3 406.8 %all-reduce.10.cloned.1.call-start = ((), (), s32[]{:S(2)}) async-start(), calls=%async_computation.16 | async-start | bytes 8388608 | tf_op jit(solution)/shard_map/psum | solution.py:525
  483.1 1.7 copy-start.21
  483.1 2.5 copy-start.23
  502.0 296.1 %reduce-scatter.16.cloned.1.call-start = ((), (), s32[]{:S(2)}) async-start(), calls=%async_computation.21 | async-start | bytes 589824
  604.2 8.0 copy-start.7
  604.2 8.1 copy-start.8
  604.2 8.3 copy-start.10
  612.5 7.0 copy-start.20
  619.5 3.7 copy-start.9
  619.5 11.7 copy-start.2
  666.3 1.0 copy-start.5
  667.3 10.3 copy-start.14
  677.1 122.5 %reduce-scatter.10.cloned.1.call-start = ((), (), s32[]{:S(2)}) async-start(), calls=%async_computation.18 | async-start | bytes 2359296 | tf_op jit(solution)/shard_map/reduce_scatter | solution.py:562
  684.6 195.2 %reduce-scatter.14.cloned.1.call-start = ((), (), s32[]{:S(2)}) async-start(), calls=%async_computation.20 | async-start | bytes 6488064 | tf_op jit(solution)/shard_map/reduce_scatter | solution.py:562
  698.0 12.8 copy-start.11
  698.0 359.5 %all-reduce.12.cloned.1.call-start = ((), (), s32[]{:S(2)}) async-start(), calls=%async_computation.22 | async-start | bytes 16777216 | tf_op jit(solution)/shard_map/psum | solution.py:512
  741.6 9.8 copy-start.16
  754.7 1.9 copy-start.12
  754.7 435.8 %reduce-scatter.8.cloned.1.call-start = ((), (), s32[]{:S(2)}) async-start(), calls=%async_computation.17 | async-start | bytes 7077888 | tf_op jit(solution)/shard_map/reduce_scatter | solution.py:562
  768.2 1.8 copy-start.22
  768.2 650.7 %reduce-scatter.12.cloned.1.call-start = ((), (), s32[]{:S(2)}) async-start(), calls=%async_computation.19 | async-start | bytes 12976128 | tf_op jit(solution)/shard_map/reduce_scatter | solution.py:562
  1096.5 325.4 %copy-start.1 = (f32[3,4,512]{2,1,0:T(4,128)S(1)}, f32[3,4,512]{2,1,0:T(4,128)}, u32[]{:S(2)}) copy-start(f32[3,4,512]{2,1,0:T(4,128)} %param.16) | copy-start | bytes 73732
Sparse Core Ops, SparseCore 0:
  9.6 67.5 all-gather.4
  78.8 29.5 all-gather.6
  196.3 102.3 all-reduce.7
  300.2 108.0 all-gather.8
  409.8 59.1 all-gather.10
  502.1 102.0 all-reduce.9
  677.2 32.4 reduce-scatter.15
  712.1 47.9 reduce-scatter.9
  762.6 117.2 reduce-scatter.13
  884.5 172.9 all-reduce.11
  1059.8 130.6 reduce-scatter.7
  1192.6 226.2 reduce-scatter.11

commit v2 on v0

--- a/solution.py
+++ b/solution.py
@@ -1,17 +1,239 @@
+import functools
 from functools import partial
 
 import jax
 import jax.numpy as jnp
 from jax import lax
+from jax.experimental import pallas as pl
+from jax.experimental.pallas import tpu as pltpu
 from jax.sharding import PartitionSpec as P
 
 HDIM = 128
 KERNEL = 4
 BLOCK = 64
-
-
+CHUNK = 128
 EPSILON = 1e-06
 PRECISE = lax.Precision.HIGHEST
+F32 = jnp.float32
+BF16 = jnp.bfloat16
+
+NT=(((1,),(1,)),((),())); NN=(((1,),(0,)),((),())); TN=(((0,),(0,)),((),()))
+
+def mm(a,b,dims=NN):
+    return lax.dot_general(a.astype(BF16), b.astype(BF16), dims, preferred_element_type=F32)
+
+def iotas():
+    return lax.broadcasted_iota(jnp.int32,(CHUNK,CHUNK),0), lax.broadcasted_iota(jnp.int32,(CHUNK,CHUNK),1)
+
+def inverses(below):
+    r,c=iotas()
+    done=[jnp.where(r==c,1.0,0.0)-jnp.where(r//2==c//2,a,0.0) for a in below]
+    size=2
+    while size<CHUNK:
+        pairs=(r//(2*size)==c//(2*size))&(r//size!=c//size)
+        half=[mm(jnp.where(pairs,a,0.0),t) for a,t in zip(below,done)]
+        done=[t-mm(t,x) for t,x in zip(done,half)]
+        size*=2
+    return done
+
+def conv_act(ext_ref, base, lanes, cw, taps):
+    total=cw[0:1]*ext_ref[pl.ds(base+8,CHUNK),lanes]
+    for j in range(1,KERNEL):
+        total=total+(cw[j:j+1]*taps[j-1])*ext_ref[pl.ds(base+8-j,CHUNK),lanes]
+    sig=jax.nn.sigmoid(total)
+    return total,sig
+
+def layout(keep_ref, count_ref, block):
+    r,_=iotas()
+    inside=r%BLOCK
+    first=r<BLOCK
+    keep0,keep1,after=keep_ref[block],keep_ref[block+1],keep_ref[block+2]
+    here=jnp.where(first,keep0,keep1)
+    later=jnp.where(first,keep1,after)
+    taps=[jnp.where(inside<j,here,1.0) for j in range(1,KERNEL)]
+    taps_later=[jnp.where(inside>=BLOCK-j,later,1.0) for j in range(1,KERNEL)]
+    real=jnp.where(inside<jnp.where(first,count_ref[block],count_ref[block+1]),1.0,0.0)
+    return taps,taps_later,jnp.where(first,1.0,keep1),jnp.where(first,keep1,1.0),real,keep0,keep1
+
+def fwd_kernel(heads, group, keep_ref, count_ref, raw_ref, cw_ref, gain_ref, normed_ref, o_ref, s_ref, t_ref, w_ref, r_ref, ext, state):
+    rows=group*CHUNK
+    step=pl.program_id(0)
+    @pl.when(step==0)
+    def _():
+        ext[0:8,:]=jnp.zeros((8,3*heads*HDIM),F32)
+        state[...]=jnp.zeros(state.shape,F32)
+    @pl.when(step>0)
+    def _():
+        ext[0:8,:]=ext[rows:rows+8,:]
+    ext[8:,:]=raw_ref[:,0:3*heads*HDIM].astype(F32)
+    r,c=iotas()
+    width=heads*HDIM
+    units=[]
+    below=[]
+    for g in range(group):
+        base=g*CHUNK
+        taps,_,m,m2,real,keep0,keep1=layout(keep_ref,count_ref,2*(step*group+g))
+        sig_b=jax.nn.sigmoid(raw_ref[pl.ds(base,CHUNK),pl.ds(3*width,HDIM)].astype(F32))*real
+        for h in range(heads):
+            act=[]
+            for s in range(3):
+                lanes=pl.ds(s*width+h*HDIM,HDIM)
+                total,sig=conv_act(ext,base,lanes,cw_ref[:,lanes],taps)
+                act.append(total*sig)
+            q=act[0]*(lax.rsqrt(jnp.sum(act[0]*act[0],axis=1,keepdims=True)+EPSILON)*HDIM**-0.5)
+            k=act[1]*lax.rsqrt(jnp.sum(act[1]*act[1],axis=1,keepdims=True)+EPSILON)
+            v=act[2]
+            b=sig_b[:,h:h+1]
+            gram=mm(k,k,NT)
+            score=mm(q,k,NT)
+            mask=jnp.where(c<BLOCK,m,1.0)
+            a=jnp.where(r>c,b*gram*mask,0.0)
+            l=jnp.where(r>=c,score*mask,0.0)
+            below.append(a)
+            units.append((g,h,q*m,k*m2,l,b*k,b*v,m,keep0,keep1))
+    done=inverses(below)
+    wus=[(mm(t,u[5])*u[7],mm(t,u[6])) for t,u in zip(done,units)]
+    for t,(w,u),(g,h,q,k,l,_,_,_,keep0,keep1) in zip(done,wus,units):
+        base=g*CHUNK
+        out=(pl.ds(base,CHUNK),pl.ds(h*HDIM,HDIM))
+        t_ref[g,h]=t.astype(BF16)
+        w_ref[out]=w.astype(BF16)
+        s=state[h]*keep0
+        s_ref[g,h]=s.astype(BF16)
+        rr=u-mm(w,s)
+        o=mm(q,s)+mm(l,rr)
+        state[h]=s*keep1+mm(k,rr,TN)
+        r_ref[out]=rr.astype(BF16)
+        o_ref[out]=o
+        stat=lax.rsqrt(jnp.mean(o*o,axis=1,keepdims=True)+EPSILON)
+        normed_ref[out]=(o*stat*gain_ref[...]).astype(BF16)
+
+def forward(keep, count, raw, cw, gain, group):
+    n=raw.shape[0]; width=cw.shape[1]//3; heads=width//HDIM; rows=group*CHUNK
+    nc=n//CHUNK
+    row=lambda w: pl.BlockSpec((rows,w),lambda i:(i,0))
+    mat=pl.BlockSpec((group,heads,HDIM,HDIM),lambda i:(i,0,0,0))
+    full=lambda a: pl.BlockSpec(a.shape,lambda i:(0,0))
+    return pl.pallas_call(functools.partial(fwd_kernel,heads,group),
+        grid=(n//rows,),
+        in_specs=[pl.BlockSpec(memory_space=pltpu.SMEM)]*2+[row(raw.shape[1]),full(cw),full(gain)],
+        out_specs=[row(width),row(width),mat,mat,row(width),row(width)],
+        out_shape=[jax.ShapeDtypeStruct((n,width),BF16),jax.ShapeDtypeStruct((n,width),F32),
+            jax.ShapeDtypeStruct((nc,heads,HDIM,HDIM),BF16),jax.ShapeDtypeStruct((nc,heads,HDIM,HDIM),BF16),
+            jax.ShapeDtypeStruct((n,width),BF16),jax.ShapeDtypeStruct((n,width),BF16)],
+        scratch_shapes=[pltpu.VMEM((rows+8,3*width),F32),pltpu.VMEM((heads,HDIM,HDIM),F32)],
+        compiler_params=pltpu.CompilerParams(vmem_limit_bytes=48<<20),
+    )(keep,count,raw,cw,gain)
+
+def bwd_kernel(heads, group, keep_ref, count_ref, raw_ref, prev_ref, cw_ref, gain_ref, gno_ref, o_ref, s_ref, t_ref, w_ref, r_ref,
+               graw_ref, gcw_ref, ggain_ref, ext, gext, grad_state):
+    rows=group*CHUNK
+    step=pl.program_id(0); steps=pl.num_programs(0)
+    width=heads*HDIM
+    @pl.when(step==0)
+    def _():
+        gext[rows:rows+8,:]=jnp.zeros((8,3*heads*HDIM),F32)
+        grad_state[...]=jnp.zeros(grad_state.shape,F32)
+        gcw_ref[...]=jnp.zeros(gcw_ref.shape,F32)
+        ggain_ref[...]=jnp.zeros(ggain_ref.shape,F32)
+    @pl.when(step>0)
+    def _():
+        gext[rows:rows+8,:]=gext[0:8,:]
+    first=jnp.where(step==steps-1,0.0,1.0)
+    ext[0:8,:]=prev_ref[:,0:3*width].astype(F32)[8:16]*first
+    ext[8:,:]=raw_ref[:,0:3*heads*HDIM].astype(F32)
+    r,c=iotas()
+    units=[]
+    for g in range(group-1,-1,-1):
+        base=g*CHUNK
+        taps,taps_later,m,m2,real,keep0,keep1=layout(keep_ref,count_ref,2*((steps-1-step)*group+g))
+        beta=jax.nn.sigmoid(raw_ref[pl.ds(base,CHUNK),pl.ds(3*width,HDIM)].astype(F32))
+        sig_b=beta*real
+        for h in range(heads):
+            out=(pl.ds(base,CHUNK),pl.ds(h*HDIM,HDIM))
+            act=[];tot=[];sigs=[]
+            for s in range(3):
+                lanes=pl.ds(s*width+h*HDIM,HDIM)
+                total,sig=conv_act(ext,base,lanes,cw_ref[:,lanes],taps)
+                act.append(total*sig);tot.append(total);sigs.append(sig)
+            rq=lax.rsqrt(jnp.sum(act[0]*act[0],axis=1,keepdims=True)+EPSILON)
+            rk=lax.rsqrt(jnp.sum(act[1]*act[1],axis=1,keepdims=True)+EPSILON)
+            qu=act[0]*rq
+            o=o_ref[out]
+            stat=lax.rsqrt(jnp.mean(o*o,axis=1,keepdims=True)+EPSILON)
+            uo=o*stat
+            gno=gno_ref[out].astype(F32)
+            ggain_ref[...]+=jnp.sum(gno*uo,axis=0,keepdims=True)
+            gu=gno*gain_ref[...]
+            do=stat*(gu-uo*jnp.mean(gu*uo,axis=1,keepdims=True))
+            units.append(dict(g=g,h=h,base=base,out=out,taps=taps,m=m,m2=m2,keep0=keep0,keep1=keep1,tot=tot,sigs=sigs,
+                rq=rq,rk=rk,qu=qu,q=qu*HDIM**-0.5,k=act[1]*rk,v=act[2],b=sig_b[:,h:h+1],do=do,
+                mask=jnp.where(c<BLOCK,m,1.0)))
+        for u in units[-heads:]: u.update(taps_later=taps_later,beta=beta,sig_b=sig_b)
+    for u in units: u['gram']=mm(u['k'],u['k'],NT)*u['mask']
+    for u in units: u['l']=jnp.where(r>=c,mm(u['q'],u['k'],NT)*u['mask'],0.0)
+    for u in units: u['dr0']=mm(u['l'],u['do'],TN)
+    for u in units: u['ds0']=mm(u['q']*u['m'],u['do'],TN)
+    for u in units:
+        dsn=grad_state[u['h']]
+        u['dsn']=dsn
+        u['dr']=u['dr0']+u['m2']*mm(u['k'],dsn)
+        ds=u['keep1']*dsn+u['ds0']-mm(w_ref[u['out']],u['dr'],TN)
+        grad_state[u['h']]=u['keep0']*ds
+    for u in units: u['df']=mm(t_ref[u['g'],u['h']],u['dr'],TN)
+    for u in units: u['dl']=jnp.where(r>=c,mm(u['do'],r_ref[u['out']],NT)*u['mask'],0.0)
+    for u in units: u['da']=jnp.where(r>c,-mm(u['df'],r_ref[u['out']],NT),0.0)
+    for u in units:
+        u['de']=u['b']*u['df']
+        u['e']=u['v']-u['m']*mm(u['k'],s_ref[u['g'],u['h']])
+        u['gb']=jnp.sum(u['df']*u['e']+u['da']*u['gram'],axis=1,keepdims=True)
+        u['dkk']=u['b']*u['da']*u['mask']
+    for u in units: u['dq']=u['m']*mm(u['do'],s_ref[u['g'],u['h']],NT)+mm(u['dl'],u['k'])
+    for u in units:
+        u['dk']=(mm(u['dl'],u['q'],TN)+u['m2']*mm(r_ref[u['out']],u['dsn'],NT)-u['m']*mm(u['de'],s_ref[u['g'],u['h']],NT)
+            +mm(u['dkk'],u['k'])+mm(u['dkk'],u['k'],TN))
+    for u in units:
+        gq=u['dq']*HDIM**-0.5
+        gq=u['rq']*(gq-u['qu']*jnp.sum(gq*u['qu'],axis=1,keepdims=True))
+        gk=u['rk']*(u['dk']-u['k']*jnp.sum(u['dk']*u['k'],axis=1,keepdims=True))
+        for i,ga in enumerate((gq,gk,u['de'])):
+            lanes=pl.ds(i*width+u['h']*HDIM,HDIM)
+            sig,tot=u['sigs'][i],u['tot'][i]
+            gc=ga*sig*(1.0+tot*(1.0-sig))
+            gext[pl.ds(u['base'],CHUNK),lanes]=gc
+            for j in range(KERNEL):
+                win=ext[pl.ds(u['base']+8-j,CHUNK),lanes]
+                prod=gc*win if j==0 else gc*win*u['taps'][j-1]
+                gcw_ref[j:j+1,lanes]+=jnp.sum(prod,axis=0,keepdims=True)
+    for at in range(0,len(units),heads):
+        glog=jnp.zeros((CHUNK,HDIM),F32)
+        for u in units[at:at+heads]:
+            glog=jnp.where(c==u['h'],u['gb'],glog)
+            for i in range(3):
+                lanes=pl.ds(i*width+u['h']*HDIM,HDIM)
+                cw=cw_ref[:,lanes]
+                total=cw[0:1]*gext[pl.ds(u['base'],CHUNK),lanes]
+                for j in range(1,KERNEL):
+                    total=total+(cw[j:j+1]*u['taps_later'][j-1])*gext[pl.ds(u['base']+j,CHUNK),lanes]
+                graw_ref[pl.ds(u['base'],CHUNK),lanes]=total.astype(BF16)
+        graw_ref[pl.ds(u['base'],CHUNK),pl.ds(3*width,HDIM)]=(glog*u['sig_b']*(1.0-u['beta'])).astype(BF16)
+
+def backward(keep, count, raw, cw, gain, gno, o, s, t, w, r, group):
+    n=raw.shape[0]; width=cw.shape[1]//3; heads=width//HDIM; rows=group*CHUNK
+    steps=n//rows
+    row=lambda w: pl.BlockSpec((rows,w),lambda i:(steps-1-i,0))
+    mat=pl.BlockSpec((group,heads,HDIM,HDIM),lambda i:(steps-1-i,0,0,0))
+    full=lambda a: pl.BlockSpec(a.shape,lambda i:(0,0))
+    prev=pl.BlockSpec((16,raw.shape[1]),lambda i:(jnp.maximum((steps-1-i)*(rows//16)-1,0),0))
+    return pl.pallas_call(functools.partial(bwd_kernel,heads,group),
+        grid=(steps,),
+        in_specs=[pl.BlockSpec(memory_space=pltpu.SMEM)]*2+[row(raw.shape[1]),prev,full(cw),full(gain),row(width),row(width),mat,mat,row(width),row(width)],
+        out_specs=[row(raw.shape[1]),pl.BlockSpec((KERNEL,3*width),lambda i:(0,0)),pl.BlockSpec((1,HDIM),lambda i:(0,0))],
+        out_shape=[jax.ShapeDtypeStruct(raw.shape,BF16),
+            jax.ShapeDtypeStruct((KERNEL,3*width),F32),jax.ShapeDtypeStruct((1,HDIM),F32)],
+        scratch_shapes=[pltpu.VMEM((rows+8,3*width),F32),pltpu.VMEM((rows+8,3*width),F32),pltpu.VMEM((heads,HDIM,HDIM),F32)],
+        compiler_params=pltpu.CompilerParams(vmem_limit_bytes=48<<20),
+    )(keep,count,raw,raw,cw,gain,gno,o,s,t,w,r)
 
 
 def passed_along(block, axis, distance):
@@ -91,7 +313,7 @@
     return (from_blocks(out_zero), from_blocks(q_prop), mapping, memory)
 
 
-def shards(
+def spread_shards(
     block_in,
     doc_lengths,
     attn_gain,
@@ -321,9 +543,247 @@
     )
 
 
+def swapped(block):
+    return lax.ppermute(block, "seq", [(0, 1), (1, 0)])
+
+
+def across(block, bit):
+    return lax.ppermute(block, "mp", [(i, i ^ bit) for i in range(4)])
+
+
+def total_over(part, axis):
+    size = lax.axis_size(axis)
+    bit = 1
+    while bit < size:
+        part = part + lax.ppermute(part, axis, [(i, i ^ bit) for i in range(size)])
+        bit *= 2
+    return part
+
+
+def sum_over_mp(parts):
+    upper, lower = parts[0], parts[1]
+    upper_in = [across(upper[1], 1), across(upper[3], 1)]
+    lower_in = [across(lower[2], 2), across(lower[3], 2)]
+    later = lambda mine, other: (mine.astype(F32) + other.astype(F32)).astype(BF16)
+    upper_last = across(later(upper[2], upper_in[1]), 2)
+    lower_last = across(later(lower[1], lower_in[1]), 1)
+    add = lambda *terms: sum(term.astype(F32) for term in terms)
+    return jnp.stack(
+        [add(upper[0], upper_in[0], upper_last), add(lower[0], lower_in[0], lower_last)]
+    )
+
+
+def gather_over_mp(own):
+    upper, lower = own[0], own[1]
+    upper_one, lower_two = across(upper, 1), across(lower, 2)
+    upper_two, lower_one = across(upper, 2), across(lower, 1)
+    upper_three, lower_three = across(upper_one, 2), across(lower_two, 1)
+    return jnp.stack(
+        [
+            jnp.stack([upper, upper_one, upper_two, upper_three]),
+            jnp.stack([lower, lower_one, lower_two, lower_three]),
+        ]
+    )
+
+
+def reordered(block, own):
+    quarters = block.reshape(4, 2, -1, block.shape[-1])
+    picked = [lax.dynamic_index_in_dim(quarters, own ^ j, 0, keepdims=False) for j in range(4)]
+    return jnp.stack(picked, axis=1)
+
+
+def restored(block, own):
+    picked = [lax.dynamic_index_in_dim(block, own ^ j, 1, keepdims=False) for j in range(4)]
+    return jnp.stack(picked).reshape(-1, block.shape[-1])
+
+
+def in_order(mine, other, core, axis):
+    first = jnp.where(core == 0, mine, other)
+    second = jnp.where(core == 0, other, mine)
+    return jnp.concatenate([first, second], axis=axis)
+
+
+def halves(block, core, axis):
+    size = block.shape[axis] // 2
+    pick = lambda i: lax.dynamic_slice_in_dim(block, i * size, size, axis=axis)
+    return pick(core), pick(1 - core)
+
+
+def joined_shards(
+    block_in,
+    doc_lengths,
+    attn_gain,
+    qkv_weight,
+    conv_weight,
+    beta_weight,
+    out_gain,
+    out_weight,
+    ffn_gain,
+    gateup_weight,
+    down_weight,
+    cotangent,
+):
+    tok_count, model = block_in.shape[1:]
+    core, own = lax.axis_index("seq"), lax.axis_index("mp")
+    width = conv_weight.shape[2] // 2
+    own_heads = width // HDIM
+    quarter = tok_count // 4
+
+    gather = lambda weight: lax.all_gather(weight, ("seq", "row"), axis=1, tiled=True)
+    qkv_full, beta_full = gather(qkv_weight), gather(beta_weight)
+    out_full, gateup_full, down_full = (
+        gather(out_weight),
+        gather(gateup_weight),
+        gather(down_weight),
+    )
+    qkv_own = lax.dynamic_slice_in_dim(qkv_full, core * width, width, axis=2)
+    beta_own = lax.dynamic_slice_in_dim(beta_full, core * own_heads, own_heads, axis=0)
+    mix_weight = jnp.concatenate(
+        [qkv_own[0], qkv_own[1], qkv_own[2], jnp.pad(beta_own.T, ((0, 0), (0, HDIM - own_heads)))],
+        axis=1,
+    )
+    conv_own = lax.dynamic_slice_in_dim(conv_weight, core * width, width, axis=2)
+    conv_own = conv_own.transpose(1, 0, 2).reshape(KERNEL, 3 * width)
+
+    residual_in = block_in[0].astype(F32)
+    stat_in = lax.rsqrt(jnp.mean(residual_in * residual_in, axis=-1, keepdims=True) + EPSILON)
+    normed_mine = (residual_in * stat_in * attn_gain).astype(BF16)
+    normed = in_order(normed_mine, swapped(normed_mine), core, 0)
+
+    positions = jnp.arange(2 * tok_count, dtype=jnp.int32)
+    doc_start, real_row = row_layout(doc_lengths[0], positions)
+    keep = jnp.pad((doc_start[::BLOCK] != positions[::BLOCK]).astype(F32), (0, 1))
+    count = jnp.sum(real_row.reshape(-1, BLOCK), axis=1).astype(jnp.int32)
+    raw = jnp.dot(normed, mix_weight, preferred_element_type=F32).astype(BF16)
+    gain = out_gain[None, :]
+    group = 4 if raw.shape[0] % (4 * CHUNK) == 0 else 1
+    heads_out, *saved = forward(keep, count, raw, conv_own, gain, group)
+
+    mine, other = halves(heads_out, core, 0)
+    normed_out = reordered(in_order(mine, swapped(other), core, 1), own)
+    branch_part = jnp.einsum("hqtc,cd->hqtd", normed_out, out_full, preferred_element_type=F32)
+    branch = sum_over_mp(branch_part.astype(BF16))
+    own_rows = lambda block: lax.dynamic_slice_in_dim(
+        block[0], own * quarter, quarter, axis=0
+    ).reshape(2, -1, model)
+    residual_own = own_rows(block_in).astype(F32)
+    hidden = residual_own + branch
+    stat_mid = lax.rsqrt(jnp.mean(hidden * hidden, axis=-1, keepdims=True) + EPSILON)
+    unit_mid = hidden * stat_mid
+    normed_mid = gather_over_mp((unit_mid * ffn_gain).astype(BF16)).reshape(tok_count, model)
+
+    grad_top = reordered(cotangent[0], own).reshape(tok_count, model)
+    gate_up = jnp.einsum("td,sdf->stf", normed_mid, gateup_full, preferred_element_type=F32)
+    gate_sig = jax.nn.sigmoid(gate_up[0])
+    product = (gate_up[0] * gate_sig * gate_up[1]).astype(BF16)
+    grad_product = jnp.dot(grad_top, down_full.T, preferred_element_type=F32)
+    grad_gate = grad_product * gate_up[1] * gate_sig * (1.0 + gate_up[0] * (1.0 - gate_sig))
+    grad_up = grad_product * gate_up[0] * gate_sig
+    grad_gate_up = jnp.stack([grad_gate, grad_up]).astype(BF16)
+    grad_mid_part = jnp.einsum("stf,sdf->td", grad_gate_up, gateup_full, preferred_element_type=F32)
+    local = lambda part: part.astype(BF16).reshape(2, 4, -1, model)
+    grad_mid = sum_over_mp(local(grad_mid_part))
+    ffn_gain_part = jnp.sum(grad_mid * unit_mid, axis=(0, 1))
+    grad_unit_mid = grad_mid * ffn_gain
+    grad_hidden = own_rows(cotangent).astype(F32) + stat_mid * (
+        grad_unit_mid - unit_mid * jnp.mean(grad_unit_mid * unit_mid, axis=-1, keepdims=True)
+    )
+    grad_branch = gather_over_mp(grad_hidden.astype(BF16))
+    grad_normed_out = jnp.einsum(
+        "hqtd,cd->hqtc", grad_branch, out_full, preferred_element_type=F32
+    ).astype(BF16)
+
+    mine, other = halves(restored(grad_normed_out, own), core, 1)
+    grad_heads = in_order(mine, swapped(other), core, 0)
+    grad_raw, grad_conv_own, out_gain_part = backward(
+        keep, count, raw, conv_own, gain, grad_heads, *saved, group
+    )
+    grad_normed = lax.dot_general(
+        grad_raw, mix_weight, (((1,), (1,)), ((), ())), preferred_element_type=F32
+    )
+    mine, other = halves(grad_normed.astype(BF16), core, 0)
+    grad_normed_sum = (mine.astype(F32) + swapped(other).astype(F32)).astype(BF16)
+    grad_normed = sum_over_mp(reordered(grad_normed_sum, own))
+    stat_own = lax.rsqrt(jnp.mean(residual_own * residual_own, axis=-1, keepdims=True) + EPSILON)
+    unit_in = residual_own * stat_own
+    attn_gain_part = jnp.sum(grad_normed * unit_in, axis=(0, 1))
+    grad_unit_in = grad_normed * attn_gain
+    grad_input = grad_hidden + stat_own * (
+        grad_unit_in - unit_in * jnp.mean(grad_unit_in * unit_in, axis=-1, keepdims=True)
+    )
+    grad_input = restored(gather_over_mp(grad_input.astype(BF16)), own).astype(F32)
+
+    ffn_part = jnp.dot(product, down_full, preferred_element_type=F32)
+    block_out = (hidden + sum_over_mp(local(ffn_part))).astype(BF16)
+    block_out = restored(gather_over_mp(block_out), own)
+
+    def summed(part, axis):
+        mine, other = halves(part.astype(BF16), core, axis)
+        pair = (mine.astype(F32) + swapped(other).astype(F32)).astype(BF16)
+        return lax.psum_scatter(pair, "row", scatter_dimension=axis, tiled=True).astype(F32)
+
+    grad_down = summed(jnp.dot(product.T, grad_top, preferred_element_type=F32), 1)
+    grad_gateup = summed(
+        jnp.einsum("td,stf->sdf", normed_mid, grad_gate_up, preferred_element_type=F32), 1
+    )
+    grad_out = summed(
+        jnp.einsum("hqtc,hqtd->cd", normed_out, grad_branch, preferred_element_type=F32), 1
+    )
+    grad_qkv = lax.dot_general(
+        normed, grad_raw[:, : 3 * width], (((0,), (0,)), ((), ())), preferred_element_type=F32
+    ).astype(BF16)
+    grad_qkv = lax.psum_scatter(
+        grad_qkv.reshape(2, -1, 3 * width), "row", scatter_dimension=1, tiled=True
+    )
+    mine, other = halves(grad_qkv, core, 0)
+    by_kind = lambda part: part[0].reshape(-1, 3, width).transpose(1, 0, 2)
+    grad_qkv = in_order(by_kind(mine), by_kind(swapped(other)), core, 2).astype(F32)
+    grad_beta = lax.dot_general(
+        grad_raw[:, 3 * width :], normed, (((0,), (0,)), ((), ())), preferred_element_type=F32
+    )[:own_heads]
+
+    per_head = jnp.concatenate([grad_conv_own.ravel(), grad_beta.ravel()]).reshape(-1, HDIM)
+    per_head = total_over(per_head, "row")
+    conv_size = grad_conv_own.size // HDIM
+
+    def unpacked(flat):
+        conv = flat[:conv_size].reshape(KERNEL, 3, width).transpose(1, 0, 2)
+        return conv, flat[conv_size:].reshape(own_heads, model)
+
+    conv_mine, beta_mine = unpacked(per_head)
+    conv_other, beta_other = unpacked(swapped(per_head))
+    grad_conv = in_order(conv_mine, conv_other, core, 2)
+    grad_beta = in_order(beta_mine, beta_other, core, 0)
+    span = beta_weight.shape[1]
+    place_no = core * lax.axis_size("row") + lax.axis_index("row")
+    grad_beta = lax.dynamic_slice_in_dim(grad_beta, place_no * span, span, axis=1)
+
+    gains = jnp.concatenate([attn_gain_part, ffn_gain_part, out_gain_part[0]]).reshape(-1, HDIM)
+    for axis in ("mp", "seq", "row"):
+        gains = total_over(gains, axis)
+    gains = gains.ravel()
+    grad_attn_gain, grad_ffn_gain = gains[:model], gains[model : 2 * model]
+    grad_out_gain = gains[2 * model :]
+    return (
+        block_out[None],
+        grad_input[None],
+        grad_attn_gain,
+        grad_qkv,
+        grad_conv,
+        grad_beta,
+        grad_out_gain,
+        grad_out,
+        grad_ffn_gain,
+        grad_gateup,
+        grad_down,
+    )
+
+
 def solution(mesh):
+    rows = mesh.shape["row"]
+    joined = mesh.shape["seq"] == 2 and mesh.shape["mp"] == 4 and rows & (rows - 1) == 0
     return jax.shard_map(
-        shards,
+        joined_shards if joined else spread_shards,
         mesh=mesh,
         in_specs=(
             P("row", "seq", None),

time: 3430 us -> 717 us (0.21)
  waiting for transfers between devices: 1440 us -> 282 us
  matrix products: 896 us -> 135 us
  other arithmetic: 820 us -> 92.9 us
  local copies, waits for them, and re-layouts: 158 us -> 48 us
  starting transfers between devices: 4.51 us -> 67.6 us
  blocking collectives: 74.6 us -> 24.5 us
  Pallas kernels: 0 us -> 47.6 us
    reduce_scatter x4, waiting for transfers between devices: 955 us -> 0.01 us  [the longest x3 0.01 us: summed(): lax.psum_scatter(pair, 'row', scatter_dimension=axis, tiled=True)]
    dot_general x518 -> x13, matrix products: 863 us -> 135 us  [the longest x1 18.7 us: joined_shards(): jnp.einsum('td,sdf->stf', normed_mid, gateup_full, preferred_element_type...]
    another operation x138 -> x27, other arithmetic: 649 us -> 26.6 us  [the longest x11 10.8 us: sum_over_mp(): jnp.stack([add(upper[0], upper_in[0], upper_last), add(lower[0], lower_in...]
    psum x3 -> x0, waiting for transfers between devices: 303 us -> none  [the longest x1 113 us: shards(): lax.psum(ffn_part.astype(jnp.bfloat16), 'mp').astype(jnp.float32)]
    ppermute x2 -> x64, waiting for transfers between devices: 0.01 us -> 205 us  [the longest x48 184 us: across(): return lax.ppermute(block, 'mp', [(i, i ^ bit) for i in range(4)])]
    all_gather x4, waiting for transfers between devices: 179 us -> 75 us  [joined_shards(): lax.all_gather(weight, ('seq', 'row'), axis=1, tiled=True)]
    ppermute x2 -> x64, starting transfers between devices: 3.78 us -> 67.1 us  [the longest x48 58.3 us: across(): return lax.ppermute(block, 'mp', [(i, i ^ bit) for i in range(4)])]
    pallas_call x0 -> x2, Pallas kernels: none -> 47.6 us  [the longest x1 26.9 us: backward(): pl.pallas_call(functools.partial(bwd_kernel, heads, group), grid=(steps,)...]
  transfers between devices with their start and end apart: 14 -> 72, of which waited for: 10 -> 41; matrix products, arithmetic and copies ran while one was open for 26% -> 31% of each run, Pallas kernels for 0% -> 7%
where the time goes in v2:
time: 717 us; the launch traced here: 713 us
  waiting for transfers between devices  282 us (39%)
  matrix products  135 us (19%)
  other arithmetic  92.9 us (13%)
  starting transfers between devices  67.6 us (9%)
  local copies, waits for them, and re-layouts  48 us (7%)
  Pallas kernels  47.6 us (7%)
  blocking collectives  24.5 us (3%)
  between operations  15.7 us (2%)
    ppermute x48, waiting for transfers between devices, across(): return lax.ppermute(block, 'mp', [(i, i ^ bit) for i in range(4)])  184 us
    all_gather x4, waiting for transfers between devices, joined_shards(): lax.all_gather(weight, ('seq', 'row'), axis=1, tiled=True)  75 us
    ppermute x48, starting transfers between devices, across(): return lax.ppermute(block, 'mp', [(i, i ^ bit) for i in range(4)])  58.3 us
    pallas_call x1, Pallas kernels, backward(): pl.pallas_call(functools.partial(bwd_kernel, heads, group), grid=(steps,)...  26.9 us
    all_gather x1, blocking collectives, joined_shards(): lax.all_gather(weight, ('seq', 'row'), axis=1, tiled=True)  24.5 us
    unnamed x121, local copies, waits for them, and re-layouts  22.3 us
    pallas_call x1, Pallas kernels, forward(): pl.pallas_call(functools.partial(fwd_kernel, heads, group), grid=(n // ro...  20.7 us
    dot_general x1, matrix products, joined_shards(): jnp.einsum('td,sdf->stf', normed_mid, gateup_full, preferred_element_type...  18.7 us
  transfers between devices with their start and end apart: 72, of which 41 were waited for; matrix products, arithmetic and copies ran while one was open for 31% of the time, Pallas kernels for 7%

profile of v2, /device:TPU:0, one launch (start us, length us, event | category | flops | bytes accessed | tf_op | source)
XLA Modules:
  0.0 713.1 jit_solution(514382321622300316)
XLA Ops:
  9.5 3.2 fusion.1
  12.9 3.0 fusion.3
  18.6 24.5 %all_gather.16 = bf16[4,2048]{1,0:T(4,128)(2,1)S(1)} all-gather(bf16[4,256]{1,0:T(4,128)(2,1)S(1)} %copy-done.54), channel_id=1, replica_groups=mesh['seq'=2,'mp'=4,'row'=4] {'seq','row'}, dimensions={1}, use_global_device_ids=true | all-gather | bytes 18432 | tf_op jit(solution)/shard_map/all_gather | solution.py:632
  43.5 7.8 %broadcast_select_fusion.1 = (bf16[1024,2048]{1,0:T(8,128)(2,1)}, bf16[1024,2048]{1,0:T(8,128)(2,1)}) fusion(bf16[1024,2048]{1,0:T(8,128)(2,1)} %collective-permute-done, pred[]{:T(512)S(6)} %eq.2, f32[2048]{0:T(1024)S(1)} %copy-done.51, f32[1024]{0:T(1024)S(1)} %add_rsqrt_fusion, bf16[1,1024,2048]{2,1,0:T(8,128)(2,1)} %param.12), kind=kLoop, calls=%fused_computation.59 | loop fusion | flops 12582912 | bytes 16789504 | tf_op jit(solution)/shard_map/jit(_where)/select_n | solution.py:601
  51.3 26.0 %all-gather.5.cloned.1.call-done = bf16[3,2048,512]{2,1,0:T(8,128)(2,1)} async-done(((bf16[3,256,512]{2,1,0:T(8,128)(2,1)}), bf16[3,2048,512]{2,1,0:T(8,128)(2,1)}) %all-gather.5.cloned.1.call-update) | async-done | bytes 6291472 | tf_op jit(solution)/shard_map/all_gather | solution.py:632
  80.5 13.1 %convolution_convert_fusion.5.raw_ref.prev_ref = bf16[2048,896]{1,0:T(8,128)(2,1)} fusion(bf16[1024,2048]{1,0:T(8,128)(2,1)} %get-tuple-element.72, bf16[1024,2048]{1,0:T(8,128)(2,1)S(1)} %copy-done.27, bf16[2048,2]{1,0:T(8,128)(2,1)S(1)} %copy.45, bf16[2048,256]{1,0:T(8,128)(2,1)S(1)} %get-tuple-element.75, bf16[2048,256]{1,0:T(8,128)(2,1)S(1)} %get-tuple-element.74, ...), kind=kOutput, calls=%fused_computation.63 | convolution fusion | flops 7553155072 | bytes 15212544 | tf_op jit(solution)/shard_map/dot_general | solution.py:657
  93.6 20.7 %shard_map.203 = (bf16[2048,256]{1,0:T(8,128)(2,1)S(1)}, f32[2048,256]{1,0:T(8,128)}, bf16[16,2,128,128]{3,2,1,0:T(8,128)(2,1)S(1)}, bf16[16,2,128,128]{3,2,1,0:...) custom-call(f32[33]{0:T(128)S(1)} %pad_convert_fusion.keep_ref, ...), custom_call_target="tpu_custom_call" | custom-call | tf_op jit(solution)/shard_map/pallas_call | solution.py:117
  121.9 4.2 convolution_convert_fusion.4
  131.0 11.1 %collective-permute-done.3 = bf16[128,2048]{1,0:T(8,128)(2,1)S(1)} collective-permute-done((bf16[128,2048]{1,0:T(8,128)(2,1)S(1)}, bf16[128,2048]{1,0:T(8,128)(2,1)S(1)}, u32[]{:S(2)}, u32[]{:S(2)}) %collective-permute-start.3) | collective-permute-done | bytes 524320 | tf_op jit(solution)/shard_map/ppermute | solution.py:551
  144.3 8.4 %collective-permute-done.2 = bf16[128,2048]{1,0:T(8,128)(2,1)S(1)} collective-permute-done((bf16[128,2048]{1,0:T(8,128)(2,1)S(1)}, bf16[128,2048]{1,0:T(8,128)(2,1)S(1)}, u32[]{:S(2)}, u32[]{:S(2)}) %collective-permute-start.2) | collective-permute-done | bytes 524320 | tf_op jit(solution)/shard_map/ppermute | solution.py:551
  152.7 4.5 collective-permute-done.4
  162.0 4.4 collective-permute-done.5
  177.9 6.5 collective-permute-done.12
  184.4 2.8 collective-permute-start.13
  191.3 2.5 pad_maximum_fusion.4
  193.8 8.1 %collective-permute-done.11 = bf16[128,2048]{1,0:T(8,128)(2,1)S(1)} collective-permute-done((bf16[128,2048]{1,0:T(8,128)(2,1)S(1)}, bf16[128,2048]{1,0:T(8,128)(2,1)S(1)}, u32[]{:S(2)}, u32[]{:S(2)}) %collective-permute-start.11) | collective-permute-done | bytes 524320 | tf_op jit(solution)/shard_map/ppermute | solution.py:551
  201.8 5.6 collective-permute-done.13
  210.3 7.1 all-gather.9.cloned.1.call-done
  217.4 18.7 %convolution_bitcast_fusion = f32[2,1024,1408]{2,1,0:T(8,128)} fusion(bf16[1024,2048,1]{1,0,2:T(8,128)(2,1)} %bitcast.406, bf16[2,2048,1408]{2,1,0:T(8,128)(2,1)} %all-gather.9.cloned.1.call-done), kind=kOutput, calls=%fused_computation.15 | convolution fusion | flops 11811160064 | bytes 27262976 | tf_op jit(solution)/shard_map/td,sdf->stf/dot_general | solution.py:676
  236.1 41.9 %all-gather.11.cloned.1.call-done = bf16[1408,2048]{1,0:T(8,128)(2,1)} async-done(((bf16[1408,256]{1,0:T(8,128)(2,1)}), bf16[1408,2048]{1,0:T(8,128)(2,1)}) %all-gather.11.cloned.1.call-update) | async-done | bytes 5767184 | tf_op jit(solution)/shard_map/all_gather | solution.py:632
  278.0 15.2 %fusion.20 = (bf16[1,1024,1408]{2,1,0:T(8,128)(2,1)S(1)}, bf16[1,1024,1408]{2,1,0:T(8,128)(2,1)}) fusion(f32[2,1024,1408]{2,1,0:T(8,128)} %convolution_bitcast_fusion, bf16[1024,2048]{1,0:T(8,128)(2,1)} %bitcast.408, bf16[1408,2048]{1,0:T(8,128)(2,1)} %all-gather.11.cloned.1.call-done), kind=kOutput, calls=%fused_computation.68 | convolution fusion | flops 5924323328 | bytes 27262976 | tf_op jit(solution)/shard_map/dot_general | solution.py:679
  294.8 16.3 %bitcast_convert_fusion = bf16[1024,2048]{1,0:T(8,128)(2,1)S(1)} fusion(bf16[2,2048,1408]{2,1,0:T(8,128)(2,1)} %all-gather.9.cloned.1.call-done, bf16[1,1024,1408]{2,1,0:T(8,128)(2,1)} %get-tuple-element.70, bf16[1,1024,1408]{2,1,0:T(8,128)(2,1)S(1)} %get-tuple-element.69), kind=kOutput, calls=%fused_computation.9 | convolution fusion | flops 11816140800 | bytes 21495808 | tf_op jit(solution)/shard_map/stf,sdf->td/dot_general | solution.py:683
  314.9 11.3 %collective-permute-done.27 = bf16[128,2048]{1,0:T(8,128)(2,1)S(1)} collective-permute-done((bf16[128,2048]{1,0:T(8,128)(2,1)S(1)}, bf16[128,2048]{1,0:T(8,128)(2,1)S(1)}, u32[]{:S(2)}, u32[]{:S(2)}) %collective-permute-start.27) | collective-permute-done | bytes 524320 | tf_op jit(solution)/shard_map/ppermute | solution.py:551
  328.3 8.4 %collective-permute-done.26 = bf16[128,2048]{1,0:T(8,128)(2,1)S(1)} collective-permute-done((bf16[128,2048]{1,0:T(8,128)(2,1)S(1)}, bf16[128,2048]{1,0:T(8,128)(2,1)S(1)}, u32[]{:S(2)}, u32[]{:S(2)}) %collective-permute-start.26) | collective-permute-done | bytes 524320 | tf_op jit(solution)/shard_map/ppermute | solution.py:551
  336.7 4.5 collective-permute-done.28
  344.5 5.7 collective-permute-done.29
  351.6 2.7 fusion.31
  359.0 7.2 %collective-permute-done.36 = bf16[128,2048]{1,0:T(8,128)(2,1)S(1)} collective-permute-done((bf16[128,2048]{1,0:T(8,128)(2,1)S(1)}, bf16[128,2048]{1,0:T(8,128)(2,1)S(1)}, u32[]{:S(2)}, u32[]{:S(2)}) %collective-permute-start.36) | collective-permute-done | bytes 524320 | tf_op jit(solution)/shard_map/ppermute | solution.py:551
  367.7 11.2 %convolution_convert_fusion.1 = bf16[1408,2048]{1,0:T(8,128)(2,1)S(1)} fusion(bf16[1024,2048]{1,0:T(8,128)(2,1)S(1)} %bitcast.409, f32[2,1024,1408]{2,1,0:T(8,128)} %convolution_bitcast_fusion), kind=kOutput, calls=%fused_computation.11 | convolution fusion | flops 5917114368 | bytes 21495808 | tf_op jit(solution)/shard_map/dot_general | solution.py:725
  380.4 2.6 collective-permute-done.32
  385.6 4.3 collective-permute-done.37
  390.1 3.7 collective-permute-done.33
  393.8 5.9 collective-permute-done.34
  402.6 2.6 collective-permute-done.61
  406.9 5.2 fusion.32
  414.3 5.7 add_convert_fusion.1
  420.1 15.9 %convolution_convert_fusion = bf16[2,1408,2048]{2,1,0:T(8,128)(2,1)S(1)} fusion(bf16[1024,2048,1]{1,0,2:T(8,128)(2,1)} %bitcast.407, bf16[1,1024,1408]{2,1,0:T(8,128)(2,1)} %get-tuple-element.70, bf16[1,1024,1408]{2,1,0:T(8,128)(2,1)} %copy-done.57), kind=kOutput, calls=%fused_computation.2 | convolution fusion | flops 11819810816 | bytes 21495808 | tf_op jit(solution)/shard_map/td,stf->sdf/dot_general | solution.py:727
  436.0 4.4 copy-done.20
  440.3 3.2 dynamic-slice_bitcast_fusion
  445.3 26.9 %shard_map.204 = (bf16[2048,896]{1,0:T(8,128)(2,1)}, f32[4,768]{1,0:T(4,128)S(1)}, f32[1,128]{1,0:T(1,128)S(1)}) custom-call(f32[33]{0:T(128)S(1)} %pad_convert_fusion.keep_ref, s32[32]{0:T(128)S(1)} %convert_element_type.332.count_ref, bf16[2048,896]{1,0:T(8,128)(2,1)} %convolution_convert_fusion.5.raw_ref.prev_ref, ...), custom_call_target="tpu_custom_call" | custom-call | tf_op jit(solution)/shard_map/pallas_call | solution.py:228
  472.1 9.2 %convolution_convert_fusion.6 = bf16[2048,768]{1,0:T(8,128)(2,1)S(1)} fusion(bf16[2048,896]{1,0:T(8,128)(2,1)} %get-tuple-element.26, bf16[1024,2048]{1,0:T(8,128)(2,1)S(1)} %copy-done.30, bf16[1024,2048]{1,0:T(8,128)(2,1)S(1)} %copy-done.28), kind=kOutput, calls=%fused_computation.64 | convolution fusion | flops 6460801024 | bytes 14680064 | tf_op jit(solution)/shard_map/dot_general | solution.py:732
  481.4 2.9 copy.35
  484.4 11.5 %convolution_convert_fusion.3 = bf16[1024,2048]{1,0:T(8,128)(2,1)S(1)} fusion(bf16[1408,2048]{1,0:T(8,128)(2,1)} %all-gather.11.cloned.1.call-done, f32[2,1024,1408]{2,1,0:T(8,128)} %convolution_bitcast_fusion), kind=kOutput, calls=%fused_computation.60 | convolution fusion | flops 5916327936 | bytes 21495808 | tf_op jit(solution)/shard_map/dot_general | solution.py:716
  495.9 9.9 %convolution_convert_fusion.2 = bf16[2048,2048]{1,0:T(8,128)(2,1)S(1)} fusion(bf16[2048,896]{1,0:T(8,128)(2,1)S(1)} %copy-done.56, bf16[2048,2]{1,0:T(8,128)(2,1)S(1)} %copy-done.46, bf16[2048,256]{1,0:T(8,128)(2,1)S(1)} %copy-done.44, bf16[2048,256]{1,0:T(8,128)(2,1)S(1)} %copy-done.42, bf16[2048,256]{1,0:T(8,128)(2,1)S(1)} %copy-done.40), kind=kOutput, calls=%fused_computation.12 | convolution fusion | flops 7538737152 | bytes 15212544 | tf_op jit(solution)/shard_map/dot_general | solution.py:701
  505.8 2.9 constant_dynamic-slice_fusion.3
  514.5 11.2 %collective-permute-done.15 = bf16[128,2048]{1,0:T(8,128)(2,1)S(1)} collective-permute-done((bf16[128,2048]{1,0:T(8,128)(2,1)S(1)}, bf16[128,2048]{1,0:T(8,128)(2,1)S(1)}, u32[]{:S(2)}, u32[]{:S(2)}) %collective-permute-start.15) | collective-permute-done | bytes 524320 | tf_op jit(solution)/shard_map/ppermute | solution.py:551
  527.4 9.0 %collective-permute-done.14 = bf16[128,2048]{1,0:T(8,128)(2,1)S(1)} collective-permute-done((bf16[128,2048]{1,0:T(8,128)(2,1)S(1)}, bf16[128,2048]{1,0:T(8,128)(2,1)S(1)}, u32[]{:S(2)}, u32[]{:S(2)}) %collective-permute-start.14) | collective-permute-done | bytes 524320 | tf_op jit(solution)/shard_map/ppermute | solution.py:551
  541.0 9.9 %fusion = bf16[2,1024,1408]{1,2,0:T(8,128)(2,1)} fusion(bf16[2,1024,1408]{1,2,0:T(8,128)(2,1)} %collective-permute-done.62, bf16[2,1408,2048]{2,1,0:T(8,128)(2,1)} %copy-done.20, s32[]{:T(128)S(6)} %select_n.205), kind=kLoop, calls=%fused_computation.1 | loop fusion | flops 11534336 | bytes 17301508 | tf_op jit(solution)/shard_map/convert_element_type | solution.py:722
  554.7 5.5 add_convert_fusion
  561.3 2.7 copy-done.29
  568.8 6.7 collective-permute-done.41
  579.0 5.8 collective-permute-done.59
  586.4 5.9 collective-permute-done.42
  594.6 6.8 collective-permute-done.43
  614.7 2.7 collective-permute-done.53
  617.5 4.6 add_convert_fusion.3
  622.0 3.8 collective-permute-start.55
  633.4 6.8 collective-permute-done.56
  645.2 8.8 %collective-permute-done.50 = bf16[128,2048]{1,0:T(8,128)(2,1)} collective-permute-done((bf16[128,2048]{1,0:T(8,128)(2,1)}, bf16[128,2048]{1,0:T(8,128)(2,1)}, u32[]{:S(2)}, u32[]{:S(2)}) %collective-permute-start.50) | collective-permute-done | bytes 524320 | tf_op jit(solution)/shard_map/ppermute | solution.py:551
  659.3 5.9 collective-permute-done.48
  669.6 6.9 collective-permute-done.24
  681.5 4.5 convert.36
  687.6 10.2 %collective-permute-done.22 = bf16[128,2048]{1,0:T(8,128)(2,1)S(1)} collective-permute-done((bf16[128,2048]{1,0:T(8,128)(2,1)}, bf16[128,2048]{1,0:T(8,128)(2,1)S(1)}, u32[]{:S(2)}, u32[]{:S(2)}) %collective-permute-start.22) | collective-permute-done | bytes 524320 | tf_op jit(solution)/shard_map/ppermute | solution.py:551
  703.1 3.0 copy.40
  (343 shorter events, 154.1 us)
Async XLA Ops:
  7.2 70.1 %all-gather.5.cloned.1.call-start = ((), (), s32[]{:S(2)}) async-start(), calls=%async_computation.4 | async-start | bytes 7077888 | tf_op jit(solution)/shard_map/all_gather | solution.py:632
  7.9 113.9 %all-gather.7.cloned.1.call-start = ((), (), s32[]{:S(2)}) async-start(), calls=%async_computation.5 | async-start | bytes 2359296 | tf_op jit(solution)/shard_map/all_gather | solution.py:632
  8.7 208.7 %all-gather.9.cloned.1.call-start = ((), (), s32[]{:S(2)}) async-start(), calls=%async_computation.6 | async-start | bytes 12976128 | tf_op jit(solution)/shard_map/all_gather | solution.py:632
  9.4 268.6 %all-gather.11.cloned.1.call-start = ((), (), s32[]{:S(2)}) async-start(), calls=%async_computation.7 | async-start | bytes 6488064 | tf_op jit(solution)/shard_map/all_gather | solution.py:632
  16.0 27.6 %collective-permute-start = (bf16[1024,2048]{1,0:T(8,128)(2,1)}, bf16[1024,2048]{1,0:T(8,128)(2,1)}, u32[]{:S(2)}, u32[]{:S(2)}) collective-permute-start(bf16[1024,2048]{1,0:T(8,128)(2,1)} %fusion.3), channel_id=1, source_target_pairs={{0,16},{16,0},{1,17},{17,1},{2,18},{18,2},{3,19},{19,3},{4,20},{20... | collective-permute-start | bytes 12582920 | tf_op jit(solution)/shard_map/ppermute | solution.py:547
  117.4 492.0 %reduce-scatter.7.cloned.1.call-start = ((), (), s32[]{:S(2)}) async-start(), calls=%async_computation.9 | async-start | bytes 1310720 | tf_op jit(solution)/shard_map/reduce_scatter | solution.py:723
  127.3 14.8 %collective-permute-start.3 = (bf16[128,2048]{1,0:T(8,128)(2,1)S(1)}, bf16[128,2048]{1,0:T(8,128)(2,1)S(1)}, u32[]{:S(2)}, u32[]{:S(2)}) collective-permute-start(bf16[128,2048]{1,0:T(8,128)(2,1)S(1)} %get-tuple-element.113), channel_id=1, source_target_pairs={{0,4},{4,0},{8,12},{12,8},{1,5},{5,1},{9,13},{13,9},{2,6},{6,2},{1... | collective-permute-start | bytes 1572872 | tf_op jit(solution)/shard_map/ppermute | solution.py:551
  129.0 23.6 %collective-permute-start.2 = (bf16[128,2048]{1,0:T(8,128)(2,1)S(1)}, bf16[128,2048]{1,0:T(8,128)(2,1)S(1)}, u32[]{:S(2)}, u32[]{:S(2)}) collective-permute-start(bf16[128,2048]{1,0:T(8,128)(2,1)S(1)} %get-tuple-element.110), channel_id=1, source_target_pairs={{0,4},{4,0},{8,12},{12,8},{1,5},{5,1},{9,13},{13,9},{2,6},{6,2},{1... | collective-permute-start | bytes 1572872 | tf_op jit(solution)/shard_map/ppermute | solution.py:551
  129.4 23.3 %collective-permute-start.6 = (bf16[128,2048]{1,0:T(8,128)(2,1)S(1)}, bf16[128,2048]{1,0:T(8,128)(2,1)S(1)}, u32[]{:S(2)}, u32[]{:S(2)}) collective-permute-start(bf16[128,2048]{1,0:T(8,128)(2,1)S(1)} %get-tuple-element.111), channel_id=1, source_target_pairs={{0,8},{4,12},{8,0},{12,4},{1,9},{5,13},{9,1},{13,5},{2,10},{6,14},... | collective-permute-start | bytes 1572872 | tf_op jit(solution)/shard_map/ppermute | solution.py:551
  142.2 14.9 %collective-permute-start.4 = (bf16[128,2048]{1,0:T(8,128)(2,1)S(1)}, bf16[128,2048]{1,0:T(8,128)(2,1)S(1)}, u32[]{:S(2)}, u32[]{:S(2)}) collective-permute-start(bf16[128,2048]{1,0:T(8,128)(2,1)S(1)} %fusion.61), channel_id=1, source_target_pairs={{0,8},{4,12},{8,0},{12,4},{1,9},{5,13},{9,1},{13,5},{2,10},{6,14},... | collective-permute-start | bytes 1572872 | tf_op jit(solution)/shard_map/ppermute | solution.py:551
  143.9 22.4 %collective-permute-start.5 = (bf16[128,2048]{1,0:T(8,128)(2,1)}, bf16[128,2048]{1,0:T(8,128)(2,1)}, u32[]{:S(2)}, u32[]{:S(2)}) collective-permute-start(bf16[128,2048]{1,0:T(8,128)(2,1)} %get-tuple-element.112), channel_id=1, source_target_pairs={{0,8},{4,12},{8,0},{12,4},{1,9},{5,13},{9,1},{13,5},{2,10},{6,14},... | collective-permute-start | bytes 1572872 | tf_op jit(solution)/shard_map/ppermute | solution.py:551
  158.7 10.1 %collective-permute-start.7 = (bf16[128,2048]{1,0:T(8,128)(2,1)}, bf16[128,2048]{1,0:T(8,128)(2,1)}, u32[]{:S(2)}, u32[]{:S(2)}) collective-permute-start(bf16[128,2048]{1,0:T(8,128)(2,1)} %get-tuple-element.109), channel_id=1, source_target_pairs={{0,4},{4,0},{8,12},{12,8},{1,5},{5,1},{9,13},{13,9},{2,6},{6,2},{1... | collective-permute-start | bytes 1572872 | tf_op jit(solution)/shard_map/ppermute | solution.py:551
  174.3 10.1 %collective-permute-start.12 = (bf16[128,2048]{1,0:T(8,128)(2,1)S(1)}, bf16[128,2048]{1,0:T(8,128)(2,1)S(1)}, u32[]{:S(2)}, u32[]{:S(2)}) collective-permute-start(bf16[128,2048]{1,0:T(8,128)(2,1)S(1)} %get-tuple-element.138), channel_id=1, source_target_pairs={{0,8},{4,12},{8,0},{12,4},{1,9},{5,13},{9,1},{13,5},{2,10},{6,14},... | collective-permute-start | bytes 1572872 | tf_op jit(solution)/shard_map/ppermute | solution.py:551
  175.9 14.9 %collective-permute-start.8 = (bf16[128,2048]{1,0:T(8,128)(2,1)S(1)}, bf16[128,2048]{1,0:T(8,128)(2,1)S(1)}, u32[]{:S(2)}, u32[]{:S(2)}) collective-permute-start(bf16[128,2048]{1,0:T(8,128)(2,1)S(1)} %get-tuple-element.137), channel_id=1, source_target_pairs={{0,4},{4,0},{8,12},{12,8},{1,5},{5,1},{9,13},{13,9},{2,6},{6,2},{1... | collective-permute-start | bytes 1572872 | tf_op jit(solution)/shard_map/ppermute | solution.py:551
  177.4 24.4 %collective-permute-start.11 = (bf16[128,2048]{1,0:T(8,128)(2,1)S(1)}, bf16[128,2048]{1,0:T(8,128)(2,1)S(1)}, u32[]{:S(2)}, u32[]{:S(2)}) collective-permute-start(bf16[128,2048]{1,0:T(8,128)(2,1)S(1)} %get-tuple-element.138), channel_id=1, source_target_pairs={{0,4},{4,0},{8,12},{12,8},{1,5},{5,1},{9,13},{13,9},{2,6},{6,2},{1... | collective-permute-start | bytes 1572872 | tf_op jit(solution)/shard_map/ppermute | solution.py:551
  184.4 23.1 %collective-permute-start.13 = (bf16[128,2048]{1,0:T(8,128)(2,1)S(1)}, bf16[128,2048]{1,0:T(8,128)(2,1)S(1)}, u32[]{:S(2)}, u32[]{:S(2)}) collective-permute-start(bf16[128,2048]{1,0:T(8,128)(2,1)S(1)} %collective-permute-done.12), channel_id=1, source_target_pairs={{0,4},{4,0},{8,12},{12,8},{1,5},{5,1},{9,13},{13,9},{2,6},{6,2},{1... | collective-permute-start | bytes 1572872 | tf_op jit(solution)/shard_map/ppermute | solution.py:551
  187.8 20.0 %collective-permute-start.9 = (bf16[128,2048]{1,0:T(8,128)(2,1)S(1)}, bf16[128,2048]{1,0:T(8,128)(2,1)S(1)}, u32[]{:S(2)}, u32[]{:S(2)}) collective-permute-start(bf16[128,2048]{1,0:T(8,128)(2,1)S(1)} %get-tuple-element.137), channel_id=1, source_target_pairs={{0,8},{4,12},{8,0},{12,4},{1,9},{5,13},{9,1},{13,5},{2,10},{6,14},... | collective-permute-start | bytes 1572872 | tf_op jit(solution)/shard_map/ppermute | solution.py:551
  190.8 17.0 %collective-permute-start.10 = (bf16[128,2048]{1,0:T(8,128)(2,1)S(1)}, bf16[128,2048]{1,0:T(8,128)(2,1)S(1)}, u32[]{:S(2)}, u32[]{:S(2)}) collective-permute-start(bf16[128,2048]{1,0:T(8,128)(2,1)S(1)} %collective-permute-done.8), channel_id=1, source_target_pairs={{0,8},{4,12},{8,0},{12,4},{1,9},{5,13},{9,1},{13,5},{2,10},{6,14},... | collective-permute-start | bytes 1572872 | tf_op jit(solution)/shard_map/ppermute | solution.py:551
  311.3 14.8 %collective-permute-start.27 = (bf16[128,2048]{1,0:T(8,128)(2,1)S(1)}, bf16[128,2048]{1,0:T(8,128)(2,1)S(1)}, u32[]{:S(2)}, u32[]{:S(2)}) collective-permute-start(bf16[128,2048]{1,0:T(8,128)(2,1)S(1)} %get-tuple-element.93), channel_id=1, source_target_pairs={{0,4},{4,0},{8,12},{12,8},{1,5},{5,1},{9,13},{13,9},{2,6},{6,2},{1... | collective-permute-start | bytes 1572872 | tf_op jit(solution)/shard_map/ppermute | solution.py:551
  312.8 23.9 %collective-permute-start.26 = (bf16[128,2048]{1,0:T(8,128)(2,1)S(1)}, bf16[128,2048]{1,0:T(8,128)(2,1)S(1)}, u32[]{:S(2)}, u32[]{:S(2)}) collective-permute-start(bf16[128,2048]{1,0:T(8,128)(2,1)S(1)} %get-tuple-element.90), channel_id=1, source_target_pairs={{0,4},{4,0},{8,12},{12,8},{1,5},{5,1},{9,13},{13,9},{2,6},{6,2},{1... | collective-permute-start | bytes 1572872 | tf_op jit(solution)/shard_map/ppermute | solution.py:551
  313.4 23.3 %collective-permute-start.30 = (bf16[128,2048]{1,0:T(8,128)(2,1)S(1)}, bf16[128,2048]{1,0:T(8,128)(2,1)S(1)}, u32[]{:S(2)}, u32[]{:S(2)}) collective-permute-start(bf16[128,2048]{1,0:T(8,128)(2,1)S(1)} %get-tuple-element.91), channel_id=1, source_target_pairs={{0,8},{4,12},{8,0},{12,4},{1,9},{5,13},{9,1},{13,5},{2,10},{6,14},... | collective-permute-start | bytes 1572872 | tf_op jit(solution)/shard_map/ppermute | solution.py:551
  326.2 14.9 %collective-permute-start.28 = (bf16[128,2048]{1,0:T(8,128)(2,1)S(1)}, bf16[128,2048]{1,0:T(8,128)(2,1)S(1)}, u32[]{:S(2)}, u32[]{:S(2)}) collective-permute-start(bf16[128,2048]{1,0:T(8,128)(2,1)S(1)} %add_convert_fusion.5), channel_id=1, source_target_pairs={{0,8},{4,12},{8,0},{12,4},{1,9},{5,13},{9,1},{13,5},{2,10},{6,14},... | collective-permute-start | bytes 1572872 | tf_op jit(solution)/shard_map/ppermute | solution.py:551
  327.8 22.4 %collective-permute-start.29 = (bf16[128,2048]{1,0:T(8,128)(2,1)S(1)}, bf16[128,2048]{1,0:T(8,128)(2,1)S(1)}, u32[]{:S(2)}, u32[]{:S(2)}) collective-permute-start(bf16[128,2048]{1,0:T(8,128)(2,1)S(1)} %get-tuple-element.92), channel_id=1, source_target_pairs={{0,8},{4,12},{8,0},{12,4},{1,9},{5,13},{9,1},{13,5},{2,10},{6,14},... | collective-permute-start | bytes 1572872 | tf_op jit(solution)/shard_map/ppermute | solution.py:551
  341.6 9.5 %collective-permute-start.31 = (bf16[128,2048]{1,0:T(8,128)(2,1)S(1)}, bf16[128,2048]{1,0:T(8,128)(2,1)S(1)}, u32[]{:S(2)}, u32[]{:S(2)}) collective-permute-start(bf16[128,2048]{1,0:T(8,128)(2,1)S(1)} %get-tuple-element.89), channel_id=1, source_target_pairs={{0,4},{4,0},{8,12},{12,8},{1,5},{5,1},{9,13},{13,9},{2,6},{6,2},{1... | collective-permute-start | bytes 1572872 | tf_op jit(solution)/shard_map/ppermute | solution.py:551
  355.4 10.8 %collective-permute-start.36 = (bf16[128,2048]{1,0:T(8,128)(2,1)S(1)}, bf16[128,2048]{1,0:T(8,128)(2,1)S(1)}, u32[]{:S(2)}, u32[]{:S(2)}) collective-permute-start(bf16[128,2048]{1,0:T(8,128)(2,1)S(1)} %get-tuple-element.130), channel_id=1, source_target_pairs={{0,8},{4,12},{8,0},{12,4},{1,9},{5,13},{9,1},{13,5},{2,10},{6,14},... | collective-permute-start | bytes 1572872 | tf_op jit(solution)/shard_map/ppermute | solution.py:551
  356.9 28.6 %collective-permute-start.35 = (bf16[128,2048]{1,0:T(8,128)(2,1)S(1)}, bf16[128,2048]{1,0:T(8,128)(2,1)S(1)}, u32[]{:S(2)}, u32[]{:S(2)}) collective-permute-start(bf16[128,2048]{1,0:T(8,128)(2,1)S(1)} %get-tuple-element.130), channel_id=1, source_target_pairs={{0,4},{4,0},{8,12},{12,8},{1,5},{5,1},{9,13},{13,9},{2,6},{6,2},{1... | collective-permute-start | bytes 1572872 | tf_op jit(solution)/shard_map/ppermute | solution.py:551
  358.4 24.6 %collective-permute-start.32 = (bf16[128,2048]{1,0:T(8,128)(2,1)S(1)}, bf16[128,2048]{1,0:T(8,128)(2,1)S(1)}, u32[]{:S(2)}, u32[]{:S(2)}) collective-permute-start(bf16[128,2048]{1,0:T(8,128)(2,1)S(1)} %get-tuple-element.129), channel_id=1, source_target_pairs={{0,4},{4,0},{8,12},{12,8},{1,5},{5,1},{9,13},{13,9},{2,6},{6,2},{1... | collective-permute-start | bytes 1572872 | tf_op jit(solution)/shard_map/ppermute | solution.py:551
  366.2 23.6 %collective-permute-start.37 = (bf16[128,2048]{1,0:T(8,128)(2,1)S(1)}, bf16[128,2048]{1,0:T(8,128)(2,1)S(1)}, u32[]{:S(2)}, u32[]{:S(2)}) collective-permute-start(bf16[128,2048]{1,0:T(8,128)(2,1)S(1)} %collective-permute-done.36), channel_id=1, source_target_pairs={{0,4},{4,0},{8,12},{12,8},{1,5},{5,1},{9,13},{13,9},{2,6},{6,2},{1... | collective-permute-start | bytes 1572872 | tf_op jit(solution)/shard_map/ppermute | solution.py:551
  378.9 14.9 %collective-permute-start.33 = (bf16[128,2048]{1,0:T(8,128)(2,1)S(1)}, bf16[128,2048]{1,0:T(8,128)(2,1)S(1)}, u32[]{:S(2)}, u32[]{:S(2)}) collective-permute-start(bf16[128,2048]{1,0:T(8,128)(2,1)S(1)} %get-tuple-element.129), channel_id=1, source_target_pairs={{0,8},{4,12},{8,0},{12,4},{1,9},{5,13},{9,1},{13,5},{2,10},{6,14},... | collective-permute-start | bytes 1572872 | tf_op jit(solution)/shard_map/ppermute | solution.py:551
  383.0 16.6 %collective-permute-start.34 = (bf16[128,2048]{1,0:T(8,128)(2,1)S(1)}, bf16[128,2048]{1,0:T(8,128)(2,1)S(1)}, u32[]{:S(2)}, u32[]{:S(2)}) collective-permute-start(bf16[128,2048]{1,0:T(8,128)(2,1)S(1)} %collective-permute-done.32), channel_id=1, source_target_pairs={{0,8},{4,12},{8,0},{12,4},{1,9},{5,13},{9,1},{13,5},{2,10},{6,14},... | collective-permute-start | bytes 1572872 | tf_op jit(solution)/shard_map/ppermute | solution.py:551
  385.6 28.8 %collective-permute-start.63 = (bf16[1408,1024]{1,0:T(8,128)(2,1)}, bf16[1408,1024]{1,0:T(8,128)(2,1)}, u32[]{:S(2)}, u32[]{:S(2)}) collective-permute-start(bf16[1408,1024]{1,0:T(8,128)(2,1)} %constant_dynamic-slice_fusion), channel_id=1, source_target_pairs={{0,16},{16,0},{1,17},{17,1},{2,18},{18,2},{3,19},{19,3},{4,20},{20... | collective-permute-start | bytes 8650760 | tf_op jit(solution)/shard_map/ppermute | solution.py:547
  406.7 204.5 %reduce-scatter.11.cloned.1.call-start = ((), (), s32[]{:S(2)}) async-start(), calls=%async_computation.11 | async-start | bytes 3604480 | tf_op jit(solution)/shard_map/reduce_scatter | solution.py:723
  414.2 29.7 %collective-permute-start.38 = (bf16[1024,256]{1,0:T(8,128)(2,1)}, bf16[1024,256]{1,0:T(8,128)(2,1)}, u32[]{:S(2)}, u32[]{:S(2)}) collective-permute-start(bf16[1024,256]{1,0:T(8,128)(2,1)} %constant_dynamic-slice_fusion.4), channel_id=1, source_target_pairs={{0,16},{16,0},{1,17},{17,1},{2,18},{18,2},{3,19},{19,3},{4,20},{20... | collective-permute-start | bytes 1572872 | tf_op jit(solution)/shard_map/ppermute | solution.py:547
  420.1 220.1 %reduce-scatter.5.cloned.1.call-start = ((), (), s32[]{:S(2)}) async-start(), calls=%async_computation.8 | async-start | bytes 3932160 | tf_op jit(solution)/shard_map/reduce_scatter | solution.py:735
  443.5 97.5 %collective-permute-start.62 = (bf16[2,1024,1408]{1,2,0:T(8,128)(2,1)}, bf16[2,1024,1408]{1,2,0:T(8,128)(2,1)}, u32[]{:S(2)}, u32[]{:S(2)}) collective-permute-start(bf16[2,1024,1408]{1,2,0:T(8,128)(2,1)} %dynamic-slice_bitcast_fusion), channel_id=1, source_target_pairs={{0,16},{16,0},{1,17},{17,1},{2,18},{18,2},{3,19},{19,3},{4,20},{20... | collective-permute-start | bytes 17301512 | tf_op jit(solution)/shard_map/ppermute | solution.py:547
  484.3 218.7 %reduce-scatter.9.cloned.1.call-start = ((), (), s32[]{:S(2)}) async-start(), calls=%async_computation.10 | async-start | bytes 7208960 | tf_op jit(solution)/shard_map/reduce_scatter | solution.py:723
  510.5 44.2 %collective-permute-start.39 = (bf16[1024,2048]{1,0:T(8,128)(2,1)}, bf16[1024,2048]{1,0:T(8,128)(2,1)}, u32[]{:S(2)}, u32[]{:S(2)}) collective-permute-start(bf16[1024,2048]{1,0:T(8,128)(2,1)} %constant_dynamic-slice_fusion.3), channel_id=1, source_target_pairs={{0,16},{16,0},{1,17},{17,1},{2,18},{18,2},{3,19},{19,3},{4,20},{20... | collective-permute-start | bytes 12582920 | tf_op jit(solution)/shard_map/ppermute | solution.py:547
  510.9 14.8 %collective-permute-start.15 = (bf16[128,2048]{1,0:T(8,128)(2,1)S(1)}, bf16[128,2048]{1,0:T(8,128)(2,1)S(1)}, u32[]{:S(2)}, u32[]{:S(2)}) collective-permute-start(bf16[128,2048]{1,0:T(8,128)(2,1)S(1)} %get-tuple-element.107), channel_id=1, source_target_pairs={{0,4},{4,0},{8,12},{12,8},{1,5},{5,1},{9,13},{13,9},{2,6},{6,2},{1... | collective-permute-start | bytes 1572872 | tf_op jit(solution)/shard_map/ppermute | solution.py:551
  511.5 24.8 %collective-permute-start.14 = (bf16[128,2048]{1,0:T(8,128)(2,1)S(1)}, bf16[128,2048]{1,0:T(8,128)(2,1)S(1)}, u32[]{:S(2)}, u32[]{:S(2)}) collective-permute-start(bf16[128,2048]{1,0:T(8,128)(2,1)S(1)} %get-tuple-element.104), channel_id=1, source_target_pairs={{0,4},{4,0},{8,12},{12,8},{1,5},{5,1},{9,13},{13,9},{2,6},{6,2},{1... | collective-permute-start | bytes 1572872 | tf_op jit(solution)/shard_map/ppermute | solution.py:551
  513.0 24.8 %collective-permute-start.18 = (bf16[128,2048]{1,0:T(8,128)(2,1)S(1)}, bf16[128,2048]{1,0:T(8,128)(2,1)S(1)}, u32[]{:S(2)}, u32[]{:S(2)}) collective-permute-start(bf16[128,2048]{1,0:T(8,128)(2,1)S(1)} %get-tuple-element.105), channel_id=1, source_target_pairs={{0,8},{4,12},{8,0},{12,4},{1,9},{5,13},{9,1},{13,5},{2,10},{6,14},... | collective-permute-start | bytes 1572872 | tf_op jit(solution)/shard_map/ppermute | solution.py:551
  525.8 13.0 %collective-permute-start.16 = (bf16[128,2048]{1,0:T(8,128)(2,1)S(1)}, bf16[128,2048]{1,0:T(8,128)(2,1)S(1)}, u32[]{:S(2)}, u32[]{:S(2)}) collective-permute-start(bf16[128,2048]{1,0:T(8,128)(2,1)S(1)} %add_convert_fusion.7), channel_id=1, source_target_pairs={{0,8},{4,12},{8,0},{12,4},{1,9},{5,13},{9,1},{13,5},{2,10},{6,14},... | collective-permute-start | bytes 1572872 | tf_op jit(solution)/shard_map/ppermute | solution.py:551
  536.3 14.6 %collective-permute-start.17 = (bf16[128,2048]{1,0:T(8,128)(2,1)S(1)}, bf16[128,2048]{1,0:T(8,128)(2,1)S(1)}, u32[]{:S(2)}, u32[]{:S(2)}) collective-permute-start(bf16[128,2048]{1,0:T(8,128)(2,1)S(1)} %get-tuple-element.106), channel_id=1, source_target_pairs={{0,8},{4,12},{8,0},{12,4},{1,9},{5,13},{9,1},{13,5},{2,10},{6,14},... | collective-permute-start | bytes 1572872 | tf_op jit(solution)/shard_map/ppermute | solution.py:551
  540.3 12.1 %collective-permute-start.19 = (bf16[128,2048]{1,0:T(8,128)(2,1)S(1)}, bf16[128,2048]{1,0:T(8,128)(2,1)S(1)}, u32[]{:S(2)}, u32[]{:S(2)}) collective-permute-start(bf16[128,2048]{1,0:T(8,128)(2,1)S(1)} %get-tuple-element.103), channel_id=1, source_target_pairs={{0,4},{4,0},{8,12},{12,8},{1,5},{5,1},{9,13},{13,9},{2,6},{6,2},{1... | collective-permute-start | bytes 1572872 | tf_op jit(solution)/shard_map/ppermute | solution.py:551
  560.6 14.9 %collective-permute-start.41 = (bf16[128,2048]{1,0:T(8,128)(2,1)S(1)}, bf16[128,2048]{1,0:T(8,128)(2,1)S(1)}, u32[]{:S(2)}, u32[]{:S(2)}) collective-permute-start(bf16[128,2048]{1,0:T(8,128)(2,1)S(1)} %get-tuple-element.85), channel_id=1, source_target_pairs={{0,4},{4,0},{8,12},{12,8},{1,5},{5,1},{9,13},{13,9},{2,6},{6,2},{1... | collective-permute-start | bytes 1572872 | tf_op jit(solution)/shard_map/ppermute | solution.py:551
  566.3 11.7 %collective-permute-start.58 = (f32[56,128]{1,0:T(8,128)S(1)}, f32[56,128]{1,0:T(8,128)S(1)}, u32[]{:S(2)}, u32[]{:S(2)}) collective-permute-start(f32[56,128]{1,0:T(8,128)S(1)} %maximum_bitcast_fusion.8), channel_id=1, source_target_pairs={{0,1},{1,0},{2,3},{3,2},{4,5},{5,4},{6,7},{7,6},{8,9},{9,8},{10,11... | collective-permute-start | bytes 86024 | tf_op jit(solution)/shard_map/ppermute | solution.py:558
  566.4 20.0 %collective-permute-start.40 = (bf16[128,2048]{1,0:T(8,128)(2,1)S(1)}, bf16[128,2048]{1,0:T(8,128)(2,1)S(1)}, u32[]{:S(2)}, u32[]{:S(2)}) collective-permute-start(bf16[128,2048]{1,0:T(8,128)(2,1)S(1)} %get-tuple-element.84), channel_id=1, source_target_pairs={{0,4},{4,0},{8,12},{12,8},{1,5},{5,1},{9,13},{13,9},{2,6},{6,2},{1... | collective-permute-start | bytes 1572872 | tf_op jit(solution)/shard_map/ppermute | solution.py:551
  567.2 19.2 %collective-permute-start.44 = (bf16[128,2048]{1,0:T(8,128)(2,1)S(1)}, bf16[128,2048]{1,0:T(8,128)(2,1)S(1)}, u32[]{:S(2)}, u32[]{:S(2)}) collective-permute-start(bf16[128,2048]{1,0:T(8,128)(2,1)S(1)} %get-tuple-element.86), channel_id=1, source_target_pairs={{0,8},{4,12},{8,0},{12,4},{1,9},{5,13},{9,1},{13,5},{2,10},{6,14},... | collective-permute-start | bytes 1572872 | tf_op jit(solution)/shard_map/ppermute | solution.py:551
  576.7 15.6 %collective-permute-start.42 = (bf16[128,2048]{1,0:T(8,128)(2,1)S(1)}, bf16[128,2048]{1,0:T(8,128)(2,1)S(1)}, u32[]{:S(2)}, u32[]{:S(2)}) collective-permute-start(bf16[128,2048]{1,0:T(8,128)(2,1)S(1)} %fusion.55), channel_id=1, source_target_pairs={{0,8},{4,12},{8,0},{12,4},{1,9},{5,13},{9,1},{13,5},{2,10},{6,14},... | collective-permute-start | bytes 1572872 | tf_op jit(solution)/shard_map/ppermute | solution.py:551
  584.8 9.7 %collective-permute-start.60 = (f32[56,128]{1,0:T(8,128)S(1)}, f32[56,128]{1,0:T(8,128)S(1)}, u32[]{:S(2)}, u32[]{:S(2)}) collective-permute-start(f32[56,128]{1,0:T(8,128)S(1)} %fusion.103), channel_id=1, source_target_pairs={{0,16},{16,0},{1,17},{17,1},{2,18},{18,2},{3,19},{19,3},{4,20},{20... | collective-permute-start | bytes 86024 | tf_op jit(solution)/shard_map/ppermute | solution.py:547
  584.8 16.6 %collective-permute-start.43 = (bf16[128,2048]{1,0:T(8,128)(2,1)S(1)}, bf16[128,2048]{1,0:T(8,128)(2,1)S(1)}, u32[]{:S(2)}, u32[]{:S(2)}) collective-permute-start(bf16[128,2048]{1,0:T(8,128)(2,1)S(1)} %get-tuple-element.87), channel_id=1, source_target_pairs={{0,8},{4,12},{8,0},{12,4},{1,9},{5,13},{9,1},{13,5},{2,10},{6,14},... | collective-permute-start | bytes 1572872 | tf_op jit(solution)/shard_map/ppermute | solution.py:551
  622.0 9.5 %collective-permute-start.55 = (f32[33,128]{1,0:T(8,128)S(1)}, f32[33,128]{1,0:T(8,128)S(1)}, u32[]{:S(2)}, u32[]{:S(2)}) collective-permute-start(f32[33,128]{1,0:T(8,128)S(1)} %add.335), channel_id=1, source_target_pairs={{0,1},{1,0},{2,3},{3,2},{4,5},{5,4},{6,7},{7,6},{8,9},{9,8},{10,11... | collective-permute-start | bytes 50696 | tf_op jit(solution)/shard_map/ppermute | solution.py:558
  627.0 15.0 %collective-permute-start.46 = (bf16[128,2048]{1,0:T(8,128)(2,1)S(1)}, bf16[128,2048]{1,0:T(8,128)(2,1)}, u32[]{:S(2)}, u32[]{:S(2)}) collective-permute-start(bf16[128,2048]{1,0:T(8,128)(2,1)S(1)} %get-tuple-element.121), channel_id=1, source_target_pairs={{0,4},{4,0},{8,12},{12,8},{1,5},{5,1},{9,13},{13,9},{2,6},{6,2},{1... | collective-permute-start | bytes 1572872 | tf_op jit(solution)/shard_map/ppermute | solution.py:551
  627.8 16.1 %collective-permute-start.47 = (bf16[128,2048]{1,0:T(8,128)(2,1)S(1)}, bf16[128,2048]{1,0:T(8,128)(2,1)S(1)}, u32[]{:S(2)}, u32[]{:S(2)}) collective-permute-start(bf16[128,2048]{1,0:T(8,128)(2,1)S(1)} %get-tuple-element.121), channel_id=1, source_target_pairs={{0,8},{4,12},{8,0},{12,4},{1,9},{5,13},{9,1},{13,5},{2,10},{6,14},... | collective-permute-start | bytes 1572872 | tf_op jit(solution)/shard_map/ppermute | solution.py:551
  629.3 24.6 %collective-permute-start.50 = (bf16[128,2048]{1,0:T(8,128)(2,1)}, bf16[128,2048]{1,0:T(8,128)(2,1)}, u32[]{:S(2)}, u32[]{:S(2)}) collective-permute-start(bf16[128,2048]{1,0:T(8,128)(2,1)} %get-tuple-element.122), channel_id=1, source_target_pairs={{0,8},{4,12},{8,0},{12,4},{1,9},{5,13},{9,1},{13,5},{2,10},{6,14},... | collective-permute-start | bytes 1572872 | tf_op jit(solution)/shard_map/ppermute | solution.py:551
  629.8 48.1 %collective-permute-start.49 = (bf16[128,2048]{1,0:T(8,128)(2,1)}, bf16[128,2048]{1,0:T(8,128)(2,1)}, u32[]{:S(2)}, u32[]{:S(2)}) collective-permute-start(bf16[128,2048]{1,0:T(8,128)(2,1)} %get-tuple-element.122), channel_id=1, source_target_pairs={{0,4},{4,0},{8,12},{12,8},{1,5},{5,1},{9,13},{13,9},{2,6},{6,2},{1... | collective-permute-start | bytes 1572872 | tf_op jit(solution)/shard_map/ppermute | solution.py:551
  641.2 14.3 %collective-permute-start.57 = (bf16[1,256,768]{1,2,0:T(8,128)(2,1)S(1)}, bf16[1,256,768]{1,2,0:T(8,128)(2,1)S(1)}, u32[]{:S(2)}, u32[]{:S(2)}) collective-permute-start(bf16[1,256,768]{1,2,0:T(8,128)(2,1)S(1)} %constant_dynamic-slice_fusion.2), channel_id=1, source_target_pairs={{0,16},{16,0},{1,17},{17,1},{2,18},{18,2},{3,19},{19,3},{4,20},{20... | collective-permute-start | bytes 1179656 | tf_op jit(solution)/shard_map/ppermute | solution.py:547
  642.0 23.2 %collective-permute-start.48 = (bf16[128,2048]{1,0:T(8,128)(2,1)}, bf16[128,2048]{1,0:T(8,128)(2,1)}, u32[]{:S(2)}, u32[]{:S(2)}) collective-permute-start(bf16[128,2048]{1,0:T(8,128)(2,1)} %collective-permute-done.46), channel_id=1, source_target_pairs={{0,8},{4,12},{8,0},{12,4},{1,9},{5,13},{9,1},{13,5},{2,10},{6,14},... | collective-permute-start | bytes 1572872 | tf_op jit(solution)/shard_map/ppermute | solution.py:551
  643.9 24.6 %collective-permute-start.20 = (bf16[128,2048]{1,0:T(8,128)(2,1)}, bf16[128,2048]{1,0:T(8,128)(2,1)}, u32[]{:S(2)}, u32[]{:S(2)}) collective-permute-start(bf16[128,2048]{1,0:T(8,128)(2,1)} %get-tuple-element.133), channel_id=1, source_target_pairs={{0,4},{4,0},{8,12},{12,8},{1,5},{5,1},{9,13},{13,9},{2,6},{6,2},{1... | collective-permute-start | bytes 1572872 | tf_op jit(solution)/shard_map/ppermute | solution.py:551
  654.0 22.5 %collective-permute-start.24 = (bf16[128,2048]{1,0:T(8,128)(2,1)}, bf16[128,2048]{1,0:T(8,128)(2,1)}, u32[]{:S(2)}, u32[]{:S(2)}) collective-permute-start(bf16[128,2048]{1,0:T(8,128)(2,1)} %get-tuple-element.134), channel_id=1, source_target_pairs={{0,8},{4,12},{8,0},{12,4},{1,9},{5,13},{9,1},{13,5},{2,10},{6,14},... | collective-permute-start | bytes 1572872 | tf_op jit(solution)/shard_map/ppermute | solution.py:551
  655.5 23.5 %collective-permute-start.51 = (bf16[128,2048]{1,0:T(8,128)(2,1)}, bf16[128,2048]{1,0:T(8,128)(2,1)}, u32[]{:S(2)}, u32[]{:S(2)}) collective-permute-start(bf16[128,2048]{1,0:T(8,128)(2,1)} %collective-permute-done.50), channel_id=1, source_target_pairs={{0,4},{4,0},{8,12},{12,8},{1,5},{5,1},{9,13},{13,9},{2,6},{6,2},{1... | collective-permute-start | bytes 1572872 | tf_op jit(solution)/shard_map/ppermute | solution.py:551
  665.2 22.4 %collective-permute-start.21 = (bf16[128,2048]{1,0:T(8,128)(2,1)}, bf16[128,2048]{1,0:T(8,128)(2,1)S(1)}, u32[]{:S(2)}, u32[]{:S(2)}) collective-permute-start(bf16[128,2048]{1,0:T(8,128)(2,1)} %get-tuple-element.133), channel_id=1, source_target_pairs={{0,8},{4,12},{8,0},{12,4},{1,9},{5,13},{9,1},{13,5},{2,10},{6,14},... | collective-permute-start | bytes 1572872 | tf_op jit(solution)/shard_map/ppermute | solution.py:551
  668.5 30.5 %collective-permute-start.23 = (bf16[128,2048]{1,0:T(8,128)(2,1)}, bf16[128,2048]{1,0:T(8,128)(2,1)S(1)}, u32[]{:S(2)}, u32[]{:S(2)}) collective-permute-start(bf16[128,2048]{1,0:T(8,128)(2,1)} %get-tuple-element.134), channel_id=1, source_target_pairs={{0,4},{4,0},{8,12},{12,8},{1,5},{5,1},{9,13},{13,9},{2,6},{6,2},{1... | collective-permute-start | bytes 1572872 | tf_op jit(solution)/shard_map/ppermute | solution.py:551
  676.4 21.3 %collective-permute-start.22 = (bf16[128,2048]{1,0:T(8,128)(2,1)}, bf16[128,2048]{1,0:T(8,128)(2,1)S(1)}, u32[]{:S(2)}, u32[]{:S(2)}) collective-permute-start(bf16[128,2048]{1,0:T(8,128)(2,1)} %collective-permute-done.20), channel_id=1, source_target_pairs={{0,8},{4,12},{8,0},{12,4},{1,9},{5,13},{9,1},{13,5},{2,10},{6,14},... | collective-permute-start | bytes 1572872 | tf_op jit(solution)/shard_map/ppermute | solution.py:551
  677.9 21.1 %collective-permute-start.25 = (bf16[128,2048]{1,0:T(8,128)(2,1)}, bf16[128,2048]{1,0:T(8,128)(2,1)S(1)}, u32[]{:S(2)}, u32[]{:S(2)}) collective-permute-start(bf16[128,2048]{1,0:T(8,128)(2,1)} %collective-permute-done.24), channel_id=1, source_target_pairs={{0,4},{4,0},{8,12},{12,8},{1,5},{5,1},{9,13},{13,9},{2,6},{6,2},{1... | collective-permute-start | bytes 1572872 | tf_op jit(solution)/shard_map/ppermute | solution.py:551
  (66 other events, 639.0 us)
Sparse Core Ops, SparseCore 0:
  9.6 67.6 all-gather.4
  78.9 29.6 all-gather.6
  110.2 107.1 all-gather.8
  218.9 59.1 all-gather.10
  406.8 24.4 reduce-scatter.6
  433.5 54.8 reduce-scatter.10
  490.8 60.0 reduce-scatter.4
  553.3 104.3 reduce-scatter.8

commit v3 on v2

--- a/solution.py
+++ b/solution.py
@@ -123,10 +123,11 @@
             jax.ShapeDtypeStruct((n,width),BF16),jax.ShapeDtypeStruct((n,width),BF16)],
         scratch_shapes=[pltpu.VMEM((rows+8,3*width),F32),pltpu.VMEM((heads,HDIM,HDIM),F32)],
         compiler_params=pltpu.CompilerParams(vmem_limit_bytes=48<<20),
+        cost_estimate=pl.CostEstimate(flops=0,bytes_accessed=120<<20,transcendentals=0),
     )(keep,count,raw,cw,gain)
 
-def bwd_kernel(heads, group, keep_ref, count_ref, raw_ref, prev_ref, cw_ref, gain_ref, gno_ref, o_ref, s_ref, t_ref, w_ref, r_ref,
-               graw_ref, gcw_ref, ggain_ref, ext, gext, grad_state):
+def bwd_kernel(heads, group, keep_ref, count_ref, raw_ref, prev_ref, cw_ref, gain_ref, gno_ref, o_ref, s_ref, t_ref, w_ref, r_ref, *rest):
+    graw_ref, gcw_ref, ggain_ref, ext, gext, grad_state = rest[-6:]
     rows=group*CHUNK
     step=pl.program_id(0); steps=pl.num_programs(0)
     width=heads*HDIM
@@ -218,7 +219,7 @@
                 graw_ref[pl.ds(u['base'],CHUNK),lanes]=total.astype(BF16)
         graw_ref[pl.ds(u['base'],CHUNK),pl.ds(3*width,HDIM)]=(glog*u['sig_b']*(1.0-u['beta'])).astype(BF16)
 
-def backward(keep, count, raw, cw, gain, gno, o, s, t, w, r, group):
+def backward(keep, count, raw, cw, gain, gno, o, s, t, w, r, group, dummies=()):
     n=raw.shape[0]; width=cw.shape[1]//3; heads=width//HDIM; rows=group*CHUNK
     steps=n//rows
     row=lambda w: pl.BlockSpec((rows,w),lambda i:(steps-1-i,0))
@@ -227,13 +228,14 @@
     prev=pl.BlockSpec((16,raw.shape[1]),lambda i:(jnp.maximum((steps-1-i)*(rows//16)-1,0),0))
     return pl.pallas_call(functools.partial(bwd_kernel,heads,group),
         grid=(steps,),
-        in_specs=[pl.BlockSpec(memory_space=pltpu.SMEM)]*2+[row(raw.shape[1]),prev,full(cw),full(gain),row(width),row(width),mat,mat,row(width),row(width)],
+        in_specs=[pl.BlockSpec(memory_space=pltpu.SMEM)]*2+[row(raw.shape[1]),prev,full(cw),full(gain),row(width),row(width),mat,mat,row(width),row(width)]+[pl.BlockSpec(memory_space=pl.ANY)]*len(dummies),
         out_specs=[row(raw.shape[1]),pl.BlockSpec((KERNEL,3*width),lambda i:(0,0)),pl.BlockSpec((1,HDIM),lambda i:(0,0))],
         out_shape=[jax.ShapeDtypeStruct(raw.shape,BF16),
             jax.ShapeDtypeStruct((KERNEL,3*width),F32),jax.ShapeDtypeStruct((1,HDIM),F32)],
         scratch_shapes=[pltpu.VMEM((rows+8,3*width),F32),pltpu.VMEM((rows+8,3*width),F32),pltpu.VMEM((heads,HDIM,HDIM),F32)],
         compiler_params=pltpu.CompilerParams(vmem_limit_bytes=48<<20),
-    )(keep,count,raw,raw,cw,gain,gno,o,s,t,w,r)
+        cost_estimate=pl.CostEstimate(flops=0,bytes_accessed=120<<20,transcendentals=0),
+    )(keep,count,raw,raw,cw,gain,gno,o,s,t,w,r,*dummies)
 
 
 def passed_along(block, axis, distance):
@@ -543,58 +545,236 @@
     )
 
 
+MESH = pl.DeviceIdType.MESH
+STRIP = 16
+
+
+def phase_kernel(middle, both_cores, small_sum, n_in, n_out, part_ref, *refs):
+    inputs, all_ref = refs[:n_in], refs[n_in]
+    outs, scratch = refs[n_in + 1 : n_in + n_out], refs[n_in + n_out :]
+    got, sums, gain_sum, send_sem, recv_sem = scratch[:5]
+    count = all_ref.shape[0]
+    rows = count // 8
+    place, core, row = lax.axis_index("mp"), lax.axis_index("seq"), lax.axis_index("row")
+    across_x = place + 1 - 2 * (place % 2)
+    across_y = (place + 2) % 4
+    across_both = 3 - place
+    ways = {"x": {"mp": across_x}, "y": {"mp": across_y}}
+    if both_cores or small_sum:
+        ways["core"] = {"seq": 1 - core}
+    steps = []
+    if small_sum:
+        bit = 1
+        while bit < lax.axis_size("row"):
+            steps.append(f"row{bit}")
+            ways[steps[-1]] = {"row": row + bit - 2 * bit * ((row // bit) % 2)}
+            bit *= 2
+        steps += ["core", "x", "y"]
+    barrier = pltpu.get_barrier_semaphore()
+    for other in ways.values():
+        pl.semaphore_signal(barrier, inc=1, device_id=other, device_id_type=MESH)
+    pl.semaphore_wait(barrier, len(ways))
+
+    def copy(index, source, target, way):
+        return pltpu.make_async_remote_copy(
+            src_ref=source,
+            dst_ref=target,
+            send_sem=send_sem.at[index],
+            recv_sem=recv_sem.at[index],
+            device_id=ways[way],
+            device_id_type=MESH,
+        )
+
+    def block(of, half):
+        return pl.ds(pl.multiple_of((2 * of + half) * rows, rows), rows)
+
+    def strips(body):
+        @pl.loop(0, rows // STRIP)
+        def _(i):
+            body(pl.multiple_of(i * STRIP, STRIP))
+
+    order = [(across_both, 0), (across_both, 1), (across_x, 0), (across_y, 1)]
+    order += [(across_y, 0), (across_x, 1), (place, 0), (place, 1)]
+    if both_cores:
+        part, incoming, local_sem = scratch[5:8]
+        mine = pltpu.make_async_copy(part_ref.at[pl.ds(core * count, count)], part, local_sem)
+        mine.start()
+        shared = []
+        for i, (of, half) in enumerate(order):
+            start = pl.multiple_of((1 - core) * count + (2 * of + half) * rows, rows)
+            shared.append(
+                copy(12 + i, part_ref.at[pl.ds(start, rows)], incoming.at[block(of, half)], "core")
+            )
+            shared[-1].start()
+        mine.wait()
+    else:
+        part = part_ref
+
+    def ready(index):
+        if both_cores:
+            of, half = order[index]
+            shared[index].wait_recv()
+
+            def add(at):
+                strip = pl.ds((2 * of + half) * rows + at, STRIP)
+                part[strip, :] = (
+                    part[strip, :].astype(F32) + incoming[strip, :].astype(F32)
+                ).astype(BF16)
+
+            strips(add)
+
+    far = [
+        copy(0, part.at[block(across_both, 0)], got.at[0], "x"),
+        copy(1, part.at[block(across_both, 1)], got.at[1], "y"),
+    ]
+    near = [
+        copy(2, part.at[block(across_x, 0)], got.at[2], "x"),
+        copy(3, part.at[block(across_y, 1)], got.at[3], "y"),
+    ]
+    last = [copy(4, sums.at[0], got.at[4], "y"), copy(5, sums.at[1], got.at[5], "x")]
+    own = [all_ref.at[block(place, 0)], all_ref.at[block(place, 1)]]
+    passed = [all_ref.at[block(across_x, 0)], all_ref.at[block(across_y, 1)]]
+    out_first = [copy(6, own[0], own[0], "x"), copy(7, own[1], own[1], "y")]
+    out_second = [copy(8, own[0], own[0], "y"), copy(9, own[1], own[1], "x")]
+    out_third = [copy(10, passed[0], passed[0], "y"), copy(11, passed[1], passed[1], "x")]
+
+    for index, step in enumerate((*far, *near)):
+        ready(index)
+        step.start()
+    gain_sum[...] = jnp.zeros_like(gain_sum)
+    for half, onward in ((0, across_y), (1, across_x)):
+        ready(4 + half)
+        far[half].wait_recv()
+
+        def add(at):
+            strip = pl.ds(at, STRIP)
+            mine = part[pl.ds((2 * onward + half) * rows + at, STRIP), :]
+            sums[half, strip, :] = (mine.astype(F32) + got[half, strip, :].astype(F32)).astype(BF16)
+
+        strips(add)
+        last[half].start()
+    for half in (0, 1):
+        ready(6 + half)
+        near[half].wait_recv()
+        last[half].wait_recv()
+
+        def finish(at):
+            strip = pl.ds(at, STRIP)
+            total = part[pl.ds((2 * place + half) * rows + at, STRIP), :].astype(F32)
+            total = total + got[2 + half, strip, :].astype(F32)
+            total = total + got[4 + half, strip, :].astype(F32)
+            result = middle(total, half, strip, inputs, outs, gain_sum)
+            all_ref[pl.ds((2 * place + half) * rows + at, STRIP), :] = result.astype(BF16)
+
+        strips(finish)
+        out_first[half].start()
+        out_second[half].start()
+
+    gain = jnp.sum(gain_sum[...], axis=0, keepdims=True)
+    small = []
+    if small_sum:
+        values, arrived = outs[-1], scratch[-1]
+        values[...] = inputs[-1 - small_sum["dummies"]][...]
+        values[0:1, :] = gain
+    elif n_out > 2:
+        outs[-1][...] = gain
+
+    def small_step(number):
+        height = 8 if steps[number] in ("x", "y") else values.shape[0]
+        step = copy(
+            20 + number,
+            arrived.at[number, 1, pl.ds(0, height)],
+            arrived.at[number, 0, pl.ds(0, height)],
+            steps[number],
+        )
+        arrived[number, 1, 0:height, :] = values[0:height, :]
+        step.start()
+        step.wait_recv()
+        values[0:height, :] = values[0:height, :] + arrived[number, 0, 0:height, :]
+        small.append(step)
+
+    for half in (0, 1):
+        out_first[half].wait_recv()
+        out_third[half].start()
+    if small_sum:
+        for number in range(len(steps)):
+            small_step(number)
+    for step in (*out_second, *out_third):
+        step.wait_recv()
+    for step in (*far, *near, *last, *out_first, *out_second, *out_third, *small):
+        step.wait_send()
+    if both_cores:
+        for step in shared:
+            step.wait_send()
+
+
+def normed_forward(total, half, strip, inputs, outs, gain_sum):
+    residual, gain = inputs[:2]
+    hidden = residual[half, strip, :].astype(F32) + total
+    outs[0][half, strip, :] = hidden
+    stat = lax.rsqrt(jnp.mean(hidden * hidden, axis=1, keepdims=True) + EPSILON)
+    return hidden * stat * gain[...]
+
+
+def normed_backward(keep, total, half, strip, inputs, outs, gain_sum):
+    value, base, gain = inputs[:3]
+    value = value[half, strip, :].astype(F32)
+    stat = lax.rsqrt(jnp.mean(value * value, axis=1, keepdims=True) + EPSILON)
+    unit = value * stat
+    gain_sum[...] += jnp.sum((total * unit).reshape(2, 8, -1), axis=0)
+    scaled = total * gain[...]
+    grad = base[half, strip, :].astype(F32) + stat * (
+        scaled - unit * jnp.mean(scaled * unit, axis=1, keepdims=True)
+    )
+    if keep:
+        outs[0][half, strip, :] = grad
+    return grad
+
+
+def mp_phase(number, middle, part, inputs, dummies, outs, both_cores=False, small=None):
+    here, there = pl.BlockSpec(memory_space=pltpu.VMEM), pl.BlockSpec(memory_space=pl.ANY)
+    count, model = part.shape[0] // (2 if both_cores else 1), part.shape[1]
+    block = (count // 8, model)
+    copies, scratch, small_sum = 12, [], None
+    if both_cores:
+        copies = 20
+        scratch += [pltpu.VMEM((count, model), BF16)] * 2 + [pltpu.SemaphoreType.DMA(())]
+    if small is not None:
+        stages = lax.axis_size("row").bit_length() - 1 + 3
+        copies = 20 + stages
+        scratch += [pltpu.VMEM((stages, 2, *small.shape), F32)]
+        small_sum = {"dummies": len(dummies)}
+        inputs = [*inputs, small]
+        outs = [*outs, jax.ShapeDtypeStruct(small.shape, F32)]
+    kernel = functools.partial(
+        phase_kernel, middle, both_cores, small_sum, len(inputs) + len(dummies), 1 + len(outs)
+    )
+    return pl.pallas_call(
+        kernel,
+        in_specs=[there if both_cores else here] + [here] * len(inputs) + [there] * len(dummies),
+        out_specs=[here] * (1 + len(outs)),
+        out_shape=[jax.ShapeDtypeStruct((count, model), BF16), *outs],
+        scratch_shapes=[
+            pltpu.VMEM((6, *block), BF16),
+            pltpu.VMEM((2, *block), BF16),
+            pltpu.VMEM((8, model), F32),
+            pltpu.SemaphoreType.DMA((copies,)),
+            pltpu.SemaphoreType.DMA((copies,)),
+            *scratch,
+        ],
+        compiler_params=pltpu.CompilerParams(
+            collective_id=number, has_side_effects=True, vmem_limit_bytes=48 << 20
+        ),
+        cost_estimate=pl.CostEstimate(flops=0, bytes_accessed=250 << 20, transcendentals=0),
+    )(part, *inputs, *dummies)
+
+
 def swapped(block):
     return lax.ppermute(block, "seq", [(0, 1), (1, 0)])
 
 
 def across(block, bit):
     return lax.ppermute(block, "mp", [(i, i ^ bit) for i in range(4)])
-
-
-def total_over(part, axis):
-    size = lax.axis_size(axis)
-    bit = 1
-    while bit < size:
-        part = part + lax.ppermute(part, axis, [(i, i ^ bit) for i in range(size)])
-        bit *= 2
-    return part
-
-
-def sum_over_mp(parts):
-    upper, lower = parts[0], parts[1]
-    upper_in = [across(upper[1], 1), across(upper[3], 1)]
-    lower_in = [across(lower[2], 2), across(lower[3], 2)]
-    later = lambda mine, other: (mine.astype(F32) + other.astype(F32)).astype(BF16)
-    upper_last = across(later(upper[2], upper_in[1]), 2)
-    lower_last = across(later(lower[1], lower_in[1]), 1)
-    add = lambda *terms: sum(term.astype(F32) for term in terms)
-    return jnp.stack(
-        [add(upper[0], upper_in[0], upper_last), add(lower[0], lower_in[0], lower_last)]
-    )
-
-
-def gather_over_mp(own):
-    upper, lower = own[0], own[1]
-    upper_one, lower_two = across(upper, 1), across(lower, 2)
-    upper_two, lower_one = across(upper, 2), across(lower, 1)
-    upper_three, lower_three = across(upper_one, 2), across(lower_two, 1)
-    return jnp.stack(
-        [
-            jnp.stack([upper, upper_one, upper_two, upper_three]),
-            jnp.stack([lower, lower_one, lower_two, lower_three]),
-        ]
-    )
-
-
-def reordered(block, own):
-    quarters = block.reshape(4, 2, -1, block.shape[-1])
-    picked = [lax.dynamic_index_in_dim(quarters, own ^ j, 0, keepdims=False) for j in range(4)]
-    return jnp.stack(picked, axis=1)
-
-
-def restored(block, own):
-    picked = [lax.dynamic_index_in_dim(block, own ^ j, 1, keepdims=False) for j in range(4)]
-    return jnp.stack(picked).reshape(-1, block.shape[-1])
 
 
 def in_order(mine, other, core, axis):
@@ -603,10 +783,40 @@
     return jnp.concatenate([first, second], axis=axis)
 
 
+def after(block, *done):
+    nothing = sum(part[(0,) * part.ndim].astype(F32) for part in done) * 0.0
+    return block + nothing.astype(block.dtype)
+
+
 def halves(block, core, axis):
     size = block.shape[axis] // 2
     pick = lambda i: lax.dynamic_slice_in_dim(block, i * size, size, axis=axis)
     return pick(core), pick(1 - core)
+
+
+def both_tokens(left, right):
+    product = lambda a, b: lax.dot_general(
+        a, b, (((0,), (0,)), ((), ())), preferred_element_type=F32
+    )
+    return (product(left[0], right[0]) + product(left[1], right[1])).astype(BF16)
+
+
+def own_columns(block, core):
+    mine, other = halves(block, core, 1)
+    return mine, swapped(other)
+
+
+def product_pair(left, right, core):
+    mine, other = halves(right, core, 1)
+    product = lambda part: lax.dot_general(
+        left, part, (((0,), (0,)), ((), ())), preferred_element_type=F32
+    )
+    incoming = swapped(product(other).astype(BF16))
+    return (product(mine) + incoming.astype(F32)).astype(BF16)
+
+
+def over_row(pair, axis):
+    return lax.psum_scatter(pair, "row", scatter_dimension=axis, tiled=True)
 
 
 def joined_shards(
@@ -630,9 +840,10 @@
     quarter = tok_count // 4
 
     gather = lambda weight: lax.all_gather(weight, ("seq", "row"), axis=1, tiled=True)
-    qkv_full, beta_full = gather(qkv_weight), gather(beta_weight)
-    out_full, gateup_full, down_full = (
-        gather(out_weight),
+    mixer_full = gather(jnp.concatenate([qkv_weight, out_weight.T[None]]))
+    qkv_full, out_full = mixer_full[:3], mixer_full[3]
+    beta_full, gateup_full, down_full = (
+        gather(beta_weight),
         gather(gateup_weight),
         gather(down_weight),
     )
@@ -660,110 +871,138 @@
     heads_out, *saved = forward(keep, count, raw, conv_own, gain, group)
 
     mine, other = halves(heads_out, core, 0)
-    normed_out = reordered(in_order(mine, swapped(other), core, 1), own)
-    branch_part = jnp.einsum("hqtc,cd->hqtd", normed_out, out_full, preferred_element_type=F32)
-    branch = sum_over_mp(branch_part.astype(BF16))
+    normed_out = in_order(mine, swapped(other), core, 1)
+    branch_part = lax.dot_general(
+        normed_out, out_full, (((1,), (1,)), ((), ())), preferred_element_type=F32
+    )
     own_rows = lambda block: lax.dynamic_slice_in_dim(
         block[0], own * quarter, quarter, axis=0
     ).reshape(2, -1, model)
-    residual_own = own_rows(block_in).astype(F32)
-    hidden = residual_own + branch
-    stat_mid = lax.rsqrt(jnp.mean(hidden * hidden, axis=-1, keepdims=True) + EPSILON)
-    unit_mid = hidden * stat_mid
-    normed_mid = gather_over_mp((unit_mid * ffn_gain).astype(BF16)).reshape(tok_count, model)
-
-    grad_top = reordered(cotangent[0], own).reshape(tok_count, model)
+    residual_own = own_rows(block_in)
+    rows_own = jax.ShapeDtypeStruct(residual_own.shape, F32)
+    normed_mid, hidden = mp_phase(
+        0,
+        normed_forward,
+        branch_part.astype(BF16),
+        [residual_own, ffn_gain[None, :]],
+        [],
+        [rows_own],
+    )
+
+    grad_top = cotangent[0]
     gate_up = jnp.einsum("td,sdf->stf", normed_mid, gateup_full, preferred_element_type=F32)
     gate_sig = jax.nn.sigmoid(gate_up[0])
     product = (gate_up[0] * gate_sig * gate_up[1]).astype(BF16)
+    down_pair = product_pair(product, grad_top, core)
+    ffn_part = jnp.dot(
+        after(product, down_pair), down_full, preferred_element_type=F32
+    ).astype(BF16)
+    ffn_parts = lax.all_to_all(ffn_part, "mp", split_axis=0, concat_axis=0, tiled=True)
+    ffn_own = jnp.sum(ffn_parts.astype(F32).reshape(4, quarter, model), axis=0)
+    block_out = (hidden.reshape(quarter, model) + ffn_own).astype(BF16)
     grad_product = jnp.dot(grad_top, down_full.T, preferred_element_type=F32)
+    grad_product = after(grad_product, ffn_part)
     grad_gate = grad_product * gate_up[1] * gate_sig * (1.0 + gate_up[0] * (1.0 - gate_sig))
     grad_up = grad_product * gate_up[0] * gate_sig
-    grad_gate_up = jnp.stack([grad_gate, grad_up]).astype(BF16)
-    grad_mid_part = jnp.einsum("stf,sdf->td", grad_gate_up, gateup_full, preferred_element_type=F32)
-    local = lambda part: part.astype(BF16).reshape(2, 4, -1, model)
-    grad_mid = sum_over_mp(local(grad_mid_part))
-    ffn_gain_part = jnp.sum(grad_mid * unit_mid, axis=(0, 1))
-    grad_unit_mid = grad_mid * ffn_gain
-    grad_hidden = own_rows(cotangent).astype(F32) + stat_mid * (
-        grad_unit_mid - unit_mid * jnp.mean(grad_unit_mid * unit_mid, axis=-1, keepdims=True)
-    )
-    grad_branch = gather_over_mp(grad_hidden.astype(BF16))
-    grad_normed_out = jnp.einsum(
-        "hqtd,cd->hqtc", grad_branch, out_full, preferred_element_type=F32
+    grad_gate, grad_up = grad_gate.astype(BF16), grad_up.astype(BF16)
+    grad_mid_part = jnp.einsum(
+        "stf,sdf->td",
+        jnp.stack([grad_gate, grad_up]),
+        gateup_full,
+        preferred_element_type=F32,
     ).astype(BF16)
-
-    mine, other = halves(restored(grad_normed_out, own), core, 1)
+    normed_halves = own_columns(normed_mid, core)
+    gate_pair = both_tokens(normed_halves, (grad_gate, swapped(grad_gate)))
+    up_pair = both_tokens(normed_halves, (grad_up, swapped(grad_up)))
+    down_sum, gate_sum, up_sum = over_row(down_pair, 1), over_row(gate_pair, 0), over_row(up_pair, 0)
+    grad_branch, grad_hidden, ffn_gain_part = mp_phase(
+        1,
+        partial(normed_backward, True),
+        grad_mid_part,
+        [hidden, own_rows(cotangent), ffn_gain[None, :]],
+        [block_out, down_pair, gate_pair, up_pair],
+        [rows_own, jax.ShapeDtypeStruct((1, model), F32)],
+    )
+    grad_normed_out = jnp.dot(grad_branch, out_full, preferred_element_type=F32).astype(BF16)
+
+    mine, other = halves(grad_normed_out, core, 1)
     grad_heads = in_order(mine, swapped(other), core, 0)
     grad_raw, grad_conv_own, out_gain_part = backward(
-        keep, count, raw, conv_own, gain, grad_heads, *saved, group
-    )
+        keep, count, raw, conv_own, gain, grad_heads, *saved, group, [down_sum, gate_sum]
+    )
+    block_outs = [block_out] + [
+        lax.ppermute(after(block_out, grad_branch), "mp", [(i, i ^ k) for i in range(4)])
+        for k in (1, 2, 3)
+    ]
+    out_pair = product_pair(after(normed_out, up_sum), grad_branch, core)
+    grad_raw = after(grad_raw, *block_outs[1:])
     grad_normed = lax.dot_general(
         grad_raw, mix_weight, (((1,), (1,)), ((), ())), preferred_element_type=F32
     )
-    mine, other = halves(grad_normed.astype(BF16), core, 0)
-    grad_normed_sum = (mine.astype(F32) + swapped(other).astype(F32)).astype(BF16)
-    grad_normed = sum_over_mp(reordered(grad_normed_sum, own))
-    stat_own = lax.rsqrt(jnp.mean(residual_own * residual_own, axis=-1, keepdims=True) + EPSILON)
-    unit_in = residual_own * stat_own
-    attn_gain_part = jnp.sum(grad_normed * unit_in, axis=(0, 1))
-    grad_unit_in = grad_normed * attn_gain
-    grad_input = grad_hidden + stat_own * (
-        grad_unit_in - unit_in * jnp.mean(grad_unit_in * unit_in, axis=-1, keepdims=True)
-    )
-    grad_input = restored(gather_over_mp(grad_input.astype(BF16)), own).astype(F32)
-
-    ffn_part = jnp.dot(product, down_full, preferred_element_type=F32)
-    block_out = (hidden + sum_over_mp(local(ffn_part))).astype(BF16)
-    block_out = restored(gather_over_mp(block_out), own)
-
-    def summed(part, axis):
-        mine, other = halves(part.astype(BF16), core, axis)
-        pair = (mine.astype(F32) + swapped(other).astype(F32)).astype(BF16)
-        return lax.psum_scatter(pair, "row", scatter_dimension=axis, tiled=True).astype(F32)
-
-    grad_down = summed(jnp.dot(product.T, grad_top, preferred_element_type=F32), 1)
-    grad_gateup = summed(
-        jnp.einsum("td,stf->sdf", normed_mid, grad_gate_up, preferred_element_type=F32), 1
-    )
-    grad_out = summed(
-        jnp.einsum("hqtc,hqtd->cd", normed_out, grad_branch, preferred_element_type=F32), 1
-    )
+    grad_normed_part = grad_normed.astype(BF16)
     grad_qkv = lax.dot_general(
-        normed, grad_raw[:, : 3 * width], (((0,), (0,)), ((), ())), preferred_element_type=F32
+        normed,
+        grad_raw[:, : 3 * width],
+        (((0,), (0,)), ((), ())),
+        preferred_element_type=F32,
     ).astype(BF16)
+    grad_beta = lax.dot_general(
+        grad_raw[:, 3 * width :], normed, (((0,), (0,)), ((), ())), preferred_element_type=F32
+    )[:own_heads]
+
+    line = lambda part: jnp.pad(part.reshape(1, -1), ((0, 0), (0, model - part.size)))
+    place = lambda part, lines: lax.dynamic_update_slice_in_dim(
+        jnp.zeros((2 * lines, model), F32), part, core * lines, axis=0
+    )
+    conv_lines = -(-grad_conv_own.size // model)
+    conv_part = jnp.pad(grad_conv_own.ravel(), (0, conv_lines * model - grad_conv_own.size))
+    small = jnp.concatenate(
+        [
+            jnp.zeros((1, model), F32),
+            ffn_gain_part,
+            line(out_gain_part[0]),
+            jnp.zeros((5, model), F32),
+            place(grad_beta, own_heads),
+            place(conv_part.reshape(conv_lines, model), conv_lines),
+        ]
+    )
+    small = jnp.pad(small, ((0, -small.shape[0] % 8), (0, 0)))
+    grad_input, small = mp_phase(
+        2,
+        partial(normed_backward, False),
+        grad_normed_part,
+        [residual_own, grad_hidden, attn_gain[None, :]],
+        [*block_outs, up_sum, out_pair, grad_qkv],
+        [],
+        both_cores=True,
+        small=small,
+    )
+    grad_input = grad_input.astype(F32)
+    block_outs = jnp.stack(block_outs)
+    block_out = jnp.concatenate(
+        [lax.dynamic_index_in_dim(block_outs, own ^ k, 0, keepdims=False) for k in range(4)]
+    )
+    grad_attn_gain, grad_ffn_gain = small[0], small[1]
+    grad_out_gain = small[2, : out_gain.shape[0]]
+    span = beta_weight.shape[1]
+    place_no = core * lax.axis_size("row") + lax.axis_index("row")
+    grad_beta = lax.dynamic_slice_in_dim(small[8 : 8 + 2 * own_heads], place_no * span, span, axis=1)
+    conv_at = 8 + 2 * own_heads
+    conv_of = lambda i: (
+        small[conv_at + i * conv_lines : conv_at + (i + 1) * conv_lines]
+        .ravel()[: grad_conv_own.size]
+        .reshape(KERNEL, 3, width)
+        .transpose(1, 0, 2)
+    )
+    grad_conv = jnp.concatenate([conv_of(0), conv_of(1)], axis=2)
+    grad_down, grad_out = down_sum.astype(F32), over_row(out_pair, 1).astype(F32)
+    grad_gateup = jnp.stack([gate_sum, up_sum]).astype(F32)
     grad_qkv = lax.psum_scatter(
         grad_qkv.reshape(2, -1, 3 * width), "row", scatter_dimension=1, tiled=True
     )
     mine, other = halves(grad_qkv, core, 0)
     by_kind = lambda part: part[0].reshape(-1, 3, width).transpose(1, 0, 2)
     grad_qkv = in_order(by_kind(mine), by_kind(swapped(other)), core, 2).astype(F32)
-    grad_beta = lax.dot_general(
-        grad_raw[:, 3 * width :], normed, (((0,), (0,)), ((), ())), preferred_element_type=F32
-    )[:own_heads]
-
-    per_head = jnp.concatenate([grad_conv_own.ravel(), grad_beta.ravel()]).reshape(-1, HDIM)
-    per_head = total_over(per_head, "row")
-    conv_size = grad_conv_own.size // HDIM
-
-    def unpacked(flat):
-        conv = flat[:conv_size].reshape(KERNEL, 3, width).transpose(1, 0, 2)
-        return conv, flat[conv_size:].reshape(own_heads, model)
-
-    conv_mine, beta_mine = unpacked(per_head)
-    conv_other, beta_other = unpacked(swapped(per_head))
-    grad_conv = in_order(conv_mine, conv_other, core, 2)
-    grad_beta = in_order(beta_mine, beta_other, core, 0)
-    span = beta_weight.shape[1]
-    place_no = core * lax.axis_size("row") + lax.axis_index("row")
-    grad_beta = lax.dynamic_slice_in_dim(grad_beta, place_no * span, span, axis=1)
-
-    gains = jnp.concatenate([attn_gain_part, ffn_gain_part, out_gain_part[0]]).reshape(-1, HDIM)
-    for axis in ("mp", "seq", "row"):
-        gains = total_over(gains, axis)
-    gains = gains.ravel()
-    grad_attn_gain, grad_ffn_gain = gains[:model], gains[model : 2 * model]
-    grad_out_gain = gains[2 * model :]
     return (
         block_out[None],
         grad_input[None],

time: 717 us -> 707 us (0.986)
  Pallas kernels: 47.6 us -> 291 us
  waiting for transfers between devices: 282 us -> 106 us
  starting transfers between devices: 67.6 us -> 10.9 us
  other arithmetic: 92.9 us -> 43.7 us
  matrix products: 135 us -> 146 us
  local copies, waits for them, and re-layouts: 48 us -> 56.1 us
    pallas_call x0 -> x3, Pallas kernels: none -> 243 us  [mp_phase(): pl.pallas_call(kernel, in_specs=[there if both_cores else here] + [here]...]
    ppermute x55 -> x3, waiting for transfers between devices: 200 us -> 34.2 us  [joined_shards(): lax.ppermute(after(block_out, grad_branch), 'mp', [(i, i ^ k) for i in ra...]
    ppermute x55 -> x3, starting transfers between devices: 65.4 us -> 3.55 us  [joined_shards(): lax.ppermute(after(block_out, grad_branch), 'mp', [(i, i ^ k) for i in ra...]
    all_gather x4 -> x3, waiting for transfers between devices: 75 us -> 43.4 us  [joined_shards(): lax.all_gather(weight, ('seq', 'row'), axis=1, tiled=True)]
    convert_element_type x15 -> x6, other arithmetic: 39.8 us -> 8.9 us  [the longest x2 2.47 us: joined_shards(): block_out = (hidden.reshape(quarter, model) + ffn_own).astype(BF16)]
    another operation x27 -> x2, other arithmetic: 26.6 us -> 0.9 us  [the longest x1 0.72 us: joined_shards(): block_outs = jnp.stack(block_outs)]
    all_to_all x0 -> x1, waiting for transfers between devices: none -> 16.6 us  [joined_shards(): lax.all_to_all(ffn_part, 'mp', split_axis=0, concat_axis=0, tiled=True)]
    dot_general x7 -> x12, matrix products: 66.6 us -> 78.5 us  [the longest x4 21.6 us: both_tokens(): lax.dot_general(a, b, (((0,), (0,)), ((), ())), preferred_element_type=F32)]
  transfers between devices with their start and end apart: 72 -> 21, of which waited for: 41 -> 9; matrix products, arithmetic and copies ran while one was open for 31% -> 30% of each run, Pallas kernels for 7% -> 42%
where the time goes in v3:
time: 707 us; the launch traced here: 697 us
  Pallas kernels  291 us (41%)
  matrix products  146 us (21%)
  waiting for transfers between devices  106 us (15%)
  local copies, waits for them, and re-layouts  56.1 us (8%)
  other arithmetic  43.7 us (6%)
  blocking collectives  24 us (3%)
  between operations  20.6 us (3%)
  starting transfers between devices  10.9 us (2%)
    pallas_call x3, Pallas kernels, mp_phase(): pl.pallas_call(kernel, in_specs=[there if both_cores else here] + [here]...  243 us
    all_gather x3, waiting for transfers between devices, joined_shards(): lax.all_gather(weight, ('seq', 'row'), axis=1, tiled=True)  43.4 us
    ppermute x3, waiting for transfers between devices, joined_shards(): lax.ppermute(after(block_out, grad_branch), 'mp', [(i, i ^ k) for i in ra...  34.2 us
    unnamed x140, local copies, waits for them, and re-layouts  33 us
    pallas_call x1, Pallas kernels, backward(): pl.pallas_call(functools.partial(bwd_kernel, heads, group), grid=(steps,)...  26.7 us
    all_gather x1, blocking collectives, joined_shards(): lax.all_gather(weight, ('seq', 'row'), axis=1, tiled=True)  24 us
    dot_general x4, matrix products, both_tokens(): lax.dot_general(a, b, (((0,), (0,)), ((), ())), preferred_element_type=F32)  21.6 us
    pallas_call x1, Pallas kernels, forward(): pl.pallas_call(functools.partial(fwd_kernel, heads, group), grid=(n // ro...  21.1 us
  transfers between devices with their start and end apart: 21, of which 9 were waited for; matrix products, arithmetic and copies ran while one was open for 30% of the time, Pallas kernels for 42%

profile of v3, /device:TPU:0, one launch (start us, length us, event | category | flops | bytes accessed | tf_op | source)
XLA Modules:
  0.0 697.4 jit_solution(99541959038193941)
XLA Ops:
  8.3 2.2 pad_maximum_fusion.7
  11.4 3.2 fusion
  14.8 3.0 fusion.2
  18.4 24.0 %all_gather.13 = bf16[4,2048]{1,0:T(4,128)(2,1)S(1)} all-gather(bf16[4,256]{1,0:T(4,128)(2,1)S(1)} %copy-done.61), channel_id=1, replica_groups=mesh['seq'=2,'mp'=4,'row'=4] {'seq','row'}, dimensions={1}, use_global_device_ids=true | all-gather | bytes 18432 | tf_op jit(solution)/shard_map/all_gather | solution.py:842
  45.0 7.7 %broadcast_select_fusion.1 = (bf16[1024,2048]{1,0:T(8,128)(2,1)}, bf16[1024,2048]{1,0:T(8,128)(2,1)}) fusion(bf16[1024,2048]{1,0:T(8,128)(2,1)} %collective-permute-done, pred[]{:T(512)S(6)} %eq.2, f32[2048]{0:T(1024)S(1)} %copy-done.27, f32[1024]{0:T(1024)S(1)} %add_rsqrt_fusion, bf16[1,1024,2048]{2,1,0:T(8,128)(2,1)} %param.12), kind=kLoop, calls=%fused_computation.43 | loop fusion | flops 12582912 | bytes 16789504 | tf_op jit(solution)/shard_map/jit(_where)/select_n | solution.py:781
  52.7 42.9 %all-gather.4.cloned.1.call-done = bf16[4,2048,512]{2,1,0:T(8,128)(2,1)} async-done(((bf16[4,256,512]{2,1,0:T(8,128)(2,1)}), bf16[4,2048,512]{2,1,0:T(8,128)(2,1)}) %all-gather.4.cloned.1.call-update) | async-done | bytes 8388624 | tf_op jit(solution)/shard_map/all_gather | solution.py:842
  95.6 2.8 slice-done
  99.6 2.6 copy-done.34
  102.2 10.8 %convolution_convert_fusion.4.raw_ref.prev_ref = bf16[2048,896]{1,0:T(8,128)(2,1)} fusion(bf16[1024,2048]{1,0:T(8,128)(2,1)S(1)} %copy-done.37, bf16[1024,2048]{1,0:T(8,128)(2,1)S(1)} %copy-done.34, bf16[2048,2]{1,0:T(8,128)(2,1)S(1)} %copy.35, bf16[2048,256]{1,0:T(8,128)(2,1)S(1)} %get-tuple-element.73, bf16[2048,256]{1,0:T(8,128)(2,1)S(1)} %get-tuple-element.72, ...), kind=kOutput, calls=%fused_computation.48 | convolution fusion | flops 7553155072 | bytes 15212544 | tf_op jit(solution)/shard_map/dot_general | solution.py:868
  113.0 21.1 %shard_map.203 = (bf16[2048,256]{1,0:T(8,128)(2,1)S(1)}, f32[2048,256]{1,0:T(8,128)}, bf16[16,2,128,128]{3,2,1,0:T(8,128)(2,1)S(1)}, bf16[16,2,128,128]{3,2,1,0:...) custom-call(f32[33]{0:T(128)S(1)} %pad_convert_fusion.keep_ref, ...), custom_call_target="tpu_custom_call" | custom-call | bytes 125829120 | tf_op jit(solution)/shard_map/pallas_call | solution.py:117
  138.4 1.3 constant_dynamic-slice_fusion.5
  140.4 6.4 convolution_convert_fusion.2.part_ref
  146.8 78.7 %shard_map.204 = (bf16[1024,2048]{1,0:T(8,128)(2,1)}, f32[2,128,2048]{2,1,0:T(8,128)S(1)}) custom-call(bf16[1024,2048]{1,0:T(8,128)(2,1)} %convolution_convert_fusion.2.part_ref, bf16[2,128,2048]{2,1,0:T(8,128)(2,1)S(1)} %bitcast.198, f32[1,2048]{1,0:T(1,128)S(1)} %bitcast.208), custom_call_target="tpu_custom_call" | custom-call | bytes 262144000 | tf_op jit(solution)/shard_map/pallas_call | solution.py:752
  225.6 17.9 %convolution_bitcast_fusion = f32[2,1024,1408]{2,1,0:T(8,128)S(1)} fusion(bf16[2,2048,1408]{2,1,0:T(8,128)(2,1)} %all-gather.6.cloned.1.call-done, bf16[1024,2048]{1,0:T(8,128)(2,1)} %get-tuple-element.29), kind=kOutput, calls=%fused_computation.11 | convolution fusion | flops 11811160064 | bytes 27262976 | tf_op jit(solution)/shard_map/td,sdf->stf/dot_general | solution.py:893
  243.5 1.7 multiply_convert_fusion
  245.2 3.7 copy-done.33
  248.9 3.4 convolution_convert_fusion.3
  252.4 5.3 collective-permute-done.2
  257.7 4.6 add_convert_fusion.2.refs_4_
  262.3 1.2 slice.129
  264.8 11.7 %convolution_convert_fusion.1 = bf16[1024,2048]{1,0:T(8,128)(2,1)S(1)} fusion(bf16[1408,2048]{1,0:T(8,128)(2,1)} %all-gather.8.cloned.1.call-done, f32[2,1024,1408]{2,1,0:T(8,128)} %copy-done.33, bf16[]{:T(256)} %bitcast.29), kind=kOutput, calls=%fused_computation.44 | convolution fusion | flops 5917769728 | bytes 21495810 | tf_op jit(solution)/shard_map/dot_general | solution.py:897
  276.5 2.0 copy-done.39
  279.6 14.7 %fusion.11 = (bf16[1024,1408]{1,0:T(8,128)(2,1)}, bf16[1024,1408]{1,0:T(8,128)(2,1)}) fusion(f32[2,1024,1408]{2,1,0:T(8,128)} %copy-done.33, f32[]{:T(128)} %bitcast.34, bf16[1408,2048]{1,0:T(8,128)(2,1)} %all-gather.8.cloned.1.call-done, bf16[1,1024,2048]{2,1,0:T(8,128)(2,1)S(1)} %copy-done.60), kind=kOutput, calls=%fused_computation.21 | convolution fusion | flops 5925765120 | bytes 27262980 | tf_op jit(solution)/shard_map/dot_general | solution.py:903
  296.2 3.5 fusion.47
  299.7 2.9 collective-permute-done.3
  302.6 1.3 copy-done.65
  303.9 5.0 add_convert_fusion.1.refs_5_
  309.3 2.3 constant_dynamic-slice_fusion.4
  311.7 4.9 all-to-all-start
  316.9 6.2 fusion.45
  323.1 6.8 add_convert_fusion.refs_6_
  330.0 18.0 %bitcast_convert_fusion.part_ref = bf16[1024,2048]{1,0:T(8,128)(2,1)} fusion(bf16[2,2048,1408]{2,1,0:T(8,128)(2,1)} %all-gather.6.cloned.1.call-done, bf16[1,1024,1408]{2,1,0:T(8,128)(2,1)} %bitcast.226, bf16[1,1024,1408]{2,1,0:T(8,128)(2,1)} %bitcast.225), kind=kOutput, calls=%fused_computation.6 | convolution fusion | flops 11816140800 | bytes 21495808 | tf_op jit(solution)/shard_map/stf,sdf->td/dot_general | solution.py:908
  348.0 16.6 %all-to-all-done = bf16[4,256,2048]{2,1,0:T(8,128)(2,1)} async-done(((bf16[4,256,2048]{2,1,0:T(8,128)(2,1)}), bf16[4,256,2048]{2,1,0:T(8,128)(2,1)}, u32[]{:S(2)}, u32[]{:S(2)}) %all-to-all-start) | async-done | bytes 4194336 | tf_op jit(solution)/shard_map/all_to_all | solution.py:900
  364.6 3.3 convert_reduce_fusion
  368.3 1.6 copy-done.12
  369.9 77.1 %shard_map.205 = (bf16[1024,2048]{1,0:T(8,128)(2,1)}, f32[2,128,2048]{2,1,0:T(8,128)S(1)}, f32[1,2048]{1,0:T(1,128)S(1)}) custom-call(bf16[1024,2048]{1,0:T(8,128)(2,1)} %bitcast_convert_fusion.part_ref, f32[2,128,2048]{2,1,0:T(8,128)} %copy-done.2, bf16[2,128,2048]{2,1,0:T(8,128)(2,1)S(1)} %bitcast.202, f32[1,2048]{1,0:T(1,128)S(1)} %bitcast.209, ...), custom_call_target="tpu_custom_call" | custom-call | bytes 262144000 | tf_op jit(solution)/shard_map/pallas_call | solution.py:752
  447.0 1.2 slice.106
  451.0 1.5 collective-permute-start.8
  452.5 5.2 fusion.52
  457.8 1.9 collective-permute-done.9
  460.0 15.0 %collective-permute-done.6.refs_5_ = bf16[256,2048]{1,0:T(8,128)(2,1)S(1)} collective-permute-done((bf16[256,2048]{1,0:T(8,128)(2,1)S(1)}, bf16[256,2048]{1,0:T(8,128)(2,1)S(1)}, u32[]{:S(2)}, u32[]{:S(2)}) %collective-permute-start.6) | collective-permute-done | bytes 1048608 | tf_op jit(solution)/shard_map/ppermute | solution.py:934
  475.6 19.2 %collective-permute-done.7.refs_6_ = bf16[256,2048]{1,0:T(8,128)(2,1)S(1)} collective-permute-done((bf16[256,2048]{1,0:T(8,128)(2,1)S(1)}, bf16[256,2048]{1,0:T(8,128)(2,1)S(1)}, u32[]{:S(2)}, u32[]{:S(2)}) %collective-permute-start.7) | collective-permute-done | bytes 1048608 | tf_op jit(solution)/shard_map/ppermute | solution.py:934
  502.1 1.2 copy-done.21
  503.3 1.2 copy-done.23
  504.5 1.2 copy-done.25
  505.7 26.7 %shard_map.206 = (bf16[2048,896]{1,0:T(8,128)(2,1)}, f32[4,768]{1,0:T(4,128)S(1)}, f32[1,128]{1,0:T(1,128)S(1)}) custom-call(f32[33]{0:T(128)S(1)} %pad_convert_fusion.keep_ref, s32[32]{0:T(128)S(1)} %convert_element_type.163.count_ref, bf16[2048,896]{1,0:T(8,128)(2,1)} %convolution_convert_fusion.4.raw_ref.prev_ref, ...), custom_call_target="tpu_custom_call" | custom-call | bytes 125829120 | tf_op jit(solution)/shard_map/pallas_call | solution.py:229
  532.4 2.5 broadcast_add_fusion
  535.7 8.5 %convolution_convert_fusion.5.refs_10_ = bf16[2048,768]{1,0:T(8,128)(2,1)} fusion(bf16[2048,896]{1,0:T(8,128)(2,1)S(1)} %broadcast_add_fusion, bf16[1024,2048]{1,0:T(8,128)(2,1)S(1)} %copy-done.38, bf16[1024,2048]{1,0:T(8,128)(2,1)S(1)} %copy-done.35), kind=kOutput, calls=%fused_computation.49 | convolution fusion | flops 6460801024 | bytes 14680064 | tf_op jit(solution)/shard_map/dot_general | solution.py:943
  544.3 4.9 copy.32
  549.3 2.1 fusion.35
  553.1 2.3 maximum_bitcast_fusion
  555.4 1.2 convert_element_type.206
  556.6 1.3 slice.135
  559.3 3.9 fusion.49
  563.3 11.4 %convolution_convert_fusion.part_ref = bf16[2048,2048]{1,0:T(8,128)(2,1)} fusion(bf16[2048,896]{1,0:T(8,128)(2,1)S(1)} %copy-done.43, bf16[2048,2]{1,0:T(8,128)(2,1)S(1)} %copy-done.52, bf16[2048,256]{1,0:T(8,128)(2,1)S(1)} %copy-done.50, bf16[2048,256]{1,0:T(8,128)(2,1)S(1)} %copy-done.48, bf16[2048,256]{1,0:T(8,128)(2,1)S(1)} %copy-done.46), kind=kOutput, calls=%fused_computation.8 | convolution fusion | flops 7538737152 | bytes 15212544 | tf_op jit(solution)/shard_map/dot_general | solution.py:939
  574.7 1.8 maximum_convert_fusion
  576.5 1.5 copy-done.36
  577.9 3.8 fusion.33
  581.9 3.6 add_convert_fusion.3.refs_9_
  585.8 1.2 copy-done.11
  588.2 87.4 %shard_map.207 = (bf16[1024,2048]{1,0:T(8,128)(2,1)}, f32[16,2048]{1,0:T(8,128)S(1)}) custom-call(bf16[2048,2048]{1,0:T(8,128)(2,1)} %convolution_convert_fusion.part_ref, bf16[2,128,2048]{2,1,0:T(8,128)(2,1)S(1)} %bitcast.199, f32[2,128,2048]{2,1,0:T(8,128)} %copy-done.19, f32[1,2048]{1,0:T(1,128)S(1)} %bitcast.207, f32[16,2048]{1,0:T(8,128)S(1)} %concatenate.37.refs_3_, ...), custom_call_target="tpu_custom_call" | custom-call | bytes 262144000 | tf_op jit(solution)/shard_map/pallas_call | solution.py:752
  677.4 6.7 bitcast_convert_fusion.1
  685.8 1.8 convert_element_type.204
  688.7 1.6 copy.33
  (229 shorter events, 32.5 us)
Async XLA Ops:
  7.2 37.8 %copy-start = (f32[3,4,512]{2,1,0:T(4,128)S(1)}, f32[3,4,512]{2,1,0:T(4,128)}, u32[]{:S(2)}) copy-start(f32[3,4,512]{2,1,0:T(4,128)} %param.16) | copy-start | bytes 73732
  7.2 88.4 %all-gather.4.cloned.1.call-start = ((), (), s32[]{:S(2)}) async-start(), calls=%async_computation.6 | async-start | bytes 9437184 | tf_op jit(solution)/shard_map/all_gather | solution.py:842
  8.3 6.3 copy-start.27
  10.6 215.0 %all-gather.6.cloned.1.call-start = ((), (), s32[]{:S(2)}) async-start(), calls=%async_computation.7 | async-start | bytes 12976128 | tf_op jit(solution)/shard_map/all_gather | solution.py:842
  11.3 253.4 %all-gather.8.cloned.1.call-start = ((), (), s32[]{:S(2)}) async-start(), calls=%async_computation.8 | async-start | bytes 6488064 | tf_op jit(solution)/shard_map/all_gather | solution.py:842
  14.8 3.6 copy-start.61
  14.8 27.9 %copy-start.62 = (s32[1,3]{1,0:T(1,128)S(1)}, s32[1,3]{1,0:T(1,128)}, u32[]{:S(2)}) copy-start(s32[1,3]{1,0:T(1,128)} %param.13) | copy-start | bytes 40
  17.9 27.2 %collective-permute-start = (bf16[1024,2048]{1,0:T(8,128)(2,1)}, bf16[1024,2048]{1,0:T(8,128)(2,1)}, u32[]{:S(2)}, u32[]{:S(2)}) collective-permute-start(bf16[1024,2048]{1,0:T(8,128)(2,1)} %fusion.2), channel_id=1, source_target_pairs={{0,16},{16,0},{1,17},{17,1},{2,18},{18,2},{3,19},{19,3},{4,20},{20... | collective-permute-start | bytes 12582920 | tf_op jit(solution)/shard_map/ppermute | solution.py:773
  18.3 481.5 %reduce-scatter.6.cloned.1.call-start = ((), (), s32[]{:S(2)}) async-start(), calls=%async_computation.9 | async-start | bytes 3604480 | tf_op jit(solution)/shard_map/reduce_scatter | solution.py:819
  42.7 55.9 %copy-start.51 = (bf16[2048,2]{1,0:T(8,128)(2,1)}, bf16[2048,2]{1,0:T(8,128)(2,1)S(1)}, u32[]{:S(2)}) copy-start(bf16[2048,2]{1,0:T(8,128)(2,1)S(1)} %copy.35) | copy-start | bytes 24580
  95.6 4.0 copy-start.37
  98.4 3.8 copy-start.34
  98.6 14.4 %copy-start.45 = (bf16[2048,256]{1,0:T(8,128)(2,1)}, bf16[2048,256]{1,0:T(8,128)(2,1)S(1)}, u32[]{:S(2)}) copy-start(bf16[2048,256]{1,0:T(8,128)(2,1)S(1)} %get-tuple-element.71) | copy-start | bytes 3145732
  98.6 14.4 %copy-start.47 = (bf16[2048,256]{1,0:T(8,128)(2,1)}, bf16[2048,256]{1,0:T(8,128)(2,1)S(1)}, u32[]{:S(2)}) copy-start(bf16[2048,256]{1,0:T(8,128)(2,1)S(1)} %get-tuple-element.72) | copy-start | bytes 3145732
  98.7 14.4 %copy-start.49 = (bf16[2048,256]{1,0:T(8,128)(2,1)}, bf16[2048,256]{1,0:T(8,128)(2,1)S(1)}, u32[]{:S(2)}) copy-start(bf16[2048,256]{1,0:T(8,128)(2,1)S(1)} %get-tuple-element.73) | copy-start | bytes 3145732
  102.2 10.8 %copy-start.30 = (f32[128]{0:T(128)S(1)}, f32[128]{0:T(128)}, u32[]{:S(2)}) copy-start(f32[128]{0:T(128)} %param.18) | copy-start | bytes 1540
  138.1 2.0 collective-permute-start.1
  139.7 7.1 %copy-start.4 = (bf16[1,256,2048]{2,1,0:T(8,128)(2,1)}, bf16[1,256,2048]{2,1,0:T(8,128)(2,1)S(1)}, u32[]{:S(2)}) copy-start(bf16[1,256,2048]{2,1,0:T(8,128)(2,1)S(1)} %constant_dynamic-slice_fusion.5) | copy-start | bytes 3145732
  140.3 6.5 copy-start.53
  140.3 6.5 copy-start.56
  140.3 6.4 copy-start.29
  225.5 142.4 %copy-start.2 = (f32[2,128,2048]{2,1,0:T(8,128)}, f32[2,128,2048]{2,1,0:T(8,128)S(1)}, u32[]{:S(2)}) copy-start(f32[2,128,2048]{2,1,0:T(8,128)S(1)} %get-tuple-element.28.refs_0_) | copy-start | bytes 6291460
  243.5 5.4 copy-start.33
  243.5 5.4 copy-start.59
  252.3 5.3 collective-permute-start.2
  263.5 236.3 %reduce-scatter.8.cloned.1.call-start = ((), (), s32[]{:S(2)}) async-start(), calls=%async_computation.10 | async-start | bytes 3604480 | tf_op jit(solution)/shard_map/reduce_scatter | solution.py:819
  264.8 14.9 %copy-start.60 = (bf16[1,1024,2048]{2,1,0:T(8,128)(2,1)S(1)}, bf16[1,1024,2048]{2,1,0:T(8,128)(2,1)}, u32[]{:S(2)}) copy-start(bf16[1,1024,2048]{2,1,0:T(8,128)(2,1)} %param.23) | copy-start | bytes 12582916
  279.6 15.0 %copy-start.44 = (bf16[1024,2048]{1,0:T(8,128)(2,1)S(1)}, bf16[1024,2048]{1,0:T(8,128)(2,1)}, u32[]{:S(2)}) copy-start(bf16[1024,2048]{1,0:T(8,128)(2,1)} %get-tuple-element.29) | copy-start | bytes 12582916
  294.3 8.3 %collective-permute-start.4 = (bf16[1024,1408]{1,0:T(8,128)(2,1)}, bf16[1024,1408]{1,0:T(8,128)(2,1)S(1)}, u32[]{:S(2)}, u32[]{:S(2)}) collective-permute-start(bf16[1024,1408]{1,0:T(8,128)(2,1)} %get-tuple-element.67), channel_id=1, source_target_pairs={{0,16},{16,0},{1,17},{17,1},{2,18},{18,2},{3,19},{19,3},{4,20},{20... | collective-permute-start | bytes 8650760 | tf_op jit(solution)/shard_map/ppermute | solution.py:773
  294.8 7.8 %collective-permute-start.3 = (bf16[1024,1024]{1,0:T(8,128)(2,1)S(1)}, bf16[1024,1024]{1,0:T(8,128)(2,1)S(1)}, u32[]{:S(2)}, u32[]{:S(2)}) collective-permute-start(bf16[1024,1024]{1,0:T(8,128)(2,1)S(1)} %constant_dynamic-slice_fusion.3), channel_id=1, source_target_pairs={{0,16},{16,0},{1,17},{17,1},{2,18},{18,2},{3,19},{19,3},{4,20},{20... | collective-permute-start | bytes 6291464 | tf_op jit(solution)/shard_map/ppermute | solution.py:773
  309.0 14.1 %collective-permute-start.5 = (bf16[1024,1408]{1,0:T(8,128)(2,1)}, bf16[1024,1408]{1,0:T(8,128)(2,1)}, u32[]{:S(2)}, u32[]{:S(2)}) collective-permute-start(bf16[1024,1408]{1,0:T(8,128)(2,1)} %get-tuple-element.68), channel_id=1, source_target_pairs={{0,16},{16,0},{1,17},{17,1},{2,18},{18,2},{3,19},{19,3},{4,20},{20... | collective-permute-start | bytes 8650760 | tf_op jit(solution)/shard_map/ppermute | solution.py:773
  311.7 52.9 %all-to-all-start = ((bf16[4,256,2048]{2,1,0:T(8,128)(2,1)}), bf16[4,256,2048]{2,1,0:T(8,128)(2,1)}, u32[]{:S(2)}, u32[]{:S(2)}) async-start(bf16[4,256,2048]{2,1,0:T(8,128)(2,1)} %bitcast.213), calls=%async_computation | async-start | bytes 8388608 | tf_op jit(solution)/shard_map/all_to_all | solution.py:900
  316.6 240.0 %reduce-scatter.10.cloned.1.call-start = ((), (), s32[]{:S(2)}) async-start(), calls=%async_computation.11 | async-start | bytes 3604480 | tf_op jit(solution)/shard_map/reduce_scatter | solution.py:819
  316.9 6.2 copy-start.66
  330.0 354.1 %reduce-scatter.12.cloned.1.call-start = ((), (), s32[]{:S(2)}) async-start(), calls=%async_computation.12 | async-start | bytes 3932160 | tf_op jit(solution)/shard_map/reduce_scatter | solution.py:1000
  367.9 79.1 %copy-start.32 = (f32[256,2048]{1,0:T(8,128)}, f32[256,2048]{1,0:T(8,128)S(1)}, u32[]{:S(2)}) copy-start(f32[256,2048]{1,0:T(8,128)S(1)} %convert_reduce_fusion) | copy-start | bytes 6291460
  447.0 10.7 %copy-start.19 = (f32[2,128,2048]{2,1,0:T(8,128)}, f32[2,128,2048]{2,1,0:T(8,128)S(1)}, u32[]{:S(2)}) copy-start(f32[2,128,2048]{2,1,0:T(8,128)S(1)} %get-tuple-element.37.refs_1_) | copy-start | bytes 6291460
  448.9 26.2 %collective-permute-start.6 = (bf16[256,2048]{1,0:T(8,128)(2,1)S(1)}, bf16[256,2048]{1,0:T(8,128)(2,1)S(1)}, u32[]{:S(2)}, u32[]{:S(2)}) collective-permute-start(bf16[256,2048]{1,0:T(8,128)(2,1)S(1)} %broadcast_add_fusion.1), channel_id=1, source_target_pairs={{0,4},{4,0},{8,12},{12,8},{1,5},{5,1},{9,13},{13,9},{2,6},{6,2},{1... | collective-permute-start | bytes 3145736 | tf_op jit(solution)/shard_map/ppermute | solution.py:934
  449.8 45.0 %collective-permute-start.7 = (bf16[256,2048]{1,0:T(8,128)(2,1)S(1)}, bf16[256,2048]{1,0:T(8,128)(2,1)S(1)}, u32[]{:S(2)}, u32[]{:S(2)}) collective-permute-start(bf16[256,2048]{1,0:T(8,128)(2,1)S(1)} %broadcast_add_fusion.1), channel_id=1, source_target_pairs={{0,8},{4,12},{8,0},{12,4},{1,9},{5,13},{9,1},{13,5},{2,10},{6,14},... | collective-permute-start | bytes 3145736 | tf_op jit(solution)/shard_map/ppermute | solution.py:934
  451.0 46.6 %collective-permute-start.8 = (bf16[256,2048]{1,0:T(8,128)(2,1)S(1)}, bf16[256,2048]{1,0:T(8,128)(2,1)S(1)}, u32[]{:S(2)}, u32[]{:S(2)}) collective-permute-start(bf16[256,2048]{1,0:T(8,128)(2,1)S(1)} %broadcast_add_fusion.1), channel_id=1, source_target_pairs={{0,12},{4,8},{8,4},{12,0},{1,13},{5,9},{9,5},{13,1},{2,14},{6,10},... | collective-permute-start | bytes 3145736 | tf_op jit(solution)/shard_map/ppermute | solution.py:934
  457.7 2.0 collective-permute-start.9
  475.1 57.3 %copy-start.6 = (bf16[256,2048]{1,0:T(8,128)(2,1)}, bf16[256,2048]{1,0:T(8,128)(2,1)S(1)}, u32[]{:S(2)}) copy-start(bf16[256,2048]{1,0:T(8,128)(2,1)S(1)} %collective-permute-done.6.refs_5_) | copy-start | bytes 3145732
  505.7 29.2 %copy-start.38 = (bf16[1024,2048]{1,0:T(8,128)(2,1)S(1)}, bf16[1024,2048]{1,0:T(8,128)(2,1)}, u32[]{:S(2)}) copy-start(bf16[1024,2048]{1,0:T(8,128)(2,1)} %get-tuple-element.70) | copy-start | bytes 12582916
  535.7 8.5 %copy-start.42 = (bf16[2048,896]{1,0:T(8,128)(2,1)}, bf16[2048,896]{1,0:T(8,128)(2,1)S(1)}, u32[]{:S(2)}) copy-start(bf16[2048,896]{1,0:T(8,128)(2,1)S(1)} %broadcast_add_fusion) | copy-start | bytes 11010052
  544.3 5.0 copy-start.3
  549.2 136.6 %reduce-scatter.14.cloned.1.call-start = ((), (), s32[]{:S(2)}) async-start(), calls=%async_computation.13 | async-start | bytes 1310720 | tf_op jit(solution)/shard_map/reduce_scatter | solution.py:819
  553.1 6.2 copy-start.54
  553.1 6.2 copy-start.57
  556.6 6.6 copy-start.52
  556.6 6.6 copy-start.43
  556.6 6.7 copy-start.46
  556.6 6.7 copy-start.48
  556.6 6.7 copy-start.50
  563.2 11.5 %copy-start.15 = (bf16[256,1408]{1,0:T(8,128)(2,1)S(1)}, bf16[256,1408]{1,0:T(8,128)(2,1)}, u32[]{:S(2)}) copy-start(bf16[256,1408]{1,0:T(8,128)(2,1)} %reduce-scatter.10.cloned.1.call-done.refs_8_) | copy-start | bytes 2162692
  563.2 11.5 %copy-start.18 = (bf16[256,1408]{1,0:T(8,128)(2,1)S(1)}, bf16[256,1408]{1,0:T(8,128)(2,1)}, u32[]{:S(2)}) copy-start(bf16[256,1408]{1,0:T(8,128)(2,1)} %reduce-scatter.8.cloned.1.call-done.rest_1_) | copy-start | bytes 2162692
  563.2 18.5 %collective-permute-start.10 = (bf16[512,1024]{1,0:T(8,128)(2,1)}, bf16[512,1024]{1,0:T(8,128)(2,1)}, u32[]{:S(2)}, u32[]{:S(2)}) collective-permute-start(bf16[512,1024]{1,0:T(8,128)(2,1)} %fusion.49), channel_id=1, source_target_pairs={{0,16},{16,0},{1,17},{17,1},{2,18},{18,2},{3,19},{19,3},{4,20},{20... | collective-permute-start | bytes 3145736 | tf_op jit(solution)/shard_map/ppermute | solution.py:773
  577.9 3.8 copy-start.55
  577.9 3.8 copy-start.58
  577.9 4.0 copy-start.63
  581.7 4.1 copy-start.5
  581.7 4.1 copy-start.8
  581.7 4.1 copy-start.28
  677.4 13.0 %copy-start.1 = (f32[3,4,512]{2,1,0:T(4,128)S(1)}, f32[3,4,512]{2,1,0:T(4,128)}, u32[]{:S(2)}) copy-start(f32[3,4,512]{2,1,0:T(4,128)} %param.16) | copy-start | bytes 73732
  685.1 2.5 collective-permute-start.11
  (25 other events, 43.2 us)
Sparse Core Ops, SparseCore 0:
  10.7 84.8 all-gather.3
  97.2 106.7 all-gather.5
  205.6 59.1 all-gather.7
  267.5 54.3 reduce-scatter.5
  324.0 56.0 reduce-scatter.7
  382.3 56.0 reduce-scatter.9
  549.3 58.4 reduce-scatter.11
  610.1 27.1 reduce-scatter.13

commit v4 on v3

--- a/solution.py
+++ b/solution.py
@@ -122,12 +122,13 @@
             jax.ShapeDtypeStruct((nc,heads,HDIM,HDIM),BF16),jax.ShapeDtypeStruct((nc,heads,HDIM,HDIM),BF16),
             jax.ShapeDtypeStruct((n,width),BF16),jax.ShapeDtypeStruct((n,width),BF16)],
         scratch_shapes=[pltpu.VMEM((rows+8,3*width),F32),pltpu.VMEM((heads,HDIM,HDIM),F32)],
-        compiler_params=pltpu.CompilerParams(vmem_limit_bytes=48<<20),
+        compiler_params=pltpu.CompilerParams(vmem_limit_bytes=56<<20),
         cost_estimate=pl.CostEstimate(flops=0,bytes_accessed=120<<20,transcendentals=0),
     )(keep,count,raw,cw,gain)
 
 def bwd_kernel(heads, group, keep_ref, count_ref, raw_ref, prev_ref, cw_ref, gain_ref, gno_ref, o_ref, s_ref, t_ref, w_ref, r_ref, *rest):
-    graw_ref, gcw_ref, ggain_ref, ext, gext, grad_state = rest[-6:]
+    block_ref=rest[0]
+    graw_ref, gcw_ref, ggain_ref, all_ref, ext, gext, grad_state, local_sem, send_sem, recv_sem = rest[-10:]
     rows=group*CHUNK
     step=pl.program_id(0); steps=pl.num_programs(0)
     width=heads*HDIM
@@ -141,6 +142,31 @@
     def _():
         gext[rows:rows+8,:]=gext[0:8,:]
     first=jnp.where(step==steps-1,0.0,1.0)
+    place=lax.axis_index("mp")
+    across_x=place+1-2*(place%2)
+    across_y=(place+2)%4
+    part=block_ref.shape[0]//2
+    at=lambda of,half: all_ref.at[pl.ds(pl.multiple_of((2*of+half)*part,part),part)]
+    def copy(index,source,target,other):
+        return pltpu.make_async_remote_copy(src_ref=source,dst_ref=target,send_sem=send_sem.at[index],recv_sem=recv_sem.at[index],
+            device_id={"mp":other},device_id_type=pl.DeviceIdType.MESH)
+    top,low=block_ref.at[pl.ds(0,part)],block_ref.at[pl.ds(part,part)]
+    keep_own=pltpu.make_async_copy(block_ref,all_ref.at[pl.ds(pl.multiple_of(2*place*part,2*part),2*part)],local_sem)
+    sends=[copy(0,top,at(place,0),across_x),copy(1,low,at(place,1),across_y),copy(2,top,at(place,0),across_y),copy(3,low,at(place,1),across_x)]
+    onward=[copy(4,at(across_x,0),at(across_x,0),across_y),copy(5,at(across_y,1),at(across_y,1),across_x)]
+    @pl.when(step==0)
+    def _():
+        barrier=pltpu.get_barrier_semaphore()
+        for other in (across_x,across_y):
+            pl.semaphore_signal(barrier,inc=1,device_id={"mp":other},device_id_type=pl.DeviceIdType.MESH)
+        pl.semaphore_wait(barrier,2)
+        keep_own.start()
+        for send in sends: send.start()
+    @pl.when(step==steps//2)
+    def _():
+        for send,follow in zip(sends[:2],onward):
+            send.wait_recv()
+            follow.start()
     ext[0:8,:]=prev_ref[:,0:3*width].astype(F32)[8:16]*first
     ext[8:,:]=raw_ref[:,0:3*heads*HDIM].astype(F32)
     r,c=iotas()
@@ -218,8 +244,13 @@
                     total=total+(cw[j:j+1]*u['taps_later'][j-1])*gext[pl.ds(u['base']+j,CHUNK),lanes]
                 graw_ref[pl.ds(u['base'],CHUNK),lanes]=total.astype(BF16)
         graw_ref[pl.ds(u['base'],CHUNK),pl.ds(3*width,HDIM)]=(glog*u['sig_b']*(1.0-u['beta'])).astype(BF16)
-
-def backward(keep, count, raw, cw, gain, gno, o, s, t, w, r, group, dummies=()):
+    @pl.when(step==steps-1)
+    def _():
+        keep_own.wait()
+        for send in (*sends[2:],*onward): send.wait_recv()
+        for send in (*sends,*onward): send.wait_send()
+
+def backward(keep, count, raw, cw, gain, gno, o, s, t, w, r, group, block, dummies=()):
     n=raw.shape[0]; width=cw.shape[1]//3; heads=width//HDIM; rows=group*CHUNK
     steps=n//rows
     row=lambda w: pl.BlockSpec((rows,w),lambda i:(steps-1-i,0))
@@ -228,14 +259,15 @@
     prev=pl.BlockSpec((16,raw.shape[1]),lambda i:(jnp.maximum((steps-1-i)*(rows//16)-1,0),0))
     return pl.pallas_call(functools.partial(bwd_kernel,heads,group),
         grid=(steps,),
-        in_specs=[pl.BlockSpec(memory_space=pltpu.SMEM)]*2+[row(raw.shape[1]),prev,full(cw),full(gain),row(width),row(width),mat,mat,row(width),row(width)]+[pl.BlockSpec(memory_space=pl.ANY)]*len(dummies),
-        out_specs=[row(raw.shape[1]),pl.BlockSpec((KERNEL,3*width),lambda i:(0,0)),pl.BlockSpec((1,HDIM),lambda i:(0,0))],
+        in_specs=[pl.BlockSpec(memory_space=pltpu.SMEM)]*2+[row(raw.shape[1]),prev,full(cw),full(gain),row(width),row(width),mat,mat,row(width),row(width)]+[pl.BlockSpec(memory_space=pl.ANY)]*(1+len(dummies)),
+        out_specs=[row(raw.shape[1]),pl.BlockSpec((KERNEL,3*width),lambda i:(0,0)),pl.BlockSpec((1,HDIM),lambda i:(0,0)),pl.BlockSpec(memory_space=pl.ANY)],
         out_shape=[jax.ShapeDtypeStruct(raw.shape,BF16),
-            jax.ShapeDtypeStruct((KERNEL,3*width),F32),jax.ShapeDtypeStruct((1,HDIM),F32)],
-        scratch_shapes=[pltpu.VMEM((rows+8,3*width),F32),pltpu.VMEM((rows+8,3*width),F32),pltpu.VMEM((heads,HDIM,HDIM),F32)],
-        compiler_params=pltpu.CompilerParams(vmem_limit_bytes=48<<20),
+            jax.ShapeDtypeStruct((KERNEL,3*width),F32),jax.ShapeDtypeStruct((1,HDIM),F32),jax.ShapeDtypeStruct((4*block.shape[0],block.shape[1]),BF16)],
+        scratch_shapes=[pltpu.VMEM((rows+8,3*width),F32),pltpu.VMEM((rows+8,3*width),F32),pltpu.VMEM((heads,HDIM,HDIM),F32),
+            pltpu.SemaphoreType.DMA(()),pltpu.SemaphoreType.DMA((6,)),pltpu.SemaphoreType.DMA((6,))],
+        compiler_params=pltpu.CompilerParams(collective_id=3,has_side_effects=True,vmem_limit_bytes=56<<20),
         cost_estimate=pl.CostEstimate(flops=0,bytes_accessed=120<<20,transcendentals=0),
-    )(keep,count,raw,raw,cw,gain,gno,o,s,t,w,r,*dummies)
+    )(keep,count,raw,raw,cw,gain,gno,o,s,t,w,r,block,*dummies)
 
 
 def passed_along(block, axis, distance):
@@ -674,8 +706,20 @@
     small = []
     if small_sum:
         values, arrived = outs[-1], scratch[-1]
-        values[...] = inputs[-1 - small_sum["dummies"]][...]
+        first = n_in - small_sum["dummies"] - 4
+        ffn_gain, out_gain, beta, conv = inputs[first : first + 4]
+        heads, taps, width = beta.shape[0], conv.shape[0], conv.shape[1]
+        middle_lane = values.shape[1] // 2
+        values[...] = jnp.zeros_like(values)
         values[0:1, :] = gain
+        values[1:2, :] = ffn_gain[...]
+        values[2:3, 0 : out_gain.shape[1]] = out_gain[...]
+        for i in (0, 1):
+            share = jnp.where(core == i, 1.0, 0.0)
+            values[8 + i * heads : 8 + (i + 1) * heads, :] = beta[...] * share
+            at = 8 + 2 * heads
+            lane = i * middle_lane
+            values[at : at + taps, lane : lane + width] = conv[...] * share
     elif n_out > 2:
         outs[-1][...] = gain
 
@@ -742,10 +786,12 @@
     if small is not None:
         stages = lax.axis_size("row").bit_length() - 1 + 3
         copies = 20 + stages
-        scratch += [pltpu.VMEM((stages, 2, *small.shape), F32)]
+        height = 8 + 2 * small[2].shape[0] + small[3].shape[0]
+        shape = (height + -height % 8, model)
+        scratch += [pltpu.VMEM((stages, 2, *shape), F32)]
         small_sum = {"dummies": len(dummies)}
-        inputs = [*inputs, small]
-        outs = [*outs, jax.ShapeDtypeStruct(small.shape, F32)]
+        inputs = [*inputs, *small]
+        outs = [*outs, jax.ShapeDtypeStruct(shape, F32)]
     kernel = functools.partial(
         phase_kernel, middle, both_cores, small_sum, len(inputs) + len(dummies), 1 + len(outs)
     )
@@ -773,10 +819,6 @@
     return lax.ppermute(block, "seq", [(0, 1), (1, 0)])
 
 
-def across(block, bit):
-    return lax.ppermute(block, "mp", [(i, i ^ bit) for i in range(4)])
-
-
 def in_order(mine, other, core, axis):
     first = jnp.where(core == 0, mine, other)
     second = jnp.where(core == 0, other, mine)
@@ -804,15 +846,6 @@
 def own_columns(block, core):
     mine, other = halves(block, core, 1)
     return mine, swapped(other)
-
-
-def product_pair(left, right, core):
-    mine, other = halves(right, core, 1)
-    product = lambda part: lax.dot_general(
-        left, part, (((0,), (0,)), ((), ())), preferred_element_type=F32
-    )
-    incoming = swapped(product(other).astype(BF16))
-    return (product(mine) + incoming.astype(F32)).astype(BF16)
 
 
 def over_row(pair, axis):
@@ -893,7 +926,7 @@
     gate_up = jnp.einsum("td,sdf->stf", normed_mid, gateup_full, preferred_element_type=F32)
     gate_sig = jax.nn.sigmoid(gate_up[0])
     product = (gate_up[0] * gate_sig * gate_up[1]).astype(BF16)
-    down_pair = product_pair(product, grad_top, core)
+    down_pair = both_tokens((product, swapped(product)), own_columns(grad_top, core))
     ffn_part = jnp.dot(
         after(product, down_pair), down_full, preferred_element_type=F32
     ).astype(BF16)
@@ -927,61 +960,45 @@
 
     mine, other = halves(grad_normed_out, core, 1)
     grad_heads = in_order(mine, swapped(other), core, 0)
-    grad_raw, grad_conv_own, out_gain_part = backward(
-        keep, count, raw, conv_own, gain, grad_heads, *saved, group, [down_sum, gate_sum]
-    )
-    block_outs = [block_out] + [
-        lax.ppermute(after(block_out, grad_branch), "mp", [(i, i ^ k) for i in range(4)])
-        for k in (1, 2, 3)
-    ]
-    out_pair = product_pair(after(normed_out, up_sum), grad_branch, core)
-    grad_raw = after(grad_raw, *block_outs[1:])
+    out_pair = both_tokens(
+        (normed_out, swapped(after(normed_out, up_sum))), own_columns(grad_branch, core)
+    )
+    grad_raw, grad_conv_own, out_gain_part, block_out = backward(
+        keep,
+        count,
+        raw,
+        conv_own,
+        gain,
+        grad_heads,
+        *saved,
+        group,
+        block_out,
+        [down_sum, gate_sum],
+    )
     grad_normed = lax.dot_general(
         grad_raw, mix_weight, (((1,), (1,)), ((), ())), preferred_element_type=F32
     )
     grad_normed_part = grad_normed.astype(BF16)
-    grad_qkv = lax.dot_general(
-        normed,
-        grad_raw[:, : 3 * width],
-        (((0,), (0,)), ((), ())),
-        preferred_element_type=F32,
+    normed_mine, normed_other = halves(normed, core, 1)
+    by_columns = lambda part: lax.dot_general(
+        part, grad_raw[:, : 3 * width], (((0,), (0,)), ((), ())), preferred_element_type=F32
     ).astype(BF16)
+    qkv_other = swapped(by_columns(normed_other))
+    qkv_mine = by_columns(normed_mine)
     grad_beta = lax.dot_general(
         grad_raw[:, 3 * width :], normed, (((0,), (0,)), ((), ())), preferred_element_type=F32
     )[:own_heads]
-
-    line = lambda part: jnp.pad(part.reshape(1, -1), ((0, 0), (0, model - part.size)))
-    place = lambda part, lines: lax.dynamic_update_slice_in_dim(
-        jnp.zeros((2 * lines, model), F32), part, core * lines, axis=0
-    )
-    conv_lines = -(-grad_conv_own.size // model)
-    conv_part = jnp.pad(grad_conv_own.ravel(), (0, conv_lines * model - grad_conv_own.size))
-    small = jnp.concatenate(
-        [
-            jnp.zeros((1, model), F32),
-            ffn_gain_part,
-            line(out_gain_part[0]),
-            jnp.zeros((5, model), F32),
-            place(grad_beta, own_heads),
-            place(conv_part.reshape(conv_lines, model), conv_lines),
-        ]
-    )
-    small = jnp.pad(small, ((0, -small.shape[0] % 8), (0, 0)))
     grad_input, small = mp_phase(
         2,
         partial(normed_backward, False),
         grad_normed_part,
         [residual_own, grad_hidden, attn_gain[None, :]],
-        [*block_outs, up_sum, out_pair, grad_qkv],
+        [up_sum, out_pair, qkv_mine, qkv_other],
         [],
         both_cores=True,
-        small=small,
+        small=[ffn_gain_part, out_gain_part, grad_beta, grad_conv_own],
     )
     grad_input = grad_input.astype(F32)
-    block_outs = jnp.stack(block_outs)
-    block_out = jnp.concatenate(
-        [lax.dynamic_index_in_dim(block_outs, own ^ k, 0, keepdims=False) for k in range(4)]
-    )
     grad_attn_gain, grad_ffn_gain = small[0], small[1]
     grad_out_gain = small[2, : out_gain.shape[0]]
     span = beta_weight.shape[1]
@@ -989,20 +1006,15 @@
     grad_beta = lax.dynamic_slice_in_dim(small[8 : 8 + 2 * own_heads], place_no * span, span, axis=1)
     conv_at = 8 + 2 * own_heads
     conv_of = lambda i: (
-        small[conv_at + i * conv_lines : conv_at + (i + 1) * conv_lines]
-        .ravel()[: grad_conv_own.size]
+        small[conv_at : conv_at + KERNEL, i * (model // 2) : i * (model // 2) + 3 * width]
         .reshape(KERNEL, 3, width)
         .transpose(1, 0, 2)
     )
     grad_conv = jnp.concatenate([conv_of(0), conv_of(1)], axis=2)
     grad_down, grad_out = down_sum.astype(F32), over_row(out_pair, 1).astype(F32)
     grad_gateup = jnp.stack([gate_sum, up_sum]).astype(F32)
-    grad_qkv = lax.psum_scatter(
-        grad_qkv.reshape(2, -1, 3 * width), "row", scatter_dimension=1, tiled=True
-    )
-    mine, other = halves(grad_qkv, core, 0)
-    by_kind = lambda part: part[0].reshape(-1, 3, width).transpose(1, 0, 2)
-    grad_qkv = in_order(by_kind(mine), by_kind(swapped(other)), core, 2).astype(F32)
+    by_kind = lambda part: over_row(part, 0).reshape(-1, 3, width).transpose(1, 0, 2)
+    grad_qkv = in_order(by_kind(qkv_mine), by_kind(qkv_other), core, 2).astype(F32)
     return (
         block_out[None],
         grad_input[None],

time: 707 us -> 676 us (0.956)
  waiting for transfers between devices: 106 us -> 78.3 us
  local copies, waits for them, and re-layouts: 56.1 us -> 40.2 us
  Pallas kernels: 291 us -> 306 us
  matrix products: 146 us -> 154 us
    ppermute x3 -> x0, waiting for transfers between devices: 34.2 us -> none  [joined_shards(): lax.ppermute(after(block_out, grad_branch), 'mp', [(i, i ^ k) for i in ra...]
    dot_general x4 -> x8, matrix products: 21.6 us -> 38.6 us  [both_tokens(): lax.dot_general(a, b, (((0,), (0,)), ((), ())), preferred_element_type=F32)]
    pallas_call x1, Pallas kernels: 26.7 us -> 40.8 us  [backward(): pl.pallas_call(functools.partial(bwd_kernel, heads, group), grid=(steps,)...]
    unnamed x140 -> x85, local copies, waits for them, and re-layouts: 33 us -> 21.4 us
    reduce_scatter x4 -> x6, waiting for transfers between devices: 0.04 us -> 9.46 us  [over_row(): return lax.psum_scatter(pair, 'row', scatter_dimension=axis, tiled=True)]
    dot_general x5 -> x2, matrix products: 24.2 us -> 15.2 us  [joined_shards(): lax.dot_general(part, grad_raw[:, :3 * width], (((0,), (0,)), ((), ())),...]
  transfers between devices with their start and end apart: 21 -> 21, of which waited for: 9 -> 9; matrix products, arithmetic and copies ran while one was open for 30% -> 26% of each run, Pallas kernels for 42% -> 46%
where the time goes in v4:
time: 676 us; the launch traced here: 672 us
  Pallas kernels  306 us (45%)
  matrix products  154 us (23%)
  waiting for transfers between devices  78.3 us (12%)
  other arithmetic  42.9 us (6%)
  local copies, waits for them, and re-layouts  40.2 us (6%)
  blocking collectives  25.4 us (4%)
  between operations  16.7 us (2%)
  starting transfers between devices  8.24 us (1%)
    pallas_call x3, Pallas kernels, mp_phase(): pl.pallas_call(kernel, in_specs=[there if both_cores else here] + [here]...  244 us
    all_gather x3, waiting for transfers between devices, joined_shards(): lax.all_gather(weight, ('seq', 'row'), axis=1, tiled=True)  43.3 us
    pallas_call x1, Pallas kernels, backward(): pl.pallas_call(functools.partial(bwd_kernel, heads, group), grid=(steps,)...  40.8 us
    dot_general x8, matrix products, both_tokens(): lax.dot_general(a, b, (((0,), (0,)), ((), ())), preferred_element_type=F32)  38.6 us
    all_gather x1, blocking collectives, joined_shards(): lax.all_gather(weight, ('seq', 'row'), axis=1, tiled=True)  25.4 us
    unnamed x85, local copies, waits for them, and re-layouts  21.4 us
    pallas_call x1, Pallas kernels, forward(): pl.pallas_call(functools.partial(fwd_kernel, heads, group), grid=(n // ro...  21.3 us
    dot_general x1, matrix products, joined_shards(): jnp.einsum('stf,sdf->td', jnp.stack([grad_gate, grad_up]), gateup_full, p...  18.3 us
  transfers between devices with their start and end apart: 21, of which 9 were waited for; matrix products, arithmetic and copies ran while one was open for 26% of the time, Pallas kernels for 46%

profile of v4, /device:TPU:0, one launch (start us, length us, event | category | flops | bytes accessed | tf_op | source)
XLA Modules:
  0.0 672.0 jit_solution(445932131154559206)
XLA Ops:
  7.2 1.1 copy.34
  8.3 2.2 pad_maximum_fusion.5
  11.4 3.2 fusion
  14.8 3.0 fusion.2
  18.4 25.4 %all_gather.13 = bf16[4,2048]{1,0:T(4,128)(2,1)S(1)} all-gather(bf16[4,256]{1,0:T(4,128)(2,1)S(1)} %copy-done.36), channel_id=1, replica_groups=mesh['seq'=2,'mp'=4,'row'=4] {'seq','row'}, dimensions={1}, use_global_device_ids=true | all-gather | bytes 18432 | tf_op jit(solution)/shard_map/all_gather | solution.py:875
  48.0 7.6 %broadcast_select_fusion.1 = (bf16[1024,2048]{1,0:T(8,128)(2,1)}, bf16[1024,2048]{1,0:T(8,128)(2,1)}) fusion(bf16[1024,2048]{1,0:T(8,128)(2,1)} %collective-permute-done, pred[]{:T(512)S(6)} %eq.2, f32[2048]{0:T(1024)S(1)} %copy-done.13, f32[1024]{0:T(1024)S(1)} %add_rsqrt_fusion, bf16[1,1024,2048]{2,1,0:T(8,128)(2,1)} %param.12), kind=kLoop, calls=%fused_computation.51 | loop fusion | flops 12582912 | bytes 16789504 | tf_op jit(solution)/shard_map/jit(_where)/select_n | solution.py:823
  55.6 40.0 %all-gather.4.cloned.1.call-done = bf16[4,2048,512]{2,1,0:T(8,128)(2,1)} async-done(((bf16[4,256,512]{2,1,0:T(8,128)(2,1)}), bf16[4,2048,512]{2,1,0:T(8,128)(2,1)}) %all-gather.4.cloned.1.call-update) | async-done | bytes 8388624 | tf_op jit(solution)/shard_map/all_gather | solution.py:875
  95.6 2.8 slice-done
  98.7 1.0 copy-done.23
  99.7 2.6 copy-done.20
  102.2 10.8 %fusion.32.raw_ref.prev_ref = bf16[2048,896]{1,0:T(8,128)(2,1)} fusion(bf16[1024,2048]{1,0:T(8,128)(2,1)S(1)} %copy-done.23, bf16[1024,2048]{1,0:T(8,128)(2,1)S(1)} %copy-done.20, bf16[2048,2]{1,0:T(8,128)(2,1)S(1)} %copy.39, bf16[2048,256]{1,0:T(8,128)(2,1)S(1)} %get-tuple-element.75, bf16[2048,256]{1,0:T(8,128)(2,1)S(1)} %get-tuple-element.74, ...), kind=kOutput, calls=%fused_computation.55 | convolution fusion | flops 7553155072 | bytes 15212544 | tf_op jit(solution)/shard_map/dot_general | solution.py:901
  113.0 21.3 %shard_map.203 = (bf16[2048,256]{1,0:T(8,128)(2,1)}, f32[2048,256]{1,0:T(8,128)}, bf16[16,2,128,128]{3,2,1,0:T(8,128)(2,1)}, bf16[16,2,128,128]{3,2,1,0:T(8,128)...) custom-call(f32[33]{0:T(128)} %pad_convert_fusion.keep_ref, s32[32]{0:T(128)} %convert_element_type.120.count_ref, ...), custom_call_target="tpu_custom_call" | custom-call | bytes 125829120 | tf_op jit(solution)/shard_map/pallas_call | solution.py:117
  134.2 1.1 constant_dynamic-slice_fusion.6
  135.6 1.3 constant_dynamic-slice_fusion.5
  137.3 1.3 broadcast_select_fusion.5
  138.6 6.0 convolution_convert_fusion.2.part_ref
  144.6 78.9 %shard_map.204 = (bf16[1024,2048]{1,0:T(8,128)(2,1)}, f32[2,128,2048]{2,1,0:T(8,128)S(1)}) custom-call(bf16[1024,2048]{1,0:T(8,128)(2,1)} %convolution_convert_fusion.2.part_ref, bf16[2,128,2048]{2,1,0:T(8,128)(2,1)S(1)} %bitcast.166, f32[1,2048]{1,0:T(1,128)S(1)} %bitcast.171), custom_call_target="tpu_custom_call" | custom-call | bytes 262144000 | tf_op jit(solution)/shard_map/pallas_call | solution.py:798
  223.6 18.0 %convolution_bitcast_fusion = f32[2,1024,1408]{2,1,0:T(8,128)S(1)} fusion(bf16[2,2048,1408]{2,1,0:T(8,128)(2,1)} %all-gather.8.cloned.1.call-done, bf16[1024,2048]{1,0:T(8,128)(2,1)} %get-tuple-element.29), kind=kOutput, calls=%fused_computation.15 | convolution fusion | flops 11811160064 | bytes 27262976 | tf_op jit(solution)/shard_map/td,sdf->stf/dot_general | solution.py:926
  241.6 2.1 fusion.8
  243.8 3.2 copy-done.28
  247.3 5.9 fusion.33
  253.2 6.4 add_convert_fusion.2.refs_4_
  259.6 1.2 slice.104
  261.5 3.3 all-gather.6.cloned.1.call-done
  264.8 10.1 %convolution_convert_fusion.1 = bf16[1024,2048]{1,0:T(8,128)(2,1)S(1)} fusion(bf16[1408,2048]{1,0:T(8,128)(2,1)} %all-gather.6.cloned.1.call-done, bf16[1024,1408]{1,0:T(8,128)(2,1)} %copy-done.26, bf16[]{:T(256)} %bitcast.30), kind=kOutput, calls=%fused_computation.52 | convolution fusion | flops 5909118976 | bytes 12845058 | tf_op jit(solution)/shard_map/dot_general | solution.py:930
  274.9 1.9 copy-done.25
  278.0 14.8 %fusion.11 = (bf16[1024,1408]{1,0:T(8,128)(2,1)}, bf16[1024,1408]{1,0:T(8,128)(2,1)}) fusion(f32[2,1024,1408]{2,1,0:T(8,128)} %copy-done.19, f32[]{:T(128)} %bitcast.31, bf16[1408,2048]{1,0:T(8,128)(2,1)} %all-gather.6.cloned.1.call-done, bf16[1,1024,2048]{2,1,0:T(8,128)(2,1)S(1)} %copy-done.29), kind=kOutput, calls=%fused_computation.25 | convolution fusion | flops 5925765120 | bytes 27262980 | tf_op jit(solution)/shard_map/dot_general | solution.py:936
  294.6 3.6 fusion.44
  298.1 3.0 collective-permute-done.4
  301.1 1.3 copy-done.39
  302.4 5.0 add_convert_fusion.refs_6_
  308.4 2.3 constant_dynamic-slice_fusion.4
  310.7 4.9 all-to-all-start
  315.6 6.1 fusion.46
  321.8 6.9 %add_convert_fusion.1.refs_5_ = bf16[1024,1408]{1,0:T(8,128)(2,1)} fusion(f32[1024,1408]{1,0:T(8,128)S(1)} %fusion.46, bf16[1024,1024]{1,0:T(8,128)(2,1)S(1)} %copy-done.40, bf16[1024,1408]{1,0:T(8,128)(2,1)} %collective-permute-done.5), kind=kOutput, calls=%fused_computation.37 | convolution fusion | flops 2955673600 | bytes 13631488 | tf_op jit(solution)/shard_map/dot_general | solution.py:840
  328.7 18.3 %bitcast_convert_fusion.part_ref = bf16[1024,2048]{1,0:T(8,128)(2,1)} fusion(bf16[2,2048,1408]{2,1,0:T(8,128)(2,1)} %all-gather.8.cloned.1.call-done, bf16[1,1024,1408]{2,1,0:T(8,128)(2,1)} %bitcast.189, bf16[1,1024,1408]{2,1,0:T(8,128)(2,1)} %bitcast.188), kind=kOutput, calls=%fused_computation.10 | convolution fusion | flops 11816140800 | bytes 21495808 | tf_op jit(solution)/shard_map/stf,sdf->td/dot_general | solution.py:941
  347.0 16.7 %all-to-all-done = bf16[4,256,2048]{2,1,0:T(8,128)(2,1)} async-done(((bf16[4,256,2048]{2,1,0:T(8,128)(2,1)}), bf16[4,256,2048]{2,1,0:T(8,128)(2,1)}, u32[]{:S(2)}, u32[]{:S(2)}) %all-to-all-start) | async-done | bytes 4194336 | tf_op jit(solution)/shard_map/all_to_all | solution.py:933
  363.7 3.3 convert_reduce_fusion
  368.1 76.8 %shard_map.205 = (bf16[1024,2048]{1,0:T(8,128)(2,1)}, f32[2,128,2048]{2,1,0:T(8,128)S(1)}, f32[1,2048]{1,0:T(1,128)S(1)}) custom-call(bf16[1024,2048]{1,0:T(8,128)(2,1)} %bitcast_convert_fusion.part_ref, f32[2,128,2048]{2,1,0:T(8,128)} %copy-done.6, bf16[2,128,2048]{2,1,0:T(8,128)(2,1)S(1)} %bitcast.168, f32[1,2048]{1,0:T(1,128)S(1)} %bitcast.172, ...), custom_call_target="tpu_custom_call" | custom-call | bytes 262144000 | tf_op jit(solution)/shard_map/pallas_call | solution.py:798
  444.9 1.4 copy-done.12
  446.3 3.1 constant_dynamic-slice_fusion.1
  449.4 1.2 slice.106
  451.2 1.2 broadcast_add_fusion
  453.8 1.8 collective-permute-done.8
  455.6 2.5 fusion.84
  458.1 2.3 add_convert_fusion.3.refs_8_
  460.5 5.2 fusion.58
  466.1 1.5 collective-permute-done.7
  467.9 1.0 pad_maximum_fusion.7.gno_ref
  469.0 9.5 %reduce-scatter.9.cloned.1.call-done.rest_2_ = bf16[256,1408]{1,0:T(8,128)(2,1)} async-done(((bf16[1024,1408]{1,0:T(8,128)(2,1)}), bf16[256,1408]{1,0:T(8,128)(2,1)}) %reduce-scatter.9.cloned.1.call-update) | async-done | bytes 720912 | tf_op jit(solution)/shard_map/reduce_scatter | solution.py:852
  478.4 40.8 %shard_map.206 = (bf16[2048,896]{1,0:T(8,128)(2,1)}, f32[4,768]{1,0:T(4,128)}, f32[1,128]{1,0:T(1,128)}, bf16[1024,2048]{1,0:T(8,128)(2,1)}) custom-call(f32[33]{0:T(128)} %pad_convert_fusion.keep_ref, s32[32]{0:T(128)} %convert_element_type.120.count_ref, bf16[2048,896]{1,0:T(8,128)(2,1)} %fusion.32.raw_ref.prev_ref, ...), custom_call_target="tpu_custom_call" | custom-call | bytes 125829120 | tf_op jit(solution)/shard_map/pallas_call | solution.py:260
  519.2 7.2 %fusion.53.refs_9_ = bf16[1024,768]{1,0:T(8,128)(2,1)} fusion(bf16[2048,896]{1,0:T(8,128)(2,1)} %get-tuple-element.38, s32[]{:T(128)S(6)} %select_n.120, bf16[1024,2048]{1,0:T(8,128)(2,1)S(1)} %copy-done.21, bf16[1024,2048]{1,0:T(8,128)(2,1)} %get-tuple-element.72), kind=kOutput, calls=%fused_computation.76 | convolution fusion | flops 3230400512 | bytes 13107204 | tf_op jit(solution)/shard_map/dot_general | solution.py:983
  526.7 8.0 %fusion.48 = bf16[1024,768]{1,0:T(8,128)(2,1)} fusion(bf16[2048,896]{1,0:T(8,128)(2,1)} %get-tuple-element.38, s32[]{:T(128)S(6)} %select_n.121, bf16[1024,2048]{1,0:T(8,128)(2,1)} %get-tuple-element.71, bf16[1024,2048]{1,0:T(8,128)(2,1)} %get-tuple-element.72), kind=kOutput, calls=%fused_computation.75 | convolution fusion | flops 3230400512 | bytes 13107204 | tf_op jit(solution)/shard_map/dot_general | solution.py:983
  534.7 1.2 convert_element_type.153
  535.9 3.4 maximum_convert_fusion
  539.3 3.7 fusion.18.refs_5_
  543.0 1.1 copy-done.8
  544.3 13.5 %convolution_convert_fusion.part_ref = bf16[2048,2048]{1,0:T(8,128)(2,1)} fusion(bf16[2048,896]{1,0:T(8,128)(2,1)} %get-tuple-element.38, bf16[2048,2]{1,0:T(8,128)(2,1)} %copy-done.35, bf16[2048,256]{1,0:T(8,128)(2,1)} %copy-done.34, bf16[2048,256]{1,0:T(8,128)(2,1)} %copy-done.33, bf16[2048,256]{1,0:T(8,128)(2,1)S(1)} %copy-done.32), kind=kOutput, calls=%fused_computation.12 | convolution fusion | flops 7538737152 | bytes 15212544 | tf_op jit(solution)/shard_map/dot_general | solution.py:978
  557.9 88.5 %shard_map.207 = (bf16[1024,2048]{1,0:T(8,128)(2,1)}, f32[16,2048]{1,0:T(8,128)S(1)}) custom-call(bf16[2048,2048]{1,0:T(8,128)(2,1)} %convolution_convert_fusion.part_ref, bf16[2,128,2048]{2,1,0:T(8,128)(2,1)S(1)} %bitcast.167, f32[2,128,2048]{2,1,0:T(8,128)} %copy-done.12, f32[1,2048]{1,0:T(1,128)S(1)} %bitcast.170, ...), custom_call_target="tpu_custom_call" | custom-call | bytes 262144000 | tf_op jit(solution)/shard_map/pallas_call | solution.py:798
  648.8 6.7 bitcast_convert_fusion.1
  655.4 1.8 convert_element_type.151
  657.2 1.2 broadcast_select_fusion.7
  658.9 1.6 copy.38
  660.5 4.8 copy.41
  (156 shorter events, 16.8 us)
Async XLA Ops:
  7.2 40.2 %copy-start = (f32[3,4,512]{2,1,0:T(4,128)S(1)}, f32[3,4,512]{2,1,0:T(4,128)}, u32[]{:S(2)}) copy-start(f32[3,4,512]{2,1,0:T(4,128)} %param.16) | copy-start | bytes 73732
  7.2 88.4 %all-gather.4.cloned.1.call-start = ((), (), s32[]{:S(2)}) async-start(), calls=%async_computation.7 | async-start | bytes 9437184 | tf_op jit(solution)/shard_map/all_gather | solution.py:875
  8.3 6.3 copy-start.13
  10.6 213.0 %all-gather.8.cloned.1.call-start = ((), (), s32[]{:S(2)}) async-start(), calls=%async_computation.9 | async-start | bytes 12976128 | tf_op jit(solution)/shard_map/all_gather | solution.py:875
  11.3 253.4 %all-gather.6.cloned.1.call-start = ((), (), s32[]{:S(2)}) async-start(), calls=%async_computation.8 | async-start | bytes 6488064 | tf_op jit(solution)/shard_map/all_gather | solution.py:875
  11.4 3.5 copy-start.18
  14.8 3.6 copy-start.36
  14.8 29.3 %copy-start.37 = (s32[1,3]{1,0:T(1,128)S(1)}, s32[1,3]{1,0:T(1,128)}, u32[]{:S(2)}) copy-start(s32[1,3]{1,0:T(1,128)} %param.13) | copy-start | bytes 40
  17.9 30.1 %collective-permute-start = (bf16[1024,2048]{1,0:T(8,128)(2,1)}, bf16[1024,2048]{1,0:T(8,128)(2,1)}, u32[]{:S(2)}, u32[]{:S(2)}) collective-permute-start(bf16[1024,2048]{1,0:T(8,128)(2,1)} %fusion.2), channel_id=1, source_target_pairs={{0,16},{16,0},{1,17},{17,1},{2,18},{18,2},{3,19},{19,3},{4,20},{20... | collective-permute-start | bytes 12582920 | tf_op jit(solution)/shard_map/ppermute | solution.py:819
  18.4 431.0 %reduce-scatter.11.cloned.1.call-start = ((), (), s32[]{:S(2)}) async-start(), calls=%async_computation.12 | async-start | bytes 3604480 | tf_op jit(solution)/shard_map/reduce_scatter | solution.py:852
  44.1 54.5 %copy-start.35 = (bf16[2048,2]{1,0:T(8,128)(2,1)}, bf16[2048,2]{1,0:T(8,128)(2,1)S(1)}, u32[]{:S(2)}) copy-start(bf16[2048,2]{1,0:T(8,128)(2,1)S(1)} %copy.39) | copy-start | bytes 24580
  95.6 2.8 slice-start
  95.6 4.0 copy-start.23
  98.4 3.8 copy-start.20
  98.6 14.3 %copy-start.31 = (bf16[2048,256]{1,0:T(8,128)(2,1)}, bf16[2048,256]{1,0:T(8,128)(2,1)S(1)}, u32[]{:S(2)}) copy-start(bf16[2048,256]{1,0:T(8,128)(2,1)S(1)} %get-tuple-element.73) | copy-start | bytes 3145732
  98.7 14.3 %copy-start.33 = (bf16[2048,256]{1,0:T(8,128)(2,1)}, bf16[2048,256]{1,0:T(8,128)(2,1)S(1)}, u32[]{:S(2)}) copy-start(bf16[2048,256]{1,0:T(8,128)(2,1)S(1)} %get-tuple-element.74) | copy-start | bytes 3145732
  98.7 14.3 %copy-start.34 = (bf16[2048,256]{1,0:T(8,128)(2,1)}, bf16[2048,256]{1,0:T(8,128)(2,1)S(1)}, u32[]{:S(2)}) copy-start(bf16[2048,256]{1,0:T(8,128)(2,1)S(1)} %get-tuple-element.75) | copy-start | bytes 3145732
  135.3 2.0 collective-permute-start.1
  137.0 7.6 %copy-start.2 = (bf16[1,256,2048]{2,1,0:T(8,128)(2,1)}, bf16[1,256,2048]{2,1,0:T(8,128)(2,1)S(1)}, u32[]{:S(2)}) copy-start(bf16[1,256,2048]{2,1,0:T(8,128)(2,1)S(1)} %constant_dynamic-slice_fusion.5) | copy-start | bytes 3145732
  138.6 6.0 copy-start.15
  223.5 143.4 %copy-start.6 = (f32[2,128,2048]{2,1,0:T(8,128)}, f32[2,128,2048]{2,1,0:T(8,128)S(1)}, u32[]{:S(2)}) copy-start(f32[2,128,2048]{2,1,0:T(8,128)S(1)} %get-tuple-element.30.refs_0_) | copy-start | bytes 6291460
  241.6 5.8 copy-start.19
  241.6 5.4 copy-start.28
  243.7 9.5 %copy-start.26 = (bf16[1024,1408]{1,0:T(8,128)(2,1)}, bf16[1024,1408]{1,0:T(8,128)(2,1)S(1)}, u32[]{:S(2)}) copy-start(bf16[1024,1408]{1,0:T(8,128)(2,1)S(1)} %fusion.8) | copy-start | bytes 8650756
  243.7 9.5 %collective-permute-start.2 = (bf16[1024,1408]{1,0:T(8,128)(2,1)S(1)}, bf16[1024,1408]{1,0:T(8,128)(2,1)S(1)}, u32[]{:S(2)}, u32[]{:S(2)}) collective-permute-start(bf16[1024,1408]{1,0:T(8,128)(2,1)S(1)} %fusion.8), channel_id=1, source_target_pairs={{0,16},{16,0},{1,17},{17,1},{2,18},{18,2},{3,19},{19,3},{4,20},{20... | collective-permute-start | bytes 8650760 | tf_op jit(solution)/shard_map/ppermute | solution.py:819
  247.2 6.0 collective-permute-start.3
  264.8 13.2 %copy-start.29 = (bf16[1,1024,2048]{2,1,0:T(8,128)(2,1)S(1)}, bf16[1,1024,2048]{2,1,0:T(8,128)(2,1)}, u32[]{:S(2)}) copy-start(bf16[1,1024,2048]{2,1,0:T(8,128)(2,1)} %param.23) | copy-start | bytes 12582916
  274.8 1.9 copy-start.25
  278.0 15.1 %copy-start.30 = (bf16[1024,2048]{1,0:T(8,128)(2,1)S(1)}, bf16[1024,2048]{1,0:T(8,128)(2,1)}, u32[]{:S(2)}) copy-start(bf16[1024,2048]{1,0:T(8,128)(2,1)} %get-tuple-element.29) | copy-start | bytes 12582916
  292.8 1.8 copy-start.38
  292.8 8.4 %collective-permute-start.6 = (bf16[1024,1408]{1,0:T(8,128)(2,1)}, bf16[1024,1408]{1,0:T(8,128)(2,1)S(1)}, u32[]{:S(2)}, u32[]{:S(2)}) collective-permute-start(bf16[1024,1408]{1,0:T(8,128)(2,1)} %get-tuple-element.70), channel_id=1, source_target_pairs={{0,16},{16,0},{1,17},{17,1},{2,18},{18,2},{3,19},{19,3},{4,20},{20... | collective-permute-start | bytes 8650760 | tf_op jit(solution)/shard_map/ppermute | solution.py:819
  293.3 7.8 %collective-permute-start.4 = (bf16[1024,1024]{1,0:T(8,128)(2,1)S(1)}, bf16[1024,1024]{1,0:T(8,128)(2,1)S(1)}, u32[]{:S(2)}, u32[]{:S(2)}) collective-permute-start(bf16[1024,1024]{1,0:T(8,128)(2,1)S(1)} %constant_dynamic-slice_fusion.3), channel_id=1, source_target_pairs={{0,16},{16,0},{1,17},{17,1},{2,18},{18,2},{3,19},{19,3},{4,20},{20... | collective-permute-start | bytes 6291464 | tf_op jit(solution)/shard_map/ppermute | solution.py:819
  301.1 1.3 copy-start.39
  307.5 161.5 %reduce-scatter.7.cloned.1.call-start = ((), (), s32[]{:S(2)}) async-start(), calls=%async_computation.10 | async-start | bytes 3604480 | tf_op jit(solution)/shard_map/reduce_scatter | solution.py:852
  308.0 13.7 %collective-permute-start.5 = (bf16[1024,1408]{1,0:T(8,128)(2,1)}, bf16[1024,1408]{1,0:T(8,128)(2,1)}, u32[]{:S(2)}, u32[]{:S(2)}) collective-permute-start(bf16[1024,1408]{1,0:T(8,128)(2,1)} %get-tuple-element.69), channel_id=1, source_target_pairs={{0,16},{16,0},{1,17},{17,1},{2,18},{18,2},{3,19},{19,3},{4,20},{20... | collective-permute-start | bytes 8650760 | tf_op jit(solution)/shard_map/ppermute | solution.py:819
  310.7 53.0 %all-to-all-start = ((bf16[4,256,2048]{2,1,0:T(8,128)(2,1)}), bf16[4,256,2048]{2,1,0:T(8,128)(2,1)}, u32[]{:S(2)}, u32[]{:S(2)}) async-start(bf16[4,256,2048]{2,1,0:T(8,128)(2,1)} %bitcast.174), calls=%async_computation | async-start | bytes 8388608 | tf_op jit(solution)/shard_map/all_to_all | solution.py:933
  315.6 162.9 %reduce-scatter.9.cloned.1.call-start = ((), (), s32[]{:S(2)}) async-start(), calls=%async_computation.11 | async-start | bytes 3604480 | tf_op jit(solution)/shard_map/reduce_scatter | solution.py:852
  315.6 6.1 copy-start.40
  328.7 326.8 %reduce-scatter.17.cloned.1.call-start = ((), (), s32[]{:S(2)}) async-start(), calls=%async_computation.15 | async-start | bytes 1310720 | tf_op jit(solution)/shard_map/reduce_scatter | solution.py:852
  366.9 1.2 copy-start.10
  367.3 77.7 %copy-start.5 = (bf16[256,2048]{1,0:T(8,128)(2,1)}, bf16[256,2048]{1,0:T(8,128)(2,1)S(1)}, u32[]{:S(2)}) copy-start(bf16[256,2048]{1,0:T(8,128)(2,1)S(1)} %fusion.38.refs_3_.rest_0_) | copy-start | bytes 3145732
  444.9 1.4 copy-start.12
  449.4 4.4 collective-permute-start.9
  452.4 3.1 collective-permute-start.8
  452.9 5.1 copy-start.24
  460.4 196.8 %reduce-scatter.13.cloned.1.call-start = ((), (), s32[]{:S(2)}) async-start(), calls=%async_computation.13 | async-start | bytes 1966080 | tf_op jit(solution)/shard_map/reduce_scatter | solution.py:852
  465.7 2.0 collective-permute-start.7
  478.4 40.8 %copy-start.21 = (bf16[1024,2048]{1,0:T(8,128)(2,1)S(1)}, bf16[1024,2048]{1,0:T(8,128)(2,1)}, u32[]{:S(2)}) copy-start(bf16[1024,2048]{1,0:T(8,128)(2,1)} %get-tuple-element.71) | copy-start | bytes 12582916
  526.5 8.2 %copy-start.27 = (bf16[1408,256]{1,0:T(8,128)(2,1)S(1)}, bf16[1408,256]{1,0:T(8,128)(2,1)}, u32[]{:S(2)}) copy-start(bf16[1408,256]{1,0:T(8,128)(2,1)} %reduce-scatter.7.cloned.1.call-done.rest_1_) | copy-start | bytes 2162692
  526.5 9.4 %copy-start.11 = (bf16[256,1408]{1,0:T(8,128)(2,1)S(1)}, bf16[256,1408]{1,0:T(8,128)(2,1)}, u32[]{:S(2)}) copy-start(bf16[256,1408]{1,0:T(8,128)(2,1)} %reduce-scatter.11.cloned.1.call-done.refs_7_) | copy-start | bytes 2162692
  526.5 130.7 %reduce-scatter.15.cloned.1.call-start = ((), (), s32[]{:S(2)}) async-start(), calls=%async_computation.14 | async-start | bytes 1966080 | tf_op jit(solution)/shard_map/reduce_scatter | solution.py:852
  534.7 8.4 %collective-permute-start.10 = (bf16[1024,768]{1,0:T(8,128)(2,1)}, bf16[1024,768]{1,0:T(8,128)(2,1)S(1)}, u32[]{:S(2)}, u32[]{:S(2)}) collective-permute-start(bf16[1024,768]{1,0:T(8,128)(2,1)} %fusion.48), channel_id=1, source_target_pairs={{0,16},{16,0},{1,17},{17,1},{2,18},{18,2},{3,19},{19,3},{4,20},{20... | collective-permute-start | bytes 4718600 | tf_op jit(solution)/shard_map/ppermute | solution.py:819
  534.7 4.7 copy-start.22
  539.3 4.9 copy-start.32
  543.0 1.1 copy-start.8
  544.2 13.6 %copy-start.3 = (bf16[1,256,2048]{2,1,0:T(8,128)(2,1)S(1)}, bf16[1,256,2048]{2,1,0:T(8,128)(2,1)}, u32[]{:S(2)}) copy-start(bf16[1,256,2048]{2,1,0:T(8,128)(2,1)} %copy-done.2) | copy-start | bytes 3145732
  544.2 13.6 %copy-start.4 = (bf16[512,1024]{1,0:T(8,128)(2,1)S(1)}, bf16[512,1024]{1,0:T(8,128)(2,1)}, u32[]{:S(2)}) copy-start(bf16[512,1024]{1,0:T(8,128)(2,1)} %add_convert_fusion.3.refs_8_) | copy-start | bytes 3145732
  544.2 13.6 %copy-start.7 = (bf16[1024,768]{1,0:T(8,128)(2,1)S(1)}, bf16[1024,768]{1,0:T(8,128)(2,1)}, u32[]{:S(2)}) copy-start(bf16[1024,768]{1,0:T(8,128)(2,1)} %fusion.53.refs_9_) | copy-start | bytes 4718596
  544.3 13.6 %copy-start.9 = (bf16[1024,768]{1,0:T(8,128)(2,1)S(1)}, bf16[1024,768]{1,0:T(8,128)(2,1)}, u32[]{:S(2)}) copy-start(bf16[1024,768]{1,0:T(8,128)(2,1)} %copy-done.8) | copy-start | bytes 4718596
  544.3 13.6 %copy-start.14 = (f32[2048]{0:T(1024)S(1)}, f32[2048]{0:T(1024)}, u32[]{:S(2)}) copy-start(f32[2048]{0:T(1024)} %param.14) | copy-start | bytes 24580
  544.3 13.6 %copy-start.16 = (f32[4,768]{1,0:T(4,128)S(1)}, f32[4,768]{1,0:T(4,128)}, u32[]{:S(2)}) copy-start(f32[4,768]{1,0:T(4,128)} %get-tuple-element.42.refs_6_) | copy-start | bytes 36868
  544.3 13.6 %copy-start.17 = (f32[1,128]{1,0:T(1,128)S(1)}, f32[1,128]{1,0:T(1,128)}, u32[]{:S(2)}) copy-start(f32[1,128]{1,0:T(1,128)} %get-tuple-element.41.refs_4_) | copy-start | bytes 1540
  660.5 4.8 copy-start.1
Sparse Core Ops, SparseCore 0:
  10.7 84.9 all-gather.3
  97.2 106.6 all-gather.7
  205.6 59.1 all-gather.5
  307.6 54.3 reduce-scatter.10
  364.1 56.0 reduce-scatter.6
  422.4 56.0 reduce-scatter.8
  480.7 26.9 reduce-scatter.16
  526.6 34.4 reduce-scatter.12
  564.1 34.2 reduce-scatter.14

commit v5 on v4

--- a/solution.py
+++ b/solution.py
@@ -122,7 +122,7 @@
             jax.ShapeDtypeStruct((nc,heads,HDIM,HDIM),BF16),jax.ShapeDtypeStruct((nc,heads,HDIM,HDIM),BF16),
             jax.ShapeDtypeStruct((n,width),BF16),jax.ShapeDtypeStruct((n,width),BF16)],
         scratch_shapes=[pltpu.VMEM((rows+8,3*width),F32),pltpu.VMEM((heads,HDIM,HDIM),F32)],
-        compiler_params=pltpu.CompilerParams(vmem_limit_bytes=56<<20),
+        compiler_params=pltpu.CompilerParams(vmem_limit_bytes=24<<20),
         cost_estimate=pl.CostEstimate(flops=0,bytes_accessed=120<<20,transcendentals=0),
     )(keep,count,raw,cw,gain)
 
@@ -153,7 +153,6 @@
     top,low=block_ref.at[pl.ds(0,part)],block_ref.at[pl.ds(part,part)]
     keep_own=pltpu.make_async_copy(block_ref,all_ref.at[pl.ds(pl.multiple_of(2*place*part,2*part),2*part)],local_sem)
     sends=[copy(0,top,at(place,0),across_x),copy(1,low,at(place,1),across_y),copy(2,top,at(place,0),across_y),copy(3,low,at(place,1),across_x)]
-    onward=[copy(4,at(across_x,0),at(across_x,0),across_y),copy(5,at(across_y,1),at(across_y,1),across_x)]
     @pl.when(step==0)
     def _():
         barrier=pltpu.get_barrier_semaphore()
@@ -162,11 +161,6 @@
         pl.semaphore_wait(barrier,2)
         keep_own.start()
         for send in sends: send.start()
-    @pl.when(step==steps//2)
-    def _():
-        for send,follow in zip(sends[:2],onward):
-            send.wait_recv()
-            follow.start()
     ext[0:8,:]=prev_ref[:,0:3*width].astype(F32)[8:16]*first
     ext[8:,:]=raw_ref[:,0:3*heads*HDIM].astype(F32)
     r,c=iotas()
@@ -247,8 +241,8 @@
     @pl.when(step==steps-1)
     def _():
         keep_own.wait()
-        for send in (*sends[2:],*onward): send.wait_recv()
-        for send in (*sends,*onward): send.wait_send()
+        for send in sends: send.wait_recv()
+        for send in sends: send.wait_send()
 
 def backward(keep, count, raw, cw, gain, gno, o, s, t, w, r, group, block, dummies=()):
     n=raw.shape[0]; width=cw.shape[1]//3; heads=width//HDIM; rows=group*CHUNK
@@ -264,8 +258,8 @@
         out_shape=[jax.ShapeDtypeStruct(raw.shape,BF16),
             jax.ShapeDtypeStruct((KERNEL,3*width),F32),jax.ShapeDtypeStruct((1,HDIM),F32),jax.ShapeDtypeStruct((4*block.shape[0],block.shape[1]),BF16)],
         scratch_shapes=[pltpu.VMEM((rows+8,3*width),F32),pltpu.VMEM((rows+8,3*width),F32),pltpu.VMEM((heads,HDIM,HDIM),F32),
-            pltpu.SemaphoreType.DMA(()),pltpu.SemaphoreType.DMA((6,)),pltpu.SemaphoreType.DMA((6,))],
-        compiler_params=pltpu.CompilerParams(collective_id=3,has_side_effects=True,vmem_limit_bytes=56<<20),
+            pltpu.SemaphoreType.DMA(()),pltpu.SemaphoreType.DMA((4,)),pltpu.SemaphoreType.DMA((4,))],
+        compiler_params=pltpu.CompilerParams(collective_id=3,has_side_effects=True,vmem_limit_bytes=24<<20),
         cost_estimate=pl.CostEstimate(flops=0,bytes_accessed=120<<20,transcendentals=0),
     )(keep,count,raw,raw,cw,gain,gno,o,s,t,w,r,block,*dummies)
 
@@ -706,9 +700,9 @@
     small = []
     if small_sum:
         values, arrived = outs[-1], scratch[-1]
-        first = n_in - small_sum["dummies"] - 4
-        ffn_gain, out_gain, beta, conv = inputs[first : first + 4]
-        heads, taps, width = beta.shape[0], conv.shape[0], conv.shape[1]
+        first = n_in - small_sum["dummies"] - 3
+        ffn_gain, out_gain, conv = inputs[first : first + 3]
+        taps, width = conv.shape
         middle_lane = values.shape[1] // 2
         values[...] = jnp.zeros_like(values)
         values[0:1, :] = gain
@@ -716,10 +710,8 @@
         values[2:3, 0 : out_gain.shape[1]] = out_gain[...]
         for i in (0, 1):
             share = jnp.where(core == i, 1.0, 0.0)
-            values[8 + i * heads : 8 + (i + 1) * heads, :] = beta[...] * share
-            at = 8 + 2 * heads
             lane = i * middle_lane
-            values[at : at + taps, lane : lane + width] = conv[...] * share
+            values[8 : 8 + taps, lane : lane + width] = conv[...] * share
     elif n_out > 2:
         outs[-1][...] = gain
 
@@ -786,7 +778,7 @@
     if small is not None:
         stages = lax.axis_size("row").bit_length() - 1 + 3
         copies = 20 + stages
-        height = 8 + 2 * small[2].shape[0] + small[3].shape[0]
+        height = 8 + small[2].shape[0]
         shape = (height + -height % 8, model)
         scratch += [pltpu.VMEM((stages, 2, *shape), F32)]
         small_sum = {"dummies": len(dummies)}
@@ -817,6 +809,10 @@
 
 def swapped(block):
     return lax.ppermute(block, "seq", [(0, 1), (1, 0)])
+
+
+def across(block, bit):
+    return lax.ppermute(block, "mp", [(i, i ^ bit) for i in range(4)])
 
 
 def in_order(mine, other, core, axis):
@@ -973,38 +969,42 @@
         *saved,
         group,
         block_out,
-        [down_sum, gate_sum],
-    )
+        [down_sum, out_pair],
+    )
+    piece = lambda of, half: lax.dynamic_slice_in_dim(
+        block_out, (2 * of + half) * (quarter // 2), quarter // 2, axis=0
+    )
+    far_rows = [across(piece(own ^ 1, 0), 2), across(piece(own ^ 2, 1), 1)]
     grad_normed = lax.dot_general(
         grad_raw, mix_weight, (((1,), (1,)), ((), ())), preferred_element_type=F32
     )
     grad_normed_part = grad_normed.astype(BF16)
     normed_mine, normed_other = halves(normed, core, 1)
     by_columns = lambda part: lax.dot_general(
-        part, grad_raw[:, : 3 * width], (((0,), (0,)), ((), ())), preferred_element_type=F32
+        part, grad_raw, (((0,), (0,)), ((), ())), preferred_element_type=F32
     ).astype(BF16)
     qkv_other = swapped(by_columns(normed_other))
     qkv_mine = by_columns(normed_mine)
-    grad_beta = lax.dot_general(
-        grad_raw[:, 3 * width :], normed, (((0,), (0,)), ((), ())), preferred_element_type=F32
-    )[:own_heads]
     grad_input, small = mp_phase(
         2,
         partial(normed_backward, False),
         grad_normed_part,
         [residual_own, grad_hidden, attn_gain[None, :]],
-        [up_sum, out_pair, qkv_mine, qkv_other],
+        [gate_sum, up_sum, qkv_mine, qkv_other, *far_rows],
         [],
         both_cores=True,
-        small=[ffn_gain_part, out_gain_part, grad_beta, grad_conv_own],
+        small=[ffn_gain_part, out_gain_part, grad_conv_own],
     )
     grad_input = grad_input.astype(F32)
+    places = jnp.arange(4)[:, None, None]
+    block_out = jnp.where(
+        places == (own ^ 3),
+        jnp.concatenate(far_rows)[None],
+        block_out.reshape(4, quarter, model),
+    ).reshape(tok_count, model)
     grad_attn_gain, grad_ffn_gain = small[0], small[1]
     grad_out_gain = small[2, : out_gain.shape[0]]
-    span = beta_weight.shape[1]
-    place_no = core * lax.axis_size("row") + lax.axis_index("row")
-    grad_beta = lax.dynamic_slice_in_dim(small[8 : 8 + 2 * own_heads], place_no * span, span, axis=1)
-    conv_at = 8 + 2 * own_heads
+    conv_at = 8
     conv_of = lambda i: (
         small[conv_at : conv_at + KERNEL, i * (model // 2) : i * (model // 2) + 3 * width]
         .reshape(KERNEL, 3, width)
@@ -1013,8 +1013,11 @@
     grad_conv = jnp.concatenate([conv_of(0), conv_of(1)], axis=2)
     grad_down, grad_out = down_sum.astype(F32), over_row(out_pair, 1).astype(F32)
     grad_gateup = jnp.stack([gate_sum, up_sum]).astype(F32)
-    by_kind = lambda part: over_row(part, 0).reshape(-1, 3, width).transpose(1, 0, 2)
-    grad_qkv = in_order(by_kind(qkv_mine), by_kind(qkv_other), core, 2).astype(F32)
+    row_sums = [over_row(part, 0) for part in (qkv_mine, qkv_other)]
+    by_kind = lambda part: part[:, : 3 * width].reshape(-1, 3, width).transpose(1, 0, 2)
+    grad_qkv = in_order(by_kind(row_sums[0]), by_kind(row_sums[1]), core, 2).astype(F32)
+    of_heads = lambda part: part[:, 3 * width : 3 * width + own_heads].T
+    grad_beta = in_order(of_heads(row_sums[0]), of_heads(row_sums[1]), core, 0).astype(F32)
     return (
         block_out[None],
         grad_input[None],

time: 676 us -> 659 us (0.975)
  Pallas kernels: 306 us -> 289 us
  local copies, waits for them, and re-layouts: 40.2 us -> 55.5 us
  waiting for transfers between devices: 78.3 us -> 65.2 us
    pallas_call x1, Pallas kernels: 40.8 us -> 26.7 us  [backward(): pl.pallas_call(functools.partial(bwd_kernel, heads, group), grid=(steps,)...]
    unnamed x85 -> x134, local copies, waits for them, and re-layouts: 21.4 us -> 35.1 us
    reduce_scatter x6, waiting for transfers between devices: 9.46 us -> 0.03 us  [over_row(): return lax.psum_scatter(pair, 'row', scatter_dimension=axis, tiled=True)]
    dot_general x3 -> x2, matrix products: 18.9 us -> 14.9 us  [joined_shards(): lax.dot_general(part, grad_raw, (((0,), (0,)), ((), ())), preferred_eleme...]
  transfers between devices with their start and end apart: 21 -> 23, of which waited for: 9 -> 8; matrix products, arithmetic and copies ran while one was open for 26% -> 27% of each run, Pallas kernels for 46% -> 44%
where the time goes in v5:
time: 659 us; the launch traced here: 655 us
  Pallas kernels  289 us (44%)
  matrix products  148 us (22%)
  waiting for transfers between devices  65.2 us (10%)
  local copies, waits for them, and re-layouts  55.5 us (8%)
  other arithmetic  43.8 us (7%)
  blocking collectives  25.4 us (4%)
  between operations  17 us (3%)
  starting transfers between devices  10.2 us (2%)
    pallas_call x3, Pallas kernels, mp_phase(): pl.pallas_call(kernel, in_specs=[there if both_cores else here] + [here]...  243 us
    all_gather x3, waiting for transfers between devices, joined_shards(): lax.all_gather(weight, ('seq', 'row'), axis=1, tiled=True)  41.8 us
    dot_general x8, matrix products, both_tokens(): lax.dot_general(a, b, (((0,), (0,)), ((), ())), preferred_element_type=F32)  37.8 us
    unnamed x134, local copies, waits for them, and re-layouts  35.1 us
    pallas_call x1, Pallas kernels, backward(): pl.pallas_call(functools.partial(bwd_kernel, heads, group), grid=(steps,)...  26.7 us
    all_gather x1, blocking collectives, joined_shards(): lax.all_gather(weight, ('seq', 'row'), axis=1, tiled=True)  25.4 us
    pallas_call x1, Pallas kernels, forward(): pl.pallas_call(functools.partial(fwd_kernel, heads, group), grid=(n // ro...  19.5 us
    dot_general x1, matrix products, joined_shards(): jnp.einsum('stf,sdf->td', jnp.stack([grad_gate, grad_up]), gateup_full, p...  18.2 us
  transfers between devices with their start and end apart: 23, of which 8 were waited for; matrix products, arithmetic and copies ran while one was open for 27% of the time, Pallas kernels for 44%

profile of v5, /device:TPU:0, one launch (start us, length us, event | category | flops | bytes accessed | tf_op | source)
XLA Modules:
  0.0 654.8 jit_solution(16005323728572406360)
XLA Ops:
  8.3 2.2 pad_maximum_fusion.4
  11.4 3.2 fusion
  14.8 3.0 fusion.2
  18.4 25.4 %all_gather.13 = bf16[4,2048]{1,0:T(4,128)(2,1)S(1)} all-gather(bf16[4,256]{1,0:T(4,128)(2,1)S(1)} %copy-done.61), channel_id=1, replica_groups=mesh['seq'=2,'mp'=4,'row'=4] {'seq','row'}, dimensions={1}, use_global_device_ids=true | all-gather | bytes 18432 | tf_op jit(solution)/shard_map/all_gather | solution.py:871
  46.4 7.6 %broadcast_select_fusion.1 = (bf16[1024,2048]{1,0:T(8,128)(2,1)}, bf16[1024,2048]{1,0:T(8,128)(2,1)}) fusion(bf16[1024,2048]{1,0:T(8,128)(2,1)} %collective-permute-done, pred[]{:T(512)S(6)} %eq.25, f32[2048]{0:T(1024)S(1)} %copy-done.29, f32[1024]{0:T(1024)S(1)} %add_rsqrt_fusion, bf16[1,1024,2048]{2,1,0:T(8,128)(2,1)} %param.12), kind=kLoop, calls=%fused_computation.51 | loop fusion | flops 12582912 | bytes 16789504 | tf_op jit(solution)/shard_map/jit(_where)/select_n | solution.py:819
  54.1 41.6 %all-gather.4.cloned.1.call-done = bf16[4,2048,512]{2,1,0:T(8,128)(2,1)} async-done(((bf16[4,256,512]{2,1,0:T(8,128)(2,1)}), bf16[4,2048,512]{2,1,0:T(8,128)(2,1)}) %all-gather.4.cloned.1.call-update) | async-done | bytes 8388624 | tf_op jit(solution)/shard_map/all_gather | solution.py:871
  95.6 2.8 slice-done
  98.7 3.1 copy-done.47
  101.8 11.7 %fusion.31.raw_ref.prev_ref = bf16[2048,896]{1,0:T(8,128)(2,1)S(1)} fusion(bf16[1024,2048]{1,0:T(8,128)(2,1)} %get-tuple-element.94, bf16[1024,2048]{1,0:T(8,128)(2,1)S(1)} %copy-done.47, bf16[2048,2]{1,0:T(8,128)(2,1)S(1)} %copy.50, bf16[2048,256]{1,0:T(8,128)(2,1)S(1)} %get-tuple-element.97, bf16[2048,256]{1,0:T(8,128)(2,1)S(1)} %get-tuple-element.96, ...), kind=kOutput, calls=%fused_computation.55 | convolution fusion | flops 7553155072 | bytes 15212544 | tf_op jit(solution)/shard_map/dot_general | solution.py:897
  113.5 19.5 %shard_map.203 = (bf16[2048,256]{1,0:T(8,128)(2,1)S(1)}, f32[2048,256]{1,0:T(8,128)S(1)}, bf16[16,2,128,128]{3,2,1,0:T(8,128)(2,1)S(1)}, bf16[16,2,128,128]{3,2,...) custom-call(f32[33]{0:T(128)S(1)} %pad_convert_fusion.keep_ref, ...), custom_call_target="tpu_custom_call" | custom-call | bytes 125829120 | tf_op jit(solution)/shard_map/pallas_call | solution.py:117
  133.0 1.9 copy-done.2
  134.9 1.3 copy-done.17
  140.5 1.3 constant_dynamic-slice_fusion.6
  142.4 6.4 convolution_convert_fusion.2.part_ref
  148.9 78.9 %shard_map.204 = (bf16[1024,2048]{1,0:T(8,128)(2,1)}, f32[2,128,2048]{2,1,0:T(8,128)S(1)}) custom-call(bf16[1024,2048]{1,0:T(8,128)(2,1)} %convolution_convert_fusion.2.part_ref, bf16[2,128,2048]{2,1,0:T(8,128)(2,1)S(1)} %bitcast.174, f32[1,2048]{1,0:T(1,128)S(1)} %bitcast.182), custom_call_target="tpu_custom_call" | custom-call | bytes 262144000 | tf_op jit(solution)/shard_map/pallas_call | solution.py:790
  227.8 1.3 copy-done.7
  229.1 17.3 %convolution_bitcast_fusion = f32[2,1024,1408]{2,1,0:T(8,128)S(1)} fusion(bf16[2,2048,1408]{2,1,0:T(8,128)(2,1)} %all-gather.8.cloned.1.call-done, bf16[1024,2048]{1,0:T(8,128)(2,1)} %get-tuple-element.29), kind=kOutput, calls=%fused_computation.16 | convolution fusion | flops 11811160064 | bytes 27262976 | tf_op jit(solution)/shard_map/td,sdf->stf/dot_general | solution.py:922
  246.5 2.1 fusion.9
  248.7 3.2 copy-done.53
  252.2 5.9 fusion.32
  258.1 5.2 add_convert_fusion.2.refs_4_
  264.8 10.1 %convolution_convert_fusion.1 = bf16[1024,2048]{1,0:T(8,128)(2,1)S(1)} fusion(bf16[1408,2048]{1,0:T(8,128)(2,1)} %all-gather.6.cloned.1.call-done, bf16[1024,1408]{1,0:T(8,128)(2,1)} %copy-done.52, bf16[]{:T(256)} %bitcast.30), kind=kOutput, calls=%fused_computation.52 | convolution fusion | flops 5909118976 | bytes 12845058 | tf_op jit(solution)/shard_map/dot_general | solution.py:926
  275.4 1.5 copy-done.51
  277.6 13.3 %fusion.12 = (bf16[1024,1408]{1,0:T(8,128)(2,1)}, bf16[1024,1408]{1,0:T(8,128)(2,1)S(1)}) fusion(f32[2,1024,1408]{2,1,0:T(8,128)S(1)} %copy-done.41, f32[]{:T(128)} %bitcast.31, bf16[1408,2048]{1,0:T(8,128)(2,1)} %all-gather.6.cloned.1.call-done, bf16[1,1024,2048]{2,1,0:T(8,128)(2,1)} %param.23), kind=kOutput, calls=%fused_computation.26 | convolution fusion | flops 5925765120 | bytes 27262980 | tf_op jit(solution)/shard_map/dot_general | solution.py:932
  291.3 3.0 constant_dynamic-slice_fusion.4
  294.7 3.6 fusion.41
  299.2 1.3 copy-done.64
  300.5 5.0 add_convert_fusion.refs_6_
  306.5 1.3 constant_dynamic-slice_fusion.5
  307.8 5.0 all-to-all-start
  312.9 6.1 fusion.43
  319.1 6.9 %add_convert_fusion.1.refs_5_ = bf16[1024,1408]{1,0:T(8,128)(2,1)} fusion(f32[1024,1408]{1,0:T(8,128)S(1)} %fusion.43, bf16[1024,1024]{1,0:T(8,128)(2,1)S(1)} %copy-done.65, bf16[1024,1408]{1,0:T(8,128)(2,1)} %collective-permute-done.5), kind=kOutput, calls=%fused_computation.38 | convolution fusion | flops 2955673600 | bytes 13631488 | tf_op jit(solution)/shard_map/dot_general | solution.py:836
  326.0 18.2 %bitcast_convert_fusion.part_ref = bf16[1024,2048]{1,0:T(8,128)(2,1)} fusion(bf16[2,2048,1408]{2,1,0:T(8,128)(2,1)} %all-gather.8.cloned.1.call-done, bf16[1,1024,1408]{2,1,0:T(8,128)(2,1)} %bitcast.196, bf16[1,1024,1408]{2,1,0:T(8,128)(2,1)} %bitcast.32), kind=kOutput, calls=%fused_computation.11 | convolution fusion | flops 11816140800 | bytes 21495808 | tf_op jit(solution)/shard_map/stf,sdf->td/dot_general | solution.py:937
  344.2 16.7 %all-to-all-done = bf16[4,256,2048]{2,1,0:T(8,128)(2,1)} async-done(((bf16[4,256,2048]{2,1,0:T(8,128)(2,1)}), bf16[4,256,2048]{2,1,0:T(8,128)(2,1)}, u32[]{:S(2)}, u32[]{:S(2)}) %all-to-all-start) | async-done | bytes 4194336 | tf_op jit(solution)/shard_map/all_to_all | solution.py:929
  360.9 3.4 convert_reduce_fusion
  364.7 77.2 %shard_map.205 = (bf16[1024,2048]{1,0:T(8,128)(2,1)}, f32[2,128,2048]{2,1,0:T(8,128)S(1)}, f32[1,2048]{1,0:T(1,128)S(1)}) custom-call(bf16[1024,2048]{1,0:T(8,128)(2,1)} %bitcast_convert_fusion.part_ref, f32[2,128,2048]{2,1,0:T(8,128)} %copy-done.7, bf16[2,128,2048]{2,1,0:T(8,128)(2,1)S(1)} %bitcast.176, f32[1,2048]{1,0:T(1,128)S(1)} %bitcast.183, ...), custom_call_target="tpu_custom_call" | custom-call | bytes 262144000 | tf_op jit(solution)/shard_map/pallas_call | solution.py:790
  441.9 1.3 copy-done.16
  443.2 3.2 constant_dynamic-slice_fusion.2
  448.3 1.2 broadcast_add_fusion
  450.9 1.6 collective-permute-done.8
  452.5 2.9 fusion.75
  455.4 2.3 add_convert_fusion.3.rest_2_
  457.7 5.2 fusion.51
  463.5 1.6 collective-permute-done.7
  465.5 2.0 copy-done.3
  468.6 1.6 copy-done.18
  470.2 1.2 copy-done.20
  471.4 1.2 copy-done.22
  472.6 1.2 copy-done.24
  473.9 1.2 copy-done.26
  475.1 26.7 %shard_map.206 = (bf16[2048,896]{1,0:T(8,128)(2,1)S(1)}, f32[4,768]{1,0:T(4,128)S(1)}, f32[1,128]{1,0:T(1,128)S(1)}, bf16[1024,2048]{1,0:T(8,128)(2,1)S(1)}) custom-call(f32[33]{0:T(128)S(1)} %copy-done.37, s32[32]{0:T(128)S(1)} %copy-done.35, bf16[2048,896]{1,0:T(8,128)(2,1)S(1)} %copy-done.3, bf16[2048,896]{1,0:T(8,128)(2,1)S(1)} %copy-done.3, ...), custom_call_target="tpu_custom_call" | custom-call | bytes 125829120 | tf_op jit(solution)/shard_map/pallas_call | solution.py:254
  501.8 2.0 copy-done.10
  503.8 1.8 copy-done.38
  505.7 5.7 fusion.48.refs_8_
  511.4 9.2 %fusion.45 = bf16[1024,896]{1,0:T(8,128)(2,1)} fusion(bf16[2048,896]{1,0:T(8,128)(2,1)} %copy-done.38, s32[]{:T(128)S(6)} %select_n.150, bf16[1024,2048]{1,0:T(8,128)(2,1)} %get-tuple-element.93, bf16[1024,2048]{1,0:T(8,128)(2,1)} %get-tuple-element.94), kind=kOutput, calls=%fused_computation.73 | convolution fusion | flops 3767402496 | bytes 13893636 | tf_op jit(solution)/shard_map/dot_general | solution.py:983
  520.8 1.2 convert_element_type.157
  522.0 3.0 maximum_convert_fusion
  525.0 2.3 constant_dynamic-slice_fusion.1
  529.4 13.5 %convolution_convert_fusion.part_ref = bf16[2048,2048]{1,0:T(8,128)(2,1)} fusion(bf16[2048,896]{1,0:T(8,128)(2,1)} %copy-done.38, bf16[2048,2]{1,0:T(8,128)(2,1)S(1)} %copy-done.60, bf16[2048,256]{1,0:T(8,128)(2,1)} %copy-done.58, bf16[2048,256]{1,0:T(8,128)(2,1)} %copy-done.57, bf16[2048,256]{1,0:T(8,128)(2,1)S(1)} %copy-done.56), kind=kOutput, calls=%fused_computation.13 | convolution fusion | flops 7538737152 | bytes 15212544 | tf_op jit(solution)/shard_map/dot_general | solution.py:978
  543.0 2.7 bitcast_select_fusion
  546.0 87.0 %shard_map.207 = (bf16[1024,2048]{1,0:T(8,128)(2,1)}, f32[16,2048]{1,0:T(8,128)S(1)}) custom-call(bf16[2048,2048]{1,0:T(8,128)(2,1)} %convolution_convert_fusion.part_ref, bf16[2,128,2048]{2,1,0:T(8,128)(2,1)S(1)} %bitcast.175, f32[2,128,2048]{2,1,0:T(8,128)} %copy-done.16, f32[1,2048]{1,0:T(1,128)S(1)} %bitcast.181, ...), custom_call_target="tpu_custom_call" | custom-call | bytes 262144000 | tf_op jit(solution)/shard_map/pallas_call | solution.py:790
  634.7 6.7 %bitcast_convert_fusion.1 = f32[1,1024,2048]{2,1,0:T(8,128)} fusion(bf16[1024,2048]{1,0:T(8,128)(2,1)} %get-tuple-element.43), kind=kLoop, calls=%fused_computation.45 | loop fusion | flops 2097152 | bytes 12582912 | tf_op jit(solution)/shard_map/broadcast_in_dim | solution.py:1023
  641.3 1.8 convert_element_type.155
  645.9 1.6 copy.49
  (216 shorter events, 27.5 us)
Async XLA Ops:
  7.2 39.2 %copy-start = (f32[3,4,512]{2,1,0:T(4,128)S(1)}, f32[3,4,512]{2,1,0:T(4,128)}, u32[]{:S(2)}) copy-start(f32[3,4,512]{2,1,0:T(4,128)} %param.16) | copy-start | bytes 73732
  7.2 88.4 %all-gather.4.cloned.1.call-start = ((), (), s32[]{:S(2)}) async-start(), calls=%async_computation.7 | async-start | bytes 9437184 | tf_op jit(solution)/shard_map/all_gather | solution.py:871
  8.3 6.3 copy-start.29
  10.6 218.5 %all-gather.8.cloned.1.call-start = ((), (), s32[]{:S(2)}) async-start(), calls=%async_computation.9 | async-start | bytes 12976128 | tf_op jit(solution)/shard_map/all_gather | solution.py:871
  11.3 253.4 %all-gather.6.cloned.1.call-start = ((), (), s32[]{:S(2)}) async-start(), calls=%async_computation.8 | async-start | bytes 6488064 | tf_op jit(solution)/shard_map/all_gather | solution.py:871
  11.4 3.5 copy-start.39
  14.8 3.6 copy-start.61
  14.8 29.3 %copy-start.62 = (s32[1,3]{1,0:T(1,128)S(1)}, s32[1,3]{1,0:T(1,128)}, u32[]{:S(2)}) copy-start(s32[1,3]{1,0:T(1,128)} %param.13) | copy-start | bytes 40
  17.9 28.6 %collective-permute-start = (bf16[1024,2048]{1,0:T(8,128)(2,1)}, bf16[1024,2048]{1,0:T(8,128)(2,1)}, u32[]{:S(2)}, u32[]{:S(2)}) collective-permute-start(bf16[1024,2048]{1,0:T(8,128)(2,1)} %fusion.2), channel_id=1, source_target_pairs={{0,16},{16,0},{1,17},{17,1},{2,18},{18,2},{3,19},{19,3},{4,20},{20... | collective-permute-start | bytes 12582920 | tf_op jit(solution)/shard_map/ppermute | solution.py:811
  18.4 428.1 %reduce-scatter.9.cloned.1.call-start = ((), (), s32[]{:S(2)}) async-start(), calls=%async_computation.11 | async-start | bytes 3604480 | tf_op jit(solution)/shard_map/reduce_scatter | solution.py:848
  44.1 54.5 %copy-start.59 = (bf16[2048,2]{1,0:T(8,128)(2,1)}, bf16[2048,2]{1,0:T(8,128)(2,1)S(1)}, u32[]{:S(2)}) copy-start(bf16[2048,2]{1,0:T(8,128)(2,1)S(1)} %copy.50) | copy-start | bytes 24580
  45.3 68.2 %copy-start.34 = (s32[32]{0:T(128)}, s32[32]{0:T(128)S(1)}, u32[]{:S(2)}) copy-start(s32[32]{0:T(128)S(1)} %convert_element_type.123.count_ref) | copy-start | bytes 388
  46.4 67.1 %copy-start.36 = (f32[33]{0:T(128)}, f32[33]{0:T(128)S(1)}, u32[]{:S(2)}) copy-start(f32[33]{0:T(128)S(1)} %pad_convert_fusion.keep_ref) | copy-start | bytes 400
  46.4 67.1 %copy-start.27 = (f32[3,4,256]{2,1,0:T(4,128)}, f32[3,4,256]{2,1,0:T(4,128)S(1)}, u32[]{:S(2)}) copy-start(f32[3,4,256]{2,1,0:T(4,128)S(1)} %constant_dynamic-slice_fusion.8) | copy-start | bytes 36868
  95.6 2.8 slice-start
  98.4 3.3 copy-start.47
  98.6 14.8 %copy-start.55 = (bf16[2048,256]{1,0:T(8,128)(2,1)}, bf16[2048,256]{1,0:T(8,128)(2,1)S(1)}, u32[]{:S(2)}) copy-start(bf16[2048,256]{1,0:T(8,128)(2,1)S(1)} %get-tuple-element.95) | copy-start | bytes 3145732
  98.6 14.8 %copy-start.57 = (bf16[2048,256]{1,0:T(8,128)(2,1)}, bf16[2048,256]{1,0:T(8,128)(2,1)S(1)}, u32[]{:S(2)}) copy-start(bf16[2048,256]{1,0:T(8,128)(2,1)S(1)} %get-tuple-element.96) | copy-start | bytes 3145732
  98.7 14.8 %copy-start.58 = (bf16[2048,256]{1,0:T(8,128)(2,1)}, bf16[2048,256]{1,0:T(8,128)(2,1)S(1)}, u32[]{:S(2)}) copy-start(bf16[2048,256]{1,0:T(8,128)(2,1)S(1)} %get-tuple-element.97) | copy-start | bytes 3145732
  101.8 11.7 %copy-start.32 = (f32[128]{0:T(128)S(1)}, f32[128]{0:T(128)}, u32[]{:S(2)}) copy-start(f32[128]{0:T(128)} %param.18) | copy-start | bytes 1540
  140.2 2.0 collective-permute-start.1
  141.8 7.1 %copy-start.4 = (bf16[1,256,2048]{2,1,0:T(8,128)(2,1)}, bf16[1,256,2048]{2,1,0:T(8,128)(2,1)S(1)}, u32[]{:S(2)}) copy-start(bf16[1,256,2048]{2,1,0:T(8,128)(2,1)S(1)} %constant_dynamic-slice_fusion.6) | copy-start | bytes 3145732
  142.4 6.5 copy-start.43
  142.4 6.5 copy-start.45
  142.4 6.5 copy-start.31
  246.5 5.7 copy-start.40
  246.5 5.4 copy-start.53
  248.6 9.5 %copy-start.52 = (bf16[1024,1408]{1,0:T(8,128)(2,1)}, bf16[1024,1408]{1,0:T(8,128)(2,1)S(1)}, u32[]{:S(2)}) copy-start(bf16[1024,1408]{1,0:T(8,128)(2,1)S(1)} %fusion.9) | copy-start | bytes 8650756
  248.6 9.5 %collective-permute-start.2 = (bf16[1024,1408]{1,0:T(8,128)(2,1)S(1)}, bf16[1024,1408]{1,0:T(8,128)(2,1)S(1)}, u32[]{:S(2)}, u32[]{:S(2)}) collective-permute-start(bf16[1024,1408]{1,0:T(8,128)(2,1)S(1)} %fusion.9), channel_id=1, source_target_pairs={{0,16},{16,0},{1,17},{17,1},{2,18},{18,2},{3,19},{19,3},{4,20},{20... | collective-permute-start | bytes 8650760 | tf_op jit(solution)/shard_map/ppermute | solution.py:811
  252.1 6.0 collective-permute-start.3
  263.3 11.5 %copy-start.42 = (bf16[1408,1024]{1,0:T(8,128)(2,1)}, bf16[1408,1024]{1,0:T(8,128)(2,1)S(1)}, u32[]{:S(2)}) copy-start(bf16[1408,1024]{1,0:T(8,128)(2,1)S(1)} %add_convert_fusion.2.refs_4_) | copy-start | bytes 8650756
  264.8 12.8 %copy-start.41 = (f32[2,1024,1408]{2,1,0:T(8,128)S(1)}, f32[2,1024,1408]{2,1,0:T(8,128)}, u32[]{:S(2)}) copy-start(f32[2,1024,1408]{2,1,0:T(8,128)} %copy-done.40) | copy-start | bytes 34603012
  290.8 7.4 %copy-start.63 = (bf16[1024,1408]{1,0:T(8,128)(2,1)}, bf16[1024,1408]{1,0:T(8,128)(2,1)S(1)}, u32[]{:S(2)}) copy-start(bf16[1024,1408]{1,0:T(8,128)(2,1)S(1)} %get-tuple-element.92) | copy-start | bytes 8650756
  290.9 3.9 copy-start.54
  290.9 8.4 %collective-permute-start.6 = (bf16[1024,1408]{1,0:T(8,128)(2,1)S(1)}, bf16[1024,1408]{1,0:T(8,128)(2,1)S(1)}, u32[]{:S(2)}, u32[]{:S(2)}) collective-permute-start(bf16[1024,1408]{1,0:T(8,128)(2,1)S(1)} %get-tuple-element.92), channel_id=1, source_target_pairs={{0,16},{16,0},{1,17},{17,1},{2,18},{18,2},{3,19},{19,3},{4,20},{20... | collective-permute-start | bytes 8650760 | tf_op jit(solution)/shard_map/ppermute | solution.py:811
  294.3 4.9 collective-permute-start.4
  305.5 159.8 %reduce-scatter.7.cloned.1.call-start = ((), (), s32[]{:S(2)}) async-start(), calls=%async_computation.10 | async-start | bytes 3604480 | tf_op jit(solution)/shard_map/reduce_scatter | solution.py:848
  306.1 12.9 %collective-permute-start.5 = (bf16[1024,1408]{1,0:T(8,128)(2,1)}, bf16[1024,1408]{1,0:T(8,128)(2,1)}, u32[]{:S(2)}, u32[]{:S(2)}) collective-permute-start(bf16[1024,1408]{1,0:T(8,128)(2,1)} %get-tuple-element.91), channel_id=1, source_target_pairs={{0,16},{16,0},{1,17},{17,1},{2,18},{18,2},{3,19},{19,3},{4,20},{20... | collective-permute-start | bytes 8650760 | tf_op jit(solution)/shard_map/ppermute | solution.py:811
  307.8 53.1 %all-to-all-start = ((bf16[4,256,2048]{2,1,0:T(8,128)(2,1)}), bf16[4,256,2048]{2,1,0:T(8,128)(2,1)}, u32[]{:S(2)}, u32[]{:S(2)}) async-start(bf16[4,256,2048]{2,1,0:T(8,128)(2,1)} %bitcast.187), calls=%async_computation | async-start | bytes 8388608 | tf_op jit(solution)/shard_map/all_to_all | solution.py:929
  312.8 209.1 %reduce-scatter.11.cloned.1.call-start = ((), (), s32[]{:S(2)}) async-start(), calls=%async_computation.12 | async-start | bytes 3604480 | tf_op jit(solution)/shard_map/reduce_scatter | solution.py:848
  312.9 6.1 copy-start.65
  325.9 315.4 %reduce-scatter.17.cloned.1.call-start = ((), (), s32[]{:S(2)}) async-start(), calls=%async_computation.15 | async-start | bytes 1310720 | tf_op jit(solution)/shard_map/reduce_scatter | solution.py:848
  360.9 3.4 copy-start.8
  443.2 5.0 copy-start.44
  443.2 5.0 copy-start.46
  446.4 4.5 collective-permute-start.9
  449.5 3.0 collective-permute-start.8
  450.0 5.4 copy-start.50
  457.7 185.4 %reduce-scatter.13.cloned.1.call-start = ((), (), s32[]{:S(2)}) async-start(), calls=%async_computation.13 | async-start | bytes 2293760 | tf_op jit(solution)/shard_map/reduce_scatter | solution.py:848
  463.1 2.0 collective-permute-start.7
  475.1 30.6 %copy-start.48 = (bf16[1024,2048]{1,0:T(8,128)(2,1)S(1)}, bf16[1024,2048]{1,0:T(8,128)(2,1)}, u32[]{:S(2)}) copy-start(bf16[1024,2048]{1,0:T(8,128)(2,1)} %get-tuple-element.93) | copy-start | bytes 12582916
  475.1 30.6 %copy-start.49 = (bf16[1024,2048]{1,0:T(8,128)(2,1)S(1)}, bf16[1024,2048]{1,0:T(8,128)(2,1)}, u32[]{:S(2)}) copy-start(bf16[1024,2048]{1,0:T(8,128)(2,1)} %get-tuple-element.94) | copy-start | bytes 12582916
  511.4 9.4 %copy-start.13 = (bf16[1408,256]{1,0:T(8,128)(2,1)S(1)}, bf16[1408,256]{1,0:T(8,128)(2,1)}, u32[]{:S(2)}) copy-start(bf16[1408,256]{1,0:T(8,128)(2,1)} %reduce-scatter.7.cloned.1.call-done.rest_1_) | copy-start | bytes 2162692
  511.4 10.6 %copy-start.14 = (bf16[256,1408]{1,0:T(8,128)(2,1)S(1)}, bf16[256,1408]{1,0:T(8,128)(2,1)}, u32[]{:S(2)}) copy-start(bf16[256,1408]{1,0:T(8,128)(2,1)} %reduce-scatter.9.cloned.1.call-done.refs_7_) | copy-start | bytes 2162692
  511.4 131.7 %reduce-scatter.15.cloned.1.call-start = ((), (), s32[]{:S(2)}) async-start(), calls=%async_computation.14 | async-start | bytes 2293760 | tf_op jit(solution)/shard_map/reduce_scatter | solution.py:848
  520.7 8.6 %collective-permute-start.12 = (bf16[1024,896]{1,0:T(8,128)(2,1)}, bf16[1024,896]{1,0:T(8,128)(2,1)}, u32[]{:S(2)}, u32[]{:S(2)}) collective-permute-start(bf16[1024,896]{1,0:T(8,128)(2,1)} %fusion.45), channel_id=1, source_target_pairs={{0,16},{16,0},{1,17},{17,1},{2,18},{18,2},{3,19},{19,3},{4,20},{20... | collective-permute-start | bytes 5505032 | tf_op jit(solution)/shard_map/ppermute | solution.py:811
  522.0 7.4 %copy-start.56 = (bf16[2048,256]{1,0:T(8,128)(2,1)S(1)}, bf16[2048,256]{1,0:T(8,128)(2,1)}, u32[]{:S(2)}) copy-start(bf16[2048,256]{1,0:T(8,128)(2,1)} %copy-done.55) | copy-start | bytes 3145732
  522.0 7.4 %copy-start.60 = (bf16[2048,2]{1,0:T(8,128)(2,1)S(1)}, bf16[2048,2]{1,0:T(8,128)(2,1)}, u32[]{:S(2)}) copy-start(bf16[2048,2]{1,0:T(8,128)(2,1)} %copy-done.59) | copy-start | bytes 24580
  527.2 15.6 %collective-permute-start.10 = (bf16[128,2048]{1,0:T(8,128)(2,1)}, bf16[128,2048]{1,0:T(8,128)(2,1)S(1)}, u32[]{:S(2)}, u32[]{:S(2)}) collective-permute-start(bf16[128,2048]{1,0:T(8,128)(2,1)} %get-tuple-element.98), channel_id=1, source_target_pairs={{0,8},{4,12},{8,0},{12,4},{1,9},{5,13},{9,1},{13,5},{2,10},{6,14},... | collective-permute-start | bytes 1572872 | tf_op jit(solution)/shard_map/ppermute | solution.py:815
  528.2 14.7 %collective-permute-start.11 = (bf16[128,2048]{1,0:T(8,128)(2,1)}, bf16[128,2048]{1,0:T(8,128)(2,1)S(1)}, u32[]{:S(2)}, u32[]{:S(2)}) collective-permute-start(bf16[128,2048]{1,0:T(8,128)(2,1)} %get-tuple-element.99), channel_id=1, source_target_pairs={{0,4},{4,0},{8,12},{12,8},{1,5},{5,1},{9,13},{13,9},{2,6},{6,2},{1... | collective-permute-start | bytes 1572872 | tf_op jit(solution)/shard_map/ppermute | solution.py:815
  529.3 13.6 %copy-start.11 = (bf16[1024,2048]{1,0:T(8,128)(2,1)S(1)}, bf16[1024,2048]{1,0:T(8,128)(2,1)}, u32[]{:S(2)}) copy-start(bf16[1024,2048]{1,0:T(8,128)(2,1)} %copy-done.10) | copy-start | bytes 12582916
  543.0 2.9 copy-start.15
  543.0 2.9 copy-start.30
  644.1 4.0 copy-start.1
  (26 other events, 44.3 us)
Sparse Core Ops, SparseCore 0:
  10.7 84.9 all-gather.3
  97.2 106.6 all-gather.7
  205.6 59.1 all-gather.5
  305.7 54.3 reduce-scatter.8
  362.2 56.0 reduce-scatter.6
  420.4 56.0 reduce-scatter.10
  478.8 26.9 reduce-scatter.16
  511.5 37.1 reduce-scatter.12
  551.1 38.5 reduce-scatter.14

commit v6 on v5

--- a/solution.py
+++ b/solution.py
@@ -573,9 +573,11 @@
 
 MESH = pl.DeviceIdType.MESH
 STRIP = 16
-
-
-def phase_kernel(middle, both_cores, small_sum, n_in, n_out, part_ref, *refs):
+TILE = 512
+WIDE = 256
+
+
+def phase_kernel(middle, both_cores, small_sum, meanwhile, n_in, n_out, part_ref, *refs):
     inputs, all_ref = refs[:n_in], refs[n_in]
     outs, scratch = refs[n_in + 1 : n_in + n_out], refs[n_in + n_out :]
     got, sums, gain_sum, send_sem, recv_sem = scratch[:5]
@@ -619,35 +621,49 @@
         def _(i):
             body(pl.multiple_of(i * STRIP, STRIP))
 
-    order = [(across_both, 0), (across_both, 1), (across_x, 0), (across_y, 1)]
-    order += [(across_y, 0), (across_x, 1), (place, 0), (place, 1)]
+    part = part_ref
+    if meanwhile:
+        fetch = pltpu.make_async_copy(inputs[3].at[3], scratch[-3], scratch[-2])
+        fetch.start()
     if both_cores:
-        part, incoming, local_sem = scratch[5:8]
-        mine = pltpu.make_async_copy(part_ref.at[pl.ds(core * count, count)], part, local_sem)
-        mine.start()
+        part, outgoing, incoming = scratch[5:8]
+        weight = inputs[3]
+        order = [across_both, across_x, across_y, place]
+
+        def product(whose, of, target):
+            start = pl.multiple_of(whose * count + 2 * of * rows, rows)
+            left = part_ref[pl.ds(start, 2 * rows), :]
+            lines = pl.ds(pl.multiple_of(2 * of * rows, rows), 2 * rows)
+
+            @pl.loop(0, weight.shape[1] // TILE)
+            def _(i):
+                tile = pl.ds(pl.multiple_of(i * TILE, TILE), TILE)
+                target[lines, tile] = jnp.dot(
+                    left, weight[:, tile], preferred_element_type=F32
+                ).astype(BF16)
+
+            return lines
+
         shared = []
-        for i, (of, half) in enumerate(order):
-            start = pl.multiple_of((1 - core) * count + (2 * of + half) * rows, rows)
-            shared.append(
-                copy(12 + i, part_ref.at[pl.ds(start, rows)], incoming.at[block(of, half)], "core")
-            )
-            shared[-1].start()
-        mine.wait()
-    else:
-        part = part_ref
-
-    def ready(index):
-        if both_cores:
-            of, half = order[index]
-            shared[index].wait_recv()
-
-            def add(at):
-                strip = pl.ds((2 * of + half) * rows + at, STRIP)
+        for number in range(4):
+            lines = pl.ds(pl.multiple_of(2 * order[number] * rows, rows), 2 * rows)
+            shared.append(copy(12 + number, outgoing.at[lines], incoming.at[lines], "core"))
+
+        def give(number):
+            product(1 - core, order[number], outgoing)
+            shared[number].start()
+
+        def take(number):
+            of = order[number]
+            product(core, of, part)
+            shared[number].wait_recv()
+
+            @pl.loop(0, 2 * rows // STRIP)
+            def _(i):
+                strip = pl.ds(pl.multiple_of(2 * of * rows + i * STRIP, STRIP), STRIP)
                 part[strip, :] = (
                     part[strip, :].astype(F32) + incoming[strip, :].astype(F32)
                 ).astype(BF16)
-
-            strips(add)
 
     far = [
         copy(0, part.at[block(across_both, 0)], got.at[0], "x"),
@@ -664,12 +680,25 @@
     out_second = [copy(8, own[0], own[0], "y"), copy(9, own[1], own[1], "x")]
     out_third = [copy(10, passed[0], passed[0], "y"), copy(11, passed[1], passed[1], "x")]
 
-    for index, step in enumerate((*far, *near)):
-        ready(index)
+    if both_cores:
+        give(0)
+        give(1)
+        take(0)
+    for step in far:
         step.start()
+    if both_cores:
+        give(2)
+        take(1)
+        near[0].start()
+        take(2)
+        near[1].start()
+        give(3)
+        take(3)
+    else:
+        for step in near:
+            step.start()
     gain_sum[...] = jnp.zeros_like(gain_sum)
     for half, onward in ((0, across_y), (1, across_x)):
-        ready(4 + half)
         far[half].wait_recv()
 
         def add(at):
@@ -680,7 +709,6 @@
         strips(add)
         last[half].start()
     for half in (0, 1):
-        ready(6 + half)
         near[half].wait_recv()
         last[half].wait_recv()
 
@@ -696,6 +724,32 @@
         out_first[half].start()
         out_second[half].start()
 
+    def use(of, first=False, last=False):
+        if not meanwhile:
+            return
+        weight, left = scratch[-3], inputs[4]
+        grad_left, products = outs[2], scratch[-1]
+        lines = pl.ds(pl.multiple_of(2 * of * rows, rows), 2 * rows)
+        grad_left[lines, :] = lax.dot_general(
+            all_ref[lines, :], weight[...], NT, preferred_element_type=F32
+        ).astype(BF16)
+
+        @pl.loop(0, products.shape[1] // TILE)
+        def _(i):
+            tile = pl.ds(pl.multiple_of(i * TILE, TILE), TILE)
+            more = lax.dot_general(
+                left[lines, :], all_ref[lines, tile], TN, preferred_element_type=F32
+            )
+            if first:
+                products[:, tile] = more
+            elif last:
+                outs[3][:, tile] = (products[:, tile] + more).astype(BF16)
+            else:
+                products[:, tile] = products[:, tile] + more
+
+    if meanwhile:
+        fetch.wait()
+    use(place, first=True)
     gain = jnp.sum(gain_sum[...], axis=0, keepdims=True)
     small = []
     if small_sum:
@@ -713,12 +767,12 @@
             lane = i * middle_lane
             values[8 : 8 + taps, lane : lane + width] = conv[...] * share
     elif n_out > 2:
-        outs[-1][...] = gain
+        outs[1][...] = gain
 
     def small_step(number):
         height = 8 if steps[number] in ("x", "y") else values.shape[0]
         step = copy(
-            20 + number,
+            16 + number,
             arrived.at[number, 1, pl.ds(0, height)],
             arrived.at[number, 0, pl.ds(0, height)],
             steps[number],
@@ -735,8 +789,13 @@
     if small_sum:
         for number in range(len(steps)):
             small_step(number)
-    for step in (*out_second, *out_third):
+    for step in out_second:
         step.wait_recv()
+    use(across_x)
+    use(across_y)
+    for step in out_third:
+        step.wait_recv()
+    use(across_both, last=True)
     for step in (*far, *near, *last, *out_first, *out_second, *out_third, *small):
         step.wait_send()
     if both_cores:
@@ -767,29 +826,47 @@
     return grad
 
 
-def mp_phase(number, middle, part, inputs, dummies, outs, both_cores=False, small=None):
+def mp_phase(
+    number, middle, part, inputs, dummies, outs, both_cores=False, small=None, meanwhile=False
+):
     here, there = pl.BlockSpec(memory_space=pltpu.VMEM), pl.BlockSpec(memory_space=pl.ANY)
-    count, model = part.shape[0] // (2 if both_cores else 1), part.shape[1]
+    count, model = part.shape
+    if both_cores:
+        count, model = count // 2, inputs[3].shape[1]
     block = (count // 8, model)
     copies, scratch, small_sum = 12, [], None
     if both_cores:
-        copies = 20
-        scratch += [pltpu.VMEM((count, model), BF16)] * 2 + [pltpu.SemaphoreType.DMA(())]
+        scratch += [pltpu.VMEM((count, model), BF16)] * 3
     if small is not None:
         stages = lax.axis_size("row").bit_length() - 1 + 3
-        copies = 20 + stages
+        copies = 16 + stages
         height = 8 + small[2].shape[0]
         shape = (height + -height % 8, model)
         scratch += [pltpu.VMEM((stages, 2, *shape), F32)]
         small_sum = {"dummies": len(dummies)}
         inputs = [*inputs, *small]
         outs = [*outs, jax.ShapeDtypeStruct(shape, F32)]
+    specs = [here] * len(inputs)
+    if meanwhile:
+        _, width, depth = inputs[3].shape
+        specs[3] = there
+        scratch += [
+            pltpu.VMEM((width, depth), BF16),
+            pltpu.SemaphoreType.DMA(()),
+            pltpu.VMEM((width, model), F32),
+        ]
     kernel = functools.partial(
-        phase_kernel, middle, both_cores, small_sum, len(inputs) + len(dummies), 1 + len(outs)
+        phase_kernel,
+        middle,
+        both_cores,
+        small_sum,
+        meanwhile,
+        len(inputs) + len(dummies),
+        1 + len(outs),
     )
     return pl.pallas_call(
         kernel,
-        in_specs=[there if both_cores else here] + [here] * len(inputs) + [there] * len(dummies),
+        in_specs=[here, *specs] + [there] * len(dummies),
         out_specs=[here] * (1 + len(outs)),
         out_shape=[jax.ShapeDtypeStruct((count, model), BF16), *outs],
         scratch_shapes=[
@@ -801,10 +878,119 @@
             *scratch,
         ],
         compiler_params=pltpu.CompilerParams(
-            collective_id=number, has_side_effects=True, vmem_limit_bytes=48 << 20
+            collective_id=number, has_side_effects=True, vmem_limit_bytes=50 << 20
         ),
         cost_estimate=pl.CostEstimate(flops=0, bytes_accessed=250 << 20, transcendentals=0),
     )(part, *inputs, *dummies)
+
+
+def pair_kernel(part_ref, hidden, left_own, left_other, gate, up, *refs):
+    block_ref, gate_pair, up_pair, got, sums, gate_in, up_in, send_sem, recv_sem = refs[-9:]
+    rows = part_ref.shape[0] // 8
+    place, core = lax.axis_index("mp"), lax.axis_index("seq")
+    across_x = place + 1 - 2 * (place % 2)
+    across_y = (place + 2) % 4
+    across_both = 3 - place
+    ways = {"x": {"mp": across_x}, "y": {"mp": across_y}, "core": {"seq": 1 - core}}
+    barrier = pltpu.get_barrier_semaphore()
+    for other in ways.values():
+        pl.semaphore_signal(barrier, inc=1, device_id=other, device_id_type=MESH)
+    pl.semaphore_wait(barrier, len(ways))
+
+    def copy(index, source, target, way):
+        return pltpu.make_async_remote_copy(
+            src_ref=source,
+            dst_ref=target,
+            send_sem=send_sem.at[index],
+            recv_sem=recv_sem.at[index],
+            device_id=ways[way],
+            device_id_type=MESH,
+        )
+
+    def block(of, half):
+        return pl.ds(pl.multiple_of((2 * of + half) * rows, rows), rows)
+
+    def strips(body):
+        @pl.loop(0, rows // STRIP)
+        def _(i):
+            body(pl.multiple_of(i * STRIP, STRIP))
+
+    far = [
+        copy(0, part_ref.at[block(across_both, 0)], got.at[0], "x"),
+        copy(1, part_ref.at[block(across_both, 1)], got.at[1], "y"),
+    ]
+    near = [
+        copy(2, part_ref.at[block(across_x, 0)], got.at[2], "x"),
+        copy(3, part_ref.at[block(across_y, 1)], got.at[3], "y"),
+    ]
+    last = [copy(4, sums.at[0], got.at[4], "y"), copy(5, sums.at[1], got.at[5], "x")]
+    shared = [copy(6, gate, gate_in, "core"), copy(7, up, up_in, "core")]
+    for step in (*shared, *far, *near):
+        step.start()
+
+    def products(own, other, target, first, count):
+        @pl.loop(first, first + count)
+        def _(i):
+            tile = pl.ds(pl.multiple_of(i * WIDE, WIDE), WIDE)
+            total = lax.dot_general(
+                left_own[:, tile], own[...], TN, preferred_element_type=F32
+            ) + lax.dot_general(left_other[:, tile], other[...], TN, preferred_element_type=F32)
+            target[tile, :] = total.astype(BF16)
+
+    tiles = left_own.shape[1] // WIDE
+    shared[0].wait_recv()
+    products(gate, gate_in, gate_pair, 0, tiles)
+    for half, onward in ((0, across_y), (1, across_x)):
+        far[half].wait_recv()
+
+        def add(at):
+            strip = pl.ds(at, STRIP)
+            mine = part_ref[pl.ds((2 * onward + half) * rows + at, STRIP), :]
+            sums[half, strip, :] = (mine.astype(F32) + got[half, strip, :].astype(F32)).astype(BF16)
+
+        strips(add)
+        last[half].start()
+    shared[1].wait_recv()
+    products(up, up_in, up_pair, 0, tiles)
+    for half in (0, 1):
+        near[half].wait_recv()
+        last[half].wait_recv()
+
+        def finish(at):
+            strip = pl.ds(at, STRIP)
+            total = part_ref[pl.ds((2 * place + half) * rows + at, STRIP), :].astype(F32)
+            total = total + got[2 + half, strip, :].astype(F32)
+            total = total + got[4 + half, strip, :].astype(F32)
+            block_ref[pl.ds(half * rows + at, STRIP), :] = (hidden[half, strip, :] + total).astype(BF16)
+
+        strips(finish)
+    for step in (*shared, *far, *near, *last):
+        step.wait_send()
+
+
+def scattered_and_pairs(number, part, hidden, left, gate, up, dummies):
+    here, there = pl.BlockSpec(memory_space=pltpu.VMEM), pl.BlockSpec(memory_space=pl.ANY)
+    count, model = part.shape
+    block = (count // 8, model)
+    pair = jax.ShapeDtypeStruct((left[0].shape[1], gate.shape[1]), BF16)
+    return pl.pallas_call(
+        pair_kernel,
+        in_specs=[here] * 6 + [there] * len(dummies),
+        out_specs=[here] * 3,
+        out_shape=[jax.ShapeDtypeStruct((2 * block[0], model), BF16), pair, pair],
+        scratch_shapes=[
+            pltpu.VMEM((6, *block), BF16),
+            pltpu.VMEM((2, *block), BF16),
+            pltpu.VMEM(gate.shape, BF16),
+            pltpu.VMEM(up.shape, BF16),
+            pltpu.SemaphoreType.DMA((8,)),
+            pltpu.SemaphoreType.DMA((8,)),
+        ],
+        compiler_params=pltpu.CompilerParams(
+            collective_id=number, has_side_effects=True, vmem_limit_bytes=50 << 20
+        ),
+        cost_estimate=pl.CostEstimate(flops=0, bytes_accessed=130 << 20, transcendentals=0),
+    )(part, hidden, *left, gate, up, *dummies)
 
 
 def swapped(block):
@@ -878,10 +1064,8 @@
     )
     qkv_own = lax.dynamic_slice_in_dim(qkv_full, core * width, width, axis=2)
     beta_own = lax.dynamic_slice_in_dim(beta_full, core * own_heads, own_heads, axis=0)
-    mix_weight = jnp.concatenate(
-        [qkv_own[0], qkv_own[1], qkv_own[2], jnp.pad(beta_own.T, ((0, 0), (0, HDIM - own_heads)))],
-        axis=1,
-    )
+    beta_rows = jnp.pad(beta_own, ((0, HDIM - own_heads), (0, 0)))
+    mix_across = jnp.concatenate([qkv_own[0].T, qkv_own[1].T, qkv_own[2].T, beta_rows])
     conv_own = lax.dynamic_slice_in_dim(conv_weight, core * width, width, axis=2)
     conv_own = conv_own.transpose(1, 0, 2).reshape(KERNEL, 3 * width)
 
@@ -894,7 +1078,9 @@
     doc_start, real_row = row_layout(doc_lengths[0], positions)
     keep = jnp.pad((doc_start[::BLOCK] != positions[::BLOCK]).astype(F32), (0, 1))
     count = jnp.sum(real_row.reshape(-1, BLOCK), axis=1).astype(jnp.int32)
-    raw = jnp.dot(normed, mix_weight, preferred_element_type=F32).astype(BF16)
+    raw = lax.dot_general(
+        normed, mix_across, (((1,), (1,)), ((), ())), preferred_element_type=F32
+    ).astype(BF16)
     gain = out_gain[None, :]
     group = 4 if raw.shape[0] % (4 * CHUNK) == 0 else 1
     heads_out, *saved = forward(keep, count, raw, conv_own, gain, group)
@@ -926,9 +1112,6 @@
     ffn_part = jnp.dot(
         after(product, down_pair), down_full, preferred_element_type=F32
     ).astype(BF16)
-    ffn_parts = lax.all_to_all(ffn_part, "mp", split_axis=0, concat_axis=0, tiled=True)
-    ffn_own = jnp.sum(ffn_parts.astype(F32).reshape(4, quarter, model), axis=0)
-    block_out = (hidden.reshape(quarter, model) + ffn_own).astype(BF16)
     grad_product = jnp.dot(grad_top, down_full.T, preferred_element_type=F32)
     grad_product = after(grad_product, ffn_part)
     grad_gate = grad_product * gate_up[1] * gate_sig * (1.0 + gate_up[0] * (1.0 - gate_sig))
@@ -940,25 +1123,28 @@
         gateup_full,
         preferred_element_type=F32,
     ).astype(BF16)
-    normed_halves = own_columns(normed_mid, core)
-    gate_pair = both_tokens(normed_halves, (grad_gate, swapped(grad_gate)))
-    up_pair = both_tokens(normed_halves, (grad_up, swapped(grad_up)))
+    block_out, gate_pair, up_pair = scattered_and_pairs(
+        4, ffn_part, hidden, own_columns(normed_mid, core), grad_gate, grad_up, []
+    )
     down_sum, gate_sum, up_sum = over_row(down_pair, 1), over_row(gate_pair, 0), over_row(up_pair, 0)
-    grad_branch, grad_hidden, ffn_gain_part = mp_phase(
+    grad_branch, grad_hidden, ffn_gain_part, grad_normed_out, grad_out_part = mp_phase(
         1,
         partial(normed_backward, True),
         grad_mid_part,
-        [hidden, own_rows(cotangent), ffn_gain[None, :]],
-        [block_out, down_pair, gate_pair, up_pair],
-        [rows_own, jax.ShapeDtypeStruct((1, model), F32)],
-    )
-    grad_normed_out = jnp.dot(grad_branch, out_full, preferred_element_type=F32).astype(BF16)
-
+        [hidden, own_rows(cotangent), ffn_gain[None, :], mixer_full.transpose(0, 2, 1), normed_out],
+        [block_out, down_sum, gate_pair, up_pair],
+        [
+            rows_own,
+            jax.ShapeDtypeStruct((1, model), F32),
+            jax.ShapeDtypeStruct(normed_out.shape, BF16),
+            jax.ShapeDtypeStruct((normed_out.shape[1], model), BF16),
+        ],
+        meanwhile=True,
+    )
     mine, other = halves(grad_normed_out, core, 1)
     grad_heads = in_order(mine, swapped(other), core, 0)
-    out_pair = both_tokens(
-        (normed_out, swapped(after(normed_out, up_sum))), own_columns(grad_branch, core)
-    )
+    mine, other = halves(grad_out_part, core, 1)
+    out_pair = after(mine.astype(F32) + swapped(other).astype(F32), up_sum).astype(BF16)
     grad_raw, grad_conv_own, out_gain_part, block_out = backward(
         keep,
         count,
@@ -969,16 +1155,12 @@
         *saved,
         group,
         block_out,
-        [down_sum, out_pair],
+        [gate_sum],
     )
     piece = lambda of, half: lax.dynamic_slice_in_dim(
         block_out, (2 * of + half) * (quarter // 2), quarter // 2, axis=0
     )
     far_rows = [across(piece(own ^ 1, 0), 2), across(piece(own ^ 2, 1), 1)]
-    grad_normed = lax.dot_general(
-        grad_raw, mix_weight, (((1,), (1,)), ((), ())), preferred_element_type=F32
-    )
-    grad_normed_part = grad_normed.astype(BF16)
     normed_mine, normed_other = halves(normed, core, 1)
     by_columns = lambda part: lax.dot_general(
         part, grad_raw, (((0,), (0,)), ((), ())), preferred_element_type=F32
@@ -988,9 +1170,9 @@
     grad_input, small = mp_phase(
         2,
         partial(normed_backward, False),
-        grad_normed_part,
-        [residual_own, grad_hidden, attn_gain[None, :]],
-        [gate_sum, up_sum, qkv_mine, qkv_other, *far_rows],
+        grad_raw,
+        [residual_own, grad_hidden, attn_gain[None, :], mix_across],
+        [up_sum, out_pair, qkv_mine, qkv_other, *far_rows],
         [],
         both_cores=True,
         small=[ffn_gain_part, out_gain_part, grad_conv_own],

time: 659 us -> 650 us (0.986)
  Pallas kernels: 289 us -> 341 us
  matrix products: 148 us -> 104 us
  waiting for transfers between devices: 65.2 us -> 48.4 us
  blocking collectives: 25.4 us -> 34 us
    pallas_call x3 -> x4, Pallas kernels: 243 us -> 295 us  [the longest x3 249 us: mp_phase(): pl.pallas_call(kernel, in_specs=[here, *specs] + [there] * len(dummies),...]
    dot_general x8 -> x2, matrix products: 37.8 us -> 12.2 us  [both_tokens(): lax.dot_general(a, b, (((0,), (0,)), ((), ())), preferred_element_type=F32)]
    dot_general x3 -> x1, matrix products: 30.4 us -> 11.8 us  [joined_shards(): lax.dot_general(normed, mix_across, (((1,), (1,)), ((), ())), preferred_e...]
    all_to_all x1 -> x0, waiting for transfers between devices: 16.7 us -> none  [joined_shards(): lax.all_to_all(ffn_part, 'mp', split_axis=0, concat_axis=0, tiled=True)]
    all_gather x1, blocking collectives: 25.4 us -> 34 us  [joined_shards(): lax.all_gather(weight, ('seq', 'row'), axis=1, tiled=True)]
    all_gather x3, waiting for transfers between devices: 41.8 us -> 34 us  [joined_shards(): lax.all_gather(weight, ('seq', 'row'), axis=1, tiled=True)]
    unnamed x134 -> x108, local copies, waits for them, and re-layouts: 35.1 us -> 32.6 us
  transfers between devices with their start and end apart: 23 -> 19, of which waited for: 8 -> 7; matrix products, arithmetic and copies ran while one was open for 27% -> 25% of each run, Pallas kernels for 44% -> 53%
where the time goes in v6:
time: 650 us; the launch traced here: 646 us
  Pallas kernels  341 us (52%)
  matrix products  104 us (16%)
  local copies, waits for them, and re-layouts  51.9 us (8%)
  waiting for transfers between devices  48.4 us (7%)
  other arithmetic  45.3 us (7%)
  blocking collectives  34 us (5%)
  between operations  16.8 us (3%)
    pallas_call x3, Pallas kernels, mp_phase(): pl.pallas_call(kernel, in_specs=[here, *specs] + [there] * len(dummies),...  249 us
    pallas_call x1, Pallas kernels, scattered_and_pairs(): pl.pallas_call(pair_kernel, in_specs=[here] * 6 + [there] * len(dummies),...  45.2 us
    all_gather x3, waiting for transfers between devices, joined_shards(): lax.all_gather(weight, ('seq', 'row'), axis=1, tiled=True)  34 us
    all_gather x1, blocking collectives, joined_shards(): lax.all_gather(weight, ('seq', 'row'), axis=1, tiled=True)  34 us
    unnamed x108, local copies, waits for them, and re-layouts  32.6 us
    pallas_call x1, Pallas kernels, backward(): pl.pallas_call(functools.partial(bwd_kernel, heads, group), grid=(steps,)...  26.4 us
    pallas_call x1, Pallas kernels, forward(): pl.pallas_call(functools.partial(fwd_kernel, heads, group), grid=(n // ro...  19.8 us
    dot_general x1, matrix products, joined_shards(): jnp.einsum('td,sdf->stf', normed_mid, gateup_full, preferred_element_type...  18 us
  transfers between devices with their start and end apart: 19, of which 7 were waited for; matrix products, arithmetic and copies ran while one was open for 25% of the time, Pallas kernels for 53%

profile of v6, /device:TPU:0, one launch (start us, length us, event | category | flops | bytes accessed | tf_op | source)
XLA Modules:
  0.0 645.9 jit_solution(4431286184271875866)
XLA Ops:
  7.2 1.4 copy.40
  8.7 2.0 pad_maximum_fusion.4
  11.5 3.2 fusion
  15.0 3.0 fusion.2
  20.8 34.0 %all_gather.13 = bf16[4,2048]{1,0:T(4,128)(2,1)S(1)} all-gather(bf16[4,256]{1,0:T(4,128)(2,1)S(1)} %copy-done.51), channel_id=1, replica_groups=mesh['seq'=2,'mp'=4,'row'=4] {'seq','row'}, dimensions={1}, use_global_device_ids=true | all-gather | bytes 18432 | tf_op jit(solution)/shard_map/all_gather | solution.py:1057
  54.8 7.6 %broadcast_select_fusion.1 = (bf16[1024,2048]{1,0:T(8,128)(2,1)}, bf16[1024,2048]{1,0:T(8,128)(2,1)}) fusion(bf16[1024,2048]{1,0:T(8,128)(2,1)} %collective-permute-done, pred[]{:T(512)S(6)} %eq.25, f32[2048]{0:T(1024)S(1)} %copy-done.28, f32[1024]{0:T(1024)S(1)} %add_rsqrt_fusion, bf16[1,1024,2048]{2,1,0:T(8,128)(2,1)} %param.12), kind=kLoop, calls=%fused_computation.47 | loop fusion | flops 12582912 | bytes 16789504 | tf_op jit(solution)/shard_map/jit(_where)/select_n | solution.py:1005
  62.4 34.0 %all-gather.4.cloned.1.call-done = bf16[4,2048,512]{1,2,0:T(8,128)(2,1)} async-done(((bf16[4,256,512]{1,2,0:T(8,128)(2,1)}), bf16[4,2048,512]{1,2,0:T(8,128)(2,1)}) %all-gather.4.cloned.1.call-update) | async-done | bytes 8388624 | tf_op jit(solution)/shard_map/all_gather | solution.py:1057
  96.4 2.8 slice-done
  99.6 2.9 copy-done.35
  102.5 11.8 %fusion.31.raw_ref.prev_ref = bf16[2048,896]{1,0:T(8,128)(2,1)S(1)} fusion(bf16[1024,2048]{1,0:T(8,128)(2,1)} %get-tuple-element.102, bf16[1024,2048]{1,0:T(8,128)(2,1)S(1)} %copy-done.35, bf16[2,2048]{1,0:T(2,128)(2,1)S(1)} %constant_dynamic-slice_fusion.10, bf16[256,2048]{1,0:T(8,128)(2,1)S(1)} %get-tuple-element.105, ...), kind=kOutput, calls=%fused_computation.51 | convolution fusion | flops 7553155072 | bytes 15212544 | tf_op jit(solution)/shard_map/dot_general | solution.py:1081
  114.3 19.8 %shard_map.203 = (bf16[2048,256]{1,0:T(8,128)(2,1)S(1)}, f32[2048,256]{1,0:T(8,128)S(1)}, bf16[16,2,128,128]{3,2,1,0:T(8,128)(2,1)S(1)}, bf16[16,2,128,128]{3,2,...) custom-call(f32[33]{0:T(128)S(1)} %pad_convert_fusion.keep_ref, ...), custom_call_target="tpu_custom_call" | custom-call | bytes 125829120 | tf_op jit(solution)/shard_map/pallas_call | solution.py:117
  134.2 1.9 copy-done.2
  136.1 1.3 copy-done.18
  137.5 1.0 copy-done.20
  138.4 1.0 copy-done.22
  139.4 1.0 copy-done.24
  140.8 1.3 constant_dynamic-slice_fusion.7
  142.7 6.4 convolution_convert_fusion.1.part_ref
  149.2 78.8 %shard_map.204 = (bf16[1024,2048]{1,0:T(8,128)(2,1)}, f32[2,128,2048]{2,1,0:T(8,128)S(1)}) custom-call(bf16[1024,2048]{1,0:T(8,128)(2,1)} %convolution_convert_fusion.1.part_ref, bf16[2,128,2048]{2,1,0:T(8,128)(2,1)S(1)} %bitcast.161, f32[1,2048]{1,0:T(1,128)S(1)} %bitcast.169), custom_call_target="tpu_custom_call" | custom-call | bytes 262144000 | tf_op jit(solution)/shard_map/pallas_call | solution.py:867
  228.0 18.0 %convolution_bitcast_fusion = f32[2,1024,1408]{2,1,0:T(8,128)S(1)} fusion(bf16[2,2048,1408]{2,1,0:T(8,128)(2,1)} %all-gather.8.cloned.1.call-done, bf16[1024,2048]{1,0:T(8,128)(2,1)} %get-tuple-element.33), kind=kOutput, calls=%fused_computation.14 | convolution fusion | flops 11811160064 | bytes 27262976 | tf_op jit(solution)/shard_map/td,sdf->stf/dot_general | solution.py:1108
  246.1 1.8 fusion.9
  248.0 3.4 copy-done.45
  251.8 5.9 fusion.32
  257.6 6.4 add_convert_fusion
  264.1 4.7 constant_dynamic-slice_fusion.4
  269.3 1.2 slice.100
  271.1 10.2 %convolution_convert_fusion.part_ref = bf16[1024,2048]{1,0:T(8,128)(2,1)S(1)} fusion(bf16[1408,2048]{1,0:T(8,128)(2,1)} %all-gather.6.cloned.1.call-done, bf16[1024,1408]{1,0:T(8,128)(2,1)} %copy-done.43, bf16[]{:T(256)} %bitcast.32), kind=kOutput, calls=%fused_computation.48 | convolution fusion | flops 5909118976 | bytes 12845058 | tf_op jit(solution)/shard_map/dot_general | solution.py:1112
  282.6 14.7 %fusion.12 = (bf16[1024,1408]{1,0:T(8,128)(2,1)}, bf16[1024,1408]{1,0:T(8,128)(2,1)}) fusion(f32[2,1024,1408]{2,1,0:T(8,128)} %copy-done.33, f32[]{:T(128)} %bitcast.33, bf16[1408,2048]{1,0:T(8,128)(2,1)} %all-gather.6.cloned.1.call-done, bf16[1,1024,2048]{2,1,0:T(8,128)(2,1)S(1)} %copy-done.46), kind=kOutput, calls=%fused_computation.24 | convolution fusion | flops 5925765120 | bytes 27262980 | tf_op jit(solution)/shard_map/dot_general | solution.py:1115
  297.4 45.2 %shard_map.205 = (bf16[256,2048]{1,0:T(8,128)(2,1)S(1)}, bf16[1024,1408]{1,0:T(8,128)(2,1)}, bf16[1024,1408]{1,0:T(8,128)(2,1)}) custom-call(bf16[1024,2048]{1,0:T(8,128)(2,1)} %copy-done.38, f32[2,128,2048]{2,1,0:T(8,128)S(1)} %get-tuple-element.34.hidden.refs_0_, bf16[1024,1024]{1,0:T(8,128)(2,1)} %get-tuple-element.109.left_own, ...), custom_call_target="tpu_custom_call" | custom-call | bytes 136314880 | tf_op jit(solution)/shard_map/pallas_call | solution.py:976
  344.3 1.5 constant_dynamic-slice_fusion.6
  345.8 1.3 pad_maximum_fusion.5.refs_4_
  347.1 17.4 %bitcast_convert_fusion.part_ref = bf16[1024,2048]{1,0:T(8,128)(2,1)} fusion(bf16[2,2048,1408]{2,1,0:T(8,128)(2,1)} %all-gather.8.cloned.1.call-done, bf16[1,1024,1408]{2,1,0:T(8,128)(2,1)} %bitcast.176, bf16[1,1024,1408]{2,1,0:T(8,128)(2,1)S(1)} %bitcast.175), kind=kOutput, calls=%fused_computation.11 | convolution fusion | flops 11816140800 | bytes 21495808 | tf_op jit(solution)/shard_map/stf,sdf->td/dot_general | solution.py:1120
  364.5 1.1 copy-done.13
  365.7 80.2 %shard_map.206 = (bf16[1024,2048]{1,0:T(8,128)(2,1)}, f32[2,128,2048]{2,1,0:T(8,128)}, f32[1,2048]{1,0:T(1,128)S(1)}, bf16[1024,512]{1,0:T(8,128)(2,1)S(1)}, bf16[512,2048]{1,0:T(8,128)(2,1)}) custom-call(bf16[1024,2048]{1,0:T(8,128)(2,1)} %bitcast_convert_fusion.part_ref, f32[2,128,2048]{2,1,0:T(8,128)} %copy-done.7, bf16[2,128,2048]{2,1,0:T(8,128)(2,1)S(1)} %bitcast.163, ...), custom_call_target="tpu_custom_call" | custom-call | bytes 262144000 | tf_op jit(solution)/shard_map/pallas_call | solution.py:867
  446.9 1.4 constant_dynamic-slice_fusion
  448.4 1.1 slice.102
  451.2 3.1 add_convert_fusion.1.refs_8_
  454.5 1.8 collective-permute-done.5
  456.7 2.0 copy-done.3
  458.7 1.1 copy-done.16
  459.8 1.6 copy-done.19
  461.4 1.2 copy-done.21
  462.7 1.4 copy-done.23
  464.0 1.2 copy-done.25
  465.3 26.4 %shard_map.207 = (bf16[2048,896]{1,0:T(8,128)(2,1)S(1)}, f32[4,768]{1,0:T(4,128)S(1)}, f32[1,128]{1,0:T(1,128)S(1)}, bf16[1024,2048]{1,0:T(8,128)(2,1)S(1)}) custom-call(f32[33]{0:T(128)S(1)} %pad_convert_fusion.keep_ref, s32[32]{0:T(128)S(1)} %convert_element_type.104.count_ref, bf16[2048,896]{1,0:T(8,128)(2,1)S(1)} %copy-done.3, ...), custom_call_target="tpu_custom_call" | custom-call | bytes 125829120 | tf_op jit(solution)/shard_map/pallas_call | solution.py:254
  491.6 2.0 copy-done.8
  493.7 1.9 copy-done.12
  495.5 5.7 fusion.40.refs_9_
  501.3 7.9 %fusion.37 = bf16[1024,896]{1,0:T(8,128)(2,1)S(1)} fusion(bf16[2048,896]{1,0:T(8,128)(2,1)} %copy-done.12, s32[]{:T(128)S(6)} %select_n.150, bf16[1024,2048]{1,0:T(8,128)(2,1)} %get-tuple-element.101, bf16[1024,2048]{1,0:T(8,128)(2,1)} %get-tuple-element.102), kind=kOutput, calls=%fused_computation.60 | convolution fusion | flops 3767402496 | bytes 13893636 | tf_op jit(solution)/shard_map/dot_general | solution.py:1165
  509.3 3.8 collective-permute-done.9.refs_10_
  513.1 1.3 copy-done.34
  514.5 1.4 constant_dynamic-slice_fusion.2
  515.9 1.1 collective-permute-start.6
  517.0 1.0 collective-permute-start.7
  518.0 3.6 fusion.30.refs_3_
  521.6 1.2 convert_element_type.132
  522.8 1.8 maximum_convert_fusion
  524.6 5.3 collective-permute-done.6.refs_11_
  530.8 2.8 bitcast_select_fusion
  533.6 90.4 %shard_map.208 = (bf16[1024,2048]{1,0:T(8,128)(2,1)}, f32[16,2048]{1,0:T(8,128)S(1)}) custom-call(bf16[2048,896]{1,0:T(8,128)(2,1)} %copy-done.12, bf16[2,128,2048]{2,1,0:T(8,128)(2,1)S(1)} %bitcast.162, f32[2,128,2048]{2,1,0:T(8,128)} %get-tuple-element.46.refs_1_, f32[1,2048]{1,0:T(1,128)S(1)} %bitcast.168, bf16[896,2048]{1,0:T(8,128)(2,1)} %fusion.30.refs_3_, ...), custom_call_target="tpu_custom_call" | custom-call | bytes 262144000 | tf_op jit(solution)/shard_map/pallas_call | solution.py:867
  625.8 6.7 %bitcast_convert_fusion.1 = f32[1,1024,2048]{2,1,0:T(8,128)} fusion(bf16[1024,2048]{1,0:T(8,128)(2,1)} %get-tuple-element.51), kind=kLoop, calls=%fused_computation.41 | loop fusion | flops 2097152 | bytes 12582912 | tf_op jit(solution)/shard_map/broadcast_in_dim | solution.py:1205
  632.5 1.8 convert_element_type.130
  635.3 1.2 broadcast_select_fusion.7
  637.0 1.6 copy.45
  (174 shorter events, 16.0 us)
Async XLA Ops:
  7.2 47.6 %copy-start = (f32[3,4,512]{2,1,0:T(4,128)S(1)}, f32[3,4,512]{2,1,0:T(4,128)}, u32[]{:S(2)}) copy-start(f32[3,4,512]{2,1,0:T(4,128)} %param.16) | copy-start | bytes 73732
  7.2 89.2 %all-gather.4.cloned.1.call-start = ((), (), s32[]{:S(2)}) async-start(), calls=%async_computation.6 | async-start | bytes 9437184 | tf_op jit(solution)/shard_map/all_gather | solution.py:1057
  8.6 6.1 copy-start.28
  10.7 217.3 %all-gather.8.cloned.1.call-start = ((), (), s32[]{:S(2)}) async-start(), calls=%async_computation.8 | async-start | bytes 12976128 | tf_op jit(solution)/shard_map/all_gather | solution.py:1057
  11.5 259.7 %all-gather.6.cloned.1.call-start = ((), (), s32[]{:S(2)}) async-start(), calls=%async_computation.7 | async-start | bytes 6488064 | tf_op jit(solution)/shard_map/all_gather | solution.py:1057
  11.5 3.5 copy-start.32
  15.0 3.6 copy-start.52
  15.0 5.8 copy-start.51
  18.0 36.8 %collective-permute-start = (bf16[1024,2048]{1,0:T(8,128)(2,1)}, bf16[1024,2048]{1,0:T(8,128)(2,1)}, u32[]{:S(2)}, u32[]{:S(2)}) collective-permute-start(bf16[1024,2048]{1,0:T(8,128)(2,1)} %fusion.2), channel_id=1, source_target_pairs={{0,16},{16,0},{1,17},{17,1},{2,18},{18,2},{3,19},{19,3},{4,20},{20... | collective-permute-start | bytes 12582920 | tf_op jit(solution)/shard_map/ppermute | solution.py:997
  18.5 346.1 %reduce-scatter.7.cloned.1.call-start = ((), (), s32[]{:S(2)}) async-start(), calls=%async_computation.9 | async-start | bytes 3604480 | tf_op jit(solution)/shard_map/reduce_scatter | solution.py:1034
  54.8 44.8 %copy-start.49 = (bf16[2,2048]{1,0:T(2,128)(2,1)}, bf16[2,2048]{1,0:T(2,128)(2,1)S(1)}, u32[]{:S(2)}) copy-start(bf16[2,2048]{1,0:T(2,128)(2,1)S(1)} %constant_dynamic-slice_fusion.10) | copy-start | bytes 24580
  96.4 2.8 slice-start
  99.2 3.3 copy-start.35
  99.6 14.7 %copy-start.39 = (bf16[256,2048]{1,0:T(8,128)(2,1)}, bf16[256,2048]{1,0:T(8,128)(2,1)S(1)}, u32[]{:S(2)}) copy-start(bf16[256,2048]{1,0:T(8,128)(2,1)S(1)} %get-tuple-element.103) | copy-start | bytes 3145732
  99.6 14.7 %copy-start.41 = (bf16[256,2048]{1,0:T(8,128)(2,1)}, bf16[256,2048]{1,0:T(8,128)(2,1)S(1)}, u32[]{:S(2)}) copy-start(bf16[256,2048]{1,0:T(8,128)(2,1)S(1)} %get-tuple-element.104) | copy-start | bytes 3145732
  99.6 14.7 %copy-start.42 = (bf16[256,2048]{1,0:T(8,128)(2,1)}, bf16[256,2048]{1,0:T(8,128)(2,1)S(1)}, u32[]{:S(2)}) copy-start(bf16[256,2048]{1,0:T(8,128)(2,1)S(1)} %get-tuple-element.105) | copy-start | bytes 3145732
  102.5 11.8 %copy-start.31 = (f32[128]{0:T(128)S(1)}, f32[128]{0:T(128)}, u32[]{:S(2)}) copy-start(f32[128]{0:T(128)} %param.18) | copy-start | bytes 1540
  134.2 1.9 copy-start.2
  136.1 1.3 copy-start.18
  140.4 2.0 collective-permute-start.1
  142.1 7.1 %copy-start.4 = (bf16[1,256,2048]{2,1,0:T(8,128)(2,1)}, bf16[1,256,2048]{2,1,0:T(8,128)(2,1)S(1)}, u32[]{:S(2)}) copy-start(bf16[1,256,2048]{2,1,0:T(8,128)(2,1)S(1)} %constant_dynamic-slice_fusion.7) | copy-start | bytes 3145732
  142.7 6.5 %copy-start.47 = (bf16[1024,256]{1,0:T(8,128)(2,1)}, bf16[1024,256]{1,0:T(8,128)(2,1)S(1)}, u32[]{:S(2)}) copy-start(bf16[1024,256]{1,0:T(8,128)(2,1)S(1)} %get-tuple-element.112) | copy-start | bytes 1572868
  142.7 6.5 copy-start.48
  142.7 6.4 copy-start.30
  228.0 69.4 %copy-start.7 = (f32[2,128,2048]{2,1,0:T(8,128)}, f32[2,128,2048]{2,1,0:T(8,128)S(1)}, u32[]{:S(2)}) copy-start(f32[2,128,2048]{2,1,0:T(8,128)S(1)} %get-tuple-element.34.hidden.refs_0_) | copy-start | bytes 6291460
  246.1 5.7 copy-start.33
  246.1 5.3 copy-start.45
  248.0 9.7 %copy-start.43 = (bf16[1024,1408]{1,0:T(8,128)(2,1)}, bf16[1024,1408]{1,0:T(8,128)(2,1)S(1)}, u32[]{:S(2)}) copy-start(bf16[1024,1408]{1,0:T(8,128)(2,1)S(1)} %fusion.9) | copy-start | bytes 8650756
  248.0 9.7 %collective-permute-start.2 = (bf16[1024,1408]{1,0:T(8,128)(2,1)S(1)}, bf16[1024,1408]{1,0:T(8,128)(2,1)S(1)}, u32[]{:S(2)}, u32[]{:S(2)}) collective-permute-start(bf16[1024,1408]{1,0:T(8,128)(2,1)S(1)} %fusion.9), channel_id=1, source_target_pairs={{0,16},{16,0},{1,17},{17,1},{2,18},{18,2},{3,19},{19,3},{4,20},{20... | collective-permute-start | bytes 8650760 | tf_op jit(solution)/shard_map/ppermute | solution.py:997
  251.7 6.0 collective-permute-start.3
  264.0 184.4 %reduce-scatter.11.cloned.1.call-start = ((), (), s32[]{:S(2)}) async-start(), calls=%async_computation.11 | async-start | bytes 3604480 | tf_op jit(solution)/shard_map/reduce_scatter | solution.py:1034
  268.8 28.6 %collective-permute-start.4 = (bf16[1024,1024]{1,0:T(8,128)(2,1)}, bf16[1024,1024]{1,0:T(8,128)(2,1)}, u32[]{:S(2)}, u32[]{:S(2)}) collective-permute-start(bf16[1024,1024]{1,0:T(8,128)(2,1)} %get-tuple-element.108), channel_id=1, source_target_pairs={{0,16},{16,0},{1,17},{17,1},{2,18},{18,2},{3,19},{19,3},{4,20},{20... | collective-permute-start | bytes 6291464 | tf_op jit(solution)/shard_map/ppermute | solution.py:997
  271.1 11.5 %copy-start.46 = (bf16[1,1024,2048]{2,1,0:T(8,128)(2,1)S(1)}, bf16[1,1024,2048]{2,1,0:T(8,128)(2,1)}, u32[]{:S(2)}) copy-start(bf16[1,1024,2048]{2,1,0:T(8,128)(2,1)} %param.23) | copy-start | bytes 12582916
  281.4 16.0 %copy-start.38 = (bf16[1024,2048]{1,0:T(8,128)(2,1)}, bf16[1024,2048]{1,0:T(8,128)(2,1)S(1)}, u32[]{:S(2)}) copy-start(bf16[1024,2048]{1,0:T(8,128)(2,1)S(1)} %convolution_convert_fusion.part_ref) | copy-start | bytes 12582916
  343.6 113.0 %reduce-scatter.9.cloned.1.call-start = ((), (), s32[]{:S(2)}) async-start(), calls=%async_computation.10 | async-start | bytes 3604480 | tf_op jit(solution)/shard_map/reduce_scatter | solution.py:1034
  344.2 288.2 %reduce-scatter.17.cloned.1.call-start = ((), (), s32[]{:S(2)}) async-start(), calls=%async_computation.14 | async-start | bytes 1310720 | tf_op jit(solution)/shard_map/reduce_scatter | solution.py:1034
  344.3 2.8 copy-start.44
  446.9 7.4 %copy-start.27 = (bf16[1024,512]{1,0:T(8,128)(2,1)S(1)}, bf16[1024,512]{1,0:T(8,128)(2,1)}, u32[]{:S(2)}) copy-start(bf16[1024,512]{1,0:T(8,128)(2,1)} %copy-done.26) | copy-start | bytes 3145732
  448.3 2.9 collective-permute-start.8
  451.2 5.5 copy-start.11
  454.2 180.0 %reduce-scatter.13.cloned.1.call-start = ((), (), s32[]{:S(2)}) async-start(), calls=%async_computation.12 | async-start | bytes 2293760 | tf_op jit(solution)/shard_map/reduce_scatter | solution.py:1034
  454.3 2.0 collective-permute-start.5
  456.7 2.0 copy-start.3
  459.8 1.6 copy-start.19
  462.7 1.4 copy-start.23
  465.2 30.3 %copy-start.36 = (bf16[1024,2048]{1,0:T(8,128)(2,1)S(1)}, bf16[1024,2048]{1,0:T(8,128)(2,1)}, u32[]{:S(2)}) copy-start(bf16[1024,2048]{1,0:T(8,128)(2,1)} %get-tuple-element.101) | copy-start | bytes 12582916
  465.2 30.3 %copy-start.37 = (bf16[1024,2048]{1,0:T(8,128)(2,1)S(1)}, bf16[1024,2048]{1,0:T(8,128)(2,1)}, u32[]{:S(2)}) copy-start(bf16[1024,2048]{1,0:T(8,128)(2,1)} %get-tuple-element.102) | copy-start | bytes 12582916
  491.6 2.0 copy-start.8
  493.6 1.9 copy-start.12
  501.3 16.7 %copy-start.50 = (bf16[2,2048]{1,0:T(2,128)(2,1)S(1)}, bf16[2,2048]{1,0:T(2,128)(2,1)}, u32[]{:S(2)}) copy-start(bf16[2,2048]{1,0:T(2,128)(2,1)} %copy-done.49) | copy-start | bytes 24580
  501.3 133.0 %reduce-scatter.15.cloned.1.call-start = ((), (), s32[]{:S(2)}) async-start(), calls=%async_computation.13 | async-start | bytes 2293760 | tf_op jit(solution)/shard_map/reduce_scatter | solution.py:1034
  509.2 8.8 %copy-start.40 = (bf16[256,2048]{1,0:T(8,128)(2,1)S(1)}, bf16[256,2048]{1,0:T(8,128)(2,1)}, u32[]{:S(2)}) copy-start(bf16[256,2048]{1,0:T(8,128)(2,1)} %copy-done.39) | copy-start | bytes 3145732
  509.2 3.9 collective-permute-start.9
  513.1 1.3 copy-start.34
  514.5 7.1 %copy-start.14 = (bf16[1408,256]{1,0:T(8,128)(2,1)S(1)}, bf16[1408,256]{1,0:T(8,128)(2,1)}, u32[]{:S(2)}) copy-start(bf16[1408,256]{1,0:T(8,128)(2,1)} %reduce-scatter.7.cloned.1.call-done.refs_6_) | copy-start | bytes 2162692
  515.9 14.0 %collective-permute-start.6 = (bf16[128,2048]{1,0:T(8,128)(2,1)S(1)}, bf16[128,2048]{1,0:T(8,128)(2,1)S(1)}, u32[]{:S(2)}, u32[]{:S(2)}) collective-permute-start(bf16[128,2048]{1,0:T(8,128)(2,1)S(1)} %get-tuple-element.106), channel_id=1, source_target_pairs={{0,8},{4,12},{8,0},{12,4},{1,9},{5,13},{9,1},{13,5},{2,10},{6,14},... | collective-permute-start | bytes 1572872 | tf_op jit(solution)/shard_map/ppermute | solution.py:1001
  517.0 5.8 copy-start.15
  517.0 5.8 copy-start.17
  517.0 13.7 %collective-permute-start.7 = (bf16[128,2048]{1,0:T(8,128)(2,1)S(1)}, bf16[128,2048]{1,0:T(8,128)(2,1)S(1)}, u32[]{:S(2)}, u32[]{:S(2)}) collective-permute-start(bf16[128,2048]{1,0:T(8,128)(2,1)S(1)} %get-tuple-element.107), channel_id=1, source_target_pairs={{0,4},{4,0},{8,12},{12,8},{1,5},{5,1},{9,13},{13,9},{2,6},{6,2},{1... | collective-permute-start | bytes 1572872 | tf_op jit(solution)/shard_map/ppermute | solution.py:1001
  521.6 9.2 %copy-start.9 = (bf16[1024,2048]{1,0:T(8,128)(2,1)S(1)}, bf16[1024,2048]{1,0:T(8,128)(2,1)}, u32[]{:S(2)}) copy-start(bf16[1024,2048]{1,0:T(8,128)(2,1)} %copy-done.8) | copy-start | bytes 12582916
  530.8 2.8 copy-start.5
  530.8 2.8 copy-start.6
  530.8 2.8 copy-start.29
  635.2 4.0 copy-start.1
  (9 other events, 9.6 us)
Sparse Core Ops, SparseCore 0:
  10.8 85.5 all-gather.3
  98.0 106.2 all-gather.7
  205.9 59.1 all-gather.5
  267.2 54.3 reduce-scatter.6
  343.8 53.3 reduce-scatter.10
  399.4 56.0 reduce-scatter.8
  457.7 26.9 reduce-scatter.16
  501.4 37.6 reduce-scatter.12
  541.5 38.5 reduce-scatter.14

commit v7 on v6

--- a/solution.py
+++ b/solution.py
@@ -621,7 +621,7 @@
         def _(i):
             body(pl.multiple_of(i * STRIP, STRIP))
 
-    part = part_ref
+    part, relayed, copies = part_ref, [], send_sem.shape[0]
     if meanwhile:
         fetch = pltpu.make_async_copy(inputs[3].at[3], scratch[-3], scratch[-2])
         fetch.start()
@@ -629,6 +629,23 @@
         part, outgoing, incoming = scratch[5:8]
         weight = inputs[3]
         order = [across_both, across_x, across_y, place]
+        passed_ref, far_ref = inputs[n_in - small_sum["dummies"] - 1], outs[-2]
+        relayed = [
+            copy(
+                copies - 2,
+                passed_ref.at[block(across_x, 0)],
+                far_ref.at[pl.ds(0, rows)],
+                "y",
+            ),
+            copy(
+                copies - 1,
+                passed_ref.at[block(across_y, 1)],
+                far_ref.at[pl.ds(rows, rows)],
+                "x",
+            ),
+        ]
+        for step in relayed:
+            step.start()
 
         def product(whose, of, target):
             start = pl.multiple_of(whose * count + 2 * of * rows, rows)
@@ -754,7 +771,7 @@
     small = []
     if small_sum:
         values, arrived = outs[-1], scratch[-1]
-        first = n_in - small_sum["dummies"] - 3
+        first = n_in - small_sum["dummies"] - 4
         ffn_gain, out_gain, conv = inputs[first : first + 3]
         taps, width = conv.shape
         middle_lane = values.shape[1] // 2
@@ -796,7 +813,9 @@
     for step in out_third:
         step.wait_recv()
     use(across_both, last=True)
-    for step in (*far, *near, *last, *out_first, *out_second, *out_third, *small):
+    for step in relayed:
+        step.wait_recv()
+    for step in (*relayed, *far, *near, *last, *out_first, *out_second, *out_third, *small):
         step.wait_send()
     if both_cores:
         for step in shared:
@@ -827,7 +846,16 @@
 
 
 def mp_phase(
-    number, middle, part, inputs, dummies, outs, both_cores=False, small=None, meanwhile=False
+    number,
+    middle,
+    part,
+    inputs,
+    dummies,
+    outs,
+    both_cores=False,
+    small=None,
+    passed=None,
+    meanwhile=False,
 ):
     here, there = pl.BlockSpec(memory_space=pltpu.VMEM), pl.BlockSpec(memory_space=pl.ANY)
     count, model = part.shape
@@ -839,14 +867,20 @@
         scratch += [pltpu.VMEM((count, model), BF16)] * 3
     if small is not None:
         stages = lax.axis_size("row").bit_length() - 1 + 3
-        copies = 16 + stages
+        copies = 16 + stages + 2
         height = 8 + small[2].shape[0]
         shape = (height + -height % 8, model)
         scratch += [pltpu.VMEM((stages, 2, *shape), F32)]
         small_sum = {"dummies": len(dummies)}
-        inputs = [*inputs, *small]
-        outs = [*outs, jax.ShapeDtypeStruct(shape, F32)]
+        inputs = [*inputs, *small, passed]
+        outs = [
+            *outs,
+            jax.ShapeDtypeStruct((2 * block[0], model), BF16),
+            jax.ShapeDtypeStruct(shape, F32),
+        ]
     specs = [here] * len(inputs)
+    if small is not None:
+        specs[-1] = there
     if meanwhile:
         _, width, depth = inputs[3].shape
         specs[3] = there
@@ -884,8 +918,8 @@
     )(part, *inputs, *dummies)
 
 
-def pair_kernel(part_ref, hidden, left_own, left_other, gate, up, *refs):
-    block_ref, gate_pair, up_pair, got, sums, gate_in, up_in, send_sem, recv_sem = refs[-9:]
+def pair_kernel(product_ref, weight, hidden, left_own, left_other, gate, up, *refs):
+    block_ref, gate_pair, up_pair, part_ref, got, sums, gate_in, up_in, send_sem, recv_sem = refs[-10:]
     rows = part_ref.shape[0] // 8
     place, core = lax.axis_index("mp"), lax.axis_index("seq")
     across_x = place + 1 - 2 * (place % 2)
@@ -925,8 +959,27 @@
     ]
     last = [copy(4, sums.at[0], got.at[4], "y"), copy(5, sums.at[1], got.at[5], "x")]
     shared = [copy(6, gate, gate_in, "core"), copy(7, up, up_in, "core")]
-    for step in (*shared, *far, *near):
+
+    def produce(of):
+        lines = pl.ds(pl.multiple_of(2 * of * rows, rows), 2 * rows)
+
+        @pl.loop(0, weight.shape[1] // TILE)
+        def _(i):
+            tile = pl.ds(pl.multiple_of(i * TILE, TILE), TILE)
+            part_ref[lines, tile] = jnp.dot(
+                product_ref[lines, :], weight[:, tile], preferred_element_type=F32
+            ).astype(BF16)
+
+    for step in shared:
         step.start()
+    produce(across_both)
+    for step in far:
+        step.start()
+    produce(across_x)
+    near[0].start()
+    produce(across_y)
+    near[1].start()
+    produce(place)
 
     def products(own, other, target, first, count):
         @pl.loop(first, first + count)
@@ -968,17 +1021,18 @@
         step.wait_send()
 
 
-def scattered_and_pairs(number, part, hidden, left, gate, up, dummies):
+def scattered_and_pairs(number, product, weight, hidden, left, gate, up, dummies):
     here, there = pl.BlockSpec(memory_space=pltpu.VMEM), pl.BlockSpec(memory_space=pl.ANY)
-    count, model = part.shape
+    count, model = product.shape[0], weight.shape[1]
     block = (count // 8, model)
     pair = jax.ShapeDtypeStruct((left[0].shape[1], gate.shape[1]), BF16)
     return pl.pallas_call(
         pair_kernel,
-        in_specs=[here] * 6 + [there] * len(dummies),
+        in_specs=[here] * 7 + [there] * len(dummies),
         out_specs=[here] * 3,
         out_shape=[jax.ShapeDtypeStruct((2 * block[0], model), BF16), pair, pair],
         scratch_shapes=[
+            pltpu.VMEM((count, model), BF16),
             pltpu.VMEM((6, *block), BF16),
             pltpu.VMEM((2, *block), BF16),
             pltpu.VMEM(gate.shape, BF16),
@@ -987,18 +1041,14 @@
             pltpu.SemaphoreType.DMA((8,)),
         ],
         compiler_params=pltpu.CompilerParams(
-            collective_id=number, has_side_effects=True, vmem_limit_bytes=50 << 20
+            collective_id=number, has_side_effects=True, vmem_limit_bytes=54 << 20
         ),
         cost_estimate=pl.CostEstimate(flops=0, bytes_accessed=130 << 20, transcendentals=0),
-    )(part, hidden, *left, gate, up, *dummies)
+    )(product, weight, hidden, *left, gate, up, *dummies)
 
 
 def swapped(block):
     return lax.ppermute(block, "seq", [(0, 1), (1, 0)])
-
-
-def across(block, bit):
-    return lax.ppermute(block, "mp", [(i, i ^ bit) for i in range(4)])
 
 
 def in_order(mine, other, core, axis):
@@ -1018,11 +1068,12 @@
     return pick(core), pick(1 - core)
 
 
-def both_tokens(left, right):
+def both_tokens(left, right, *done):
     product = lambda a, b: lax.dot_general(
         a, b, (((0,), (0,)), ((), ())), preferred_element_type=F32
     )
-    return (product(left[0], right[0]) + product(left[1], right[1])).astype(BF16)
+    total = product(left[0], right[0]) + product(left[1], right[1])
+    return (after(total, *done) if done else total).astype(BF16)
 
 
 def own_columns(block, core):
@@ -1108,12 +1159,12 @@
     gate_up = jnp.einsum("td,sdf->stf", normed_mid, gateup_full, preferred_element_type=F32)
     gate_sig = jax.nn.sigmoid(gate_up[0])
     product = (gate_up[0] * gate_sig * gate_up[1]).astype(BF16)
-    down_pair = both_tokens((product, swapped(product)), own_columns(grad_top, core))
-    ffn_part = jnp.dot(
-        after(product, down_pair), down_full, preferred_element_type=F32
-    ).astype(BF16)
+    normed_halves = own_columns(normed_mid, core)
+    down_pair = both_tokens(
+        (product, swapped(product)), own_columns(grad_top, core), normed_halves[1]
+    )
     grad_product = jnp.dot(grad_top, down_full.T, preferred_element_type=F32)
-    grad_product = after(grad_product, ffn_part)
+    grad_product = after(grad_product, down_pair)
     grad_gate = grad_product * gate_up[1] * gate_sig * (1.0 + gate_up[0] * (1.0 - gate_sig))
     grad_up = grad_product * gate_up[0] * gate_sig
     grad_gate, grad_up = grad_gate.astype(BF16), grad_up.astype(BF16)
@@ -1124,7 +1175,14 @@
         preferred_element_type=F32,
     ).astype(BF16)
     block_out, gate_pair, up_pair = scattered_and_pairs(
-        4, ffn_part, hidden, own_columns(normed_mid, core), grad_gate, grad_up, []
+        4,
+        product,
+        down_full,
+        hidden,
+        normed_halves,
+        grad_gate,
+        grad_up,
+        [down_pair],
     )
     down_sum, gate_sum, up_sum = over_row(down_pair, 1), over_row(gate_pair, 0), over_row(up_pair, 0)
     grad_branch, grad_hidden, ffn_gain_part, grad_normed_out, grad_out_part = mp_phase(
@@ -1157,31 +1215,28 @@
         block_out,
         [gate_sum],
     )
-    piece = lambda of, half: lax.dynamic_slice_in_dim(
-        block_out, (2 * of + half) * (quarter // 2), quarter // 2, axis=0
-    )
-    far_rows = [across(piece(own ^ 1, 0), 2), across(piece(own ^ 2, 1), 1)]
     normed_mine, normed_other = halves(normed, core, 1)
     by_columns = lambda part: lax.dot_general(
         part, grad_raw, (((0,), (0,)), ((), ())), preferred_element_type=F32
     ).astype(BF16)
     qkv_other = swapped(by_columns(normed_other))
     qkv_mine = by_columns(normed_mine)
-    grad_input, small = mp_phase(
+    grad_input, far_rows, small = mp_phase(
         2,
         partial(normed_backward, False),
         grad_raw,
         [residual_own, grad_hidden, attn_gain[None, :], mix_across],
-        [up_sum, out_pair, qkv_mine, qkv_other, *far_rows],
+        [up_sum, out_pair, qkv_mine, qkv_other],
         [],
         both_cores=True,
         small=[ffn_gain_part, out_gain_part, grad_conv_own],
+        passed=block_out,
     )
     grad_input = grad_input.astype(F32)
     places = jnp.arange(4)[:, None, None]
     block_out = jnp.where(
         places == (own ^ 3),
-        jnp.concatenate(far_rows)[None],
+        far_rows[None],
         block_out.reshape(4, quarter, model),
     ).reshape(tok_count, model)
     grad_attn_gain, grad_ffn_gain = small[0], small[1]

time: 650 us -> 642 us (0.988)
  Pallas kernels: 341 us -> 354 us
  matrix products: 104 us -> 95.3 us
    dot_general x1 -> x0, matrix products: 10.2 us -> none  [joined_shards(): jnp.dot(after(product, down_pair), down_full, preferred_element_type=F32)]
    pallas_call x3, Pallas kernels: 249 us -> 258 us  [mp_phase(): pl.pallas_call(kernel, in_specs=[here, *specs] + [there] * len(dummies),...]
    unnamed x108 -> x100, local copies, waits for them, and re-layouts: 32.6 us -> 32 us
  transfers between devices with their start and end apart: 19 -> 17, of which waited for: 7 -> 5; matrix products, arithmetic and copies ran while one was open for 25% -> 23% of each run, Pallas kernels for 53% -> 55%
where the time goes in v7:
time: 642 us; the launch traced here: 638 us
  Pallas kernels  354 us (55%)
  matrix products  95.3 us (15%)
  local copies, waits for them, and re-layouts  50.6 us (8%)
  other arithmetic  43 us (7%)
  waiting for transfers between devices  42.4 us (7%)
  blocking collectives  34 us (5%)
  between operations  16.7 us (3%)
    pallas_call x3, Pallas kernels, mp_phase(): pl.pallas_call(kernel, in_specs=[here, *specs] + [there] * len(dummies),...  258 us
    pallas_call x1, Pallas kernels, scattered_and_pairs(): pl.pallas_call(pair_kernel, in_specs=[here] * 7 + [there] * len(dummies),...  49.2 us
    all_gather x3, waiting for transfers between devices, joined_shards(): lax.all_gather(weight, ('seq', 'row'), axis=1, tiled=True)  34 us
    all_gather x1, blocking collectives, joined_shards(): lax.all_gather(weight, ('seq', 'row'), axis=1, tiled=True)  34 us
    unnamed x100, local copies, waits for them, and re-layouts  32 us
    pallas_call x1, Pallas kernels, backward(): pl.pallas_call(functools.partial(bwd_kernel, heads, group), grid=(steps,)...  26.4 us
    pallas_call x1, Pallas kernels, forward(): pl.pallas_call(functools.partial(fwd_kernel, heads, group), grid=(n // ro...  19.9 us
    dot_general x1, matrix products, joined_shards(): jnp.einsum('stf,sdf->td', jnp.stack([grad_gate, grad_up]), gateup_full, p...  17.4 us
  transfers between devices with their start and end apart: 17, of which 5 were waited for; matrix products, arithmetic and copies ran while one was open for 23% of the time, Pallas kernels for 55%

profile of v7, /device:TPU:0, one launch (start us, length us, event | category | flops | bytes accessed | tf_op | source)
XLA Modules:
  0.0 638.1 jit_solution(11984498758396691229)
XLA Ops:
  7.2 1.4 copy.40
  8.7 2.0 pad_maximum_fusion.4
  11.5 3.2 fusion
  15.0 3.0 fusion.2
  19.7 0.7 pad_add_fusion
  20.8 34.0 %all_gather.13 = bf16[4,2048]{1,0:T(4,128)(2,1)S(1)} all-gather(bf16[4,256]{1,0:T(4,128)(2,1)S(1)} %copy-done.47), channel_id=1, replica_groups=mesh['seq'=2,'mp'=4,'row'=4] {'seq','row'}, dimensions={1}, use_global_device_ids=true | all-gather | bytes 18432 | tf_op jit(solution)/shard_map/all_gather | solution.py:1108
  54.8 7.6 %broadcast_select_fusion.1 = (bf16[1024,2048]{1,0:T(8,128)(2,1)}, bf16[1024,2048]{1,0:T(8,128)(2,1)}) fusion(bf16[1024,2048]{1,0:T(8,128)(2,1)} %collective-permute-done, pred[]{:T(512)S(6)} %eq.25, f32[2048]{0:T(1024)S(1)} %copy-done.27, f32[1024]{0:T(1024)S(1)} %add_rsqrt_fusion, bf16[1,1024,2048]{2,1,0:T(8,128)(2,1)} %param.12), kind=kLoop, calls=%fused_computation.47 | loop fusion | flops 12582912 | bytes 16789504 | tf_op jit(solution)/shard_map/jit(_where)/select_n | solution.py:1055
  62.4 34.0 %all-gather.4.cloned.1.call-done = bf16[4,2048,512]{1,2,0:T(8,128)(2,1)} async-done(((bf16[4,256,512]{1,2,0:T(8,128)(2,1)}), bf16[4,2048,512]{1,2,0:T(8,128)(2,1)}) %all-gather.4.cloned.1.call-update) | async-done | bytes 8388624 | tf_op jit(solution)/shard_map/all_gather | solution.py:1108
  96.4 2.8 slice-done
  99.5 3.0 copy-done.34
  102.5 11.7 %fusion.31.raw_ref.prev_ref = bf16[2048,896]{1,0:T(8,128)(2,1)S(1)} fusion(bf16[1024,2048]{1,0:T(8,128)(2,1)} %get-tuple-element.104, bf16[1024,2048]{1,0:T(8,128)(2,1)S(1)} %copy-done.34, bf16[2,2048]{1,0:T(2,128)(2,1)S(1)} %constant_dynamic-slice_fusion.8, bf16[256,2048]{1,0:T(8,128)(2,1)S(1)} %get-tuple-element.107, ...), kind=kOutput, calls=%fused_computation.50 | convolution fusion | flops 7553155072 | bytes 15212544 | tf_op jit(solution)/shard_map/dot_general | solution.py:1132
  114.3 19.9 %shard_map.203 = (bf16[2048,256]{1,0:T(8,128)(2,1)S(1)}, f32[2048,256]{1,0:T(8,128)S(1)}, bf16[16,2,128,128]{3,2,1,0:T(8,128)(2,1)S(1)}, bf16[16,2,128,128]{3,2,...) custom-call(f32[33]{0:T(128)S(1)} %pad_convert_fusion.keep_ref, ...), custom_call_target="tpu_custom_call" | custom-call | bytes 125829120 | tf_op jit(solution)/shard_map/pallas_call | solution.py:117
  134.2 1.8 copy-done.2
  136.0 1.3 copy-done.15
  137.3 1.0 copy-done.17
  138.3 1.0 copy-done.19
  139.3 1.0 copy-done.21
  140.3 1.0 copy-done.23
  141.6 1.3 constant_dynamic-slice_fusion.5
  143.5 6.4 convolution_convert_fusion.part_ref
  149.9 78.9 %shard_map.204 = (bf16[1024,2048]{1,0:T(8,128)(2,1)}, f32[2,128,2048]{2,1,0:T(8,128)S(1)}) custom-call(bf16[1024,2048]{1,0:T(8,128)(2,1)} %convolution_convert_fusion.part_ref, bf16[2,128,2048]{2,1,0:T(8,128)(2,1)S(1)} %bitcast.160, f32[1,2048]{1,0:T(1,128)S(1)} %bitcast.168), custom_call_target="tpu_custom_call" | custom-call | bytes 262144000 | tf_op jit(solution)/shard_map/pallas_call | solution.py:901
  228.9 5.4 constant_dynamic-slice_fusion.2
  234.4 17.2 %convolution_bitcast_fusion = f32[2,1024,1408]{2,1,0:T(8,128)S(1)} fusion(bf16[2,2048,1408]{2,1,0:T(8,128)(2,1)} %all-gather.8.cloned.1.call-done, bf16[1024,2048]{1,0:T(8,128)(2,1)} %get-tuple-element.34), kind=kOutput, calls=%fused_computation.14 | convolution fusion | flops 11811160064 | bytes 27262976 | tf_op jit(solution)/shard_map/td,sdf->stf/dot_general | solution.py:1159
  251.6 1.9 fusion.9.product_ref
  254.1 2.9 copy-done.43
  259.0 6.0 fusion.32
  265.1 6.4 add_convert_fusion.refs_0_
  271.5 1.2 slice.101
  273.4 16.5 %fusion.12 = (bf16[1024,1408]{1,0:T(8,128)(2,1)}, bf16[1024,1408]{1,0:T(8,128)(2,1)}) fusion(f32[2,1024,1408]{2,1,0:T(8,128)} %copy-done.32, f32[]{:T(128)} %bitcast.33, bf16[1408,2048]{1,0:T(8,128)(2,1)} %all-gather.6.cloned.1.call-done.weight, bf16[1,1024,2048]{2,1,0:T(8,128)(2,1)} %param.23), kind=kOutput, calls=%fused_computation.24 | convolution fusion | flops 5925765120 | bytes 27262980 | tf_op jit(solution)/shard_map/dot_general | solution.py:1166
  289.9 49.2 %shard_map.205 = (bf16[256,2048]{1,0:T(8,128)(2,1)}, bf16[1024,1408]{1,0:T(8,128)(2,1)}, bf16[1024,1408]{1,0:T(8,128)(2,1)}) custom-call(bf16[1024,1408]{1,0:T(8,128)(2,1)} %copy-done.33, bf16[1408,2048]{1,0:T(8,128)(2,1)} %all-gather.6.cloned.1.call-done.weight, f32[2,128,2048]{2,1,0:T(8,128)} %copy-done.7, bf16[1024,1024]{1,0:T(8,128)(2,1)} %get-tuple-element.108.left_own, ...), custom_call_target="tpu_custom_call" | custom-call | bytes 136314880 | tf_op jit(solution)/shard_map/pallas_call | solution.py:1029
  339.7 1.5 constant_dynamic-slice_fusion.3
  341.2 1.3 pad_maximum_fusion.5.refs_4_
  342.6 17.4 %bitcast_convert_fusion.part_ref = bf16[1024,2048]{1,0:T(8,128)(2,1)} fusion(bf16[2,2048,1408]{2,1,0:T(8,128)(2,1)} %all-gather.8.cloned.1.call-done, bf16[1,1024,1408]{2,1,0:T(8,128)(2,1)} %bitcast.175, bf16[1,1024,1408]{2,1,0:T(8,128)(2,1)S(1)} %bitcast.174), kind=kOutput, calls=%fused_computation.11 | convolution fusion | flops 11816140800 | bytes 21495808 | tf_op jit(solution)/shard_map/stf,sdf->td/dot_general | solution.py:1171
  360.0 1.1 copy-done.10
  361.1 80.4 %shard_map.206 = (bf16[1024,2048]{1,0:T(8,128)(2,1)}, f32[2,128,2048]{2,1,0:T(8,128)}, f32[1,2048]{1,0:T(1,128)S(1)}, bf16[1024,512]{1,0:T(8,128)(2,1)S(1)}, bf16[512,2048]{1,0:T(8,128)(2,1)}) custom-call(bf16[1024,2048]{1,0:T(8,128)(2,1)} %bitcast_convert_fusion.part_ref, f32[2,128,2048]{2,1,0:T(8,128)} %copy-done.7, bf16[2,128,2048]{2,1,0:T(8,128)(2,1)S(1)} %bitcast.162, ...), custom_call_target="tpu_custom_call" | custom-call | bytes 262144000 | tf_op jit(solution)/shard_map/pallas_call | solution.py:901
  441.5 1.0 copy-done.25
  442.5 1.4 constant_dynamic-slice_fusion
  444.0 1.2 slice.102
  445.8 0.9 collective-permute-done.6
  446.7 3.0 add_convert_fusion.1.refs_9_
  450.1 1.8 collective-permute-done.5
  452.3 2.0 copy-done.3
  454.3 1.1 copy-done.12
  455.4 1.6 copy-done.16
  457.0 1.2 copy-done.18
  458.2 1.3 copy-done.20
  459.6 1.2 copy-done.22
  460.8 1.2 copy-done.24
  462.0 26.4 %shard_map.207 = (bf16[2048,896]{1,0:T(8,128)(2,1)S(1)}, f32[4,768]{1,0:T(4,128)S(1)}, f32[1,128]{1,0:T(1,128)S(1)}, bf16[1024,2048]{1,0:T(8,128)(2,1)S(1)}) custom-call(f32[33]{0:T(128)S(1)} %pad_convert_fusion.keep_ref, s32[32]{0:T(128)S(1)} %convert_element_type.94.count_ref, bf16[2048,896]{1,0:T(8,128)(2,1)S(1)} %copy-done.3, ...), custom_call_target="tpu_custom_call" | custom-call | bytes 125829120 | tf_op jit(solution)/shard_map/pallas_call | solution.py:254
  488.5 2.0 copy-done.4
  490.5 1.9 copy-done.9
  492.3 5.7 fusion.39.refs_10_
  498.1 8.0 %fusion.36 = bf16[1024,896]{1,0:T(8,128)(2,1)S(1)} fusion(bf16[2048,896]{1,0:T(8,128)(2,1)} %copy-done.9, s32[]{:T(128)S(6)} %select_n.144, bf16[1024,2048]{1,0:T(8,128)(2,1)} %get-tuple-element.103, bf16[1024,2048]{1,0:T(8,128)(2,1)} %get-tuple-element.104), kind=kOutput, calls=%fused_computation.58 | convolution fusion | flops 3767402496 | bytes 13893636 | tf_op jit(solution)/shard_map/dot_general | solution.py:1219
  506.2 3.9 collective-permute-done.7.refs_11_
  510.2 3.6 fusion.30.refs_3_
  513.8 1.2 convert_element_type.119
  515.1 1.8 maximum_convert_fusion
  516.8 98.9 %shard_map.208 = (bf16[1024,2048]{1,0:T(8,128)(2,1)}, bf16[256,2048]{1,0:T(8,128)(2,1)S(1)}, f32[16,2048]{1,0:T(8,128)S(1)}) custom-call(bf16[2048,896]{1,0:T(8,128)(2,1)} %copy-done.9, bf16[2,128,2048]{2,1,0:T(8,128)(2,1)S(1)} %bitcast.161, f32[2,128,2048]{2,1,0:T(8,128)} %get-tuple-element.46.refs_1_, f32[1,2048]{1,0:T(1,128)S(1)} %bitcast.167, ...), custom_call_target="tpu_custom_call" | custom-call | bytes 262144000 | tf_op jit(solution)/shard_map/pallas_call | solution.py:901
  615.8 2.6 bitcast_select_fusion
  620.1 4.5 bitcast_convert_fusion.1
  624.6 1.8 convert_element_type.117
  626.4 0.9 select_bitcast_fusion.1
  627.5 1.2 broadcast_select_fusion.7
  629.2 1.6 copy.45
  (159 shorter events, 10.9 us)
Async XLA Ops:
  7.2 47.6 %copy-start = (f32[3,4,512]{2,1,0:T(4,128)S(1)}, f32[3,4,512]{2,1,0:T(4,128)}, u32[]{:S(2)}) copy-start(f32[3,4,512]{2,1,0:T(4,128)} %param.16) | copy-start | bytes 73732
  7.2 89.2 %all-gather.4.cloned.1.call-start = ((), (), s32[]{:S(2)}) async-start(), calls=%async_computation.6 | async-start | bytes 9437184 | tf_op jit(solution)/shard_map/all_gather | solution.py:1108
  8.6 6.1 copy-start.27
  10.7 223.6 %all-gather.8.cloned.1.call-start = ((), (), s32[]{:S(2)}) async-start(), calls=%async_computation.8 | async-start | bytes 12976128 | tf_op jit(solution)/shard_map/all_gather | solution.py:1108
  11.5 261.9 %all-gather.6.cloned.1.call-start = ((), (), s32[]{:S(2)}) async-start(), calls=%async_computation.7 | async-start | bytes 6488064 | tf_op jit(solution)/shard_map/all_gather | solution.py:1108
  11.5 3.5 copy-start.31
  15.0 3.6 copy-start.48
  15.0 5.8 copy-start.47
  18.0 36.8 %collective-permute-start = (bf16[1024,2048]{1,0:T(8,128)(2,1)}, bf16[1024,2048]{1,0:T(8,128)(2,1)}, u32[]{:S(2)}, u32[]{:S(2)}) collective-permute-start(bf16[1024,2048]{1,0:T(8,128)(2,1)} %fusion.2), channel_id=1, source_target_pairs={{0,16},{16,0},{1,17},{17,1},{2,18},{18,2},{3,19},{19,3},{4,20},{20... | collective-permute-start | bytes 12582920 | tf_op jit(solution)/shard_map/ppermute | solution.py:1051
  18.5 341.5 %reduce-scatter.7.cloned.1.call-start = ((), (), s32[]{:S(2)}) async-start(), calls=%async_computation.9 | async-start | bytes 3604480 | tf_op jit(solution)/shard_map/reduce_scatter | solution.py:1085
  96.4 2.8 slice-start
  99.2 3.3 copy-start.34
  99.5 14.8 %copy-start.38 = (bf16[256,2048]{1,0:T(8,128)(2,1)}, bf16[256,2048]{1,0:T(8,128)(2,1)S(1)}, u32[]{:S(2)}) copy-start(bf16[256,2048]{1,0:T(8,128)(2,1)S(1)} %get-tuple-element.105) | copy-start | bytes 3145732
  99.5 14.8 %copy-start.40 = (bf16[256,2048]{1,0:T(8,128)(2,1)}, bf16[256,2048]{1,0:T(8,128)(2,1)S(1)}, u32[]{:S(2)}) copy-start(bf16[256,2048]{1,0:T(8,128)(2,1)S(1)} %get-tuple-element.106) | copy-start | bytes 3145732
  99.5 14.8 %copy-start.41 = (bf16[256,2048]{1,0:T(8,128)(2,1)}, bf16[256,2048]{1,0:T(8,128)(2,1)S(1)}, u32[]{:S(2)}) copy-start(bf16[256,2048]{1,0:T(8,128)(2,1)S(1)} %get-tuple-element.107) | copy-start | bytes 3145732
  102.5 11.8 %copy-start.30 = (f32[128]{0:T(128)S(1)}, f32[128]{0:T(128)}, u32[]{:S(2)}) copy-start(f32[128]{0:T(128)} %param.18) | copy-start | bytes 1540
  134.2 1.8 copy-start.2
  136.0 1.3 copy-start.15
  138.3 1.0 copy-start.19
  139.3 1.0 copy-start.21
  141.3 2.0 collective-permute-start.1
  143.5 6.4 %copy-start.45 = (bf16[1024,256]{1,0:T(8,128)(2,1)}, bf16[1024,256]{1,0:T(8,128)(2,1)S(1)}, u32[]{:S(2)}) copy-start(bf16[1024,256]{1,0:T(8,128)(2,1)S(1)} %get-tuple-element.112) | copy-start | bytes 1572868
  143.5 6.4 %copy-start.46 = (bf16[1024,256]{1,0:T(8,128)(2,1)}, bf16[1024,256]{1,0:T(8,128)(2,1)S(1)}, u32[]{:S(2)}) copy-start(bf16[1024,256]{1,0:T(8,128)(2,1)S(1)} %get-tuple-element.113) | copy-start | bytes 1572868
  143.5 6.4 %copy-start.29 = (f32[2048]{0:T(1024)S(1)}, f32[2048]{0:T(1024)}, u32[]{:S(2)}) copy-start(f32[2048]{0:T(1024)} %param.20) | copy-start | bytes 24580
  228.9 5.4 copy-start.7
  234.3 23.4 %collective-permute-start.4 = (bf16[1024,1024]{1,0:T(8,128)(2,1)}, bf16[1024,1024]{1,0:T(8,128)(2,1)S(1)}, u32[]{:S(2)}, u32[]{:S(2)}) collective-permute-start(bf16[1024,1024]{1,0:T(8,128)(2,1)} %get-tuple-element.109), channel_id=1, source_target_pairs={{0,16},{16,0},{1,17},{17,1},{2,18},{18,2},{3,19},{19,3},{4,20},{20... | collective-permute-start | bytes 6291464 | tf_op jit(solution)/shard_map/ppermute | solution.py:1051
  251.6 7.4 %copy-start.32 = (f32[2,1024,1408]{2,1,0:T(8,128)}, f32[2,1024,1408]{2,1,0:T(8,128)S(1)}, u32[]{:S(2)}) copy-start(f32[2,1024,1408]{2,1,0:T(8,128)S(1)} %convolution_bitcast_fusion) | copy-start | bytes 34603012
  251.6 5.4 copy-start.43
  253.5 11.5 %copy-start.33 = (bf16[1024,1408]{1,0:T(8,128)(2,1)}, bf16[1024,1408]{1,0:T(8,128)(2,1)S(1)}, u32[]{:S(2)}) copy-start(bf16[1024,1408]{1,0:T(8,128)(2,1)S(1)} %fusion.9.product_ref) | copy-start | bytes 8650756
  253.6 11.5 %collective-permute-start.2 = (bf16[1024,1408]{1,0:T(8,128)(2,1)S(1)}, bf16[1024,1408]{1,0:T(8,128)(2,1)S(1)}, u32[]{:S(2)}, u32[]{:S(2)}) collective-permute-start(bf16[1024,1408]{1,0:T(8,128)(2,1)S(1)} %fusion.9.product_ref), channel_id=1, source_target_pairs={{0,16},{16,0},{1,17},{17,1},{2,18},{18,2},{3,19},{19,3},{4,20},{20... | collective-permute-start | bytes 8650760 | tf_op jit(solution)/shard_map/ppermute | solution.py:1051
  257.3 7.8 %collective-permute-start.3 = (bf16[1024,1024]{1,0:T(8,128)(2,1)S(1)}, bf16[1024,1024]{1,0:T(8,128)(2,1)S(1)}, u32[]{:S(2)}, u32[]{:S(2)}) collective-permute-start(bf16[1024,1024]{1,0:T(8,128)(2,1)S(1)} %dynamic-slice_bitcast_fusion), channel_id=1, source_target_pairs={{0,16},{16,0},{1,17},{17,1},{2,18},{18,2},{3,19},{19,3},{4,20},{20... | collective-permute-start | bytes 6291464 | tf_op jit(solution)/shard_map/ppermute | solution.py:1051
  257.8 7.3 %copy-start.44 = (bf16[1024,1024]{1,0:T(8,128)(2,1)}, bf16[1024,1024]{1,0:T(8,128)(2,1)S(1)}, u32[]{:S(2)}) copy-start(bf16[1024,1024]{1,0:T(8,128)(2,1)S(1)} %collective-permute-done.4.left_other) | copy-start | bytes 6291460
  271.5 172.5 %reduce-scatter.11.cloned.1.call-start = ((), (), s32[]{:S(2)}) async-start(), calls=%async_computation.11 | async-start | bytes 3604480 | tf_op jit(solution)/shard_map/reduce_scatter | solution.py:1085
  339.1 113.1 %reduce-scatter.9.cloned.1.call-start = ((), (), s32[]{:S(2)}) async-start(), calls=%async_computation.10 | async-start | bytes 3604480 | tf_op jit(solution)/shard_map/reduce_scatter | solution.py:1085
  339.7 284.9 %reduce-scatter.17.cloned.1.call-start = ((), (), s32[]{:S(2)}) async-start(), calls=%async_computation.14 | async-start | bytes 1310720 | tf_op jit(solution)/shard_map/reduce_scatter | solution.py:1085
  339.7 2.8 copy-start.42
  360.0 1.1 copy-start.10
  442.5 7.4 %copy-start.26 = (bf16[1024,512]{1,0:T(8,128)(2,1)S(1)}, bf16[1024,512]{1,0:T(8,128)(2,1)}, u32[]{:S(2)}) copy-start(bf16[1024,512]{1,0:T(8,128)(2,1)} %copy-done.25) | copy-start | bytes 3145732
  443.9 2.9 collective-permute-start.6
  446.7 5.5 copy-start.8
  449.8 176.6 %reduce-scatter.13.cloned.1.call-start = ((), (), s32[]{:S(2)}) async-start(), calls=%async_computation.12 | async-start | bytes 2293760 | tf_op jit(solution)/shard_map/reduce_scatter | solution.py:1085
  449.9 2.0 collective-permute-start.5
  452.3 2.0 copy-start.3
  454.3 1.1 copy-start.12
  455.4 1.6 copy-start.16
  457.0 1.2 copy-start.18
  458.2 1.4 copy-start.20
  459.6 1.2 copy-start.22
  460.8 1.2 copy-start.24
  462.0 30.3 %copy-start.35 = (bf16[1024,2048]{1,0:T(8,128)(2,1)S(1)}, bf16[1024,2048]{1,0:T(8,128)(2,1)}, u32[]{:S(2)}) copy-start(bf16[1024,2048]{1,0:T(8,128)(2,1)} %get-tuple-element.103) | copy-start | bytes 12582916
  462.0 30.3 %copy-start.36 = (bf16[1024,2048]{1,0:T(8,128)(2,1)S(1)}, bf16[1024,2048]{1,0:T(8,128)(2,1)}, u32[]{:S(2)}) copy-start(bf16[1024,2048]{1,0:T(8,128)(2,1)} %get-tuple-element.104) | copy-start | bytes 12582916
  488.4 2.0 copy-start.4
  490.5 1.9 copy-start.9
  498.1 12.1 %copy-start.39 = (bf16[256,2048]{1,0:T(8,128)(2,1)S(1)}, bf16[256,2048]{1,0:T(8,128)(2,1)}, u32[]{:S(2)}) copy-start(bf16[256,2048]{1,0:T(8,128)(2,1)} %copy-done.38) | copy-start | bytes 3145732
  498.1 128.3 %reduce-scatter.15.cloned.1.call-start = ((), (), s32[]{:S(2)}) async-start(), calls=%async_computation.13 | async-start | bytes 2293760 | tf_op jit(solution)/shard_map/reduce_scatter | solution.py:1085
  506.1 4.0 collective-permute-start.7
  510.1 3.8 copy-start.11
  510.2 4.9 copy-start.13
  510.2 4.9 copy-start.14
  513.8 3.0 copy-start.6
  513.8 3.0 copy-start.28
  516.8 98.9 %copy-start.5 = (bf16[1024,2048]{1,0:T(8,128)(2,1)S(1)}, bf16[1024,2048]{1,0:T(8,128)(2,1)}, u32[]{:S(2)}) copy-start(bf16[1024,2048]{1,0:T(8,128)(2,1)} %copy-done.4) | copy-start | bytes 12582916
  615.8 4.4 copy-start.37
  627.4 4.0 copy-start.1
  (3 other events, 2.9 us)
Sparse Core Ops, SparseCore 0:
  10.8 85.5 all-gather.3
  98.0 106.2 all-gather.7
  205.9 59.1 all-gather.5
  271.6 53.4 reduce-scatter.6
  339.2 53.4 reduce-scatter.10
  394.8 56.0 reduce-scatter.8
  453.2 26.9 reduce-scatter.16
  498.2 37.5 reduce-scatter.12
  538.2 38.5 reduce-scatter.14

commit v8 on v7

--- a/solution.py
+++ b/solution.py
@@ -55,7 +55,7 @@
     real=jnp.where(inside<jnp.where(first,count_ref[block],count_ref[block+1]),1.0,0.0)
     return taps,taps_later,jnp.where(first,1.0,keep1),jnp.where(first,keep1,1.0),real,keep0,keep1
 
-def fwd_kernel(heads, group, keep_ref, count_ref, raw_ref, cw_ref, gain_ref, normed_ref, o_ref, s_ref, t_ref, w_ref, r_ref, ext, state):
+def fwd_kernel(heads, group, keep_ref, count_ref, raw_ref, cw_ref, gain_ref, normed_ref, o_ref, st_ref, wr_ref, ext, state):
     rows=group*CHUNK
     step=pl.program_id(0)
     @pl.when(step==0)
@@ -96,14 +96,14 @@
     for t,(w,u),(g,h,q,k,l,_,_,_,keep0,keep1) in zip(done,wus,units):
         base=g*CHUNK
         out=(pl.ds(base,CHUNK),pl.ds(h*HDIM,HDIM))
-        t_ref[g,h]=t.astype(BF16)
-        w_ref[out]=w.astype(BF16)
+        st_ref[g,h,1]=t.astype(BF16)
+        wr_ref[out]=w.astype(BF16)
         s=state[h]*keep0
-        s_ref[g,h]=s.astype(BF16)
+        st_ref[g,h,0]=s.astype(BF16)
         rr=u-mm(w,s)
         o=mm(q,s)+mm(l,rr)
         state[h]=s*keep1+mm(k,rr,TN)
-        r_ref[out]=rr.astype(BF16)
+        wr_ref[pl.ds(base,CHUNK),pl.ds(width+h*HDIM,HDIM)]=rr.astype(BF16)
         o_ref[out]=o
         stat=lax.rsqrt(jnp.mean(o*o,axis=1,keepdims=True)+EPSILON)
         normed_ref[out]=(o*stat*gain_ref[...]).astype(BF16)
@@ -112,21 +112,20 @@
     n=raw.shape[0]; width=cw.shape[1]//3; heads=width//HDIM; rows=group*CHUNK
     nc=n//CHUNK
     row=lambda w: pl.BlockSpec((rows,w),lambda i:(i,0))
-    mat=pl.BlockSpec((group,heads,HDIM,HDIM),lambda i:(i,0,0,0))
+    mat=pl.BlockSpec((group,heads,2,HDIM,HDIM),lambda i:(i,0,0,0,0))
     full=lambda a: pl.BlockSpec(a.shape,lambda i:(0,0))
     return pl.pallas_call(functools.partial(fwd_kernel,heads,group),
         grid=(n//rows,),
         in_specs=[pl.BlockSpec(memory_space=pltpu.SMEM)]*2+[row(raw.shape[1]),full(cw),full(gain)],
-        out_specs=[row(width),row(width),mat,mat,row(width),row(width)],
+        out_specs=[row(width),row(width),mat,row(2*width)],
         out_shape=[jax.ShapeDtypeStruct((n,width),BF16),jax.ShapeDtypeStruct((n,width),F32),
-            jax.ShapeDtypeStruct((nc,heads,HDIM,HDIM),BF16),jax.ShapeDtypeStruct((nc,heads,HDIM,HDIM),BF16),
-            jax.ShapeDtypeStruct((n,width),BF16),jax.ShapeDtypeStruct((n,width),BF16)],
+            jax.ShapeDtypeStruct((nc,heads,2,HDIM,HDIM),BF16),jax.ShapeDtypeStruct((n,2*width),BF16)],
         scratch_shapes=[pltpu.VMEM((rows+8,3*width),F32),pltpu.VMEM((heads,HDIM,HDIM),F32)],
         compiler_params=pltpu.CompilerParams(vmem_limit_bytes=24<<20),
         cost_estimate=pl.CostEstimate(flops=0,bytes_accessed=120<<20,transcendentals=0),
     )(keep,count,raw,cw,gain)
 
-def bwd_kernel(heads, group, keep_ref, count_ref, raw_ref, prev_ref, cw_ref, gain_ref, gno_ref, o_ref, s_ref, t_ref, w_ref, r_ref, *rest):
+def bwd_kernel(heads, group, keep_ref, count_ref, raw_ref, prev_ref, cw_ref, gain_ref, gno_ref, o_ref, st_ref, wr_ref, *rest):
     block_ref=rest[0]
     graw_ref, gcw_ref, ggain_ref, all_ref, ext, gext, grad_state, local_sem, send_sem, recv_sem = rest[-10:]
     rows=group*CHUNK
@@ -187,7 +186,7 @@
             ggain_ref[...]+=jnp.sum(gno*uo,axis=0,keepdims=True)
             gu=gno*gain_ref[...]
             do=stat*(gu-uo*jnp.mean(gu*uo,axis=1,keepdims=True))
-            units.append(dict(g=g,h=h,base=base,out=out,taps=taps,m=m,m2=m2,keep0=keep0,keep1=keep1,tot=tot,sigs=sigs,
+            units.append(dict(g=g,h=h,base=base,out=out,second=(pl.ds(base,CHUNK),pl.ds(width+h*HDIM,HDIM)),taps=taps,m=m,m2=m2,keep0=keep0,keep1=keep1,tot=tot,sigs=sigs,
                 rq=rq,rk=rk,qu=qu,q=qu*HDIM**-0.5,k=act[1]*rk,v=act[2],b=sig_b[:,h:h+1],do=do,
                 mask=jnp.where(c<BLOCK,m,1.0)))
         for u in units[-heads:]: u.update(taps_later=taps_later,beta=beta,sig_b=sig_b)
@@ -199,19 +198,19 @@
         dsn=grad_state[u['h']]
         u['dsn']=dsn
         u['dr']=u['dr0']+u['m2']*mm(u['k'],dsn)
-        ds=u['keep1']*dsn+u['ds0']-mm(w_ref[u['out']],u['dr'],TN)
+        ds=u['keep1']*dsn+u['ds0']-mm(wr_ref[u['out']],u['dr'],TN)
         grad_state[u['h']]=u['keep0']*ds
-    for u in units: u['df']=mm(t_ref[u['g'],u['h']],u['dr'],TN)
-    for u in units: u['dl']=jnp.where(r>=c,mm(u['do'],r_ref[u['out']],NT)*u['mask'],0.0)
-    for u in units: u['da']=jnp.where(r>c,-mm(u['df'],r_ref[u['out']],NT),0.0)
+    for u in units: u['df']=mm(st_ref[u['g'],u['h'],1],u['dr'],TN)
+    for u in units: u['dl']=jnp.where(r>=c,mm(u['do'],wr_ref[u['second']],NT)*u['mask'],0.0)
+    for u in units: u['da']=jnp.where(r>c,-mm(u['df'],wr_ref[u['second']],NT),0.0)
     for u in units:
         u['de']=u['b']*u['df']
-        u['e']=u['v']-u['m']*mm(u['k'],s_ref[u['g'],u['h']])
+        u['e']=u['v']-u['m']*mm(u['k'],st_ref[u['g'],u['h'],0])
         u['gb']=jnp.sum(u['df']*u['e']+u['da']*u['gram'],axis=1,keepdims=True)
         u['dkk']=u['b']*u['da']*u['mask']
-    for u in units: u['dq']=u['m']*mm(u['do'],s_ref[u['g'],u['h']],NT)+mm(u['dl'],u['k'])
+    for u in units: u['dq']=u['m']*mm(u['do'],st_ref[u['g'],u['h'],0],NT)+mm(u['dl'],u['k'])
     for u in units:
-        u['dk']=(mm(u['dl'],u['q'],TN)+u['m2']*mm(r_ref[u['out']],u['dsn'],NT)-u['m']*mm(u['de'],s_ref[u['g'],u['h']],NT)
+        u['dk']=(mm(u['dl'],u['q'],TN)+u['m2']*mm(wr_ref[u['second']],u['dsn'],NT)-u['m']*mm(u['de'],st_ref[u['g'],u['h'],0],NT)
             +mm(u['dkk'],u['k'])+mm(u['dkk'],u['k'],TN))
     for u in units:
         gq=u['dq']*HDIM**-0.5
@@ -244,16 +243,16 @@
         for send in sends: send.wait_recv()
         for send in sends: send.wait_send()
 
-def backward(keep, count, raw, cw, gain, gno, o, s, t, w, r, group, block, dummies=()):
+def backward(keep, count, raw, cw, gain, gno, o, st, wr, group, block, dummies=()):
     n=raw.shape[0]; width=cw.shape[1]//3; heads=width//HDIM; rows=group*CHUNK
     steps=n//rows
     row=lambda w: pl.BlockSpec((rows,w),lambda i:(steps-1-i,0))
-    mat=pl.BlockSpec((group,heads,HDIM,HDIM),lambda i:(steps-1-i,0,0,0))
+    mat=pl.BlockSpec((group,heads,2,HDIM,HDIM),lambda i:(steps-1-i,0,0,0,0))
     full=lambda a: pl.BlockSpec(a.shape,lambda i:(0,0))
     prev=pl.BlockSpec((16,raw.shape[1]),lambda i:(jnp.maximum((steps-1-i)*(rows//16)-1,0),0))
     return pl.pallas_call(functools.partial(bwd_kernel,heads,group),
         grid=(steps,),
-        in_specs=[pl.BlockSpec(memory_space=pltpu.SMEM)]*2+[row(raw.shape[1]),prev,full(cw),full(gain),row(width),row(width),mat,mat,row(width),row(width)]+[pl.BlockSpec(memory_space=pl.ANY)]*(1+len(dummies)),
+        in_specs=[pl.BlockSpec(memory_space=pltpu.SMEM)]*2+[row(raw.shape[1]),prev,full(cw),full(gain),row(width),row(width),mat,row(2*width)]+[pl.BlockSpec(memory_space=pl.ANY)]*(1+len(dummies)),
         out_specs=[row(raw.shape[1]),pl.BlockSpec((KERNEL,3*width),lambda i:(0,0)),pl.BlockSpec((1,HDIM),lambda i:(0,0)),pl.BlockSpec(memory_space=pl.ANY)],
         out_shape=[jax.ShapeDtypeStruct(raw.shape,BF16),
             jax.ShapeDtypeStruct((KERNEL,3*width),F32),jax.ShapeDtypeStruct((1,HDIM),F32),jax.ShapeDtypeStruct((4*block.shape[0],block.shape[1]),BF16)],
@@ -261,7 +260,7 @@
             pltpu.SemaphoreType.DMA(()),pltpu.SemaphoreType.DMA((4,)),pltpu.SemaphoreType.DMA((4,))],
         compiler_params=pltpu.CompilerParams(collective_id=3,has_side_effects=True,vmem_limit_bytes=24<<20),
         cost_estimate=pl.CostEstimate(flops=0,bytes_accessed=120<<20,transcendentals=0),
-    )(keep,count,raw,raw,cw,gain,gno,o,s,t,w,r,block,*dummies)
+    )(keep,count,raw,raw,cw,gain,gno,o,st,wr,block,*dummies)
 
 
 def passed_along(block, axis, distance):
@@ -626,8 +625,20 @@
         fetch = pltpu.make_async_copy(inputs[3].at[3], scratch[-3], scratch[-2])
         fetch.start()
     if both_cores:
-        part, outgoing, incoming = scratch[5:8]
-        weight = inputs[3]
+        part, outgoing, incoming, weight, weight_sem = scratch[5:10]
+        mixer, beta = inputs[3:5]
+        width = (weight.shape[0] - beta.shape[0]) // 3
+        fetches = [
+            pltpu.make_async_copy(
+                mixer.at[s, pl.ds(pl.multiple_of(core * width, width), width)],
+                weight.at[pl.ds(s * width, width)],
+                weight_sem.at[s],
+            )
+            for s in range(3)
+        ]
+        for step in fetches:
+            step.start()
+        weight[3 * width :, :] = beta[...]
         order = [across_both, across_x, across_y, place]
         passed_ref, far_ref = inputs[n_in - small_sum["dummies"] - 1], outs[-2]
         relayed = [
@@ -665,6 +676,9 @@
         for number in range(4):
             lines = pl.ds(pl.multiple_of(2 * order[number] * rows, rows), 2 * rows)
             shared.append(copy(12 + number, outgoing.at[lines], incoming.at[lines], "core"))
+
+        for step in fetches:
+            step.wait()
 
         def give(number):
             product(1 - core, order[number], outgoing)
@@ -860,11 +874,12 @@
     here, there = pl.BlockSpec(memory_space=pltpu.VMEM), pl.BlockSpec(memory_space=pl.ANY)
     count, model = part.shape
     if both_cores:
-        count, model = count // 2, inputs[3].shape[1]
+        count, depth, model = count // 2, model, inputs[3].shape[2]
     block = (count // 8, model)
     copies, scratch, small_sum = 12, [], None
     if both_cores:
         scratch += [pltpu.VMEM((count, model), BF16)] * 3
+        scratch += [pltpu.VMEM((depth, model), BF16), pltpu.SemaphoreType.DMA((3,))]
     if small is not None:
         stages = lax.axis_size("row").bit_length() - 1 + 3
         copies = 16 + stages + 2
@@ -880,7 +895,7 @@
         ]
     specs = [here] * len(inputs)
     if small is not None:
-        specs[-1] = there
+        specs[3] = specs[-1] = there
     if meanwhile:
         _, width, depth = inputs[3].shape
         specs[3] = there
@@ -1108,6 +1123,7 @@
     gather = lambda weight: lax.all_gather(weight, ("seq", "row"), axis=1, tiled=True)
     mixer_full = gather(jnp.concatenate([qkv_weight, out_weight.T[None]]))
     qkv_full, out_full = mixer_full[:3], mixer_full[3]
+    mixer_rows = mixer_full.transpose(0, 2, 1)
     beta_full, gateup_full, down_full = (
         gather(beta_weight),
         gather(gateup_weight),
@@ -1189,7 +1205,7 @@
         1,
         partial(normed_backward, True),
         grad_mid_part,
-        [hidden, own_rows(cotangent), ffn_gain[None, :], mixer_full.transpose(0, 2, 1), normed_out],
+        [hidden, own_rows(cotangent), ffn_gain[None, :], mixer_rows, normed_out],
         [block_out, down_sum, gate_pair, up_pair],
         [
             rows_own,
@@ -1225,7 +1241,7 @@
         2,
         partial(normed_backward, False),
         grad_raw,
-        [residual_own, grad_hidden, attn_gain[None, :], mix_across],
+        [residual_own, grad_hidden, attn_gain[None, :], mixer_rows, beta_rows],
         [up_sum, out_pair, qkv_mine, qkv_other],
         [],
         both_cores=True,

time: 642 us -> 634 us (0.988)
    unnamed x100 -> x84, local copies, waits for them, and re-layouts: 32 us -> 25.7 us
  transfers between devices with their start and end apart: 17 -> 17, of which waited for: 5 -> 5; matrix products, arithmetic and copies ran while one was open for 23% -> 24% of each run, Pallas kernels for 55% -> 56%
where the time goes in v8:
time: 634 us; the launch traced here: 631 us
  Pallas kernels  352 us (56%)
  matrix products  96.8 us (15%)
  local copies, waits for them, and re-layouts  45.1 us (7%)
  waiting for transfers between devices  42.3 us (7%)
  other arithmetic  40.7 us (6%)
  blocking collectives  34 us (5%)
  between operations  17 us (3%)
    pallas_call x3, Pallas kernels, mp_phase(): pl.pallas_call(kernel, in_specs=[here, *specs] + [there] * len(dummies),...  257 us
    pallas_call x1, Pallas kernels, scattered_and_pairs(): pl.pallas_call(pair_kernel, in_specs=[here] * 7 + [there] * len(dummies),...  49.3 us
    all_gather x1, blocking collectives, joined_shards(): lax.all_gather(weight, ('seq', 'row'), axis=1, tiled=True)  34 us
    all_gather x3, waiting for transfers between devices, joined_shards(): lax.all_gather(weight, ('seq', 'row'), axis=1, tiled=True)  33.8 us
    pallas_call x1, Pallas kernels, backward(): pl.pallas_call(functools.partial(bwd_kernel, heads, group), grid=(steps,)...  26.2 us
    unnamed x84, local copies, waits for them, and re-layouts  25.7 us
    pallas_call x1, Pallas kernels, forward(): pl.pallas_call(functools.partial(fwd_kernel, heads, group), grid=(n // ro...  19.5 us
    dot_general x1, matrix products, joined_shards(): jnp.einsum('stf,sdf->td', jnp.stack([grad_gate, grad_up]), gateup_full, p...  17.4 us
  transfers between devices with their start and end apart: 17, of which 5 were waited for; matrix products, arithmetic and copies ran while one was open for 24% of the time, Pallas kernels for 56%

profile of v8, /device:TPU:0, one launch (start us, length us, event | category | flops | bytes accessed | tf_op | source)
XLA Modules:
  0.0 630.7 jit_solution(4688801841633445863)
XLA Ops:
  7.2 1.4 copy.40
  8.7 2.0 pad_maximum_fusion.4
  10.8 0.7 all-gather.8.cloned.1.call-update
  11.5 3.2 fusion
  15.0 3.0 fusion.2
  19.7 0.7 pad_add_fusion
  20.8 34.0 %all_gather.13 = bf16[4,2048]{1,0:T(4,128)(2,1)S(1)} all-gather(bf16[4,256]{1,0:T(4,128)(2,1)S(1)} %copy-done.39), channel_id=1, replica_groups=mesh['seq'=2,'mp'=4,'row'=4] {'seq','row'}, dimensions={1}, use_global_device_ids=true | all-gather | bytes 18432 | tf_op jit(solution)/shard_map/all_gather | solution.py:1123
  54.9 7.8 %broadcast_select_fusion.1 = (bf16[1024,2048]{1,0:T(8,128)(2,1)}, bf16[1024,2048]{1,0:T(8,128)(2,1)}) fusion(bf16[1024,2048]{1,0:T(8,128)(2,1)} %collective-permute-done, pred[]{:T(512)S(6)} %eq.25, f32[2048]{0:T(1024)S(1)} %copy-done.24, f32[1024]{0:T(1024)S(1)} %add_rsqrt_fusion, bf16[1,1024,2048]{2,1,0:T(8,128)(2,1)} %param.12), kind=kLoop, calls=%fused_computation.45 | loop fusion | flops 12582912 | bytes 16789504 | tf_op jit(solution)/shard_map/jit(_where)/select_n | solution.py:1070
  62.7 33.8 %all-gather.4.cloned.1.call-done = bf16[4,2048,512]{1,2,0:T(8,128)(2,1)} async-done(((bf16[4,256,512]{1,2,0:T(8,128)(2,1)}), bf16[4,2048,512]{1,2,0:T(8,128)(2,1)}) %all-gather.4.cloned.1.call-update) | async-done | bytes 8388624 | tf_op jit(solution)/shard_map/all_gather | solution.py:1123
  96.4 2.8 slice-done
  99.2 1.2 dynamic-slice_bitcast_fusion.3
  100.4 13.2 %fusion.36.raw_ref.prev_ref = bf16[2048,896]{1,0:T(8,128)(2,1)S(1)} fusion(bf16[128,2048]{1,0:T(8,128)(2,1)S(1)} %pad.12.refs_4_, bf16[256,2048]{1,0:T(8,128)(2,1)} %get-tuple-element.103, bf16[256,2048]{1,0:T(8,128)(2,1)S(1)} %get-tuple-element.102, bf16[256,2048]{1,0:T(8,128)(2,1)S(1)} %get-tuple-element.101, bf16[1024,2048]{1,0:T(8,128)(2,1)} %get-tuple-element.100, ...), kind=kOutput, calls=%fused_computation.54 | convolution fusion | flops 7549485056 | bytes 15728640 | tf_op jit(solution)/shard_map/dot_general | solution.py:1148
  113.6 19.5 %shard_map.203 = (bf16[2048,256]{1,0:T(8,128)(2,1)S(1)}, f32[2048,256]{1,0:T(8,128)S(1)}, bf16[16,2,2,128,128]{4,3,2,1,0:T(8,128)(2,1)S(1)}, bf16[2048,512]{1,0:T(8,128)(2,1)S(1)}) custom-call(f32[33]{0:T(128)S(1)} %pad_convert_fusion.keep_ref, s32[32]{0:T(128)S(1)} %convert_element_type.94.count_ref, bf16[2048,896]{1,0:T(8,128)(2,1)S(1)} %fusion.36.raw_ref.prev_ref, ...), custom_call_target="tpu_custom_call" | custom-call | bytes 125829120 | tf_op jit(solution)/shard_map/pallas_call | solution.py:117
  133.1 1.8 copy-done.2
  134.9 1.3 copy-done.14
  136.2 1.3 copy-done.16
  137.5 1.3 copy-done.18
  139.1 1.3 constant_dynamic-slice_fusion.5
  140.9 1.3 broadcast_select_fusion.5
  142.2 6.4 %convolution_convert_fusion.part_ref = bf16[1024,2048]{1,0:T(8,128)(2,1)} fusion(bf16[4,2048,512]{1,2,0:T(8,128)(2,1)} %all-gather.4.cloned.1.call-done, bf16[1024,256]{1,0:T(8,128)(2,1)S(1)} %get-tuple-element.109, bf16[1024,256]{1,0:T(8,128)(2,1)S(1)} %get-tuple-element.108), kind=kOutput, calls=%fused_computation.46 | convolution fusion | flops 2151677952 | bytes 7340032 | tf_op jit(solution)/shard_map/dot_general | solution.py:1157
  148.6 79.2 %shard_map.204 = (bf16[1024,2048]{1,0:T(8,128)(2,1)}, f32[2,128,2048]{2,1,0:T(8,128)S(1)}) custom-call(bf16[1024,2048]{1,0:T(8,128)(2,1)} %convolution_convert_fusion.part_ref, bf16[2,128,2048]{2,1,0:T(8,128)(2,1)S(1)} %bitcast.160, f32[1,2048]{1,0:T(1,128)S(1)} %bitcast.168), custom_call_target="tpu_custom_call" | custom-call | bytes 262144000 | tf_op jit(solution)/shard_map/pallas_call | solution.py:916
  227.8 5.4 constant_dynamic-slice_fusion.2
  233.2 17.3 %convolution_bitcast_fusion = f32[2,1024,1408]{2,1,0:T(8,128)S(1)} fusion(bf16[2,2048,1408]{2,1,0:T(8,128)(2,1)} %all-gather.8.cloned.1.call-done, bf16[1024,2048]{1,0:T(8,128)(2,1)} %get-tuple-element.32), kind=kOutput, calls=%fused_computation.12 | convolution fusion | flops 11811160064 | bytes 27262976 | tf_op jit(solution)/shard_map/td,sdf->stf/dot_general | solution.py:1175
  250.5 2.1 fusion.8.product_ref
  253.2 2.8 copy-done.35
  257.9 5.9 fusion.39
  263.8 6.4 %add_convert_fusion.refs_0_ = bf16[1408,1024]{1,0:T(8,128)(2,1)} fusion(f32[1408,1024]{1,0:T(8,128)} %fusion.39, f32[]{:T(128)} %bitcast.32, bf16[1024,1408]{1,0:T(8,128)(2,1)S(1)} %collective-permute-done.2, bf16[1024,1024]{1,0:T(8,128)(2,1)S(1)} %collective-permute-done.3), kind=kOutput, calls=%fused_computation.33 | convolution fusion | flops 2957115392 | bytes 13631492 | tf_op jit(solution)/shard_map/dot_general | solution.py:1087
  270.3 1.2 slice.101
  272.2 16.6 %fusion.11 = (bf16[1024,1408]{1,0:T(8,128)(2,1)}, bf16[1024,1408]{1,0:T(8,128)(2,1)}) fusion(f32[2,1024,1408]{2,1,0:T(8,128)} %copy-done.29, f32[]{:T(128)} %bitcast.33, bf16[1408,2048]{1,0:T(8,128)(2,1)} %all-gather.6.cloned.1.call-done.weight, bf16[1,1024,2048]{2,1,0:T(8,128)(2,1)} %param.23), kind=kOutput, calls=%fused_computation.22 | convolution fusion | flops 5925765120 | bytes 27262980 | tf_op jit(solution)/shard_map/dot_general | solution.py:1182
  288.8 49.3 %shard_map.205 = (bf16[256,2048]{1,0:T(8,128)(2,1)}, bf16[1024,1408]{1,0:T(8,128)(2,1)}, bf16[1024,1408]{1,0:T(8,128)(2,1)}) custom-call(bf16[1024,1408]{1,0:T(8,128)(2,1)} %copy-done.30, bf16[1408,2048]{1,0:T(8,128)(2,1)} %all-gather.6.cloned.1.call-done.weight, f32[2,128,2048]{2,1,0:T(8,128)} %copy-done.6, bf16[1024,1024]{1,0:T(8,128)(2,1)} %get-tuple-element.104.left_own, ...), custom_call_target="tpu_custom_call" | custom-call | bytes 136314880 | tf_op jit(solution)/shard_map/pallas_call | solution.py:1044
  338.8 1.5 constant_dynamic-slice_fusion.3
  340.3 1.3 pad_maximum_fusion.5.refs_4_
  341.6 17.4 %bitcast_convert_fusion.part_ref = bf16[1024,2048]{1,0:T(8,128)(2,1)} fusion(bf16[2,2048,1408]{2,1,0:T(8,128)(2,1)} %all-gather.8.cloned.1.call-done, bf16[1,1024,1408]{2,1,0:T(8,128)(2,1)} %bitcast.176, bf16[1,1024,1408]{2,1,0:T(8,128)(2,1)S(1)} %bitcast.175), kind=kOutput, calls=%fused_computation.11 | convolution fusion | flops 11816140800 | bytes 21495808 | tf_op jit(solution)/shard_map/stf,sdf->td/dot_general | solution.py:1187
  359.0 1.1 copy-done.9
  360.1 80.5 %shard_map.206 = (bf16[1024,2048]{1,0:T(8,128)(2,1)}, f32[2,128,2048]{2,1,0:T(8,128)}, f32[1,2048]{1,0:T(1,128)S(1)}, bf16[1024,512]{1,0:T(8,128)(2,1)S(1)}, bf16[512,2048]{1,0:T(8,128)(2,1)}) custom-call(bf16[1024,2048]{1,0:T(8,128)(2,1)} %bitcast_convert_fusion.part_ref, f32[2,128,2048]{2,1,0:T(8,128)} %copy-done.6, bf16[2,128,2048]{2,1,0:T(8,128)(2,1)S(1)} %bitcast.162, ...), custom_call_target="tpu_custom_call" | custom-call | bytes 262144000 | tf_op jit(solution)/shard_map/pallas_call | solution.py:916
  440.6 1.0 copy-done.22
  441.6 1.4 constant_dynamic-slice_fusion
  443.1 1.1 slice.102
  444.9 0.9 collective-permute-done.6
  445.9 3.0 add_convert_fusion.1.refs_10_
  449.2 1.8 collective-permute-done.5
  451.4 2.0 copy-done.3
  453.4 1.1 copy-done.12
  454.5 1.6 copy-done.15
  456.1 1.6 copy-done.17
  457.7 1.8 copy-done.19
  459.5 26.2 %shard_map.207 = (bf16[2048,896]{1,0:T(8,128)(2,1)S(1)}, f32[4,768]{1,0:T(4,128)S(1)}, f32[1,128]{1,0:T(1,128)S(1)}, bf16[1024,2048]{1,0:T(8,128)(2,1)S(1)}) custom-call(f32[33]{0:T(128)S(1)} %pad_convert_fusion.keep_ref, s32[32]{0:T(128)S(1)} %convert_element_type.94.count_ref, bf16[2048,896]{1,0:T(8,128)(2,1)S(1)} %copy-done.3, ...), custom_call_target="tpu_custom_call" | custom-call | bytes 125829120 | tf_op jit(solution)/shard_map/pallas_call | solution.py:253
  485.7 2.0 copy-done.4
  487.7 1.8 copy-done.8
  489.5 5.7 fusion.46.refs_11_
  495.3 7.9 %fusion.43 = bf16[1024,896]{1,0:T(8,128)(2,1)S(1)} fusion(bf16[2048,896]{1,0:T(8,128)(2,1)} %copy-done.8, s32[]{:T(128)S(6)} %select_n.144, bf16[1024,2048]{1,0:T(8,128)(2,1)} %get-tuple-element.99, bf16[1024,2048]{1,0:T(8,128)(2,1)} %get-tuple-element.100), kind=kOutput, calls=%fused_computation.62 | convolution fusion | flops 3767402496 | bytes 13893636 | tf_op jit(solution)/shard_map/dot_general | solution.py:1235
  503.4 3.9 collective-permute-done.7.refs_12_
  507.4 1.2 convert_element_type.119
  508.6 1.8 maximum_convert_fusion
  510.4 97.6 %shard_map.208 = (bf16[1024,2048]{1,0:T(8,128)(2,1)}, bf16[256,2048]{1,0:T(8,128)(2,1)S(1)}, f32[16,2048]{1,0:T(8,128)S(1)}) custom-call(bf16[2048,896]{1,0:T(8,128)(2,1)} %copy-done.8, bf16[2,128,2048]{2,1,0:T(8,128)(2,1)S(1)} %bitcast.161, f32[2,128,2048]{2,1,0:T(8,128)} %get-tuple-element.42.refs_1_, f32[1,2048]{1,0:T(1,128)S(1)} %bitcast.167, ...), custom_call_target="tpu_custom_call" | custom-call | bytes 262144000 | tf_op jit(solution)/shard_map/pallas_call | solution.py:916
  608.1 2.6 bitcast_select_fusion
  610.7 0.6 pad_maximum_fusion.7
  611.8 0.6 fusion.60
  612.4 4.5 bitcast_convert_fusion.1
  616.9 1.8 convert_element_type.117
  618.7 0.9 select_bitcast_fusion.1
  619.8 1.2 broadcast_select_fusion.7
  621.5 1.6 copy.45
  623.1 0.6 maximum_convert_fusion.2
  (143 shorter events, 8.0 us)
Async XLA Ops:
  7.2 47.7 %copy-start = (f32[3,4,512]{2,1,0:T(4,128)S(1)}, f32[3,4,512]{2,1,0:T(4,128)}, u32[]{:S(2)}) copy-start(f32[3,4,512]{2,1,0:T(4,128)} %param.16) | copy-start | bytes 73732
  7.2 89.2 %all-gather.4.cloned.1.call-start = ((), (), s32[]{:S(2)}) async-start(), calls=%async_computation.6 | async-start | bytes 9437184 | tf_op jit(solution)/shard_map/all_gather | solution.py:1123
  8.6 6.1 copy-start.24
  10.7 222.5 %all-gather.8.cloned.1.call-start = ((), (), s32[]{:S(2)}) async-start(), calls=%async_computation.8 | async-start | bytes 12976128 | tf_op jit(solution)/shard_map/all_gather | solution.py:1123
  11.5 260.7 %all-gather.6.cloned.1.call-start = ((), (), s32[]{:S(2)}) async-start(), calls=%async_computation.7 | async-start | bytes 6488064 | tf_op jit(solution)/shard_map/all_gather | solution.py:1123
  11.5 3.5 copy-start.28
  15.0 3.6 copy-start.40
  15.0 5.8 copy-start.39
  18.0 36.9 %collective-permute-start = (bf16[1024,2048]{1,0:T(8,128)(2,1)}, bf16[1024,2048]{1,0:T(8,128)(2,1)}, u32[]{:S(2)}, u32[]{:S(2)}) collective-permute-start(bf16[1024,2048]{1,0:T(8,128)(2,1)} %fusion.2), channel_id=1, source_target_pairs={{0,16},{16,0},{1,17},{17,1},{2,18},{18,2},{3,19},{19,3},{4,20},{20... | collective-permute-start | bytes 12582920 | tf_op jit(solution)/shard_map/ppermute | solution.py:1066
  18.5 340.6 %reduce-scatter.7.cloned.1.call-start = ((), (), s32[]{:S(2)}) async-start(), calls=%async_computation.9 | async-start | bytes 3604480 | tf_op jit(solution)/shard_map/reduce_scatter | solution.py:1100
  54.8 45.6 %copy-start.20 = (bf16[128,2048]{1,0:T(8,128)(2,1)}, bf16[128,2048]{1,0:T(8,128)(2,1)S(1)}, u32[]{:S(2)}) copy-start(bf16[128,2048]{1,0:T(8,128)(2,1)S(1)} %pad.12.refs_4_) | copy-start | bytes 1572868
  96.4 2.8 slice-start
  100.4 13.2 %copy-start.27 = (f32[128]{0:T(128)S(1)}, f32[128]{0:T(128)}, u32[]{:S(2)}) copy-start(f32[128]{0:T(128)} %param.18) | copy-start | bytes 1540
  133.1 1.8 copy-start.2
  134.9 1.3 copy-start.14
  136.2 1.3 copy-start.16
  137.5 1.3 copy-start.18
  138.8 2.1 collective-permute-start.1
  142.2 6.4 %copy-start.37 = (bf16[1024,256]{1,0:T(8,128)(2,1)}, bf16[1024,256]{1,0:T(8,128)(2,1)S(1)}, u32[]{:S(2)}) copy-start(bf16[1024,256]{1,0:T(8,128)(2,1)S(1)} %get-tuple-element.108) | copy-start | bytes 1572868
  142.2 6.4 %copy-start.38 = (bf16[1024,256]{1,0:T(8,128)(2,1)}, bf16[1024,256]{1,0:T(8,128)(2,1)S(1)}, u32[]{:S(2)}) copy-start(bf16[1024,256]{1,0:T(8,128)(2,1)S(1)} %get-tuple-element.109) | copy-start | bytes 1572868
  142.2 6.4 %copy-start.26 = (f32[2048]{0:T(1024)S(1)}, f32[2048]{0:T(1024)}, u32[]{:S(2)}) copy-start(f32[2048]{0:T(1024)} %param.20) | copy-start | bytes 24580
  227.8 5.4 copy-start.6
  233.2 23.5 %collective-permute-start.4 = (bf16[1024,1024]{1,0:T(8,128)(2,1)}, bf16[1024,1024]{1,0:T(8,128)(2,1)S(1)}, u32[]{:S(2)}, u32[]{:S(2)}) collective-permute-start(bf16[1024,1024]{1,0:T(8,128)(2,1)} %get-tuple-element.105), channel_id=1, source_target_pairs={{0,16},{16,0},{1,17},{17,1},{2,18},{18,2},{3,19},{19,3},{4,20},{20... | collective-permute-start | bytes 6291464 | tf_op jit(solution)/shard_map/ppermute | solution.py:1066
  250.5 7.4 %copy-start.29 = (f32[2,1024,1408]{2,1,0:T(8,128)}, f32[2,1024,1408]{2,1,0:T(8,128)S(1)}, u32[]{:S(2)}) copy-start(f32[2,1024,1408]{2,1,0:T(8,128)S(1)} %convolution_bitcast_fusion) | copy-start | bytes 34603012
  250.5 5.4 copy-start.35
  252.7 11.1 %copy-start.30 = (bf16[1024,1408]{1,0:T(8,128)(2,1)}, bf16[1024,1408]{1,0:T(8,128)(2,1)S(1)}, u32[]{:S(2)}) copy-start(bf16[1024,1408]{1,0:T(8,128)(2,1)S(1)} %fusion.8.product_ref) | copy-start | bytes 8650756
  252.7 11.1 %collective-permute-start.2 = (bf16[1024,1408]{1,0:T(8,128)(2,1)S(1)}, bf16[1024,1408]{1,0:T(8,128)(2,1)S(1)}, u32[]{:S(2)}, u32[]{:S(2)}) collective-permute-start(bf16[1024,1408]{1,0:T(8,128)(2,1)S(1)} %fusion.8.product_ref), channel_id=1, source_target_pairs={{0,16},{16,0},{1,17},{17,1},{2,18},{18,2},{3,19},{19,3},{4,20},{20... | collective-permute-start | bytes 8650760 | tf_op jit(solution)/shard_map/ppermute | solution.py:1066
  256.2 7.6 %collective-permute-start.3 = (bf16[1024,1024]{1,0:T(8,128)(2,1)S(1)}, bf16[1024,1024]{1,0:T(8,128)(2,1)S(1)}, u32[]{:S(2)}, u32[]{:S(2)}) collective-permute-start(bf16[1024,1024]{1,0:T(8,128)(2,1)S(1)} %dynamic-slice_bitcast_fusion), channel_id=1, source_target_pairs={{0,16},{16,0},{1,17},{17,1},{2,18},{18,2},{3,19},{19,3},{4,20},{20... | collective-permute-start | bytes 6291464 | tf_op jit(solution)/shard_map/ppermute | solution.py:1066
  256.7 7.1 %copy-start.36 = (bf16[1024,1024]{1,0:T(8,128)(2,1)}, bf16[1024,1024]{1,0:T(8,128)(2,1)S(1)}, u32[]{:S(2)}) copy-start(bf16[1024,1024]{1,0:T(8,128)(2,1)S(1)} %collective-permute-done.4.left_other) | copy-start | bytes 6291460
  270.2 172.9 %reduce-scatter.11.cloned.1.call-start = ((), (), s32[]{:S(2)}) async-start(), calls=%async_computation.11 | async-start | bytes 3604480 | tf_op jit(solution)/shard_map/reduce_scatter | solution.py:1100
  338.2 113.2 %reduce-scatter.9.cloned.1.call-start = ((), (), s32[]{:S(2)}) async-start(), calls=%async_computation.10 | async-start | bytes 3604480 | tf_op jit(solution)/shard_map/reduce_scatter | solution.py:1100
  338.8 278.1 %reduce-scatter.17.cloned.1.call-start = ((), (), s32[]{:S(2)}) async-start(), calls=%async_computation.14 | async-start | bytes 1310720 | tf_op jit(solution)/shard_map/reduce_scatter | solution.py:1100
  338.8 2.8 copy-start.34
  359.0 1.1 copy-start.9
  440.6 1.0 copy-start.22
  441.6 7.4 %copy-start.23 = (bf16[1024,512]{1,0:T(8,128)(2,1)S(1)}, bf16[1024,512]{1,0:T(8,128)(2,1)}, u32[]{:S(2)}) copy-start(bf16[1024,512]{1,0:T(8,128)(2,1)} %copy-done.22) | copy-start | bytes 3145732
  443.0 2.9 collective-permute-start.6
  445.9 5.5 copy-start.7
  448.9 169.8 %reduce-scatter.13.cloned.1.call-start = ((), (), s32[]{:S(2)}) async-start(), calls=%async_computation.12 | async-start | bytes 2293760 | tf_op jit(solution)/shard_map/reduce_scatter | solution.py:1100
  449.0 2.0 collective-permute-start.5
  451.4 2.0 copy-start.3
  453.4 1.1 copy-start.12
  454.5 1.6 copy-start.15
  456.1 1.6 copy-start.17
  457.7 1.8 copy-start.19
  459.5 30.0 %copy-start.31 = (bf16[1024,2048]{1,0:T(8,128)(2,1)S(1)}, bf16[1024,2048]{1,0:T(8,128)(2,1)}, u32[]{:S(2)}) copy-start(bf16[1024,2048]{1,0:T(8,128)(2,1)} %get-tuple-element.99) | copy-start | bytes 12582916
  459.5 30.0 %copy-start.32 = (bf16[1024,2048]{1,0:T(8,128)(2,1)S(1)}, bf16[1024,2048]{1,0:T(8,128)(2,1)}, u32[]{:S(2)}) copy-start(bf16[1024,2048]{1,0:T(8,128)(2,1)} %get-tuple-element.100) | copy-start | bytes 12582916
  485.7 2.0 copy-start.4
  487.7 1.8 copy-start.8
  495.3 12.2 %copy-start.10 = (bf16[1408,256]{1,0:T(8,128)(2,1)S(1)}, bf16[1408,256]{1,0:T(8,128)(2,1)}, u32[]{:S(2)}) copy-start(bf16[1408,256]{1,0:T(8,128)(2,1)} %reduce-scatter.7.cloned.1.call-done.refs_6_) | copy-start | bytes 2162692
  495.3 123.4 %reduce-scatter.15.cloned.1.call-start = ((), (), s32[]{:S(2)}) async-start(), calls=%async_computation.13 | async-start | bytes 2293760 | tf_op jit(solution)/shard_map/reduce_scatter | solution.py:1100
  503.3 5.4 copy-start.11
  503.3 5.4 copy-start.13
  503.3 7.1 %copy-start.25 = (f32[2048]{0:T(1024)S(1)}, f32[2048]{0:T(1024)}, u32[]{:S(2)}) copy-start(f32[2048]{0:T(1024)} %param.14) | copy-start | bytes 24580
  503.3 4.0 collective-permute-start.7
  507.4 3.0 copy-start.21
  510.4 97.6 %copy-start.5 = (bf16[1024,2048]{1,0:T(8,128)(2,1)S(1)}, bf16[1024,2048]{1,0:T(8,128)(2,1)}, u32[]{:S(2)}) copy-start(bf16[1024,2048]{1,0:T(8,128)(2,1)} %copy-done.4) | copy-start | bytes 12582916
  608.1 4.4 copy-start.33
  619.7 4.0 copy-start.1
Sparse Core Ops, SparseCore 0:
  10.8 85.5 all-gather.3
  98.0 106.2 all-gather.7
  205.9 59.1 all-gather.5
  270.4 53.4 reduce-scatter.6
  338.3 53.3 reduce-scatter.10
  393.9 56.0 reduce-scatter.8
  452.8 26.9 reduce-scatter.16
  495.4 37.4 reduce-scatter.12
  535.3 38.5 reduce-scatter.14

commit v9 on v8

--- a/solution.py
+++ b/solution.py
@@ -756,6 +756,12 @@
         out_second[half].start()
 
     def use(of, first=False, last=False):
+        if middle is normed_forward:
+            lines = pl.ds(pl.multiple_of(2 * of * rows, rows), 2 * rows)
+            half = all_ref.shape[1] // 2
+            for target, whose in ((outs[1], core), (outs[2], 1 - core)):
+                columns = pl.ds(pl.multiple_of(whose * half, half), half)
+                target[lines, :] = all_ref[lines, columns]
         if not meanwhile:
             return
         weight, left = scratch[-3], inputs[4]
@@ -797,7 +803,7 @@
             share = jnp.where(core == i, 1.0, 0.0)
             lane = i * middle_lane
             values[8 : 8 + taps, lane : lane + width] = conv[...] * share
-    elif n_out > 2:
+    elif middle is not normed_forward:
         outs[1][...] = gain
 
     def small_step(number):
@@ -1162,20 +1168,20 @@
     ).reshape(2, -1, model)
     residual_own = own_rows(block_in)
     rows_own = jax.ShapeDtypeStruct(residual_own.shape, F32)
-    normed_mid, hidden = mp_phase(
+    normed_mid, hidden, normed_mine, normed_other = mp_phase(
         0,
         normed_forward,
         branch_part.astype(BF16),
         [residual_own, ffn_gain[None, :]],
         [],
-        [rows_own],
+        [rows_own] + [jax.ShapeDtypeStruct((tok_count, model // 2), BF16)] * 2,
     )
 
     grad_top = cotangent[0]
     gate_up = jnp.einsum("td,sdf->stf", normed_mid, gateup_full, preferred_element_type=F32)
     gate_sig = jax.nn.sigmoid(gate_up[0])
     product = (gate_up[0] * gate_sig * gate_up[1]).astype(BF16)
-    normed_halves = own_columns(normed_mid, core)
+    normed_halves = normed_mine, swapped(normed_other)
     down_pair = both_tokens(
         (product, swapped(product)), own_columns(grad_top, core), normed_halves[1]
     )

time: 634 us -> 631 us (level)
  transfers between devices with their start and end apart: 17 -> 17, of which waited for: 5 -> 5; matrix products, arithmetic and copies ran while one was open for 24% -> 23% of each run, Pallas kernels for 56% -> 56%
where the time goes in v9:
time: 631 us; the launch traced here: 627 us
  Pallas kernels  353 us (56%)
  matrix products  96.9 us (15%)
  waiting for transfers between devices  42.3 us (7%)
  local copies, waits for them, and re-layouts  40.9 us (6%)
  other arithmetic  40.7 us (6%)
  blocking collectives  34 us (5%)
  between operations  16.9 us (3%)
    pallas_call x3, Pallas kernels, mp_phase(): pl.pallas_call(kernel, in_specs=[here, *specs] + [there] * len(dummies),...  258 us
    pallas_call x1, Pallas kernels, scattered_and_pairs(): pl.pallas_call(pair_kernel, in_specs=[here] * 7 + [there] * len(dummies),...  49.2 us
    all_gather x1, blocking collectives, joined_shards(): lax.all_gather(weight, ('seq', 'row'), axis=1, tiled=True)  34 us
    all_gather x3, waiting for transfers between devices, joined_shards(): lax.all_gather(weight, ('seq', 'row'), axis=1, tiled=True)  33.8 us
    unnamed x84, local copies, waits for them, and re-layouts  26.8 us
    pallas_call x1, Pallas kernels, backward(): pl.pallas_call(functools.partial(bwd_kernel, heads, group), grid=(steps,)...  26.3 us
    pallas_call x1, Pallas kernels, forward(): pl.pallas_call(functools.partial(fwd_kernel, heads, group), grid=(n // ro...  19.5 us
    dot_general x1, matrix products, joined_shards(): jnp.einsum('stf,sdf->td', jnp.stack([grad_gate, grad_up]), gateup_full, p...  17.4 us
  transfers between devices with their start and end apart: 17, of which 5 were waited for; matrix products, arithmetic and copies ran while one was open for 23% of the time, Pallas kernels for 56%

profile of v9, /device:TPU:0, one launch (start us, length us, event | category | flops | bytes accessed | tf_op | source)
XLA Modules:
  0.0 627.1 jit_solution(12109469518114260893)
XLA Ops:
  7.2 1.4 copy.40
  8.7 2.0 pad_maximum_fusion.4
  10.8 0.7 all-gather.8.cloned.1.call-update
  11.5 3.2 fusion
  15.0 3.0 fusion.2
  19.7 0.7 pad_add_fusion
  20.8 34.0 %all_gather.13 = bf16[4,2048]{1,0:T(4,128)(2,1)S(1)} all-gather(bf16[4,256]{1,0:T(4,128)(2,1)S(1)} %copy-done.39), channel_id=1, replica_groups=mesh['seq'=2,'mp'=4,'row'=4] {'seq','row'}, dimensions={1}, use_global_device_ids=true | all-gather | bytes 18432 | tf_op jit(solution)/shard_map/all_gather | solution.py:1129
  54.9 7.8 %broadcast_select_fusion.1 = (bf16[1024,2048]{1,0:T(8,128)(2,1)}, bf16[1024,2048]{1,0:T(8,128)(2,1)}) fusion(bf16[1024,2048]{1,0:T(8,128)(2,1)} %collective-permute-done, pred[]{:T(512)S(6)} %eq.25, f32[2048]{0:T(1024)S(1)} %copy-done.24, f32[1024]{0:T(1024)S(1)} %add_rsqrt_fusion, bf16[1,1024,2048]{2,1,0:T(8,128)(2,1)} %param.12), kind=kLoop, calls=%fused_computation.45 | loop fusion | flops 12582912 | bytes 16789504 | tf_op jit(solution)/shard_map/jit(_where)/select_n | solution.py:1076
  62.7 33.8 %all-gather.4.cloned.1.call-done = bf16[4,2048,512]{1,2,0:T(8,128)(2,1)} async-done(((bf16[4,256,512]{1,2,0:T(8,128)(2,1)}), bf16[4,2048,512]{1,2,0:T(8,128)(2,1)}) %all-gather.4.cloned.1.call-update) | async-done | bytes 8388624 | tf_op jit(solution)/shard_map/all_gather | solution.py:1129
  96.4 2.8 slice-done
  99.2 1.2 dynamic-slice_bitcast_fusion.3
  100.4 13.2 %fusion.36.raw_ref.prev_ref = bf16[2048,896]{1,0:T(8,128)(2,1)S(1)} fusion(bf16[128,2048]{1,0:T(8,128)(2,1)S(1)} %pad.12.refs_4_, bf16[256,2048]{1,0:T(8,128)(2,1)} %get-tuple-element.107, bf16[256,2048]{1,0:T(8,128)(2,1)S(1)} %get-tuple-element.106, bf16[256,2048]{1,0:T(8,128)(2,1)S(1)} %get-tuple-element.105, bf16[1024,2048]{1,0:T(8,128)(2,1)} %get-tuple-element.104, ...), kind=kOutput, calls=%fused_computation.54 | convolution fusion | flops 7549485056 | bytes 15728640 | tf_op jit(solution)/shard_map/dot_general | solution.py:1154
  113.6 19.5 %shard_map.203 = (bf16[2048,256]{1,0:T(8,128)(2,1)S(1)}, f32[2048,256]{1,0:T(8,128)S(1)}, bf16[16,2,2,128,128]{4,3,2,1,0:T(8,128)(2,1)S(1)}, bf16[2048,512]{1,0:T(8,128)(2,1)S(1)}) custom-call(f32[33]{0:T(128)S(1)} %pad_convert_fusion.keep_ref, s32[32]{0:T(128)S(1)} %convert_element_type.94.count_ref, bf16[2048,896]{1,0:T(8,128)(2,1)S(1)} %fusion.36.raw_ref.prev_ref, ...), custom_call_target="tpu_custom_call" | custom-call | bytes 125829120 | tf_op jit(solution)/shard_map/pallas_call | solution.py:117
  133.1 1.8 copy-done.2
  134.9 1.3 copy-done.14
  136.2 1.3 copy-done.16
  137.5 1.3 copy-done.18
  139.1 1.3 constant_dynamic-slice_fusion.3
  140.9 1.3 broadcast_select_fusion.5
  142.2 6.4 %convolution_convert_fusion.part_ref = bf16[1024,2048]{1,0:T(8,128)(2,1)} fusion(bf16[4,2048,512]{1,2,0:T(8,128)(2,1)} %all-gather.4.cloned.1.call-done, bf16[1024,256]{1,0:T(8,128)(2,1)S(1)} %get-tuple-element.111, bf16[1024,256]{1,0:T(8,128)(2,1)S(1)} %get-tuple-element.110), kind=kOutput, calls=%fused_computation.46 | convolution fusion | flops 2151677952 | bytes 7340032 | tf_op jit(solution)/shard_map/dot_general | solution.py:1163
  148.6 80.7 %shard_map.204 = (bf16[1024,2048]{1,0:T(8,128)(2,1)}, f32[2,128,2048]{2,1,0:T(8,128)S(1)}, bf16[1024,1024]{1,0:T(8,128)(2,1)}, bf16[1024,1024]{1,0:T(8,128)(2,1)}) custom-call(bf16[1024,2048]{1,0:T(8,128)(2,1)} %convolution_convert_fusion.part_ref, bf16[2,128,2048]{2,1,0:T(8,128)(2,1)S(1)} %bitcast.160, f32[1,2048]{1,0:T(1,128)S(1)} %bitcast.168), custom_call_target="tpu_custom_call" | custom-call | bytes 262144000 | tf_op jit(solution)/shard_map/pallas_call | solution.py:922
  229.3 1.3 copy-done.6
  230.7 17.4 %convolution_bitcast_fusion = f32[2,1024,1408]{2,1,0:T(8,128)S(1)} fusion(bf16[2,2048,1408]{2,1,0:T(8,128)(2,1)} %all-gather.8.cloned.1.call-done, bf16[1024,2048]{1,0:T(8,128)(2,1)} %get-tuple-element.34), kind=kOutput, calls=%fused_computation.12 | convolution fusion | flops 11811160064 | bytes 27262976 | tf_op jit(solution)/shard_map/td,sdf->stf/dot_general | solution.py:1181
  248.1 2.1 fusion.8.product_ref
  250.8 2.6 copy-done.35
  255.5 5.9 fusion.39
  261.4 6.3 %add_convert_fusion.refs_0_ = bf16[1408,1024]{1,0:T(8,128)(2,1)} fusion(f32[1408,1024]{1,0:T(8,128)} %fusion.39, f32[]{:T(128)} %bitcast.32, bf16[1024,1408]{1,0:T(8,128)(2,1)S(1)} %collective-permute-done.2, bf16[1024,1024]{1,0:T(8,128)(2,1)S(1)} %collective-permute-done.3), kind=kOutput, calls=%fused_computation.33 | convolution fusion | flops 2957115392 | bytes 13631492 | tf_op jit(solution)/shard_map/dot_general | solution.py:1093
  267.8 1.2 slice.101
  269.7 16.6 %fusion.11 = (bf16[1024,1408]{1,0:T(8,128)(2,1)}, bf16[1024,1408]{1,0:T(8,128)(2,1)}) fusion(f32[2,1024,1408]{2,1,0:T(8,128)} %copy-done.29, f32[]{:T(128)} %bitcast.33, bf16[1408,2048]{1,0:T(8,128)(2,1)} %all-gather.6.cloned.1.call-done.weight, bf16[1,1024,2048]{2,1,0:T(8,128)(2,1)} %param.23), kind=kOutput, calls=%fused_computation.22 | convolution fusion | flops 5925765120 | bytes 27262980 | tf_op jit(solution)/shard_map/dot_general | solution.py:1188
  286.3 49.2 %shard_map.205 = (bf16[256,2048]{1,0:T(8,128)(2,1)}, bf16[1024,1408]{1,0:T(8,128)(2,1)}, bf16[1024,1408]{1,0:T(8,128)(2,1)}) custom-call(bf16[1024,1408]{1,0:T(8,128)(2,1)} %copy-done.30, bf16[1408,2048]{1,0:T(8,128)(2,1)} %all-gather.6.cloned.1.call-done.weight, f32[2,128,2048]{2,1,0:T(8,128)} %copy-done.6, bf16[1024,1024]{1,0:T(8,128)(2,1)} %get-tuple-element.37.left_own, ...), custom_call_target="tpu_custom_call" | custom-call | bytes 136314880 | tf_op jit(solution)/shard_map/pallas_call | solution.py:1050
  336.2 1.5 constant_dynamic-slice_fusion.2
  337.6 1.3 pad_maximum_fusion.5.refs_4_
  339.0 17.4 %bitcast_convert_fusion.part_ref = bf16[1024,2048]{1,0:T(8,128)(2,1)} fusion(bf16[2,2048,1408]{2,1,0:T(8,128)(2,1)} %all-gather.8.cloned.1.call-done, bf16[1,1024,1408]{2,1,0:T(8,128)(2,1)} %bitcast.176, bf16[1,1024,1408]{2,1,0:T(8,128)(2,1)S(1)} %bitcast.175), kind=kOutput, calls=%fused_computation.11 | convolution fusion | flops 11816140800 | bytes 21495808 | tf_op jit(solution)/shard_map/stf,sdf->td/dot_general | solution.py:1193
  356.4 1.1 copy-done.9
  357.5 80.8 %shard_map.206 = (bf16[1024,2048]{1,0:T(8,128)(2,1)}, f32[2,128,2048]{2,1,0:T(8,128)}, f32[1,2048]{1,0:T(1,128)S(1)}, bf16[1024,512]{1,0:T(8,128)(2,1)S(1)}, bf16[512,2048]{1,0:T(8,128)(2,1)}) custom-call(bf16[1024,2048]{1,0:T(8,128)(2,1)} %bitcast_convert_fusion.part_ref, f32[2,128,2048]{2,1,0:T(8,128)} %copy-done.6, bf16[2,128,2048]{2,1,0:T(8,128)(2,1)S(1)} %bitcast.162, ...), custom_call_target="tpu_custom_call" | custom-call | bytes 262144000 | tf_op jit(solution)/shard_map/pallas_call | solution.py:922
  438.3 1.0 copy-done.22
  439.3 1.4 constant_dynamic-slice_fusion
  440.8 1.2 slice.102
  442.6 0.9 collective-permute-done.6
  443.5 3.0 add_convert_fusion.1.refs_10_
  446.9 1.8 collective-permute-done.5
  449.1 2.0 copy-done.3
  451.1 1.1 copy-done.12
  452.2 1.6 copy-done.15
  453.8 1.6 copy-done.17
  455.4 1.7 copy-done.19
  457.1 26.3 %shard_map.207 = (bf16[2048,896]{1,0:T(8,128)(2,1)S(1)}, f32[4,768]{1,0:T(4,128)S(1)}, f32[1,128]{1,0:T(1,128)S(1)}, bf16[1024,2048]{1,0:T(8,128)(2,1)S(1)}) custom-call(f32[33]{0:T(128)S(1)} %pad_convert_fusion.keep_ref, s32[32]{0:T(128)S(1)} %convert_element_type.94.count_ref, bf16[2048,896]{1,0:T(8,128)(2,1)S(1)} %copy-done.3, ...), custom_call_target="tpu_custom_call" | custom-call | bytes 125829120 | tf_op jit(solution)/shard_map/pallas_call | solution.py:253
  483.4 2.0 copy-done.4
  485.4 1.8 copy-done.8
  487.2 5.8 fusion.46.refs_11_
  493.0 7.9 %fusion.43 = bf16[1024,896]{1,0:T(8,128)(2,1)S(1)} fusion(bf16[2048,896]{1,0:T(8,128)(2,1)} %copy-done.8, s32[]{:T(128)S(6)} %select_n.142, bf16[1024,2048]{1,0:T(8,128)(2,1)} %get-tuple-element.103, bf16[1024,2048]{1,0:T(8,128)(2,1)} %get-tuple-element.104), kind=kOutput, calls=%fused_computation.62 | convolution fusion | flops 3767402496 | bytes 13893636 | tf_op jit(solution)/shard_map/dot_general | solution.py:1241
  501.1 3.9 collective-permute-done.7.refs_12_
  505.1 1.2 convert_element_type.119
  506.3 1.8 maximum_convert_fusion
  508.1 96.3 %shard_map.208 = (bf16[1024,2048]{1,0:T(8,128)(2,1)}, bf16[256,2048]{1,0:T(8,128)(2,1)S(1)}, f32[16,2048]{1,0:T(8,128)S(1)}) custom-call(bf16[2048,896]{1,0:T(8,128)(2,1)} %copy-done.8, bf16[2,128,2048]{2,1,0:T(8,128)(2,1)S(1)} %bitcast.161, f32[2,128,2048]{2,1,0:T(8,128)} %get-tuple-element.46.refs_1_, f32[1,2048]{1,0:T(1,128)S(1)} %bitcast.167, ...), custom_call_target="tpu_custom_call" | custom-call | bytes 262144000 | tf_op jit(solution)/shard_map/pallas_call | solution.py:922
  604.4 2.6 bitcast_select_fusion
  607.0 0.6 pad_maximum_fusion.7
  608.2 0.6 fusion.60
  608.8 4.5 bitcast_convert_fusion.1
  613.3 1.8 convert_element_type.117
  615.1 0.9 select_bitcast_fusion.1
  616.1 1.2 broadcast_select_fusion.7
  617.8 1.6 copy.45
  619.4 0.6 maximum_convert_fusion.2
  (142 shorter events, 8.2 us)
Async XLA Ops:
  7.2 47.7 %copy-start = (f32[3,4,512]{2,1,0:T(4,128)S(1)}, f32[3,4,512]{2,1,0:T(4,128)}, u32[]{:S(2)}) copy-start(f32[3,4,512]{2,1,0:T(4,128)} %param.16) | copy-start | bytes 73732
  7.2 89.2 %all-gather.4.cloned.1.call-start = ((), (), s32[]{:S(2)}) async-start(), calls=%async_computation.6 | async-start | bytes 9437184 | tf_op jit(solution)/shard_map/all_gather | solution.py:1129
  8.6 6.1 copy-start.24
  10.7 220.0 %all-gather.8.cloned.1.call-start = ((), (), s32[]{:S(2)}) async-start(), calls=%async_computation.8 | async-start | bytes 12976128 | tf_op jit(solution)/shard_map/all_gather | solution.py:1129
  11.5 258.2 %all-gather.6.cloned.1.call-start = ((), (), s32[]{:S(2)}) async-start(), calls=%async_computation.7 | async-start | bytes 6488064 | tf_op jit(solution)/shard_map/all_gather | solution.py:1129
  11.5 3.5 copy-start.28
  15.0 3.6 copy-start.40
  15.0 5.8 copy-start.39
  18.0 36.9 %collective-permute-start = (bf16[1024,2048]{1,0:T(8,128)(2,1)}, bf16[1024,2048]{1,0:T(8,128)(2,1)}, u32[]{:S(2)}, u32[]{:S(2)}) collective-permute-start(bf16[1024,2048]{1,0:T(8,128)(2,1)} %fusion.2), channel_id=1, source_target_pairs={{0,16},{16,0},{1,17},{17,1},{2,18},{18,2},{3,19},{19,3},{4,20},{20... | collective-permute-start | bytes 12582920 | tf_op jit(solution)/shard_map/ppermute | solution.py:1072
  18.5 337.9 %reduce-scatter.7.cloned.1.call-start = ((), (), s32[]{:S(2)}) async-start(), calls=%async_computation.9 | async-start | bytes 3604480 | tf_op jit(solution)/shard_map/reduce_scatter | solution.py:1106
  54.8 45.6 %copy-start.20 = (bf16[128,2048]{1,0:T(8,128)(2,1)}, bf16[128,2048]{1,0:T(8,128)(2,1)S(1)}, u32[]{:S(2)}) copy-start(bf16[128,2048]{1,0:T(8,128)(2,1)S(1)} %pad.12.refs_4_) | copy-start | bytes 1572868
  96.4 2.8 slice-start
  100.4 13.2 %copy-start.27 = (f32[128]{0:T(128)S(1)}, f32[128]{0:T(128)}, u32[]{:S(2)}) copy-start(f32[128]{0:T(128)} %param.18) | copy-start | bytes 1540
  133.1 1.8 copy-start.2
  134.9 1.3 copy-start.14
  136.2 1.3 copy-start.16
  137.5 1.3 copy-start.18
  138.8 2.1 collective-permute-start.1
  142.2 6.4 %copy-start.37 = (bf16[1024,256]{1,0:T(8,128)(2,1)}, bf16[1024,256]{1,0:T(8,128)(2,1)S(1)}, u32[]{:S(2)}) copy-start(bf16[1024,256]{1,0:T(8,128)(2,1)S(1)} %get-tuple-element.110) | copy-start | bytes 1572868
  142.2 6.4 %copy-start.38 = (bf16[1024,256]{1,0:T(8,128)(2,1)}, bf16[1024,256]{1,0:T(8,128)(2,1)S(1)}, u32[]{:S(2)}) copy-start(bf16[1024,256]{1,0:T(8,128)(2,1)S(1)} %get-tuple-element.111) | copy-start | bytes 1572868
  142.2 6.4 %copy-start.26 = (f32[2048]{0:T(1024)S(1)}, f32[2048]{0:T(1024)}, u32[]{:S(2)}) copy-start(f32[2048]{0:T(1024)} %param.20) | copy-start | bytes 24580
  229.3 1.3 copy-start.6
  230.6 23.6 %collective-permute-start.4 = (bf16[1024,1024]{1,0:T(8,128)(2,1)}, bf16[1024,1024]{1,0:T(8,128)(2,1)S(1)}, u32[]{:S(2)}, u32[]{:S(2)}) collective-permute-start(bf16[1024,1024]{1,0:T(8,128)(2,1)} %get-tuple-element.35), channel_id=1, source_target_pairs={{0,16},{16,0},{1,17},{17,1},{2,18},{18,2},{3,19},{19,3},{4,20},{20... | collective-permute-start | bytes 6291464 | tf_op jit(solution)/shard_map/ppermute | solution.py:1072
  248.0 7.5 %copy-start.29 = (f32[2,1024,1408]{2,1,0:T(8,128)}, f32[2,1024,1408]{2,1,0:T(8,128)S(1)}, u32[]{:S(2)}) copy-start(f32[2,1024,1408]{2,1,0:T(8,128)S(1)} %convolution_bitcast_fusion) | copy-start | bytes 34603012
  248.0 5.4 copy-start.35
  250.2 11.2 %copy-start.30 = (bf16[1024,1408]{1,0:T(8,128)(2,1)}, bf16[1024,1408]{1,0:T(8,128)(2,1)S(1)}, u32[]{:S(2)}) copy-start(bf16[1024,1408]{1,0:T(8,128)(2,1)S(1)} %fusion.8.product_ref) | copy-start | bytes 8650756
  250.2 11.2 %collective-permute-start.2 = (bf16[1024,1408]{1,0:T(8,128)(2,1)S(1)}, bf16[1024,1408]{1,0:T(8,128)(2,1)S(1)}, u32[]{:S(2)}, u32[]{:S(2)}) collective-permute-start(bf16[1024,1408]{1,0:T(8,128)(2,1)S(1)} %fusion.8.product_ref), channel_id=1, source_target_pairs={{0,16},{16,0},{1,17},{17,1},{2,18},{18,2},{3,19},{19,3},{4,20},{20... | collective-permute-start | bytes 8650760 | tf_op jit(solution)/shard_map/ppermute | solution.py:1072
  253.7 7.7 %collective-permute-start.3 = (bf16[1024,1024]{1,0:T(8,128)(2,1)S(1)}, bf16[1024,1024]{1,0:T(8,128)(2,1)S(1)}, u32[]{:S(2)}, u32[]{:S(2)}) collective-permute-start(bf16[1024,1024]{1,0:T(8,128)(2,1)S(1)} %dynamic-slice_bitcast_fusion), channel_id=1, source_target_pairs={{0,16},{16,0},{1,17},{17,1},{2,18},{18,2},{3,19},{19,3},{4,20},{20... | collective-permute-start | bytes 6291464 | tf_op jit(solution)/shard_map/ppermute | solution.py:1072
  254.3 7.1 %copy-start.36 = (bf16[1024,1024]{1,0:T(8,128)(2,1)}, bf16[1024,1024]{1,0:T(8,128)(2,1)S(1)}, u32[]{:S(2)}) copy-start(bf16[1024,1024]{1,0:T(8,128)(2,1)S(1)} %collective-permute-done.4.left_other) | copy-start | bytes 6291460
  267.8 173.0 %reduce-scatter.11.cloned.1.call-start = ((), (), s32[]{:S(2)}) async-start(), calls=%async_computation.11 | async-start | bytes 3604480 | tf_op jit(solution)/shard_map/reduce_scatter | solution.py:1106
  335.5 113.5 %reduce-scatter.9.cloned.1.call-start = ((), (), s32[]{:S(2)}) async-start(), calls=%async_computation.10 | async-start | bytes 3604480 | tf_op jit(solution)/shard_map/reduce_scatter | solution.py:1106
  336.1 277.2 %reduce-scatter.17.cloned.1.call-start = ((), (), s32[]{:S(2)}) async-start(), calls=%async_computation.14 | async-start | bytes 1310720 | tf_op jit(solution)/shard_map/reduce_scatter | solution.py:1106
  336.2 2.8 copy-start.34
  356.4 1.1 copy-start.9
  438.3 1.0 copy-start.22
  439.3 7.3 %copy-start.23 = (bf16[1024,512]{1,0:T(8,128)(2,1)S(1)}, bf16[1024,512]{1,0:T(8,128)(2,1)}, u32[]{:S(2)}) copy-start(bf16[1024,512]{1,0:T(8,128)(2,1)} %copy-done.22) | copy-start | bytes 3145732
  440.7 2.9 collective-permute-start.6
  443.5 5.5 copy-start.7
  446.6 168.5 %reduce-scatter.13.cloned.1.call-start = ((), (), s32[]{:S(2)}) async-start(), calls=%async_computation.12 | async-start | bytes 2293760 | tf_op jit(solution)/shard_map/reduce_scatter | solution.py:1106
  446.7 2.0 collective-permute-start.5
  449.0 2.0 copy-start.3
  451.1 1.1 copy-start.12
  452.2 1.6 copy-start.15
  453.8 1.6 copy-start.17
  455.4 1.7 copy-start.19
  457.1 30.1 %copy-start.31 = (bf16[1024,2048]{1,0:T(8,128)(2,1)S(1)}, bf16[1024,2048]{1,0:T(8,128)(2,1)}, u32[]{:S(2)}) copy-start(bf16[1024,2048]{1,0:T(8,128)(2,1)} %get-tuple-element.103) | copy-start | bytes 12582916
  457.1 30.1 %copy-start.32 = (bf16[1024,2048]{1,0:T(8,128)(2,1)S(1)}, bf16[1024,2048]{1,0:T(8,128)(2,1)}, u32[]{:S(2)}) copy-start(bf16[1024,2048]{1,0:T(8,128)(2,1)} %get-tuple-element.104) | copy-start | bytes 12582916
  483.4 2.0 copy-start.4
  485.4 1.8 copy-start.8
  493.0 12.2 %copy-start.10 = (bf16[1408,256]{1,0:T(8,128)(2,1)S(1)}, bf16[1408,256]{1,0:T(8,128)(2,1)}, u32[]{:S(2)}) copy-start(bf16[1408,256]{1,0:T(8,128)(2,1)} %reduce-scatter.7.cloned.1.call-done.refs_6_) | copy-start | bytes 2162692
  493.0 122.1 %reduce-scatter.15.cloned.1.call-start = ((), (), s32[]{:S(2)}) async-start(), calls=%async_computation.13 | async-start | bytes 2293760 | tf_op jit(solution)/shard_map/reduce_scatter | solution.py:1106
  501.0 5.4 copy-start.11
  501.0 5.4 copy-start.13
  501.0 7.1 %copy-start.25 = (f32[2048]{0:T(1024)S(1)}, f32[2048]{0:T(1024)}, u32[]{:S(2)}) copy-start(f32[2048]{0:T(1024)} %param.14) | copy-start | bytes 24580
  501.0 4.0 collective-permute-start.7
  505.1 3.0 copy-start.21
  508.1 96.3 %copy-start.5 = (bf16[1024,2048]{1,0:T(8,128)(2,1)S(1)}, bf16[1024,2048]{1,0:T(8,128)(2,1)}, u32[]{:S(2)}) copy-start(bf16[1024,2048]{1,0:T(8,128)(2,1)} %copy-done.4) | copy-start | bytes 12582916
  604.4 4.4 copy-start.33
  616.0 4.0 copy-start.1
Sparse Core Ops, SparseCore 0:
  10.8 85.5 all-gather.3
  98.0 106.2 all-gather.7
  205.9 59.1 all-gather.5
  267.9 54.2 reduce-scatter.6
  335.7 53.3 reduce-scatter.10
  391.3 56.0 reduce-scatter.8
  450.2 26.9 reduce-scatter.16
  493.1 37.1 reduce-scatter.12
  532.6 38.5 reduce-scatter.14
